TPU v7x, 32 devices: a whole 2x2x4 slice. The times are simulated.
32 devices in a mesh: batch: 8 (over z, x), head: 4 (over y, core).
Axes of the slice: x: 2, y: 2, z: 4, core: 2. Of those that a mesh axis runs over, the one named last changes fastest.
Arguments:
- patches: bfloat16 [8, 3136, 768], P('batch', 'head'), may hold values from -8 to 8
- bucket: int32 [8], P('batch'), may hold values from 0 to 1
- labels: int32 [8], P('batch'), may hold values from 0 to 399
- partner: int32 [8], P('batch'), may hold values from 0 to 7, as said below
- patch_weight: float32 [768, 768], P(('batch', 'head')), may hold values from -0.21875 to 0.21875
- norm_params: float32 [8, 768], P(None, ('batch', 'head')), may hold values from -2.5 to 2.5
- head_weight: float32 [768, 400], P(('batch', 'head')), may hold values from -0.4375 to 0.4375
- proj_weight: float32 [768, 256], P(('batch', 'head')), may hold values from -0.21875 to 0.21875
- attn_in: float32 [2, 768, 3, 768], P(None, 'batch', None, 'head'), may hold values from -0.21875 to 0.21875
- attn_out: float32 [2, 768, 768], P(None, 'head', 'batch'), may hold values from -0.875 to 0.875
- mlp_up: float32 [768, 3072], P('batch', 'head'), may hold values from -0.21875 to 0.21875
- mlp_down: float32 [3072, 768], P('head', 'batch'), may hold values from -0.109375 to 0.109375
- first_patch: float32 [768, 768], P(('batch', 'head')), may hold values from -0.001953125 to 0.001953125
- first_norms: float32 [8, 768], P(None, ('batch', 'head')), may hold values from -0.009765625 to 0.009765625
- first_head: float32 [768, 400], P(('batch', 'head')), may hold values from -0.001953125 to 0.001953125
- first_proj: float32 [768, 256], P(('batch', 'head')), may hold values from -0.001953125 to 0.001953125
- first_qkv: float32 [2, 768, 3, 768], P(None, 'batch', None, 'head'), may hold values from -0.001953125 to 0.001953125
- first_out: float32 [2, 768, 768], P(None, 'head', 'batch'), may hold values from -0.001953125 to 0.001953125
- first_up: float32 [768, 3072], P('batch', 'head'), may hold values from -0.00036621094 to 0.00036621094
- first_down: float32 [3072, 768], P('head', 'batch'), may hold values from -0.001953125 to 0.001953125
- second_patch: float32 [768, 768], P(('batch', 'head')), may hold values from 9.490403e-08 to 3.7961613e-07
- second_norms: float32 [8, 768], P(None, ('batch', 'head')), may hold values from 2.3726009e-06 to 9.4904035e-06
- second_head: float32 [768, 400], P(('batch', 'head')), may hold values from 9.490403e-08 to 3.7961613e-07
- second_proj: float32 [768, 256], P(('batch', 'head')), may hold values from 9.490403e-08 to 3.7961613e-07
- second_qkv: float32 [2, 768, 3, 768], P(None, 'batch', None, 'head'), may hold values from 9.490403e-08 to 3.7961613e-07
- second_out: float32 [2, 768, 768], P(None, 'head', 'batch'), may hold values from 9.490403e-08 to 3.7961613e-07
- second_up: float32 [768, 3072], P('batch', 'head'), may hold values from 4.7452016e-09 to 1.8980806e-08
- second_down: float32 [3072, 768], P('head', 'batch'), may hold values from 9.490403e-08 to 3.7961613e-07
Outputs:
- loss_sum: float32 [], replicated
- grad_norm: float32 [], replicated
- new_patch: float32 [768, 768], P(('batch', 'head'))
- new_first_patch: float32 [768, 768], P(('batch', 'head'))
- new_second_patch: float32 [768, 768], P(('batch', 'head'))
- new_norms: float32 [8, 768], P(None, ('batch', 'head'))
- new_first_norms: float32 [8, 768], P(None, ('batch', 'head'))
- new_second_norms: float32 [8, 768], P(None, ('batch', 'head'))
- new_head: float32 [768, 400], P(('batch', 'head'))
- new_first_head: float32 [768, 400], P(('batch', 'head'))
- new_second_head: float32 [768, 400], P(('batch', 'head'))
- new_proj: float32 [768, 256], P(('batch', 'head'))
- new_first_proj: float32 [768, 256], P(('batch', 'head'))
- new_second_proj: float32 [768, 256], P(('batch', 'head'))
- new_qkv: float32 [2, 768, 3, 768], P(None, 'batch', None, 'head')
- new_first_qkv: float32 [2, 768, 3, 768], P(None, 'batch', None, 'head')
- new_second_qkv: float32 [2, 768, 3, 768], P(None, 'batch', None, 'head')
- new_out: float32 [2, 768, 768], P(None, 'head', 'batch')
- new_first_out: float32 [2, 768, 768], P(None, 'head', 'batch')
- new_second_out: float32 [2, 768, 768], P(None, 'head', 'batch')
- new_up: float32 [768, 3072], P('batch', 'head')
- new_first_up: float32 [768, 3072], P('batch', 'head')
- new_second_up: float32 [768, 3072], P('batch', 'head')
- new_down: float32 [3072, 768], P('head', 'batch')
- new_first_down: float32 [3072, 768], P('head', 'batch')
- new_second_down: float32 [3072, 768], P('head', 'batch')
Inputs may be any that keep to these rules, and one draw needn't show every extreme that they name: partner[partner[c]] = c and partner[c] != c: the clips form 8 // 2 pairs.
All inputs are finite; a program needn't handle non-finite values.
Results may differ from a plain program's by a relative error of at most 0.012.
The roundings to bfloat16 on the way count: a program that leaves them out, or rounds other values in their place, can miss the bound.
Values may be sent and summed in bfloat16 or wider, within the bound.
No kernel may reach another device: no remote copies, remote signals or barrier semaphores. Data moves between devices by JAX's collectives and lax.ppermute only.
A program may use at most 192 MiB of HBM per device.

v0:
```python
import jax
import jax.numpy as jnp
from jax import lax
from jax.sharding import PartitionSpec as P

HD = 64
FRAMES = 4
PMAX = 784
PSMALL = 196
STEP = 5


EXACT = lax.Precision.HIGHEST
TEMPER = 0.05
BETA_ONE = 0.5
BETA_TWO = 0.5
RATE = 0.04
NORM_RATE = 0.3
DECAY = 0.05
ADAM_EPS = 1e-08
CLIP_AT = 1.0
LOWER = jnp.bfloat16
SINGLE = jnp.float32


def layer_norm(value, gain, bias):
    center = value - jnp.mean(value, axis=-1, keepdims=True)
    spread = jnp.mean(center * center, axis=-1, keepdims=True)
    return center * lax.rsqrt(spread + 1e-06) * gain + bias


def gather_small(masters):
    return (
        lax.all_gather(masters[0].astype(LOWER), ("batch", "head"), axis=0, tiled=True),
        lax.all_gather(masters[1].astype(LOWER), ("batch", "head"), axis=1, tiled=True),
        lax.all_gather(masters[2].astype(LOWER), ("batch", "head"), axis=0, tiled=True),
        lax.all_gather(masters[3].astype(LOWER), ("batch", "head"), axis=0, tiled=True),
    )


def gather_wide(masters):
    pieces = (
        lax.all_gather(masters[0].astype(LOWER), "batch", axis=1, tiled=True),
        lax.all_gather(masters[1].astype(LOWER), "batch", axis=2, tiled=True),
        lax.all_gather(masters[2].astype(LOWER), "batch", axis=0, tiled=True),
        lax.all_gather(masters[3].astype(LOWER), "batch", axis=1, tiled=True),
    )
    return pieces


def spread_norm(normed):
    return lax.all_gather(normed, "head", axis=1, tiled=True)


def collect_branch(partial_value):
    return lax.psum_scatter(
        partial_value.astype(jnp.bfloat16), "head", scatter_dimension=1, tiled=True
    ).astype(jnp.float32)


def spread_back(grad):
    return lax.all_gather(grad.astype(LOWER), "head", axis=1, tiled=True)


def collect_back(partial_value):
    return lax.psum_scatter(
        partial_value.astype(jnp.bfloat16), "head", scatter_dimension=1, tiled=True
    ).astype(jnp.float32)


def to_blocks(tensor, spatial):
    clip_count, row_count, width = tensor.shape
    frame_count = row_count // PMAX
    tensor = tensor.reshape(clip_count, frame_count, PMAX, width // HD, HD)
    if spatial:
        return tensor.reshape(clip_count * frame_count, PMAX, width // HD, HD)
    return tensor.transpose(0, 2, 1, 3, 4).reshape(clip_count * PMAX, frame_count, width // HD, HD)


def from_blocks(tensor, clip_count, spatial):
    block_count, span, head_count, head_size = tensor.shape
    if spatial:
        return tensor.reshape(clip_count, block_count // clip_count * span, head_count * head_size)
    tensor = tensor.reshape(clip_count, PMAX, span, head_count, head_size)
    return tensor.transpose(0, 2, 1, 3, 4).reshape(clip_count, span * PMAX, head_count * head_size)


def block_mask(key_mask, spatial, block_count):
    if spatial:
        slot_count = key_mask.shape[1]
        frame_count = block_count // key_mask.shape[0]
        return jnp.broadcast_to(
            key_mask[:, None, :], (key_mask.shape[0], frame_count, slot_count)
        ).reshape(block_count, slot_count)
    return jnp.ones((block_count, FRAMES), bool)


def attn_prob(query, keys, key_mask):
    score = jnp.einsum("blhe,bmhe->bhlm", query, keys, preferred_element_type=SINGLE) * HD ** (-0.5)
    score = jnp.where(key_mask[:, None, None, :], score, -1e30)
    return jax.nn.softmax(score, axis=-1)


def attend(query, keys, values, key_mask):
    weights_soft = attn_prob(query, keys, key_mask)
    return jnp.einsum(
        "bhlm,bmhe->blhe", weights_soft.astype(LOWER), values, preferred_element_type=SINGLE
    ).astype(LOWER)


def attend_back(query, keys, values, key_mask, d_mixed):
    weights_soft = attn_prob(query, keys, key_mask)
    d_prob = jnp.einsum("blhe,bmhe->bhlm", d_mixed, values, preferred_element_type=SINGLE)
    d_score = (
        weights_soft * (d_prob - jnp.sum(weights_soft * d_prob, axis=-1, keepdims=True))
    ).astype(LOWER)
    scale = HD ** (-0.5)
    d_query = (
        jnp.einsum("bhlm,bmhe->blhe", d_score, keys, preferred_element_type=SINGLE) * scale
    ).astype(LOWER)
    d_keys = (
        jnp.einsum("bhlm,blhe->bmhe", d_score, query, preferred_element_type=SINGLE) * scale
    ).astype(LOWER)
    d_values = jnp.einsum(
        "bhlm,blhe->bmhe", weights_soft.astype(LOWER), d_mixed, preferred_element_type=SINGLE
    ).astype(LOWER)
    return (d_query, d_keys, d_values)


def mix_heads(qkv_rows, key_mask, spatial):
    query, keys, values = (to_blocks(qkv_rows[:, :, which], spatial) for which in range(3))
    masks = block_mask(key_mask, spatial, query.shape[0])
    if spatial:
        mixed = lax.map(
            lambda block_item: attend(*(piece[None] for piece in block_item))[0],
            (query, keys, values, masks),
        )
    else:
        mixed = attend(query, keys, values, masks)
    return from_blocks(mixed, qkv_rows.shape[0], spatial)


def mix_heads_back(qkv_rows, d_mixed, key_mask, spatial):
    query, keys, values = (to_blocks(qkv_rows[:, :, which], spatial) for which in range(3))
    d_blocks = to_blocks(d_mixed, spatial)
    masks = block_mask(key_mask, spatial, query.shape[0])
    if spatial:
        grad_list = lax.map(
            lambda block_item: tuple(
                (piece[0] for piece in attend_back(*(part_of[None] for part_of in block_item)))
            ),
            (query, keys, values, masks, d_blocks),
        )
    else:
        grad_list = attend_back(query, keys, values, masks, d_blocks)
    return jnp.stack([from_blocks(grad, qkv_rows.shape[0], spatial) for grad in grad_list], axis=2)


def mix_any(qkv_rows, key_mask, spatial):
    return mix_heads(qkv_rows, key_mask, spatial)


def mix_any_back(qkv_rows, d_mixed, key_mask, spatial):
    return mix_heads_back(qkv_rows, d_mixed, key_mask, spatial)


def block_forward(resid, wide_copies, norms, key_mask):
    qkv_w, out_w, up_w, down_w = wide_copies
    saved_inputs = []
    for which in range(2):
        saved_inputs.append(resid)
        gathered = spread_norm(
            layer_norm(resid, norms[2 * which], norms[2 * which + 1]).astype(LOWER)
        )
        qkv_rows = jnp.einsum(
            "crd,dkf->crkf", gathered, qkv_w[which], preferred_element_type=SINGLE
        ).astype(LOWER)
        mixed = mix_any(qkv_rows, key_mask, which == 1)
        resid = resid + collect_branch(
            jnp.einsum("crf,fd->crd", mixed, out_w[which], preferred_element_type=SINGLE)
        )
    saved_inputs.append(resid)
    gathered = spread_norm(layer_norm(resid, norms[4], norms[5]).astype(LOWER))
    hidden = jnp.einsum("crd,df->crf", gathered, up_w, preferred_element_type=SINGLE)
    activated = jax.nn.gelu(hidden).astype(LOWER)
    resid = resid + collect_branch(
        jnp.einsum("crf,fd->crd", activated, down_w, preferred_element_type=SINGLE)
    )
    return (resid, saved_inputs)


def block_backward(saved_inputs, d_resid, wide_copies, norms, key_mask):
    qkv_w, out_w, up_w, down_w = wide_copies
    normed, norm_back = jax.vjp(layer_norm, saved_inputs[2], norms[4], norms[5])
    gathered = spread_norm(normed.astype(LOWER))
    hidden = jnp.einsum("crd,df->crf", gathered, up_w, preferred_element_type=SINGLE)
    activated, gelu_back = jax.vjp(jax.nn.gelu, hidden)
    d_rows = spread_back(d_resid)
    d_down = jnp.einsum(
        "crf,crd->fd", activated.astype(LOWER), d_rows, preferred_element_type=SINGLE
    )
    d_hidden = gelu_back(jnp.einsum("crd,fd->crf", d_rows, down_w, preferred_element_type=SINGLE))[
        0
    ].astype(LOWER)
    d_up = jnp.einsum("crd,crf->df", gathered, d_hidden, preferred_element_type=SINGLE)
    d_local, d_gain, d_bias = norm_back(
        collect_back(jnp.einsum("crf,df->crd", d_hidden, up_w, preferred_element_type=SINGLE))
    )
    d_resid = d_resid + d_local
    norm_grads = [d_gain, d_bias]
    d_in_list = []
    d_out_list = []
    for which in (1, 0):
        normed, norm_back = jax.vjp(
            layer_norm, saved_inputs[which], norms[2 * which], norms[2 * which + 1]
        )
        gathered = spread_norm(normed.astype(LOWER))
        qkv_rows = jnp.einsum(
            "crd,dkf->crkf", gathered, qkv_w[which], preferred_element_type=SINGLE
        ).astype(LOWER)
        mixed = mix_any(qkv_rows, key_mask, which == 1)
        d_rows = spread_back(d_resid)
        d_out_list.insert(
            0, jnp.einsum("crf,crd->fd", mixed, d_rows, preferred_element_type=SINGLE)
        )
        d_mixed = jnp.einsum(
            "crd,fd->crf", d_rows, out_w[which], preferred_element_type=SINGLE
        ).astype(LOWER)
        d_qkv = mix_any_back(qkv_rows, d_mixed, key_mask, which == 1)
        d_in_list.insert(
            0, jnp.einsum("crd,crkf->dkf", gathered, d_qkv, preferred_element_type=SINGLE)
        )
        d_local, d_gain, d_bias = norm_back(
            collect_back(
                jnp.einsum("crkf,dkf->crd", d_qkv, qkv_w[which], preferred_element_type=SINGLE)
            )
        )
        d_resid = d_resid + d_local
        norm_grads = [d_gain, d_bias] + norm_grads
    return (d_resid, norm_grads, (jnp.stack(d_in_list), jnp.stack(d_out_list), d_up, d_down))


def adam_step(master, first, second, grad, factor, rate):
    clipped = grad * factor
    first_new = BETA_ONE * first + (1.0 - BETA_ONE) * clipped
    second_new = BETA_TWO * second + (1.0 - BETA_TWO) * clipped * clipped
    first_hat = first_new / (1.0 - BETA_ONE**STEP)
    second_hat = second_new / (1.0 - BETA_TWO**STEP)
    master_new = master - rate * (first_hat / (jnp.sqrt(second_hat) + ADAM_EPS) + DECAY * master)
    return (master_new, first_new, second_new)


def body(
    patches,
    bucket,
    labels,
    partner,
    patch_weight,
    norm_params,
    head_weight,
    proj_weight,
    attn_in,
    attn_out,
    mlp_up,
    mlp_down,
    first_patch,
    first_norms,
    first_head,
    first_proj,
    first_qkv,
    first_out,
    first_up,
    first_down,
    second_patch,
    second_norms,
    second_head,
    second_proj,
    second_qkv,
    second_out,
    second_up,
    second_down,
):
    masters = (
        patch_weight,
        norm_params,
        head_weight,
        proj_weight,
        attn_in,
        attn_out,
        mlp_up,
        mlp_down,
    )
    firsts = (
        first_patch,
        first_norms,
        first_head,
        first_proj,
        first_qkv,
        first_out,
        first_up,
        first_down,
    )
    seconds = (
        second_patch,
        second_norms,
        second_head,
        second_proj,
        second_qkv,
        second_out,
        second_up,
        second_down,
    )
    patch_copy, norms_copy, head_copy, proj_copy = gather_small(masters[:4])
    wide_copies = gather_wide(masters[4:])
    norms = norms_copy.astype(SINGLE)
    clip_count, local_rows = (patches.shape[0], patches.shape[1])
    patch_count = jnp.where(bucket == 1, PMAX, PSMALL)
    key_mask = jnp.arange(PMAX)[None, :] < patch_count[:, None]
    rows_here = lax.axis_index("head") * local_rows + jnp.arange(local_rows)
    row_mask = ((rows_here % PMAX)[None, :] < patch_count[:, None]).astype(SINGLE)[:, :, None]
    row_count = (FRAMES * patch_count).astype(SINGLE)[:, None]
    start = jnp.einsum("crp,pd->crd", patches, patch_copy, preferred_element_type=SINGLE) * row_mask
    top, saved_inputs = block_forward(start, wide_copies, norms, key_mask)
    final_norm, final_back = jax.vjp(layer_norm, top, norms[6], norms[7])
    pooled = lax.psum(jnp.sum(final_norm * row_mask, axis=1), "head") / row_count
    pooled_low = pooled.astype(LOWER)
    logits = jnp.dot(pooled_low, head_copy, preferred_element_type=SINGLE)
    label_hot = (jnp.arange(logits.shape[1])[None, :] == labels[:, None]).astype(SINGLE)
    cross_loss = jax.nn.logsumexp(logits, axis=1) - jnp.sum(logits * label_hot, axis=1)
    d_logits = (jax.nn.softmax(logits, axis=1) - label_hot).astype(LOWER)
    embedding = jnp.dot(pooled_low, proj_copy, preferred_element_type=SINGLE)
    inverse = lax.rsqrt(jnp.sum(embedding * embedding, axis=1, keepdims=True) + 1e-06)
    unit_embed = embedding * inverse
    all_units = lax.all_gather(unit_embed, "batch", axis=0, tiled=True)
    own_ids = lax.axis_index("batch") * clip_count + jnp.arange(clip_count)
    other_ids = jnp.arange(all_units.shape[0])
    own_pair = other_ids[None, :] == own_ids[:, None]
    mate_hot = (other_ids[None, :] == partner[:, None]).astype(SINGLE)
    similar = jnp.dot(unit_embed, all_units.T, precision=EXACT) / TEMPER
    masked = jnp.where(own_pair, -1e30, similar)
    contrast = jax.nn.logsumexp(masked, axis=1) - jnp.sum(similar * mate_hot, axis=1)
    local_loss = jnp.sum(cross_loss + contrast)
    loss_sum = lax.psum(local_loss, "batch")
    d_similar = (jax.nn.softmax(masked, axis=1) - mate_hot) / TEMPER
    column_part = lax.psum_scatter(
        jnp.dot(d_similar.T, unit_embed, precision=EXACT), "batch", scatter_dimension=0, tiled=True
    )
    d_unit = jnp.dot(d_similar, all_units, precision=EXACT) + column_part
    d_embed = (
        inverse * d_unit
        - embedding
        * (inverse * inverse * inverse)
        * jnp.sum(embedding * d_unit, axis=1, keepdims=True)
    ).astype(LOWER)
    lead_flag = (lax.axis_index("head") == 0).astype(SINGLE)
    d_head = jnp.dot(pooled_low.T, d_logits, preferred_element_type=SINGLE) * lead_flag
    d_proj = jnp.dot(pooled_low.T, d_embed, preferred_element_type=SINGLE) * lead_flag
    d_pooled = jnp.dot(d_logits, head_copy.T, preferred_element_type=SINGLE) + jnp.dot(
        d_embed, proj_copy.T, preferred_element_type=SINGLE
    )
    d_top, d_gain_final, d_bias_final = final_back(row_mask * (d_pooled / row_count)[:, None, :])
    wide_copies = gather_wide(masters[4:])
    d_start, norm_grads, d_wide = block_backward(saved_inputs, d_top, wide_copies, norms, key_mask)
    d_patch = jnp.einsum(
        "crp,crd->pd", patches, (d_start * row_mask).astype(LOWER), preferred_element_type=SINGLE
    )
    d_norms = jnp.stack(norm_grads + [d_gain_final, d_bias_final])
    owned_small = (
        lax.psum_scatter(d_patch, ("batch", "head"), scatter_dimension=0, tiled=True),
        lax.psum_scatter(d_norms, ("batch", "head"), scatter_dimension=1, tiled=True),
        lax.psum_scatter(d_head, ("batch", "head"), scatter_dimension=0, tiled=True),
        lax.psum_scatter(d_proj, ("batch", "head"), scatter_dimension=0, tiled=True),
    )
    owned_wide = (
        lax.psum_scatter(d_wide[0], "batch", scatter_dimension=1, tiled=True),
        lax.psum_scatter(d_wide[1], "batch", scatter_dimension=2, tiled=True),
        lax.psum_scatter(d_wide[2], "batch", scatter_dimension=0, tiled=True),
        lax.psum_scatter(d_wide[3], "batch", scatter_dimension=1, tiled=True),
    )
    grad_list = tuple(owned_small) + tuple(owned_wide)
    squares = sum((jnp.sum(grad * grad) for grad in grad_list))
    total_square = lax.psum(squares, ("batch", "head"))
    grad_norm = jnp.sqrt(total_square)
    factor = jnp.minimum(1.0, CLIP_AT / (grad_norm + 1e-06))
    updates = []
    for number, (master, first, second, grad) in enumerate(
        zip(masters, firsts, seconds, grad_list)
    ):
        rate = NORM_RATE if number == 1 else RATE
        updates.extend(adam_step(master, first, second, grad, factor, rate))
    return (loss_sum, grad_norm, *updates)


def solution(mesh):
    placed = (
        P("batch", "head", None),
        P("batch"),
        P("batch"),
        P("batch"),
        P(("batch", "head"), None),
        P(None, ("batch", "head")),
        P(("batch", "head"), None),
        P(("batch", "head"), None),
        P(None, "batch", None, "head"),
        P(None, "head", "batch"),
        P("batch", "head"),
        P("head", "batch"),
        P(("batch", "head"), None),
        P(None, ("batch", "head")),
        P(("batch", "head"), None),
        P(("batch", "head"), None),
        P(None, "batch", None, "head"),
        P(None, "head", "batch"),
        P("batch", "head"),
        P("head", "batch"),
        P(("batch", "head"), None),
        P(None, ("batch", "head")),
        P(("batch", "head"), None),
        P(("batch", "head"), None),
        P(None, "batch", None, "head"),
        P(None, "head", "batch"),
        P("batch", "head"),
        P("head", "batch"),
    )
    return jax.shard_map(
        body,
        mesh=mesh,
        in_specs=placed,
        out_specs=(
            P(),
            P(),
            P(("batch", "head"), None),
            P(("batch", "head"), None),
            P(("batch", "head"), None),
            P(None, ("batch", "head")),
            P(None, ("batch", "head")),
            P(None, ("batch", "head")),
            P(("batch", "head"), None),
            P(("batch", "head"), None),
            P(("batch", "head"), None),
            P(("batch", "head"), None),
            P(("batch", "head"), None),
            P(("batch", "head"), None),
            P(None, "batch", None, "head"),
            P(None, "batch", None, "head"),
            P(None, "batch", None, "head"),
            P(None, "head", "batch"),
            P(None, "head", "batch"),
            P(None, "head", "batch"),
            P("batch", "head"),
            P("batch", "head"),
            P("batch", "head"),
            P("head", "batch"),
            P("head", "batch"),
            P("head", "batch"),
        ),
        check_vma=False,
    )
```

profile of v0, /device:TPU:0, one launch (start us, length us, event | category | flops | bytes accessed | tf_op | source)
XLA Modules:
  0.0 1951.5 jit_solution(5253758208351722327)
XLA Ops:
  12.6 43.4 %all-gather.2 = bf16[32,24,8]{1,2,0:T(8,128)(2,1)S(1)} all-gather(bf16[1,24,8]{1,2,0:T(8,128)(2,1)S(1)} %convert_bitcast_fusion.4), channel_id=1, replica_groups=mesh['batch'=8,'head'=4] {'batch','head'}, dimensions={0}, use_global_device_ids=true | all-gather | bytes 12672 | tf_op jit(solution)/shard_map/all_gather | solution.py:35
  57.0 11.4 all-gather.15.cloned.1.call-done
  74.1 32.8 %all_gather.56 = bf16[2,192,768]{1,0,2:T(2,128)(2,1)S(1)} all-gather(bf16[2,192,96]{1,0,2:T(2,128)(2,1)S(1)} %copy.233), channel_id=1, replica_groups=mesh['batch'=8,'head'=4] {'batch'}, dimensions={2}, use_global_device_ids=true | all-gather | bytes 663552 | tf_op jit(solution)/shard_map/all_gather | solution.py:44
  109.8 16.9 all-gather.17.cloned.1.call-done
  126.7 8.7 fusion.227
  135.4 5.5 copy.276
  140.9 24.5 %all-gather.33.cloned.1.call-done = bf16[3136,768]{1,0:T(8,128)(2,1)} async-done(((bf16[784,768]{1,0:T(8,128)(2,1)}), bf16[3136,768]{1,0:T(8,128)(2,1)}) %all-gather.33.cloned.1.call-update) | async-done | bytes 4816912 | tf_op jit(solution)/shard_map/all_gather | solution.py:52
  165.4 5.5 fusion.230
  199.9 8.9 fusion.229
  211.0 5.5 convert_bitcast_fusion.3
  228.9 48.2 %reduce-scatter.21.cloned.1.call-done = bf16[1,784,768]{2,1,0:T(8,128)(2,1)} async-done(((bf16[1,3136,768]{2,1,0:T(8,128)(2,1)}), bf16[1,784,768]{2,1,0:T(8,128)(2,1)}) %reduce-scatter.21.cloned.1.call-update) | async-done | bytes 1204240 | tf_op jit(solution)/shard_map/reduce_scatter | solution.py:56
  284.8 5.5 copy.278
  290.3 31.1 %all-gather.19.cloned.1.call-done = bf16[1,3136,768]{2,1,0:T(8,128)(2,1)} async-done(((bf16[1,784,768]{2,1,0:T(8,128)(2,1)}), bf16[1,3136,768]{2,1,0:T(8,128)(2,1)}) %all-gather.19.cloned.1.call-update) | async-done | bytes 4816912 | tf_op jit(solution)/shard_map/all_gather | solution.py:52
  321.3 5.5 fusion.97
  347.5 35.4 %while.28 = (s32[]{:T(128)}, bf16[4,784,3,64]{1,3,2,0:T(8,128)(2,1)}, bf16[4,784,3,64]{1,3,2,0:T(8,128)(2,1)}, pred[4,784]{1,0:T(4,128)(4,1)S(1)}, bf16[4,784,3,...) while((s32[]{:T(128)}, bf16[4,784,3,64]{1,3,2,0:T(8,128)(2,1)}, ...), condition=%wide.region_10.11_spmd, body=%wide.region_7.10_spmd.sunk | while | flops 486958848 | bytes 30903048 | solution.py:134
  396.8 46.9 %reduce-scatter.23.cloned.1.call-done = bf16[1,784,768]{2,1,0:T(8,128)(2,1)} async-done(((bf16[1,3136,768]{2,1,0:T(8,128)(2,1)}), bf16[1,784,768]{2,1,0:T(8,128)(2,1)}) %reduce-scatter.23.cloned.1.call-update) | async-done | bytes 1204240 | tf_op jit(solution)/shard_map/reduce_scatter | solution.py:56
  450.0 37.5 %all-gather.23.cloned.1.call-done = bf16[768,768]{1,0:T(8,128)(2,1)} async-done(((bf16[96,768]{1,0:T(8,128)(2,1)}), bf16[768,768]{1,0:T(8,128)(2,1)}) %all-gather.23.cloned.1.call-update) | async-done | bytes 1179664 | tf_op jit(solution)/shard_map/all_gather | solution.py:45
  487.5 38.4 %all-gather.21.cloned.1.call-done = bf16[1,3136,768]{2,1,0:T(8,128)(2,1)} async-done(((bf16[1,784,768]{2,1,0:T(8,128)(2,1)}), bf16[1,3136,768]{2,1,0:T(8,128)(2,1)}) %all-gather.21.cloned.1.call-update) | async-done | bytes 4816912 | tf_op jit(solution)/shard_map/all_gather | solution.py:52
  525.9 10.2 fusion.93
  536.2 33.6 %all-gather.25.cloned.1.call-done = bf16[768,768]{0,1:T(8,128)(2,1)} async-done(((bf16[768,96]{0,1:T(8,128)(2,1)}), bf16[768,768]{0,1:T(8,128)(2,1)}) %all-gather.25.cloned.1.call-update) | async-done | bytes 1179664 | tf_op jit(solution)/shard_map/all_gather | solution.py:46
  569.8 10.1 fusion.75
  581.9 43.5 %all_gather.62 = bf16[768,256]{1,0:T(8,128)(2,1)} all-gather(bf16[24,256]{1,0:T(8,128)(2,1)S(1)} %convert_element_type.291), channel_id=1, replica_groups=mesh['batch'=8,'head'=4] {'batch','head'}, dimensions={0}, use_global_device_ids=true | all-gather | bytes 405504 | tf_op jit(solution)/shard_map/all_gather | solution.py:37
  625.5 38.7 %all_gather.61 = bf16[768,400]{1,0:T(8,128)(2,1)S(1)} all-gather(bf16[24,400]{1,0:T(8,128)(2,1)S(1)} %convert_element_type.290), channel_id=1, replica_groups=mesh['batch'=8,'head'=4] {'batch','head'}, dimensions={0}, use_global_device_ids=true | all-gather | bytes 633600 | tf_op jit(solution)/shard_map/all_gather | solution.py:36
  668.0 7.3 psum.21
  684.1 16.8 all-gather.3
  707.6 20.2 %all-reduce.2 = (f32[]{:T(128)}, f32[8,256]{1,0:T(8,128)S(1)}) all-reduce(f32[]{:T(128)} %bitcast.61, f32[8,256]{1,0:T(8,128)S(1)} %broadcast_multiply_fusion), channel_id=1, replica_groups=mesh['batch'=8,'head'=4] {'batch'}, use_global_device_ids=true, to_apply=%region_26.27 | all-reduce | flops 2049 | bytes 16392 | tf_op jit(solution)/shard_map/psum | solution.py:343
  738.8 34.1 %all-gather.27.cloned.1.call-done = bf16[1,3136,768]{2,1,0:T(8,128)(2,1)} async-done(((bf16[1,784,768]{2,1,0:T(8,128)(2,1)}), bf16[1,3136,768]{2,1,0:T(8,128)(2,1)}) %all-gather.27.cloned.1.call-update) | async-done | bytes 4816912 | tf_op jit(solution)/shard_map/all_gather | solution.py:62
  772.8 12.3 fusion.72
  787.2 5.6 fusion.76
  792.9 48.6 %reduce-scatter.27.cloned.1.call-done = bf16[1,784,768]{2,1,0:T(8,128)(2,1)} async-done(((bf16[1,3136,768]{2,1,0:T(8,128)(2,1)}), bf16[1,784,768]{2,1,0:T(8,128)(2,1)}) %reduce-scatter.27.cloned.1.call-update) | async-done | bytes 1204240 | tf_op jit(solution)/shard_map/reduce_scatter | solution.py:66
  849.4 38.1 %all-gather.29.cloned.1.call-done = bf16[1,3136,768]{2,1,0:T(8,128)(2,1)} async-done(((bf16[1,784,768]{2,1,0:T(8,128)(2,1)}), bf16[1,3136,768]{2,1,0:T(8,128)(2,1)}) %all-gather.29.cloned.1.call-update) | async-done | bytes 4816912 | tf_op jit(solution)/shard_map/all_gather | solution.py:62
  887.6 5.2 convolution_convert_fusion.5
  903.6 124.9 %while.29 = (s32[]{:T(128)}, bf16[4,784,3,64]{1,3,2,0:T(8,128)(2,1)}, bf16[4,784,3,64]{1,3,2,0:T(8,128)(2,1)}, bf16[4,784,3,64]{1,3,2,0:T(8,128)(2,1)}, bf16[4,7...) while((s32[]{:T(128)}, ...), condition=%wide.region_40.41_spmd, body=%wide.region_36.40_spmd.sunk | while | flops 1208550144 | bytes 125291760 | solution.py:148
  913.3 5.7 multiply_reduce_fusion.21
  918.9 8.8 multiply_convert_fusion.9
  944.5 5.7 multiply_reduce_fusion.21
  950.1 8.8 multiply_convert_fusion.9
  975.6 5.7 multiply_reduce_fusion.21
  981.3 8.8 multiply_convert_fusion.9
  1006.8 5.7 multiply_reduce_fusion.21
  1012.5 8.8 multiply_convert_fusion.9
  1049.5 5.9 fusion.77
  1055.4 48.6 %reduce-scatter.29.cloned.1.call-done = bf16[1,784,768]{2,1,0:T(8,128)(2,1)} async-done(((bf16[1,3136,768]{2,1,0:T(8,128)(2,1)}), bf16[1,784,768]{2,1,0:T(8,128)(2,1)}) %reduce-scatter.29.cloned.1.call-update) | async-done | bytes 1204240 | tf_op jit(solution)/shard_map/reduce_scatter | solution.py:66
  1111.1 38.1 %all-gather.31.cloned.1.call-done = bf16[1,3136,768]{2,1,0:T(8,128)(2,1)} async-done(((bf16[1,784,768]{2,1,0:T(8,128)(2,1)}), bf16[1,3136,768]{2,1,0:T(8,128)(2,1)}) %all-gather.31.cloned.1.call-update) | async-done | bytes 4816912 | tf_op jit(solution)/shard_map/all_gather | solution.py:62
  1149.2 5.2 convolution_convert_fusion.4
  1162.0 7.8 convert_bitcast_fusion.2
  1169.8 11.2 multiply_reduce_fusion.1
  1206.2 5.8 copy.251
  1221.5 5.8 fusion.78
  1230.6 10.3 fusion.91
  1241.1 11.5 fusion.85
  1266.3 6.8 fusion.95
  1273.1 5.5 fusion.231
  1280.7 6.9 copy.271
  1287.5 8.0 reshape.1006
  1311.1 65.2 %reduce-scatter.35.cloned.1.call-done = f32[24,256]{1,0:T(8,128)} async-done(((f32[768,256]{1,0:T(8,128)}), f32[24,256]{1,0:T(8,128)}) %reduce-scatter.35.cloned.1.call-update) | async-done | bytes 24592 | tf_op jit(solution)/shard_map/reduce_scatter | solution.py:372
  1377.7 99.9 %reduce-scatter.33.cloned.1.call-done = f32[24,400]{1,0:T(8,128)} async-done(((f32[768,400]{1,0:T(8,128)}), f32[24,400]{1,0:T(8,128)}) %reduce-scatter.33.cloned.1.call-update) | async-done | bytes 38416 | tf_op jit(solution)/shard_map/reduce_scatter | solution.py:371
  1479.0 70.1 %reduce-scatter.37.cloned.1.call-done = f32[96,768]{1,0:T(8,128)} async-done(((f32[768,768]{1,0:T(8,128)}), f32[96,768]{1,0:T(8,128)}) %reduce-scatter.37.cloned.1.call-update) | async-done | bytes 294928 | tf_op jit(solution)/shard_map/reduce_scatter | solution.py:377
  1550.7 69.7 %reduce-scatter.39.cloned.1.call-done = f32[768,96]{0,1:T(8,128)} async-done(((f32[768,768]{0,1:T(8,128)}), f32[768,96]{0,1:T(8,128)}) %reduce-scatter.39.cloned.1.call-update) | async-done | bytes 294928 | tf_op jit(solution)/shard_map/reduce_scatter | solution.py:378
  1622.1 64.7 %reduce-scatter.45.cloned.1.call-done = f32[96,384]{1,0:T(8,128)} async-done(((f32[768,384]{1,0:T(8,128)}), f32[96,384]{1,0:T(8,128)}) %reduce-scatter.45.cloned.1.call-update) | async-done | bytes 147472
  1688.7 79.7 %reduce-scatter.43.cloned.1.call-done = f32[96,1152]{1,0:T(8,128)} async-done(((f32[768,1152]{1,0:T(8,128)}), f32[96,1152]{1,0:T(8,128)}) %reduce-scatter.43.cloned.1.call-update) | async-done | bytes 442384
  1771.1 40.4 %all-reduce.1 = f32[8,768]{1,0:T(8,128)S(1)} all-reduce(f32[8,768]{1,0:T(8,128)S(1)} %stack.61), channel_id=12, replica_groups=mesh['batch'=8,'head'=4] {'batch','head'}, use_global_device_ids=true, to_apply=%region_58.59.clone | all-reduce | flops 6144 | bytes 49152
  1812.3 60.1 %reduce-scatter.41.cloned.1.call-done = f32[24,768]{1,0:T(8,128)} async-done(((f32[768,768]{1,0:T(8,128)}), f32[24,768]{1,0:T(8,128)}) %reduce-scatter.41.cloned.1.call-update) | async-done | bytes 73744 | tf_op jit(solution)/shard_map/reduce_scatter | solution.py:369
  1883.2 40.0 %psum.23 = f32[]{:T(128)} all-reduce(f32[]{:T(128)S(6)} %add.397), channel_id=1, replica_groups=mesh['batch'=8,'head'=4] {'batch','head'}, use_global_device_ids=true, to_apply=%region_72.73 | all-reduce | flops 1 | bytes 8 | tf_op jit(solution)/shard_map/psum | solution.py:382
  (492 shorter events, 394.3 us)
Async XLA Ops:
  7.2 61.2 %copy-start = (bf16[1,784,768]{2,1,0:T(8,128)(2,1)S(1)}, bf16[1,784,768]{2,1,0:T(8,128)(2,1)}, u32[]{:S(2)}) copy-start(bf16[1,784,768]{2,1,0:T(8,128)(2,1)} %param.32) | copy-start | bytes 3612676
  7.2 61.2 %all-gather.15.cloned.1.call-start = ((), (), s32[]{:S(2)}) async-start(), calls=%async_computation.13 | async-start | bytes 1216512 | tf_op jit(solution)/shard_map/all_gather | solution.py:34
  8.9 117.8 %all-gather.17.cloned.1.call-start = ((), (), s32[]{:S(2)}) async-start(), calls=%async_computation.14 | async-start | bytes 2654208 | tf_op jit(solution)/shard_map/all_gather | solution.py:43
  11.2 154.2 %all-gather.33.cloned.1.call-start = ((), (), s32[]{:S(2)}) async-start(), calls=%async_computation.32 | async-start | bytes 6021120 | tf_op jit(solution)/shard_map/all_gather | solution.py:52
  56.3 678.3 %copy-start.52 = (f32[784]{0:T(1024)}, f32[784]{0:T(1024)S(1)}, u32[]{:S(2)}) copy-start(f32[784]{0:T(1024)S(1)} %fusion.184) | copy-start | bytes 9412
  57.0 15.3 copy-start.74
  57.0 224.0 %copy-start.69 = (f32[768]{0:T(1024)}, f32[768]{0:T(1024)S(1)}, u32[]{:S(2)}) copy-start(f32[768]{0:T(1024)S(1)} %get-tuple-element.345) | copy-start | bytes 9220
  73.9 203.1 %reduce-scatter.21.cloned.1.call-start = ((), (), s32[]{:S(2)}) async-start(), calls=%async_computation.15 | async-start | bytes 6021120 | tf_op jit(solution)/shard_map/reduce_scatter | solution.py:56
  140.9 30.0 %copy-start.42 = (bf16[1,768,3,192]{1,3,2,0:T(8,128)(2,1)}, bf16[1,768,3,192]{1,3,2,0:T(8,128)(2,1)S(1)}, u32[]{:S(2)}) copy-start(bf16[1,768,3,192]{1,3,2,0:T(8,128)(2,1)S(1)} %copy.276) | copy-start | bytes 2654212
  199.9 11.1 copy-start.29
  228.4 92.9 %all-gather.19.cloned.1.call-start = ((), (), s32[]{:S(2)}) async-start(), calls=%async_computation.16 | async-start | bytes 6021120 | tf_op jit(solution)/shard_map/all_gather | solution.py:52
  283.1 160.6 %reduce-scatter.23.cloned.1.call-start = ((), (), s32[]{:S(2)}) async-start(), calls=%async_computation.17 | async-start | bytes 6021120 | tf_op jit(solution)/shard_map/reduce_scatter | solution.py:56
  290.2 36.6 %copy-start.44 = (bf16[1,768,3,192]{1,3,2,0:T(8,128)(2,1)}, bf16[1,768,3,192]{1,3,2,0:T(8,128)(2,1)S(1)}, u32[]{:S(2)}) copy-start(bf16[1,768,3,192]{1,3,2,0:T(8,128)(2,1)S(1)} %copy.278) | copy-start | bytes 2654212
  383.0 7.2 copy-start.59
  395.1 92.4 %all-gather.23.cloned.1.call-start = ((), (), s32[]{:S(2)}) async-start(), calls=%async_computation.19 | async-start | bytes 1327104 | tf_op jit(solution)/shard_map/all_gather | solution.py:45
  396.7 129.2 %all-gather.21.cloned.1.call-start = ((), (), s32[]{:S(2)}) async-start(), calls=%async_computation.18 | async-start | bytes 6021120 | tf_op jit(solution)/shard_map/all_gather | solution.py:52
  449.0 120.8 %all-gather.25.cloned.1.call-start = ((), (), s32[]{:S(2)}) async-start(), calls=%async_computation.20 | async-start | bytes 1327104 | tf_op jit(solution)/shard_map/all_gather | solution.py:46
  449.7 214.5 %reduce-scatter.25.cloned.1.call-start = ((), (), s32[]{:S(2)}) async-start(), calls=%async_computation.21 | async-start | bytes 6021120 | tf_op jit(solution)/shard_map/reduce_scatter | solution.py:56
  579.9 192.9 %all-gather.27.cloned.1.call-start = ((), (), s32[]{:S(2)}) async-start(), calls=%async_computation.22 | async-start | bytes 6021120 | tf_op jit(solution)/shard_map/all_gather | solution.py:62
  675.3 59.3 %copy-start.78 = (f32[1,768]{1,0:T(1,128)}, f32[1,768]{1,0:T(1,128)S(1)}, u32[]{:S(2)}) copy-start(f32[1,768]{1,0:T(1,128)S(1)} %psum.21) | copy-start | bytes 9220
  727.8 6.8 copy-start.10
  730.0 5.6 copy-start.94
  738.3 103.2 %reduce-scatter.27.cloned.1.call-start = ((), (), s32[]{:S(2)}) async-start(), calls=%async_computation.23 | async-start | bytes 6021120 | tf_op jit(solution)/shard_map/reduce_scatter | solution.py:66
  772.8 14.4 copy-start.99
  792.9 94.7 %all-gather.29.cloned.1.call-start = ((), (), s32[]{:S(2)}) async-start(), calls=%async_computation.24 | async-start | bytes 6021120 | tf_op jit(solution)/shard_map/all_gather | solution.py:62
  847.0 40.5 %copy-start.60 = (bf16[1,192,768]{2,1,0:T(8,128)(2,1)S(1)}, bf16[1,192,768]{2,1,0:T(8,128)(2,1)}, u32[]{:S(2)}) copy-start(bf16[1,192,768]{2,1,0:T(8,128)(2,1)} %copy.279) | copy-start | bytes 884740
  849.4 254.6 %reduce-scatter.29.cloned.1.call-start = ((), (), s32[]{:S(2)}) async-start(), calls=%async_computation.25 | async-start | bytes 6021120 | tf_op jit(solution)/shard_map/reduce_scatter | solution.py:66
  1032.8 7.2 copy-start.20
  1055.4 48.7 %copy-start.64 = (f32[784]{0:T(1024)S(1)}, f32[784]{0:T(1024)}, u32[]{:S(2)}) copy-start(f32[784]{0:T(1024)} %copy-done.63) | copy-start | bytes 9412
  1055.4 48.7 %copy-start.70 = (f32[768]{0:T(1024)S(1)}, f32[768]{0:T(1024)}, u32[]{:S(2)}) copy-start(f32[768]{0:T(1024)} %copy-done.69) | copy-start | bytes 9220
  1055.4 48.7 %copy-start.72 = (f32[784]{0:T(1024)S(1)}, f32[784]{0:T(1024)}, u32[]{:S(2)}) copy-start(f32[784]{0:T(1024)} %copy-done.71) | copy-start | bytes 9412
  1055.4 51.9 %copy-start.84 = (f32[784]{0:T(1024)S(1)}, f32[784]{0:T(1024)}, u32[]{:S(2)}) copy-start(f32[784]{0:T(1024)} %copy-done.83) | copy-start | bytes 9412
  1055.4 93.8 %all-gather.31.cloned.1.call-start = ((), (), s32[]{:S(2)}) async-start(), calls=%async_computation.26 | async-start | bytes 6021120 | tf_op jit(solution)/shard_map/all_gather | solution.py:62
  1109.7 39.5 %copy-start.58 = (bf16[1,192,768]{2,1,0:T(8,128)(2,1)S(1)}, bf16[1,192,768]{2,1,0:T(8,128)(2,1)}, u32[]{:S(2)}) copy-start(bf16[1,192,768]{2,1,0:T(8,128)(2,1)} %copy.277) | copy-start | bytes 884740
  1111.1 184.9 %reduce-scatter.31.cloned.1.call-start = ((), (), s32[]{:S(2)}) async-start(), calls=%async_computation.27 | async-start | bytes 6021120 | tf_op jit(solution)/shard_map/reduce_scatter | solution.py:66
  1162.0 7.8 copy-start.30
  1162.0 19.0 slice-start
  1169.8 11.2 slice-start.1
  1181.0 5.0 copy-start.19
  1227.3 149.1 %reduce-scatter.35.cloned.1.call-start = ((), (), s32[]{:S(2)}) async-start(), calls=%async_computation.29 | async-start | bytes 811008 | tf_op jit(solution)/shard_map/reduce_scatter | solution.py:372
  1229.1 248.5 %reduce-scatter.33.cloned.1.call-start = ((), (), s32[]{:S(2)}) async-start(), calls=%async_computation.28 | async-start | bytes 1622016 | tf_op jit(solution)/shard_map/reduce_scatter | solution.py:371
  1230.5 318.5 %reduce-scatter.37.cloned.1.call-start = ((), (), s32[]{:S(2)}) async-start(), calls=%async_computation.30 | async-start | bytes 2654208 | tf_op jit(solution)/shard_map/reduce_scatter | solution.py:377
  1240.9 379.6 %reduce-scatter.39.cloned.1.call-start = ((), (), s32[]{:S(2)}) async-start(), calls=%async_computation.31 | async-start | bytes 2654208 | tf_op jit(solution)/shard_map/reduce_scatter | solution.py:378
  1252.7 434.2 %reduce-scatter.45.cloned.1.call-start = ((), (), s32[]{:S(2)}) async-start(), calls=%async_computation.35 | async-start | bytes 1327104
  1266.2 502.2 %reduce-scatter.43.cloned.1.call-start = ((), (), s32[]{:S(2)}) async-start(), calls=%async_computation.34 | async-start | bytes 3981312
  1266.3 6.8 copy-start.51
  1295.6 576.8 %reduce-scatter.41.cloned.1.call-start = ((), (), s32[]{:S(2)}) async-start(), calls=%async_computation.33 | async-start | bytes 2433024 | tf_op jit(solution)/shard_map/reduce_scatter | solution.py:369
  1309.0 313.1 %copy-start.89 = (f32[768]{0:T(1024)S(1)}, f32[768]{0:T(1024)}, u32[]{:S(2)}) copy-start(f32[768]{0:T(1024)} %get-tuple-element.336) | copy-start | bytes 9220
  1309.0 313.1 %copy-start.90 = (f32[768]{0:T(1024)S(1)}, f32[768]{0:T(1024)}, u32[]{:S(2)}) copy-start(f32[768]{0:T(1024)} %get-tuple-element.328) | copy-start | bytes 9220
  1770.3 153.6 %copy-start.31 = (f32[2,96,3,192]{1,3,2,0:T(8,128)S(1)}, f32[2,96,3,192]{1,3,2,0:T(8,128)}, u32[]{:S(2)}) copy-start(f32[2,96,3,192]{1,3,2,0:T(8,128)} %copy.254) | copy-start | bytes 1327108
  1811.6 115.0 %copy-start.80 = (f32[8,768]{1,0:T(8,128)}, f32[8,768]{1,0:T(8,128)S(1)}, u32[]{:S(2)}) copy-start(f32[8,768]{1,0:T(8,128)S(1)} %all-reduce.1) | copy-start | bytes 73732
  1926.6 5.6 copy-start.91
  1926.6 5.6 copy-start.97
  1926.6 5.5 copy-start.98
  1926.6 7.1 copy-start.47
  1926.6 9.0 copy-start.68
  1928.8 9.7 copy-start.56
  1928.8 9.7 copy-start.57
  1928.8 11.3 copy-start.37
  1928.8 11.3 copy-start.41
  1932.1 10.2 copy-start.39
  1932.1 10.2 copy-start.40
  1932.1 10.2 copy-start.54
  1932.2 10.2 copy-start.55
  (72 other events, 164.4 us)
Sparse Core Ops, SparseCore 0:
  11.5 56.7 all-gather.14
  71.1 55.5 all-gather.16
  128.3 37.0 all-gather.32
  228.5 48.4 reduce-scatter.20
  283.3 38.0 all-gather.18
  395.2 48.4 reduce-scatter.22
  446.4 41.0 all-gather.22
  489.1 36.7 all-gather.20
  528.7 41.0 all-gather.24
  580.0 49.4 reduce-scatter.24
  738.4 34.3 all-gather.26
  793.0 48.4 reduce-scatter.26
  849.5 38.0 all-gather.28
  1055.5 48.4 reduce-scatter.28
  1111.2 38.0 all-gather.30
  1227.4 48.4 reduce-scatter.30
  1280.9 95.4 reduce-scatter.34
  1381.5 96.0 reduce-scatter.32
  1481.1 67.9 reduce-scatter.36
  1552.4 67.9 reduce-scatter.38
  1623.8 62.9 reduce-scatter.44
  1690.5 77.9 reduce-scatter.42
  1773.8 98.5 reduce-scatter.40
where the time goes:
time: 1960 us; the launch traced here: 1950 us
  waiting for transfers between devices  1010 us (52%)
  blocking collectives  283 us (14%)
  matrix products  263 us (13%)
  local copies, waits for them, and re-layouts  207 us (11%)
  other arithmetic  159 us (8%)
  between operations  30.7 us (2%)
    unnamed x25, waiting for transfers between devices  145 us
    all_gather x3, waiting for transfers between devices, spread_back(): return lax.all_gather(grad.astype(LOWER), 'head', axis=1, tiled=True)  110 us
    reduce_scatter x1, waiting for transfers between devices, body(): lax.psum_scatter(d_head, ('batch', 'head'), scatter_dimension=0, tiled=True)  99.9 us
    reduce_scatter x3, waiting for transfers between devices, collect_back(): lax.psum_scatter(partial_value.astype(jnp.bfloat16), 'head', scatter_dime...  97.2 us
    reduce_scatter x3, waiting for transfers between devices, collect_branch(): lax.psum_scatter(partial_value.astype(jnp.bfloat16), 'head', scatter_dime...  95.1 us
    all_gather x3, waiting for transfers between devices, spread_norm(): return lax.all_gather(normed, 'head', axis=1, tiled=True)  93.9 us
    unnamed x229, local copies, waits for them, and re-layouts  76.3 us
    reduce_scatter x1, waiting for transfers between devices, body(): lax.psum_scatter(d_wide[2], 'batch', scatter_dimension=0, tiled=True)  70.1 us
  transfers between devices with their start and end apart: 23, of which 21 were waited for; matrix products, arithmetic and copies ran while one was open for 7% of the time, Pallas kernels for 0%

commit v1 on v0

v1 whole, which is shorter than its diff:
```python
import functools

import jax
import jax.numpy as jnp
from jax import lax
from jax.experimental import pallas as pl
from jax.experimental.pallas import tpu as pltpu
from jax.sharding import PartitionSpec as P

HD = 64
FRAMES = 4
PMAX = 784
PSMALL = 196
STEP = 5
SLOTS = 208
ROWS = FRAMES * SLOTS
GROUP = 192
QKV = 3 * GROUP


EXACT = lax.Precision.HIGHEST
TEMPER = 0.05
BETA_ONE = 0.5
BETA_TWO = 0.5
RATE = 0.04
NORM_RATE = 0.3
DECAY = 0.05
ADAM_EPS = 1e-08
CLIP_AT = 1.0
LOWER = jnp.bfloat16
SINGLE = jnp.float32
ALL = ("batch", "head")
GRANT = 56 << 20

NN = (((1,), (0,)), ((), ()))
NT = (((1,), (1,)), ((), ()))
TN = (((0,), (0,)), ((), ()))


def dot(left, right, dims=NN):
    return lax.dot_general(left, right, dims, preferred_element_type=SINGLE)


def low(value):
    return value.astype(LOWER)


def layer_norm(value, gain, bias):
    center = value - jnp.mean(value, axis=-1, keepdims=True)
    spread = jnp.mean(center * center, axis=-1, keepdims=True)
    return center * lax.rsqrt(spread + 1e-06) * gain + bias


def three_parts(value):
    high = low(value)
    rest = value - high.astype(SINGLE)
    middle = low(rest)
    return high, middle, low(rest - middle.astype(SINGLE))


def frame_scores(left, right, heads):
    product = left.astype(SINGLE) * right.astype(SINGLE)
    high = low(product)
    rest = low(product - high.astype(SINGLE))
    return dot(high, heads) + dot(rest, heads)


def frame_probs(query, keys, heads):
    scores = [frame_scores(query, key, heads) * HD ** (-0.5) for key in keys]
    top = functools.reduce(jnp.maximum, scores)
    raised = [jnp.exp(score - top) for score in scores]
    total = functools.reduce(jnp.add, raised)
    return [value / total for value in raised]


def split_frames(rows):
    return [rows[SLOTS * f : SLOTS * (f + 1)] for f in range(FRAMES)]


def temporal_fwd_kernel(normed_ref, weight_ref, heads_ref, qkv_ref, mixed_ref):
    qkv_ref[0] = low(dot(normed_ref[...], weight_ref[0, :, :QKV]))
    heads = heads_ref[...]
    query, keys, values = (
        split_frames(qkv_ref[0, :, GROUP * i : GROUP * (i + 1)]) for i in range(3)
    )
    for f in range(FRAMES):
        probs = frame_probs(query[f], keys, heads)
        mixed = sum(
            dot(low(prob), heads, NT) * value.astype(SINGLE) for prob, value in zip(probs, values)
        )
        mixed_ref[0, SLOTS * f : SLOTS * (f + 1), :] = low(mixed)


def temporal_bwd_kernel(
    normed_ref, grad_ref, weight_ref, qkv_ref, mixed_ref, heads_ref, dweight_ref, dnormed_ref, dqkv
):
    heads = heads_ref[...]
    d_mixed = split_frames(low(dot(grad_ref[...], weight_ref[0, :, QKV:])))
    query, keys, values = (
        split_frames(qkv_ref[0, :, GROUP * i : GROUP * (i + 1)]) for i in range(3)
    )
    d_keys = [jnp.zeros((SLOTS, GROUP), SINGLE) for _ in range(FRAMES)]
    d_values = [jnp.zeros((SLOTS, GROUP), SINGLE) for _ in range(FRAMES)]
    scale = HD ** (-0.5)
    for f in range(FRAMES):
        probs = frame_probs(query[f], keys, heads)
        d_probs = [frame_scores(d_mixed[f], value, heads) for value in values]
        row = sum(prob * d_prob for prob, d_prob in zip(probs, d_probs))
        d_query = jnp.zeros((SLOTS, GROUP), SINGLE)
        for g in range(FRAMES):
            d_score = dot(low(probs[g] * (d_probs[g] - row)), heads, NT)
            d_query = d_query + d_score * keys[g].astype(SINGLE)
            d_keys[g] = d_keys[g] + d_score * query[f].astype(SINGLE)
            d_values[g] = d_values[g] + dot(low(probs[g]), heads, NT) * d_mixed[f].astype(SINGLE)
        dqkv[SLOTS * f : SLOTS * (f + 1), :GROUP] = low(d_query * scale)
    for g in range(FRAMES):
        dqkv[SLOTS * g : SLOTS * (g + 1), GROUP : 2 * GROUP] = low(d_keys[g] * scale)
        dqkv[SLOTS * g : SLOTS * (g + 1), 2 * GROUP :] = low(d_values[g])
    finish_backward(normed_ref, grad_ref, weight_ref, mixed_ref, dweight_ref, dnormed_ref, dqkv)


def finish_backward(
    normed_ref, grad_ref, weight_ref, mixed_ref, dweight_ref, dnormed_ref, dqkv
):
    dweight_ref[0, :, :QKV] = low(dot(normed_ref[...], dqkv[...], TN))
    dweight_ref[0, :, QKV:] = low(dot(grad_ref[...], mixed_ref[0], TN))
    d_normed = dot(dqkv[...], weight_ref[0, :, :QKV], NT)

    @pl.when(pl.program_id(0) == 0)
    def _():
        dnormed_ref[...] = d_normed

    @pl.when(pl.program_id(0) != 0)
    def _():
        dnormed_ref[...] += d_normed


def lane_pieces(pieces, rows):
    lane = lax.broadcasted_iota(jnp.int32, (rows, HD), 1)
    result = jnp.zeros((rows, HD), SINGLE)
    for number, piece in enumerate(pieces):
        result = jnp.where(lane == number, piece.astype(SINGLE), result)
    return low(result)


def spatial_fwd_kernel(
    normed_ref, weight_ref, key_extra_ref, qkv_ref, mixed_ref, extra_ref, branch_ref
):
    qkv_ref[0] = low(dot(normed_ref[...], weight_ref[0, :, :QKV]))
    one = jnp.ones((ROWS, 1), SINGLE)
    for head in range(GROUP // HD):
        at = HD * head
        query = qkv_ref[0, :, at : at + HD] * jnp.asarray(HD ** (-0.5), LOWER)
        query = jnp.concatenate([query, lane_pieces([one], ROWS)], axis=1)
        keys = jnp.concatenate(
            [qkv_ref[0, :, GROUP + at : GROUP + at + HD], key_extra_ref[...]], axis=1
        )
        values = jnp.concatenate(
            [qkv_ref[0, :, 2 * GROUP + at : 2 * GROUP + at + HD], lane_pieces([one], ROWS)], axis=1
        )
        for part in range(FRAMES):
            rows = slice(SLOTS * part, SLOTS * (part + 1))
            score = dot(query[rows], keys, NT)
            top = jnp.max(score, axis=1, keepdims=True)
            mixed = dot(low(jnp.exp(score - top)), values)
            total = mixed[:, HD : HD + 1]
            mixed_ref[0, rows, at : at + HD] = low(mixed[:, :HD] / total)
            logsum = -(top + jnp.log(total))
            extra_ref[0, rows, at : at + HD] = lane_pieces(
                [one[rows], *three_parts(logsum)], SLOTS
            )
    branch = dot(mixed_ref[0], weight_ref[0, :, QKV:], NT)

    @pl.when(pl.program_id(0) == 0)
    def _():
        branch_ref[...] = branch

    @pl.when(pl.program_id(0) != 0)
    def _():
        branch_ref[...] += branch


def spatial_bwd_kernel(
    normed_ref,
    grad_ref,
    weight_ref,
    qkv_ref,
    mixed_ref,
    extra_ref,
    key_extra_ref,
    dweight_ref,
    dnormed_ref,
    dqkv,
):
    scale = HD ** (-0.5)
    d_mixed_all = low(dot(grad_ref[...], weight_ref[0, :, QKV:]))
    one = jnp.ones((ROWS, 1), SINGLE)
    for head in range(GROUP // HD):
        at = HD * head
        query = qkv_ref[0, :, at : at + HD]
        query_long = jnp.concatenate(
            [query * jnp.asarray(scale, LOWER), extra_ref[0, :, at : at + HD]], axis=1
        )
        d_mixed = d_mixed_all[:, at : at + HD]
        delta = -jnp.sum(
            d_mixed.astype(SINGLE) * mixed_ref[0, :, at : at + HD].astype(SINGLE),
            axis=1,
            keepdims=True,
        )
        d_mixed_long = jnp.concatenate([d_mixed, lane_pieces(three_parts(delta), ROWS)], axis=1)
        d_query = jnp.zeros((ROWS, HD), SINGLE)
        for part in range(FRAMES):
            rows = slice(SLOTS * part, SLOTS * (part + 1))
            keys = qkv_ref[0, rows, GROUP + at : GROUP + at + HD]
            values = qkv_ref[0, rows, 2 * GROUP + at : 2 * GROUP + at + HD]
            keys_long = jnp.concatenate([keys, key_extra_ref[rows, :]], axis=1)
            values_long = jnp.concatenate(
                [values, lane_pieces([one[rows]] * 3, SLOTS)], axis=1
            )
            prob = jnp.exp(dot(keys_long, query_long, NT))
            d_score = low(prob * dot(values_long, d_mixed_long, NT))
            dqkv[rows, 2 * GROUP + at : 2 * GROUP + at + HD] = low(dot(low(prob), d_mixed))
            dqkv[rows, GROUP + at : GROUP + at + HD] = low(dot(d_score, query) * scale)
            d_query = d_query + dot(d_score, keys, TN)
        dqkv[:, at : at + HD] = low(d_query * scale)
    finish_backward(normed_ref, grad_ref, weight_ref, mixed_ref, dweight_ref, dnormed_ref, dqkv)


def whole(shape):
    return pl.BlockSpec(shape, lambda g: (0,) * len(shape))


def per_group(rows, width):
    return pl.BlockSpec((1, rows, width), lambda g: (g, 0, 0))


def call(kernel, inputs, in_specs, outputs, out_specs, scratch, flops, name):
    return pl.pallas_call(
        kernel,
        grid=(2,),
        in_specs=in_specs,
        out_specs=out_specs,
        out_shape=outputs,
        scratch_shapes=scratch,
        compiler_params=pltpu.CompilerParams(vmem_limit_bytes=GRANT),
        cost_estimate=pl.CostEstimate(flops=flops, bytes_accessed=16 << 20, transcendentals=0),
        name=name,
    )(*inputs)


def grouped(width, dtype=LOWER, rows=ROWS):
    return jax.ShapeDtypeStruct((2, rows, width), dtype)


def temporal_forward(normed, weight, heads):
    dim = normed.shape[1]
    return call(
        temporal_fwd_kernel,
        (normed, weight, heads),
        [whole(normed.shape), per_group(dim, dim), whole(heads.shape)],
        [grouped(QKV), grouped(GROUP)],
        [per_group(ROWS, QKV), per_group(ROWS, GROUP)],
        [],
        5 * 10**9,
        "temporal_forward",
    )


def temporal_backward(normed, grad, weight, qkv, mixed, heads):
    dim = normed.shape[1]
    return call(
        temporal_bwd_kernel,
        (normed, grad, weight, qkv, mixed, heads),
        [
            whole(normed.shape),
            whole(grad.shape),
            per_group(dim, dim),
            per_group(ROWS, QKV),
            per_group(ROWS, GROUP),
            whole(heads.shape),
        ],
        [grouped(dim, LOWER, dim), jax.ShapeDtypeStruct((ROWS, dim), SINGLE)],
        [per_group(dim, dim), whole((ROWS, dim))],
        [pltpu.VMEM((ROWS, QKV), LOWER)],
        12 * 10**9,
        "temporal_backward",
    )


def spatial_forward(normed, weight, key_extra):
    dim = normed.shape[1]
    return call(
        spatial_fwd_kernel,
        (normed, weight, key_extra),
        [whole(normed.shape), per_group(dim, dim), whole(key_extra.shape)],
        [
            grouped(QKV),
            grouped(GROUP),
            grouped(GROUP),
            jax.ShapeDtypeStruct((ROWS, dim), SINGLE),
        ],
        [
            per_group(ROWS, QKV),
            per_group(ROWS, GROUP),
            per_group(ROWS, GROUP),
            whole((ROWS, dim)),
        ],
        [],
        10 * 10**9,
        "spatial_forward",
    )


def spatial_backward(normed, grad, weight, qkv, mixed, extra, key_extra):
    dim = normed.shape[1]
    return call(
        spatial_bwd_kernel,
        (normed, grad, weight, qkv, mixed, extra, key_extra),
        [
            whole(normed.shape),
            whole(grad.shape),
            per_group(dim, dim),
            per_group(ROWS, QKV),
            per_group(ROWS, GROUP),
            per_group(ROWS, GROUP),
            whole(key_extra.shape),
        ],
        [grouped(dim, LOWER, dim), jax.ShapeDtypeStruct((ROWS, dim), SINGLE)],
        [per_group(dim, dim), whole((ROWS, dim))],
        [pltpu.VMEM((ROWS, QKV), LOWER)],
        30 * 10**9,
        "spatial_backward",
    )


class Cube:
    def __init__(self, sizes):
        self.count = sizes["batch"] * sizes["head"]
        self.mine = lax.axis_index(ALL)
        batch_bits = sizes["batch"].bit_length() - 1
        self.head_masks = [2, 1]
        self.batch_masks = [4 << k for k in reversed(range(batch_bits))]

    def swap(self, value, mask):
        return lax.ppermute(value, ALL, [(i, i ^ mask) for i in range(self.count)])

    def has(self, mask):
        return (self.mine & mask) != 0

    def join(self, value, mask):
        other = self.swap(value, mask)
        has = self.has(mask)
        both = jnp.stack([jnp.where(has, other, value), jnp.where(has, value, other)], axis=-3)
        shape = value.shape
        return both.reshape(*shape[:-3], 2 * shape[-3], *shape[-2:])

    def shed(self, value, mask):
        shape = value.shape
        pair = value.reshape(*shape[:-3], shape[-3] // 2, 2, *shape[-2:])
        first, last = pair[..., 0, :, :], pair[..., 1, :, :]
        has = self.has(mask)
        send = low(jnp.where(has, first, last))
        keep = jnp.where(has, last, first).astype(SINGLE)
        return keep + self.swap(send, mask).astype(SINGLE)

    def gather_block(self, shard, late):
        value = shard[None]
        for mask in self.batch_masks[:-1]:
            value = self.join(value, mask)
        if late:
            value = jnp.stack([value, self.swap(value, 2)])
            value = self.join(value, self.batch_masks[-1])
        else:
            value = self.join(value, self.batch_masks[-1])
            value = jnp.stack([value, self.swap(value, 2)])
        value = value.reshape(2, -1, shard.shape[-1])
        return value, self.swap(value, 1)

    def reduce_block(self, own, other, rows, late):
        value = own.astype(SINGLE) + self.swap(other, 1).astype(SINGLE)
        value = value.reshape(2, -1, rows, own.shape[-1])
        masks = self.batch_masks[::-1]
        if late:
            value = self.shed(value, masks[0])
        value = value[0] + self.swap(low(value[1]), 2).astype(SINGLE)
        if not late:
            value = self.shed(value, masks[0])
        for mask in masks[1:]:
            value = self.shed(value, mask)
        return value[0]

    def gather_rows(self, shard):
        value = shard[None]
        for mask in self.batch_masks + self.head_masks:
            value = self.join(value, mask)
        return value.reshape(-1, shard.shape[-1])

    def reduce_rows(self, value, rows):
        value = value.reshape(-1, rows, value.shape[-1])
        for mask in (self.batch_masks + self.head_masks)[::-1]:
            value = self.shed(value, mask)
        return value[0]

    def total(self, value):
        for mask in (self.batch_masks + self.head_masks)[::-1]:
            value = value + self.swap(value, mask)
        return value

    def swap_frames(self, parts):
        return [parts[0]] + [self.swap(parts[r], r) for r in range(1, FRAMES)]


def adam_step(master, first, second, grad, factor, rate):
    clipped = grad * factor
    first_new = BETA_ONE * first + (1.0 - BETA_ONE) * clipped
    second_new = BETA_TWO * second + (1.0 - BETA_TWO) * clipped * clipped
    first_hat = first_new / (1.0 - BETA_ONE**STEP)
    second_hat = second_new / (1.0 - BETA_TWO**STEP)
    master_new = master - rate * (first_hat / (jnp.sqrt(second_hat) + ADAM_EPS) + DECAY * master)
    return (master_new, first_new, second_new)


def gelu_slope(hidden):
    _, back = jax.vjp(jax.nn.gelu, hidden)
    return back(jnp.ones_like(hidden))[0]


def body(sizes, *args):
    patches, bucket, labels, partner = args[:4]
    masters, firsts, seconds = (args[4:12], args[12:20], args[20:28])
    patch_weight, norm_params, head_weight, proj_weight, attn_in, attn_out, up, down = masters
    cube = Cube(sizes)
    clips = sizes["batch"]
    dim = norm_params.shape[1] * cube.count
    classes, proj = head_weight.shape[1], proj_weight.shape[1]
    rows_wide, rows_small = attn_in.shape[1], patch_weight.shape[0]
    place = lax.axis_index("head")

    early = jnp.concatenate(
        [low(patch_weight), low(norm_params).T, jnp.zeros((rows_small, 120), LOWER)], axis=1
    )
    early = cube.gather_rows(early)
    patch_copy, norms = early[:, :dim], early[:, dim : dim + 8].astype(SINGLE).T
    attn_shards = [
        jnp.concatenate(
            [low(attn_in[i]).reshape(rows_wide, QKV), low(attn_out[i]).T], axis=1
        )
        for i in range(2)
    ]
    attn_w = [cube.gather_block(attn_shards[i], i == 1) for i in range(2)]
    up_w = cube.gather_block(low(up), False)
    down_w = cube.gather_block(low(down).T, True)
    small = jnp.concatenate(
        [
            low(head_weight),
            low(proj_weight),
            jnp.zeros((rows_small, -(classes + proj) % 128), LOWER),
        ],
        axis=1,
    )
    small = cube.gather_rows(small)
    head_copy, proj_copy = small[:, :classes], small[:, classes : classes + proj]

    patch_count = jnp.where(bucket == 1, PMAX, PSMALL)
    blocks = jnp.pad(patches[0], ((0, ROWS - PMAX), (0, 0))).reshape(FRAMES, SLOTS, -1)
    blocks = jnp.where((place & 1) != 0, blocks[jnp.array([1, 0, 3, 2])], blocks)
    blocks = jnp.where((place & 2) != 0, blocks[jnp.array([2, 3, 0, 1])], blocks)
    by_frame = blocks.reshape(ROWS, -1)
    by_slot = jnp.concatenate(cube.swap_frames(list(blocks)))
    offset = jnp.arange(SLOTS)[None, :]
    number = (place ^ jnp.arange(FRAMES))[:, None]
    frame_valid = ((number * SLOTS + offset) < patch_count).reshape(ROWS, 1).astype(SINGLE)
    slot_valid = (jnp.broadcast_to(place * SLOTS + offset, (FRAMES, SLOTS)) < patch_count).reshape(
        ROWS, 1
    ).astype(SINGLE)
    heads = (
        jnp.arange(GROUP)[:, None] // HD == jnp.arange(128)[None, :]
    ).astype(LOWER)
    lane = jnp.arange(HD)[None, :]
    key_extra = low(
        jnp.where(lane == 0, jnp.where(frame_valid > 0, 0.0, -1e30), (lane < 4).astype(SINGLE))
    )

    start_slot = dot(by_slot, patch_copy) * slot_valid
    start_frame = dot(by_frame, patch_copy) * frame_valid
    normed_t = low(layer_norm(start_slot, norms[0], norms[1]))
    qkv_t, mixed_t = zip(*(temporal_forward(normed_t, weight, heads) for weight in attn_w[0]))
    order = (0, 2, 1, 3)
    pieces = {m: mixed_t[m % 2][m // 2] for m in range(4)}
    parts = [
        jnp.concatenate(
            [pieces[m ^ r][SLOTS * r : SLOTS * (r + 1)] for m in order], axis=1
        )
        for r in range(FRAMES)
    ]
    mixed_frame = jnp.concatenate(cube.swap_frames(parts))
    out_first = jnp.concatenate(
        [attn_w[0][m % 2][m // 2][:, QKV:] for m in order], axis=1
    )
    resid_one = start_frame + dot(mixed_frame, out_first, NT)
    normed_s = low(layer_norm(resid_one, norms[2], norms[3]))
    qkv_s, mixed_s, extra_s, branch_s = zip(
        *(spatial_forward(normed_s, weight, key_extra) for weight in attn_w[1])
    )
    resid_two = resid_one + (branch_s[0] + branch_s[1])
    normed_m = low(layer_norm(resid_two, norms[4], norms[5]))
    hidden = [[dot(normed_m, up_w[c][y]) for y in range(2)] for c in range(2)]
    activated = [[low(jax.nn.gelu(hidden[c][y])) for y in range(2)] for c in range(2)]
    slope = [[low(gelu_slope(hidden[c][y])) for y in range(2)] for c in range(2)]
    resid_three = resid_two + sum(
        dot(activated[c][y], down_w[c][y], NT) for c in range(2) for y in range(2)
    )
    final_norm, final_back = jax.vjp(layer_norm, resid_three, norms[6], norms[7])
    sums = jnp.sum(final_norm * frame_valid, axis=0, keepdims=True)

    for mask in cube.head_masks[::-1]:
        sums = sums + cube.swap(sums, mask)
    facts = jnp.stack([labels[0], partner[0], FRAMES * patch_count[0]]).astype(SINGLE)
    gathered = jnp.concatenate([sums, jnp.pad(facts, (0, 125))[None]], axis=1)[None]
    for mask in cube.batch_masks:
        gathered = cube.join(gathered, mask)
    gathered = gathered[:, 0]
    all_labels, all_partners = (gathered[:, dim + i].astype(jnp.int32) for i in range(2))
    pooled_low = low(gathered[:, :dim] / gathered[:, dim + 2 : dim + 3])
    logits = dot(pooled_low, head_copy)
    label_hot = (jnp.arange(classes)[None, :] == all_labels[:, None]).astype(SINGLE)
    cross = jax.nn.logsumexp(logits, axis=1) - jnp.sum(logits * label_hot, axis=1)
    d_logits = low(jax.nn.softmax(logits, axis=1) - label_hot)
    embedding = dot(pooled_low, proj_copy)
    inverse = lax.rsqrt(jnp.sum(embedding * embedding, axis=1, keepdims=True) + 1e-06)
    unit = embedding * inverse
    ids = jnp.arange(clips)
    mate_hot = (ids[None, :] == all_partners[:, None]).astype(SINGLE)
    similar = jnp.dot(unit, unit.T, precision=EXACT) / TEMPER
    masked = jnp.where(ids[None, :] == ids[:, None], -1e30, similar)
    contrast = jax.nn.logsumexp(masked, axis=1) - jnp.sum(similar * mate_hot, axis=1)
    loss_sum = jnp.sum(cross + contrast)
    d_similar = (jax.nn.softmax(masked, axis=1) - mate_hot) / TEMPER
    d_unit = jnp.dot(d_similar + d_similar.T, unit, precision=EXACT)
    d_embed = low(
        inverse * d_unit
        - embedding
        * (inverse * inverse * inverse)
        * jnp.sum(embedding * d_unit, axis=1, keepdims=True)
    )
    d_head = lax.dynamic_slice_in_dim(
        dot(pooled_low, d_logits, TN), cube.mine * rows_small, rows_small, 0
    )
    d_proj = lax.dynamic_slice_in_dim(
        dot(pooled_low, d_embed, TN), cube.mine * rows_small, rows_small, 0
    )
    d_pooled = dot(d_logits, head_copy, NT) + dot(d_embed, proj_copy, NT)
    d_pooled = lax.dynamic_slice_in_dim(d_pooled, lax.axis_index("batch"), 1, 0)
    row_count = (FRAMES * patch_count[0]).astype(SINGLE)

    d_resid, d_gain_f, d_bias_f = final_back(frame_valid * (d_pooled / row_count))
    d_rows = low(d_resid)
    d_hidden = [
        [low(dot(d_rows, down_w[c][y]) * slope[c][y].astype(SINGLE)) for y in range(2)]
        for c in range(2)
    ]
    d_down = [
        jnp.stack([low(dot(d_rows, activated[c][y], TN)) for y in range(2)]) for c in range(2)
    ]
    d_down = cube.reduce_block(d_down[0], d_down[1], rows_wide, True)
    d_up = [
        jnp.stack([low(dot(normed_m, d_hidden[c][y], TN)) for y in range(2)]) for c in range(2)
    ]
    d_up = cube.reduce_block(d_up[0], d_up[1], rows_wide, False)
    d_normed = sum(dot(d_hidden[c][y], up_w[c][y], NT) for c in range(2) for y in range(2))
    _, back = jax.vjp(layer_norm, resid_two, norms[4], norms[5])
    d_local, d_gain_m, d_bias_m = back(d_normed)
    d_resid = d_resid + d_local
    d_rows = low(d_resid)
    d_second, d_normed = [None, None], []
    for c in (1, 0):
        d_second[c], part = spatial_backward(
            normed_s, d_rows, attn_w[1][c], qkv_s[c], mixed_s[c], extra_s[c], key_extra
        )
        d_normed.append(part)
    d_second = cube.reduce_block(d_second[0], d_second[1], rows_wide, True)
    _, back = jax.vjp(layer_norm, resid_one, norms[2], norms[3])
    d_local, d_gain_s, d_bias_s = back(d_normed[0] + d_normed[1])
    d_resid = d_resid + d_local
    d_rows = jnp.concatenate(cube.swap_frames(split_frames(low(d_resid))))
    d_first, d_normed = [None, None], []
    for c in (1, 0):
        d_first[c], part = temporal_backward(
            normed_t, d_rows, attn_w[0][c], qkv_t[c], mixed_t[c], heads
        )
        d_normed.append(part)
    d_first = cube.reduce_block(d_first[0], d_first[1], rows_wide, False)
    _, back = jax.vjp(layer_norm, start_slot, norms[0], norms[1])
    d_local, d_gain_t, d_bias_t = back(d_normed[0] + d_normed[1])
    d_start = low((d_rows.astype(SINGLE) + d_local) * slot_valid)
    d_patch = cube.reduce_rows(low(dot(by_slot, d_start, TN)), rows_small)
    d_norms = cube.total(
        jnp.stack(
            [d_gain_t, d_bias_t, d_gain_s, d_bias_s, d_gain_m, d_bias_m, d_gain_f, d_bias_f]
        )
    )
    d_norms = lax.dynamic_slice_in_dim(
        d_norms.reshape(8, cube.count, rows_small), cube.mine, 1, 1
    )[:, 0]
    d_in = jnp.stack([d_first[:, :QKV], d_second[:, :QKV]]).reshape(attn_in.shape)
    d_out = jnp.stack([d_first[:, QKV:].T, d_second[:, QKV:].T])
    grads = (d_patch, d_norms, d_head, d_proj, d_in, d_out, d_up, d_down.T)

    squares = sum(jnp.sum(grad * grad) for grad in grads)
    grad_norm = jnp.sqrt(cube.total(squares.reshape(1, 1)))[0, 0]
    factor = jnp.minimum(1.0, CLIP_AT / (grad_norm + 1e-06))
    updates = []
    for index, (master, first, second, grad) in enumerate(zip(masters, firsts, seconds, grads)):
        rate = NORM_RATE if index == 1 else RATE
        updates.extend(adam_step(master, first, second, grad, factor, rate))
    return (loss_sum, grad_norm, *updates)


def solution(mesh):
    placed = (
        P("batch", "head", None),
        P("batch"),
        P("batch"),
        P("batch"),
        P(("batch", "head"), None),
        P(None, ("batch", "head")),
        P(("batch", "head"), None),
        P(("batch", "head"), None),
        P(None, "batch", None, "head"),
        P(None, "head", "batch"),
        P("batch", "head"),
        P("head", "batch"),
        P(("batch", "head"), None),
        P(None, ("batch", "head")),
        P(("batch", "head"), None),
        P(("batch", "head"), None),
        P(None, "batch", None, "head"),
        P(None, "head", "batch"),
        P("batch", "head"),
        P("head", "batch"),
        P(("batch", "head"), None),
        P(None, ("batch", "head")),
        P(("batch", "head"), None),
        P(("batch", "head"), None),
        P(None, "batch", None, "head"),
        P(None, "head", "batch"),
        P("batch", "head"),
        P("head", "batch"),
    )
    return jax.shard_map(
        functools.partial(body, dict(mesh.shape)),
        mesh=mesh,
        in_specs=placed,
        out_specs=(
            P(),
            P(),
            P(("batch", "head"), None),
            P(("batch", "head"), None),
            P(("batch", "head"), None),
            P(None, ("batch", "head")),
            P(None, ("batch", "head")),
            P(None, ("batch", "head")),
            P(("batch", "head"), None),
            P(("batch", "head"), None),
            P(("batch", "head"), None),
            P(("batch", "head"), None),
            P(("batch", "head"), None),
            P(("batch", "head"), None),
            P(None, "batch", None, "head"),
            P(None, "batch", None, "head"),
            P(None, "batch", None, "head"),
            P(None, "head", "batch"),
            P(None, "head", "batch"),
            P(None, "head", "batch"),
            P("batch", "head"),
            P("batch", "head"),
            P("batch", "head"),
            P("head", "batch"),
            P("head", "batch"),
            P("head", "batch"),
        ),
        check_vma=False,
    )
```

time: 1960 us -> 696 us (0.36)
  waiting for transfers between devices: 1010 us -> 203 us
  blocking collectives: 283 us -> 0 us
  matrix products: 263 us -> 78.4 us
  Pallas kernels: 0 us -> 158 us
  local copies, waits for them, and re-layouts: 207 us -> 51.5 us
  starting transfers between devices: 2.44 us -> 87.6 us
  other arithmetic: 159 us -> 90.8 us
    reduce_scatter x11 -> x0, waiting for transfers between devices: 557 us -> none  [the longest x1 99.9 us: body(): lax.psum_scatter(d_head, ('batch', 'head'), scatter_dimension=0, tiled=True)]
    all_gather x10 -> x0, waiting for transfers between devices: 304 us -> none  [the longest x3 110 us: spread_back(): return lax.all_gather(grad.astype(LOWER), 'head', axis=1, tiled=True)]
    ppermute x0 -> x79, waiting for transfers between devices: none -> 203 us  [swap(): return lax.ppermute(value, ALL, [(i, i ^ mask) for i in range(self.count)])]
    all_gather x5 -> x0, blocking collectives: 175 us -> none  [the longest x1 43.5 us: gather_small(): lax.all_gather(masters[3].astype(LOWER), ('batch', 'head'), axis=0, tiled...]
    dot_general x56 -> x36, matrix products: 239 us -> 78.4 us  [the longest x34 77.9 us: dot(): return lax.dot_general(left, right, dims, preferred_element_type=SINGLE)]
    pallas_call x0 -> x8, Pallas kernels: none -> 158 us  [call(): pl.pallas_call(kernel, grid=(2,), in_specs=in_specs, out_specs=out_specs,...]
    unnamed x25 -> x0, waiting for transfers between devices: 145 us -> none
    ppermute x0 -> x79, starting transfers between devices: none -> 87.6 us  [swap(): return lax.ppermute(value, ALL, [(i, i ^ mask) for i in range(self.count)])]
  transfers between devices with their start and end apart: 23 -> 79, of which waited for: 21 -> 42; matrix products, arithmetic and copies ran while one was open for 7% -> 17% of each run, Pallas kernels for 0% -> 9%
where the time goes in v1:
time: 696 us; the launch traced here: 685 us
  waiting for transfers between devices  203 us (29%)
  Pallas kernels  158 us (23%)
  other arithmetic  90.8 us (13%)
  starting transfers between devices  87.6 us (13%)
  matrix products  78.4 us (11%)
  local copies, waits for them, and re-layouts  51.5 us (7%)
  between operations  16 us (2%)
    ppermute x79, waiting for transfers between devices, swap(): return lax.ppermute(value, ALL, [(i, i ^ mask) for i in range(self.count)])  203 us
    pallas_call x8, Pallas kernels, call(): pl.pallas_call(kernel, grid=(2,), in_specs=in_specs, out_specs=out_specs,...  158 us
    ppermute x79, starting transfers between devices, swap(): return lax.ppermute(value, ALL, [(i, i ^ mask) for i in range(self.count)])  87.6 us
    dot_general x34, matrix products, dot(): return lax.dot_general(left, right, dims, preferred_element_type=SINGLE)  77.9 us
    unnamed x316, local copies, waits for them, and re-layouts  28.8 us
  transfers between devices with their start and end apart: 79, of which 42 were waited for; matrix products, arithmetic and copies ran while one was open for 17% of the time, Pallas kernels for 9%

profile of v1, /device:TPU:0, one launch (start us, length us, event | category | flops | bytes accessed | tf_op | source)
XLA Modules:
  0.0 685.1 jit_solution(16573689683947486108)
XLA Ops:
  2.5 4.0 collective-permute-start.36
  11.0 2.9 collective-permute-start.8
  28.8 3.2 collective-permute-done.37
  33.2 3.3 collective-permute-done.1
  42.3 6.3 collective-permute-done.24
  54.2 6.0 collective-permute-done.9
  60.9 5.6 collective-permute-done.17
  67.9 4.8 collective-permute-done.25
  74.2 2.8 collective-permute-done.22
  81.5 2.4 collective-permute-start.23
  84.2 9.0 %collective-permute-done.10 = bf16[4,96,768]{2,1,0:T(8,128)(2,1)S(1)} collective-permute-done((bf16[4,96,768]{2,1,0:T(8,128)(2,1)S(1)}, bf16[4,96,768]{2,1,0:T(8,128)(2,1)S(1)}, u32[]{:S(2)}, u32[]{:S(2)}) %collective-permute-start.10) | collective-permute-done | bytes 589856 | tf_op jit(solution)/shard_map/ppermute | solution.py:345
  95.9 7.4 %collective-permute-done.23 = bf16[4,96,768]{2,1,0:T(8,128)(2,1)S(1)} collective-permute-done((bf16[4,96,768]{2,1,0:T(8,128)(2,1)S(1)}, bf16[4,96,768]{2,1,0:T(8,128)(2,1)S(1)}, u32[]{:S(2)}, u32[]{:S(2)}) %collective-permute-start.23) | collective-permute-done | bytes 589856 | tf_op jit(solution)/shard_map/ppermute | solution.py:345
  115.4 19.4 %collective-permute-done.11 = bf16[8,96,768]{2,1,0:T(8,128)(2,1)S(1)} collective-permute-done((bf16[8,96,768]{2,1,0:T(8,128)(2,1)S(1)}, bf16[8,96,768]{2,1,0:T(8,128)(2,1)S(1)}, u32[]{:S(2)}, u32[]{:S(2)}) %collective-permute-start.11) | collective-permute-done | bytes 1179680 | tf_op jit(solution)/shard_map/ppermute | solution.py:345
  138.0 3.0 fusion.79
  143.4 15.4 %collective-permute-done.27 = bf16[2,4,96,768]{3,2,1,0:T(8,128)(2,1)S(1)} collective-permute-done((bf16[2,4,96,768]{3,2,1,0:T(8,128)(2,1)S(1)}, bf16[2,4,96,768]{3,2,1,0:T(8,128)(2,1)S(1)}, u32[]{:S(2)}, u32[]{:S(2)}) %collective-permute-start.27) | collective-permute-done | bytes 1179680 | tf_op jit(solution)/shard_map/ppermute | solution.py:345
  160.8 8.8 %temporal_forward.2 = (bf16[2,832,576]{2,1,0:T(8,128)(2,1)}, bf16[2,832,192]{2,1,0:T(8,128)(2,1)}) custom-call(bf16[832,768]{1,0:T(8,128)(2,1)} %add_convert_fusion.3.normed_ref, bf16[2,768,768]{2,1,0:T(8,128)(2,1)} %pad_maximum_fusion.1.weight_ref, bf16[192,128]{1,0:T(8,128)(2,1)} %fusion.122.heads_ref), custom_call_target="tpu_custom_call" | custom-call | flops 5000000000 | bytes 16777216 | tf_op jit(solution)/shard_map/temporal_forward/pallas_call | solution.py:238
  171.9 8.9 %temporal_forward.3 = (bf16[2,832,576]{2,1,0:T(8,128)(2,1)}, bf16[2,832,192]{2,1,0:T(8,128)(2,1)}) custom-call(bf16[832,768]{1,0:T(8,128)(2,1)} %add_convert_fusion.3.normed_ref, bf16[2,768,768]{2,1,0:T(8,128)(2,1)} %collective-permute-done.12.weight_ref, bf16[192,128]{1,0:T(8,128)(2,1)} %fusion.122.heads_ref), custom_call_target="tpu_custom_call" | custom-call | flops 5000000000 | bytes 16777216 | tf_op jit(solution)/shard_map/temporal_forward/pallas_call | solution.py:238
  184.8 2.9 pad_maximum_fusion.3
  193.1 5.9 collective-permute-done.14
  202.5 27.4 %spatial_forward.2 = (bf16[2,832,576]{2,1,0:T(8,128)(2,1)}, bf16[2,832,192]{2,1,0:T(8,128)(2,1)}, bf16[2,832,192]{2,1,0:T(8,128)(2,1)}, f32[832,768]{1,0:T(8,128)}) custom-call(bf16[832,768]{1,0:T(8,128)(2,1)} %add_convert_fusion.2.normed_ref, bf16[2,768,768]{2,1,0:T(8,128)(2,1)} %bitcast.77.weight_ref, bf16[832,64]{1,0:T(8,128)(2,1)} %select_convert_fusion.9.key_extra_ref), custom_call_target="tpu_custom_call" | custom-call | flops 10000000000 | bytes 16777216 | tf_op jit(solution)/shard_map/spatial_forward/pallas_call | solution.py:238
  229.9 18.4 %spatial_forward.3 = (bf16[2,832,576]{2,1,0:T(8,128)(2,1)}, bf16[2,832,192]{2,1,0:T(8,128)(2,1)}, bf16[2,832,192]{2,1,0:T(8,128)(2,1)}, f32[832,768]{1,0:T(8,128)}) custom-call(bf16[832,768]{1,0:T(8,128)(2,1)} %add_convert_fusion.2.normed_ref, bf16[2,768,768]{2,1,0:T(8,128)(2,1)} %collective-permute-done.20.weight_ref, ...), custom_call_target="tpu_custom_call" | custom-call | flops 10000000000 | bytes 16777216 | tf_op jit(solution)/shard_map/spatial_forward/pallas_call | solution.py:238
  248.3 2.9 fusion.193
  253.5 3.3 fusion.205
  256.8 3.3 fusion.75
  260.2 3.4 fusion.72
  267.4 2.9 fusion.73
  270.4 3.4 fusion.197
  281.2 4.4 collective-permute-start.33
  310.9 3.4 fusion.31
  323.2 2.6 fusion.39
  325.8 3.1 fusion.38
  328.9 2.6 fusion.37
  332.7 2.5 fusion.207
  335.1 3.6 multiply_convert_fusion.1
  338.7 2.5 fusion.35
  341.2 3.5 multiply_convert_fusion.2
  344.7 2.5 fusion.34
  347.2 2.5 fusion.71
  349.7 3.5 multiply_reduce_fusion.1
  356.1 27.7 %spatial_backward.3 = (bf16[2,768,768]{2,1,0:T(8,128)(2,1)}, f32[832,768]{1,0:T(8,128)}) custom-call(bf16[832,768]{1,0:T(8,128)(2,1)} %add_convert_fusion.2.normed_ref, bf16[832,768]{1,0:T(8,128)(2,1)} %fusion.178.grad_ref, bf16[2,768,768]{2,1,0:T(8,128)(2,1)} %bitcast.77.weight_ref, bf16[2,832,576]{2,1,0:T(8,128)(2,1)} %get-tuple-element.54.qkv_ref, ...), custom_call_target="tpu_custom_call" | custom-call | flops 30000001024 | bytes 16777216 | tf_op jit(solution)/shard_map/spatial_backward/pallas_call | solution.py:238
  383.8 28.5 %spatial_backward.2 = (bf16[2,768,768]{2,1,0:T(8,128)(2,1)}, f32[832,768]{1,0:T(8,128)}) custom-call(bf16[832,768]{1,0:T(8,128)(2,1)} %add_convert_fusion.2.normed_ref, bf16[832,768]{1,0:T(8,128)(2,1)} %fusion.178.grad_ref, bf16[2,768,768]{2,1,0:T(8,128)(2,1)} %collective-permute-done.20.weight_ref, bf16[2,832,576]{2,1,0:T(8,128)(2,1)} %get-tuple-element.50.qkv_ref, ...), custom_call_target="tpu_custom_call" | custom-call | flops 30000001024 | bytes 16777216 | tf_op jit(solution)/shard_map/spatial_backward/pallas_call | solution.py:238
  412.4 2.9 multiply_reduce_fusion.2
  420.4 2.5 fusion.33
  422.9 5.5 collective-permute-done.43
  428.4 6.5 collective-permute-done.42
  436.7 18.9 %temporal_backward.3 = (bf16[2,768,768]{2,1,0:T(8,128)(2,1)}, f32[832,768]{1,0:T(8,128)}) custom-call(bf16[832,768]{1,0:T(8,128)(2,1)} %add_convert_fusion.3.normed_ref, bf16[832,768]{1,0:T(8,128)(2,1)} %pad_maximum_fusion.8.grad_ref, bf16[2,768,768]{2,1,0:T(8,128)(2,1)} %pad_maximum_fusion.1.weight_ref, bf16[2,832,576]{2,1,0:T(8,128)(2,1)} %get-tuple-element.60.qkv_ref, ...), custom_call_target="tpu_custom_call" | custom-call | flops 12000000000 | bytes 16777216 | tf_op jit(solution)/shard_map/temporal_backward/pallas_call | solution.py:238
  455.6 19.3 %temporal_backward.2 = (bf16[2,768,768]{2,1,0:T(8,128)(2,1)}, f32[832,768]{1,0:T(8,128)}) custom-call(bf16[832,768]{1,0:T(8,128)(2,1)} %add_convert_fusion.3.normed_ref, bf16[832,768]{1,0:T(8,128)(2,1)} %pad_maximum_fusion.8.grad_ref, bf16[2,768,768]{2,1,0:T(8,128)(2,1)} %collective-permute-done.12.weight_ref, ...), custom_call_target="tpu_custom_call" | custom-call | flops 12000000000 | bytes 16777216 | tf_op jit(solution)/shard_map/temporal_backward/pallas_call | solution.py:238
  475.0 3.1 multiply_reduce_fusion.3
  479.4 2.8 convolution_convert_fusion.8
  483.2 2.5 fusion.32
  492.9 6.2 collective-permute-done.50
  510.9 4.0 collective-permute-done.53
  525.1 2.9 convert_add_fusion.2
  543.6 13.6 %collective-permute-done.60 = bf16[2,4,96,768]{3,2,1,0:T(8,128)(2,1)S(1)} collective-permute-done((bf16[2,4,96,768]{3,2,1,0:T(8,128)(2,1)S(1)}, bf16[2,4,96,768]{3,2,1,0:T(8,128)(2,1)S(1)}, u32[]{:S(2)}, u32[]{:S(2)}) %collective-permute-start.60) | collective-permute-done | bytes 1179680 | tf_op jit(solution)/shard_map/ppermute | solution.py:345
  562.2 20.3 %collective-permute-done.70 = bf16[2,4,96,768]{3,2,1,0:T(8,128)(2,1)S(1)} collective-permute-done((bf16[2,4,96,768]{3,2,1,0:T(8,128)(2,1)S(1)}, bf16[2,4,96,768]{3,2,1,0:T(8,128)(2,1)S(1)}, u32[]{:S(2)}, u32[]{:S(2)}) %collective-permute-start.70) | collective-permute-done | bytes 1179680 | tf_op jit(solution)/shard_map/ppermute | solution.py:345
  587.4 11.4 %collective-permute-done.61 = bf16[4,96,768]{2,1,0:T(8,128)(2,1)S(1)} collective-permute-done((bf16[4,96,768]{2,1,0:T(8,128)(2,1)S(1)}, bf16[4,96,768]{2,1,0:T(8,128)(2,1)S(1)}, u32[]{:S(2)}, u32[]{:S(2)}) %collective-permute-start.61) | collective-permute-done | bytes 589856 | tf_op jit(solution)/shard_map/ppermute | solution.py:345
  601.4 6.2 collective-permute-done.71
  608.9 2.7 collective-permute-start.63
  611.6 4.4 collective-permute-done.67
  620.1 2.5 collective-permute-start.73
  623.6 2.6 collective-permute-start.57
  626.3 3.5 collective-permute-done.68
  635.4 6.3 collective-permute-done.58
  652.0 2.5 collective-permute-start.76
  (722 shorter events, 236.2 us)
Async XLA Ops:
  2.5 23.2 %collective-permute-start.36 = (bf16[1,24,768]{2,1,0:T(8,128)(2,1)S(1)}, bf16[1,24,768]{2,1,0:T(8,128)(2,1)S(1)}, u32[]{:S(2)}, u32[]{:S(2)}) collective-permute-start(bf16[1,24,768]{2,1,0:T(8,128)(2,1)S(1)} %maximum_bitcast_fusion.9), channel_id=1, source_target_pairs={{0,16},{1,17},{2,18},{3,19},{4,20},{5,21},{6,22},{7,23},{8,24},{9,... | collective-permute-start | bytes 110600 | tf_op jit(solution)/shard_map/ppermute | solution.py:345
  9.9 28.7 %collective-permute-start.16 = (bf16[1,96,768]{2,1,0:T(8,128)(2,1)}, bf16[1,96,768]{2,1,0:T(8,128)(2,1)}, u32[]{:S(2)}, u32[]{:S(2)}) collective-permute-start(bf16[1,96,768]{2,1,0:T(8,128)(2,1)} %maximum_bitcast_fusion.5), channel_id=1, source_target_pairs={{0,16},{1,17},{2,18},{3,19},{4,20},{5,21},{6,22},{7,23},{8,24},{9,... | collective-permute-start | bytes 442376 | tf_op jit(solution)/shard_map/ppermute | solution.py:345
  11.0 28.6 %collective-permute-start.8 = (bf16[1,96,768]{2,1,0:T(8,128)(2,1)}, bf16[1,96,768]{2,1,0:T(8,128)(2,1)}, u32[]{:S(2)}, u32[]{:S(2)}) collective-permute-start(bf16[1,96,768]{2,1,0:T(8,128)(2,1)} %maximum_bitcast_fusion.4), channel_id=1, source_target_pairs={{0,16},{1,17},{2,18},{3,19},{4,20},{5,21},{6,22},{7,23},{8,24},{9,... | collective-permute-start | bytes 442376 | tf_op jit(solution)/shard_map/ppermute | solution.py:345
  14.1 13.5 %collective-permute-start = (bf16[1,24,896]{2,1,0:T(8,128)(2,1)S(1)}, bf16[1,24,896]{2,1,0:T(8,128)(2,1)S(1)}, u32[]{:S(2)}, u32[]{:S(2)}) collective-permute-start(bf16[1,24,896]{2,1,0:T(8,128)(2,1)S(1)} %maximum_bitcast_fusion.8), channel_id=1, source_target_pairs={{0,16},{1,17},{2,18},{3,19},{4,20},{5,21},{6,22},{7,23},{8,24},{9,... | collective-permute-start | bytes 129032 | tf_op jit(solution)/shard_map/ppermute | solution.py:345
  18.0 91.4 %collective-permute-start.7 = (bf16[208,768]{1,0:T(8,128)(2,1)}, bf16[208,768]{1,0:T(8,128)(2,1)}, u32[]{:S(2)}, u32[]{:S(2)}) collective-permute-start(bf16[208,768]{1,0:T(8,128)(2,1)} %get-tuple-element.281), channel_id=1, source_target_pairs={{0,3},{1,2},{2,1},{3,0},{4,7},{5,6},{6,5},{7,4},{8,11},{9,10},{10,... | collective-permute-start | bytes 958472 | tf_op jit(solution)/shard_map/ppermute | solution.py:345
  25.7 84.3 %collective-permute-start.6 = (bf16[208,768]{1,0:T(8,128)(2,1)}, bf16[208,768]{1,0:T(8,128)(2,1)S(1)}, u32[]{:S(2)}, u32[]{:S(2)}) collective-permute-start(bf16[208,768]{1,0:T(8,128)(2,1)} %get-tuple-element.282), channel_id=1, source_target_pairs={{0,2},{1,3},{2,0},{3,1},{4,6},{5,7},{6,4},{7,5},{8,10},{9,11},{10,... | collective-permute-start | bytes 958472 | tf_op jit(solution)/shard_map/ppermute | solution.py:345
  32.0 4.5 collective-permute-start.1
  36.5 12.1 %collective-permute-start.24 = (bf16[1,96,768]{2,1,0:T(8,128)(2,1)S(1)}, bf16[1,96,768]{2,1,0:T(8,128)(2,1)S(1)}, u32[]{:S(2)}, u32[]{:S(2)}) collective-permute-start(bf16[1,96,768]{2,1,0:T(8,128)(2,1)S(1)} %convert_bitcast_fusion.1), channel_id=1, source_target_pairs={{0,16},{1,17},{2,18},{3,19},{4,20},{5,21},{6,22},{7,23},{8,24},{9,... | collective-permute-start | bytes 442376 | tf_op jit(solution)/shard_map/ppermute | solution.py:345
  38.7 11.5 %collective-permute-start.21 = (bf16[1,96,768]{2,1,0:T(8,128)(2,1)S(1)}, bf16[1,96,768]{2,1,0:T(8,128)(2,1)S(1)}, u32[]{:S(2)}, u32[]{:S(2)}) collective-permute-start(bf16[1,96,768]{2,1,0:T(8,128)(2,1)S(1)} %convert_bitcast_fusion.2), channel_id=1, source_target_pairs={{0,16},{1,17},{2,18},{3,19},{4,20},{5,21},{6,22},{7,23},{8,24},{9,... | collective-permute-start | bytes 442376 | tf_op jit(solution)/shard_map/ppermute | solution.py:345
  39.6 11.4 %collective-permute-start.38 = (bf16[4,24,768]{2,1,0:T(8,128)(2,1)S(1)}, bf16[4,24,768]{2,1,0:T(8,128)(2,1)S(1)}, u32[]{:S(2)}, u32[]{:S(2)}) collective-permute-start(bf16[4,24,768]{2,1,0:T(8,128)(2,1)S(1)} %bitcast.815), channel_id=1, source_target_pairs={{0,4},{1,5},{2,6},{3,7},{4,0},{5,1},{6,2},{7,3},{8,12},{9,13},{10,... | collective-permute-start | bytes 442376 | tf_op jit(solution)/shard_map/ppermute | solution.py:345
  48.6 5.4 collective-permute-start.2
  50.2 9.9 %collective-permute-start.9 = (bf16[2,96,768]{2,1,0:T(8,128)(2,1)S(1)}, bf16[2,96,768]{2,1,0:T(8,128)(2,1)S(1)}, u32[]{:S(2)}, u32[]{:S(2)}) collective-permute-start(bf16[2,96,768]{2,1,0:T(8,128)(2,1)S(1)} %maximum_bitcast_fusion), channel_id=1, source_target_pairs={{0,8},{1,9},{2,10},{3,11},{4,12},{5,13},{6,14},{7,15},{8,0},{9,1},... | collective-permute-start | bytes 884744 | tf_op jit(solution)/shard_map/ppermute | solution.py:345
  51.0 15.4 %collective-permute-start.17 = (bf16[2,96,768]{2,1,0:T(8,128)(2,1)S(1)}, bf16[2,96,768]{2,1,0:T(8,128)(2,1)S(1)}, u32[]{:S(2)}, u32[]{:S(2)}) collective-permute-start(bf16[2,96,768]{2,1,0:T(8,128)(2,1)S(1)} %maximum_bitcast_fusion.1), channel_id=1, source_target_pairs={{0,8},{1,9},{2,10},{3,11},{4,12},{5,13},{6,14},{7,15},{8,0},{9,1},... | collective-permute-start | bytes 884744 | tf_op jit(solution)/shard_map/ppermute | solution.py:345
  54.0 18.8 %collective-permute-start.25 = (bf16[2,96,768]{2,1,0:T(8,128)(2,1)S(1)}, bf16[2,96,768]{2,1,0:T(8,128)(2,1)S(1)}, u32[]{:S(2)}, u32[]{:S(2)}) collective-permute-start(bf16[2,96,768]{2,1,0:T(8,128)(2,1)S(1)} %maximum_bitcast_fusion.3), channel_id=1, source_target_pairs={{0,8},{1,9},{2,10},{3,11},{4,12},{5,13},{6,14},{7,15},{8,0},{9,1},... | collective-permute-start | bytes 884744 | tf_op jit(solution)/shard_map/ppermute | solution.py:345
  60.1 16.9 %collective-permute-start.22 = (bf16[2,96,768]{2,1,0:T(8,128)(2,1)S(1)}, bf16[2,96,768]{2,1,0:T(8,128)(2,1)S(1)}, u32[]{:S(2)}, u32[]{:S(2)}) collective-permute-start(bf16[2,96,768]{2,1,0:T(8,128)(2,1)S(1)} %maximum_bitcast_fusion.2), channel_id=1, source_target_pairs={{0,8},{1,9},{2,10},{3,11},{4,12},{5,13},{6,14},{7,15},{8,0},{9,1},... | collective-permute-start | bytes 884744 | tf_op jit(solution)/shard_map/ppermute | solution.py:345
  66.4 12.2 %collective-permute-start.39 = (bf16[8,24,768]{2,1,0:T(8,128)(2,1)S(1)}, bf16[8,24,768]{2,1,0:T(8,128)(2,1)S(1)}, u32[]{:S(2)}, u32[]{:S(2)}) collective-permute-start(bf16[8,24,768]{2,1,0:T(8,128)(2,1)S(1)} %bitcast.811), channel_id=1, source_target_pairs={{0,2},{1,3},{2,0},{3,1},{4,6},{5,7},{6,4},{7,5},{8,10},{9,11},{10,... | collective-permute-start | bytes 884744 | tf_op jit(solution)/shard_map/ppermute | solution.py:345
  72.8 8.8 %collective-permute-start.3 = (bf16[8,24,896]{2,1,0:T(8,128)(2,1)S(1)}, bf16[8,24,896]{2,1,0:T(8,128)(2,1)S(1)}, u32[]{:S(2)}, u32[]{:S(2)}) collective-permute-start(bf16[8,24,896]{2,1,0:T(8,128)(2,1)S(1)} %bitcast.804), channel_id=1, source_target_pairs={{0,2},{1,3},{2,0},{3,1},{4,6},{5,7},{6,4},{7,5},{8,10},{9,11},{10,... | collective-permute-start | bytes 1032200 | tf_op jit(solution)/shard_map/ppermute | solution.py:345
  77.0 16.3 %collective-permute-start.10 = (bf16[4,96,768]{2,1,0:T(8,128)(2,1)S(1)}, bf16[4,96,768]{2,1,0:T(8,128)(2,1)S(1)}, u32[]{:S(2)}, u32[]{:S(2)}) collective-permute-start(bf16[4,96,768]{2,1,0:T(8,128)(2,1)S(1)} %bitcast.790), channel_id=1, source_target_pairs={{0,4},{1,5},{2,6},{3,7},{4,0},{5,1},{6,2},{7,3},{8,12},{9,13},{10,... | collective-permute-start | bytes 1769480 | tf_op jit(solution)/shard_map/ppermute | solution.py:345
  78.7 25.0 %collective-permute-start.18 = (bf16[4,96,768]{2,1,0:T(8,128)(2,1)S(1)}, bf16[4,96,768]{2,1,0:T(8,128)(2,1)S(1)}, u32[]{:S(2)}, u32[]{:S(2)}) collective-permute-start(bf16[4,96,768]{2,1,0:T(8,128)(2,1)S(1)} %bitcast.765), channel_id=1, source_target_pairs={{0,2},{1,3},{2,0},{3,1},{4,6},{5,7},{6,4},{7,5},{8,10},{9,11},{10,... | collective-permute-start | bytes 1769480 | tf_op jit(solution)/shard_map/ppermute | solution.py:345
  81.5 21.8 %collective-permute-start.23 = (bf16[4,96,768]{2,1,0:T(8,128)(2,1)S(1)}, bf16[4,96,768]{2,1,0:T(8,128)(2,1)S(1)}, u32[]{:S(2)}, u32[]{:S(2)}) collective-permute-start(bf16[4,96,768]{2,1,0:T(8,128)(2,1)S(1)} %bitcast.792), channel_id=1, source_target_pairs={{0,4},{1,5},{2,6},{3,7},{4,0},{5,1},{6,2},{7,3},{8,12},{9,13},{10,... | collective-permute-start | bytes 1769480 | tf_op jit(solution)/shard_map/ppermute | solution.py:345
  93.3 12.6 %collective-permute-start.26 = (bf16[4,96,768]{2,1,0:T(8,128)(2,1)S(1)}, bf16[4,96,768]{2,1,0:T(8,128)(2,1)S(1)}, u32[]{:S(2)}, u32[]{:S(2)}) collective-permute-start(bf16[4,96,768]{2,1,0:T(8,128)(2,1)S(1)} %bitcast.768), channel_id=1, source_target_pairs={{0,2},{1,3},{2,0},{3,1},{4,6},{5,7},{6,4},{7,5},{8,10},{9,11},{10,... | collective-permute-start | bytes 1769480 | tf_op jit(solution)/shard_map/ppermute | solution.py:345
  103.7 7.0 %collective-permute-start.5 = (bf16[208,768]{1,0:T(8,128)(2,1)}, bf16[208,768]{1,0:T(8,128)(2,1)S(1)}, u32[]{:S(2)}, u32[]{:S(2)}) collective-permute-start(bf16[208,768]{1,0:T(8,128)(2,1)} %get-tuple-element.283), channel_id=1, source_target_pairs={{0,1},{1,0},{2,3},{3,2},{4,5},{5,4},{6,7},{7,6},{8,9},{9,8},{10,11... | collective-permute-start | bytes 958472 | tf_op jit(solution)/shard_map/ppermute | solution.py:345
  105.8 28.9 %collective-permute-start.11 = (bf16[8,96,768]{2,1,0:T(8,128)(2,1)S(1)}, bf16[8,96,768]{2,1,0:T(8,128)(2,1)S(1)}, u32[]{:S(2)}, u32[]{:S(2)}) collective-permute-start(bf16[8,96,768]{2,1,0:T(8,128)(2,1)S(1)} %bitcast.763), channel_id=1, source_target_pairs={{0,2},{1,3},{2,0},{3,1},{4,6},{5,7},{6,4},{7,5},{8,10},{9,11},{10,... | collective-permute-start | bytes 3538952 | tf_op jit(solution)/shard_map/ppermute | solution.py:345
  107.3 33.7 %collective-permute-start.19 = (bf16[2,4,96,768]{3,2,1,0:T(8,128)(2,1)S(1)}, bf16[2,4,96,768]{3,2,1,0:T(8,128)(2,1)S(1)}, u32[]{:S(2)}, u32[]{:S(2)}) collective-permute-start(bf16[2,4,96,768]{3,2,1,0:T(8,128)(2,1)S(1)} %pad_maximum_fusion.10), channel_id=1, source_target_pairs={{0,4},{1,5},{2,6},{3,7},{4,0},{5,1},{6,2},{7,3},{8,12},{9,13},{10,... | collective-permute-start | bytes 3538952 | tf_op jit(solution)/shard_map/ppermute | solution.py:345
  109.4 49.5 %collective-permute-start.27 = (bf16[2,4,96,768]{3,2,1,0:T(8,128)(2,1)S(1)}, bf16[2,4,96,768]{3,2,1,0:T(8,128)(2,1)S(1)}, u32[]{:S(2)}, u32[]{:S(2)}) collective-permute-start(bf16[2,4,96,768]{3,2,1,0:T(8,128)(2,1)S(1)} %pad_maximum_fusion.12), channel_id=1, source_target_pairs={{0,4},{1,5},{2,6},{3,7},{4,0},{5,1},{6,2},{7,3},{8,12},{9,13},{10,... | collective-permute-start | bytes 3538952 | tf_op jit(solution)/shard_map/ppermute | solution.py:345
  110.0 74.8 %collective-permute-start.28 = (bf16[8,96,768]{2,1,0:T(8,128)(2,1)S(1)}, bf16[8,96,768]{2,1,0:T(8,128)(2,1)}, u32[]{:S(2)}, u32[]{:S(2)}) collective-permute-start(bf16[8,96,768]{2,1,0:T(8,128)(2,1)S(1)} %bitcast.775), channel_id=1, source_target_pairs={{0,2},{1,3},{2,0},{3,1},{4,6},{5,7},{6,4},{7,5},{8,10},{9,11},{10,... | collective-permute-start | bytes 3538952 | tf_op jit(solution)/shard_map/ppermute | solution.py:345
  136.3 35.5 %collective-permute-start.12 = (bf16[2,768,768]{2,1,0:T(8,128)(2,1)}, bf16[2,768,768]{2,1,0:T(8,128)(2,1)}, u32[]{:S(2)}, u32[]{:S(2)}) collective-permute-start(bf16[2,768,768]{2,1,0:T(8,128)(2,1)} %pad_maximum_fusion.1.weight_ref), channel_id=1, source_target_pairs={{0,1},{1,0},{2,3},{3,2},{4,5},{5,4},{6,7},{7,6},{8,9},{9,8},{10,11... | collective-permute-start | bytes 7077896 | tf_op jit(solution)/shard_map/ppermute | solution.py:345
  142.9 87.0 %collective-permute-start.20 = (bf16[2,768,768]{2,1,0:T(8,128)(2,1)}, bf16[2,768,768]{2,1,0:T(8,128)(2,1)}, u32[]{:S(2)}, u32[]{:S(2)}) collective-permute-start(bf16[2,768,768]{2,1,0:T(8,128)(2,1)} %bitcast.77.weight_ref), channel_id=1, source_target_pairs={{0,1},{1,0},{2,3},{3,2},{4,5},{5,4},{6,7},{7,6},{8,9},{9,8},{10,11... | collective-permute-start | bytes 7077896 | tf_op jit(solution)/shard_map/ppermute | solution.py:345
  160.8 106.6 %collective-permute-start.30 = (bf16[2,768,768]{2,1,0:T(8,128)(2,1)}, bf16[2,768,768]{2,1,0:T(8,128)(2,1)}, u32[]{:S(2)}, u32[]{:S(2)}) collective-permute-start(bf16[2,768,768]{2,1,0:T(8,128)(2,1)} %bitcast.108), channel_id=1, source_target_pairs={{0,1},{1,0},{2,3},{3,2},{4,5},{5,4},{6,7},{7,6},{8,9},{9,8},{10,11... | collective-permute-start | bytes 7077896 | tf_op jit(solution)/shard_map/ppermute | solution.py:345
  182.2 10.3 %collective-permute-start.15 = (bf16[208,768]{1,0:T(8,128)(2,1)S(1)}, bf16[208,768]{1,0:T(8,128)(2,1)S(1)}, u32[]{:S(2)}, u32[]{:S(2)}) collective-permute-start(bf16[208,768]{1,0:T(8,128)(2,1)S(1)} %pad_maximum_fusion.24), channel_id=1, source_target_pairs={{0,3},{1,2},{2,1},{3,0},{4,7},{5,6},{6,5},{7,4},{8,11},{9,10},{10,... | collective-permute-start | bytes 958472 | tf_op jit(solution)/shard_map/ppermute | solution.py:345
  183.8 15.2 %collective-permute-start.14 = (bf16[208,768]{1,0:T(8,128)(2,1)S(1)}, bf16[208,768]{1,0:T(8,128)(2,1)S(1)}, u32[]{:S(2)}, u32[]{:S(2)}) collective-permute-start(bf16[208,768]{1,0:T(8,128)(2,1)S(1)} %pad_maximum_fusion.23), channel_id=1, source_target_pairs={{0,2},{1,3},{2,0},{3,1},{4,6},{5,7},{6,4},{7,5},{8,10},{9,11},{10,... | collective-permute-start | bytes 958472 | tf_op jit(solution)/shard_map/ppermute | solution.py:345
  184.8 14.2 %collective-permute-start.13 = (bf16[208,768]{1,0:T(8,128)(2,1)S(1)}, bf16[208,768]{1,0:T(8,128)(2,1)S(1)}, u32[]{:S(2)}, u32[]{:S(2)}) collective-permute-start(bf16[208,768]{1,0:T(8,128)(2,1)S(1)} %pad_maximum_fusion.22), channel_id=1, source_target_pairs={{0,1},{1,0},{2,3},{3,2},{4,5},{5,4},{6,7},{7,6},{8,9},{9,8},{10,11... | collective-permute-start | bytes 958472 | tf_op jit(solution)/shard_map/ppermute | solution.py:345
  192.5 64.3 %collective-permute-start.29 = (bf16[2,768,768]{2,1,0:T(8,128)(2,1)}, bf16[2,768,768]{2,1,0:T(8,128)(2,1)}, u32[]{:S(2)}, u32[]{:S(2)}) collective-permute-start(bf16[2,768,768]{2,1,0:T(8,128)(2,1)} %pad_maximum_fusion.3), channel_id=1, source_target_pairs={{0,1},{1,0},{2,3},{3,2},{4,5},{5,4},{6,7},{7,6},{8,9},{9,8},{10,11... | collective-permute-start | bytes 7077896 | tf_op jit(solution)/shard_map/ppermute | solution.py:345
  275.6 20.3 %collective-permute-start.40 = (bf16[16,24,768]{2,1,0:T(8,128)(2,1)S(1)}, bf16[16,24,768]{2,1,0:T(8,128)(2,1)}, u32[]{:S(2)}, u32[]{:S(2)}) collective-permute-start(bf16[16,24,768]{2,1,0:T(8,128)(2,1)S(1)} %bitcast.791), channel_id=1, source_target_pairs={{0,1},{1,0},{2,3},{3,2},{4,5},{5,4},{6,7},{7,6},{8,9},{9,8},{10,11... | collective-permute-start | bytes 1769480 | tf_op jit(solution)/shard_map/ppermute | solution.py:345
  281.2 12.4 %collective-permute-start.33 = (f32[1,1,896]{2,1,0:T(1,128)}, f32[1,1,896]{2,1,0:T(1,128)}, u32[]{:S(2)}, u32[]{:S(2)}) collective-permute-start(f32[1,1,896]{2,1,0:T(1,128)} %maximum_bitcast_fusion.11), channel_id=1, source_target_pairs={{0,16},{1,17},{2,18},{3,19},{4,20},{5,21},{6,22},{7,23},{8,24},{9,... | collective-permute-start | bytes 10760 | tf_op jit(solution)/shard_map/ppermute | solution.py:345
  418.5 9.9 %collective-permute-start.43 = (bf16[208,768]{1,0:T(8,128)(2,1)S(1)}, bf16[208,768]{1,0:T(8,128)(2,1)S(1)}, u32[]{:S(2)}, u32[]{:S(2)}) collective-permute-start(bf16[208,768]{1,0:T(8,128)(2,1)S(1)} %get-tuple-element.277), channel_id=1, source_target_pairs={{0,3},{1,2},{2,1},{3,0},{4,7},{5,6},{6,5},{7,4},{8,11},{9,10},{10,... | collective-permute-start | bytes 958472 | tf_op jit(solution)/shard_map/ppermute | solution.py:345
  418.5 16.3 %collective-permute-start.42 = (bf16[208,768]{1,0:T(8,128)(2,1)S(1)}, bf16[208,768]{1,0:T(8,128)(2,1)S(1)}, u32[]{:S(2)}, u32[]{:S(2)}) collective-permute-start(bf16[208,768]{1,0:T(8,128)(2,1)S(1)} %get-tuple-element.278), channel_id=1, source_target_pairs={{0,2},{1,3},{2,0},{3,1},{4,6},{5,7},{6,4},{7,5},{8,10},{9,11},{10,... | collective-permute-start | bytes 958472 | tf_op jit(solution)/shard_map/ppermute | solution.py:345
  419.9 15.0 %collective-permute-start.41 = (bf16[208,768]{1,0:T(8,128)(2,1)S(1)}, bf16[208,768]{1,0:T(8,128)(2,1)S(1)}, u32[]{:S(2)}, u32[]{:S(2)}) collective-permute-start(bf16[208,768]{1,0:T(8,128)(2,1)S(1)} %get-tuple-element.279), channel_id=1, source_target_pairs={{0,1},{1,0},{2,3},{3,2},{4,5},{5,4},{6,7},{7,6},{8,9},{9,8},{10,11... | collective-permute-start | bytes 958472 | tf_op jit(solution)/shard_map/ppermute | solution.py:345
  483.1 5.0 collective-permute-start.44
  489.6 10.7 %collective-permute-start.45 = (bf16[8,24,768]{2,1,0:T(8,128)(2,1)S(1)}, bf16[8,24,768]{2,1,0:T(8,128)(2,1)S(1)}, u32[]{:S(2)}, u32[]{:S(2)}) collective-permute-start(bf16[8,24,768]{2,1,0:T(8,128)(2,1)S(1)} %fusion.104), channel_id=1, source_target_pairs={{0,2},{1,3},{2,0},{3,1},{4,6},{5,7},{6,4},{7,5},{8,10},{9,11},{10,... | collective-permute-start | bytes 884744 | tf_op jit(solution)/shard_map/ppermute | solution.py:345
  490.4 34.6 %collective-permute-start.59 = (bf16[2,768,768]{2,1,0:T(8,128)(2,1)}, bf16[2,768,768]{2,1,0:T(8,128)(2,1)}, u32[]{:S(2)}, u32[]{:S(2)}) collective-permute-start(bf16[2,768,768]{2,1,0:T(8,128)(2,1)} %get-tuple-element.65), channel_id=1, source_target_pairs={{0,1},{1,0},{2,3},{3,2},{4,5},{5,4},{6,7},{7,6},{8,9},{9,8},{10,11... | collective-permute-start | bytes 7077896 | tf_op jit(solution)/shard_map/ppermute | solution.py:345
  490.7 8.4 %collective-permute-start.50 = (f32[8,768]{1,0:T(8,128)S(1)}, f32[8,768]{1,0:T(8,128)S(1)}, u32[]{:S(2)}, u32[]{:S(2)}) collective-permute-start(f32[8,768]{1,0:T(8,128)S(1)} %add.568), channel_id=1, source_target_pairs={{0,2},{1,3},{2,0},{3,1},{4,6},{5,7},{6,4},{7,5},{8,10},{9,11},{10,... | collective-permute-start | bytes 73736 | tf_op jit(solution)/shard_map/ppermute | solution.py:345
  492.6 36.5 %collective-permute-start.64 = (bf16[2,768,768]{2,1,0:T(8,128)(2,1)S(1)}, bf16[2,768,768]{2,1,0:T(8,128)(2,1)}, u32[]{:S(2)}, u32[]{:S(2)}) collective-permute-start(bf16[2,768,768]{2,1,0:T(8,128)(2,1)S(1)} %pad_maximum_fusion.4), channel_id=1, source_target_pairs={{0,1},{1,0},{2,3},{3,2},{4,5},{5,4},{6,7},{7,6},{8,9},{9,8},{10,11... | collective-permute-start | bytes 7077896 | tf_op jit(solution)/shard_map/ppermute | solution.py:345
  500.5 5.2 collective-permute-start.46
  503.1 29.9 %collective-permute-start.69 = (bf16[2,768,768]{2,1,0:T(8,128)(2,1)}, bf16[2,768,768]{2,1,0:T(8,128)(2,1)}, u32[]{:S(2)}, u32[]{:S(2)}) collective-permute-start(bf16[2,768,768]{2,1,0:T(8,128)(2,1)} %pad_maximum_fusion.5), channel_id=1, source_target_pairs={{0,1},{1,0},{2,3},{3,2},{4,5},{5,4},{6,7},{7,6},{8,9},{9,8},{10,11... | collective-permute-start | bytes 7077896 | tf_op jit(solution)/shard_map/ppermute | solution.py:345
  507.7 29.8 %collective-permute-start.54 = (bf16[2,768,768]{2,1,0:T(8,128)(2,1)}, bf16[2,768,768]{2,1,0:T(8,128)(2,1)}, u32[]{:S(2)}, u32[]{:S(2)}) collective-permute-start(bf16[2,768,768]{2,1,0:T(8,128)(2,1)} %get-tuple-element.63), channel_id=1, source_target_pairs={{0,1},{1,0},{2,3},{3,2},{4,5},{5,4},{6,7},{7,6},{8,9},{9,8},{10,11... | collective-permute-start | bytes 7077896 | tf_op jit(solution)/shard_map/ppermute | solution.py:345
  510.2 4.7 collective-permute-start.53
  514.9 5.4 collective-permute-start.48
  528.2 29.0 %collective-permute-start.60 = (bf16[2,4,96,768]{3,2,1,0:T(8,128)(2,1)S(1)}, bf16[2,4,96,768]{3,2,1,0:T(8,128)(2,1)S(1)}, u32[]{:S(2)}, u32[]{:S(2)}) collective-permute-start(bf16[2,4,96,768]{3,2,1,0:T(8,128)(2,1)S(1)} %fusion.56), channel_id=1, source_target_pairs={{0,4},{1,5},{2,6},{3,7},{4,0},{5,1},{6,2},{7,3},{8,12},{9,13},{10,... | collective-permute-start | bytes 3538952 | tf_op jit(solution)/shard_map/ppermute | solution.py:345
  531.9 29.0 %collective-permute-start.65 = (bf16[8,96,768]{2,1,0:T(8,128)(2,1)S(1)}, bf16[8,96,768]{2,1,0:T(8,128)(2,1)S(1)}, u32[]{:S(2)}, u32[]{:S(2)}) collective-permute-start(bf16[8,96,768]{2,1,0:T(8,128)(2,1)S(1)} %bitcast.809), channel_id=1, source_target_pairs={{0,2},{1,3},{2,0},{3,1},{4,6},{5,7},{6,4},{7,5},{8,10},{9,11},{10,... | collective-permute-start | bytes 3538952 | tf_op jit(solution)/shard_map/ppermute | solution.py:345
  536.5 45.9 %collective-permute-start.70 = (bf16[2,4,96,768]{3,2,1,0:T(8,128)(2,1)S(1)}, bf16[2,4,96,768]{3,2,1,0:T(8,128)(2,1)S(1)}, u32[]{:S(2)}, u32[]{:S(2)}) collective-permute-start(bf16[2,4,96,768]{3,2,1,0:T(8,128)(2,1)S(1)} %fusion.57), channel_id=1, source_target_pairs={{0,4},{1,5},{2,6},{3,7},{4,0},{5,1},{6,2},{7,3},{8,12},{9,13},{10,... | collective-permute-start | bytes 3538952 | tf_op jit(solution)/shard_map/ppermute | solution.py:345
  542.6 43.6 %collective-permute-start.55 = (bf16[8,96,768]{2,1,0:T(8,128)(2,1)S(1)}, bf16[8,96,768]{2,1,0:T(8,128)(2,1)S(1)}, u32[]{:S(2)}, u32[]{:S(2)}) collective-permute-start(bf16[8,96,768]{2,1,0:T(8,128)(2,1)S(1)} %bitcast.810), channel_id=1, source_target_pairs={{0,2},{1,3},{2,0},{3,1},{4,6},{5,7},{6,4},{7,5},{8,10},{9,11},{10,... | collective-permute-start | bytes 3538952 | tf_op jit(solution)/shard_map/ppermute | solution.py:345
  557.6 41.2 %collective-permute-start.61 = (bf16[4,96,768]{2,1,0:T(8,128)(2,1)S(1)}, bf16[4,96,768]{2,1,0:T(8,128)(2,1)S(1)}, u32[]{:S(2)}, u32[]{:S(2)}) collective-permute-start(bf16[4,96,768]{2,1,0:T(8,128)(2,1)S(1)} %fusion.88), channel_id=1, source_target_pairs={{0,2},{1,3},{2,0},{3,1},{4,6},{5,7},{6,4},{7,5},{8,10},{9,11},{10,... | collective-permute-start | bytes 1769480 | tf_op jit(solution)/shard_map/ppermute | solution.py:345
  561.3 39.6 %collective-permute-start.66 = (bf16[4,96,768]{2,1,0:T(8,128)(2,1)S(1)}, bf16[4,96,768]{2,1,0:T(8,128)(2,1)S(1)}, u32[]{:S(2)}, u32[]{:S(2)}) collective-permute-start(bf16[4,96,768]{2,1,0:T(8,128)(2,1)S(1)} %fusion.87), channel_id=1, source_target_pairs={{0,4},{1,5},{2,6},{3,7},{4,0},{5,1},{6,2},{7,3},{8,12},{9,13},{10,... | collective-permute-start | bytes 1769480 | tf_op jit(solution)/shard_map/ppermute | solution.py:345
  582.9 24.7 %collective-permute-start.71 = (bf16[4,96,768]{2,1,0:T(8,128)(2,1)S(1)}, bf16[4,96,768]{2,1,0:T(8,128)(2,1)S(1)}, u32[]{:S(2)}, u32[]{:S(2)}) collective-permute-start(bf16[4,96,768]{2,1,0:T(8,128)(2,1)S(1)} %fusion.89), channel_id=1, source_target_pairs={{0,2},{1,3},{2,0},{3,1},{4,6},{5,7},{6,4},{7,5},{8,10},{9,11},{10,... | collective-permute-start | bytes 1769480 | tf_op jit(solution)/shard_map/ppermute | solution.py:345
  586.5 36.1 %collective-permute-start.56 = (bf16[4,96,768]{2,1,0:T(8,128)(2,1)S(1)}, bf16[4,96,768]{2,1,0:T(8,128)(2,1)S(1)}, u32[]{:S(2)}, u32[]{:S(2)}) collective-permute-start(bf16[4,96,768]{2,1,0:T(8,128)(2,1)S(1)} %fusion.86), channel_id=1, source_target_pairs={{0,4},{1,5},{2,6},{3,7},{4,0},{5,1},{6,2},{7,3},{8,12},{9,13},{10,... | collective-permute-start | bytes 1769480 | tf_op jit(solution)/shard_map/ppermute | solution.py:345
  599.0 9.7 %collective-permute-start.62 = (bf16[2,96,768]{2,1,0:T(8,128)(2,1)S(1)}, bf16[2,96,768]{2,1,0:T(8,128)(2,1)S(1)}, u32[]{:S(2)}, u32[]{:S(2)}) collective-permute-start(bf16[2,96,768]{2,1,0:T(8,128)(2,1)S(1)} %fusion.106), channel_id=1, source_target_pairs={{0,8},{1,9},{2,10},{3,11},{4,12},{5,13},{6,14},{7,15},{8,0},{9,1},... | collective-permute-start | bytes 884744 | tf_op jit(solution)/shard_map/ppermute | solution.py:345
  601.1 14.8 %collective-permute-start.67 = (bf16[2,96,768]{2,1,0:T(8,128)(2,1)S(1)}, bf16[2,96,768]{2,1,0:T(8,128)(2,1)S(1)}, u32[]{:S(2)}, u32[]{:S(2)}) collective-permute-start(bf16[2,96,768]{2,1,0:T(8,128)(2,1)S(1)} %fusion.107), channel_id=1, source_target_pairs={{0,8},{1,9},{2,10},{3,11},{4,12},{5,13},{6,14},{7,15},{8,0},{9,1},... | collective-permute-start | bytes 884744 | tf_op jit(solution)/shard_map/ppermute | solution.py:345
  607.7 12.2 %collective-permute-start.72 = (bf16[2,96,768]{2,1,0:T(8,128)(2,1)S(1)}, bf16[2,96,768]{2,1,0:T(8,128)(2,1)S(1)}, u32[]{:S(2)}, u32[]{:S(2)}) collective-permute-start(bf16[2,96,768]{2,1,0:T(8,128)(2,1)S(1)} %fusion.108), channel_id=1, source_target_pairs={{0,8},{1,9},{2,10},{3,11},{4,12},{5,13},{6,14},{7,15},{8,0},{9,1},... | collective-permute-start | bytes 884744 | tf_op jit(solution)/shard_map/ppermute | solution.py:345
  608.9 17.4 %collective-permute-start.63 = (bf16[1,96,768]{2,1,0:T(8,128)(2,1)S(1)}, bf16[1,96,768]{2,1,0:T(8,128)(2,1)S(1)}, u32[]{:S(2)}, u32[]{:S(2)}) collective-permute-start(bf16[1,96,768]{2,1,0:T(8,128)(2,1)S(1)} %fusion.116), channel_id=1, source_target_pairs={{0,16},{1,17},{2,18},{3,19},{4,20},{5,21},{6,22},{7,23},{8,24},{9,... | collective-permute-start | bytes 442376 | tf_op jit(solution)/shard_map/ppermute | solution.py:345
  616.0 13.7 %collective-permute-start.68 = (bf16[1,96,768]{2,1,0:T(8,128)(2,1)S(1)}, bf16[1,96,768]{2,1,0:T(8,128)(2,1)S(1)}, u32[]{:S(2)}, u32[]{:S(2)}) collective-permute-start(bf16[1,96,768]{2,1,0:T(8,128)(2,1)S(1)} %fusion.117), channel_id=1, source_target_pairs={{0,16},{1,17},{2,18},{3,19},{4,20},{5,21},{6,22},{7,23},{8,24},{9,... | collective-permute-start | bytes 442376 | tf_op jit(solution)/shard_map/ppermute | solution.py:345
  620.1 11.7 %collective-permute-start.73 = (bf16[1,96,768]{2,1,0:T(8,128)(2,1)S(1)}, bf16[1,96,768]{2,1,0:T(8,128)(2,1)S(1)}, u32[]{:S(2)}, u32[]{:S(2)}) collective-permute-start(bf16[1,96,768]{2,1,0:T(8,128)(2,1)S(1)} %fusion.118), channel_id=1, source_target_pairs={{0,16},{1,17},{2,18},{3,19},{4,20},{5,21},{6,22},{7,23},{8,24},{9,... | collective-permute-start | bytes 442376 | tf_op jit(solution)/shard_map/ppermute | solution.py:345
  623.6 10.2 %collective-permute-start.57 = (bf16[2,96,768]{2,1,0:T(8,128)(2,1)}, bf16[2,96,768]{2,1,0:T(8,128)(2,1)}, u32[]{:S(2)}, u32[]{:S(2)}) collective-permute-start(bf16[2,96,768]{2,1,0:T(8,128)(2,1)} %fusion.105), channel_id=1, source_target_pairs={{0,8},{1,9},{2,10},{3,11},{4,12},{5,13},{6,14},{7,15},{8,0},{9,1},... | collective-permute-start | bytes 884744 | tf_op jit(solution)/shard_map/ppermute | solution.py:345
  635.0 6.7 collective-permute-start.58
  (169 other events, 2023.1 us)

commit v2 on v1

v2 whole, which is shorter than its diff:
```python
import functools

import jax
import jax.numpy as jnp
from jax import lax
from jax.experimental import pallas as pl
from jax.experimental.pallas import tpu as pltpu
from jax.sharding import PartitionSpec as P

HD = 64
FRAMES = 4
PMAX = 784
PSMALL = 196
STEP = 5
SLOTS = 208
ROWS = FRAMES * SLOTS
GROUP = 192
QKV = 3 * GROUP


EXACT = lax.Precision.HIGHEST
TEMPER = 0.05
BETA_ONE = 0.5
BETA_TWO = 0.5
RATE = 0.04
NORM_RATE = 0.3
DECAY = 0.05
ADAM_EPS = 1e-08
CLIP_AT = 1.0
LOWER = jnp.bfloat16
SINGLE = jnp.float32
ALL = ("batch", "head")
GRANT = 56 << 20

NN = (((1,), (0,)), ((), ()))
NT = (((1,), (1,)), ((), ()))
TN = (((0,), (0,)), ((), ()))


def dot(left, right, dims=NN):
    return lax.dot_general(left, right, dims, preferred_element_type=SINGLE)


def low(value):
    return value.astype(LOWER)


def layer_norm(value, gain, bias):
    center = value - jnp.mean(value, axis=-1, keepdims=True)
    spread = jnp.mean(center * center, axis=-1, keepdims=True)
    return center * lax.rsqrt(spread + 1e-06) * gain + bias


def three_parts(value):
    high = low(value)
    rest = value - high.astype(SINGLE)
    middle = low(rest)
    return high, middle, low(rest - middle.astype(SINGLE))


def frame_probs(query, keys):
    scores = [jnp.sum(query * key, axis=0, keepdims=True) * HD ** (-0.5) for key in keys]
    top = functools.reduce(jnp.maximum, scores)
    raised = [jnp.exp(score - top) for score in scores]
    total = functools.reduce(jnp.add, raised)
    return [value / total for value in raised]


def rounded(value):
    return low(value).astype(SINGLE)


def frame_rows(f):
    return slice(SLOTS * f, SLOTS * (f + 1))


def split_frames(rows):
    return [rows[frame_rows(f)] for f in range(FRAMES)]


def head_features(which, head):
    return slice(GROUP * which + HD * head, GROUP * which + HD * (head + 1))


def temporal_fwd_kernel(normed_ref, weight_ref, qkv_ref, mixed_ref, out):
    for f in range(FRAMES):
        qkv_ref[0, f] = low(dot(normed_ref[frame_rows(f), :], weight_ref[0, :, :QKV])).T
    for head in range(GROUP // HD):
        query, keys, values = (
            [qkv_ref[0, f, head_features(i, head), :].astype(SINGLE) for f in range(FRAMES)]
            for i in range(3)
        )
        for f in range(FRAMES):
            probs = frame_probs(query[f], keys)
            mixed = sum(rounded(prob) * value for prob, value in zip(probs, values))
            out[f, head_features(0, head), :] = low(mixed)
    for f in range(FRAMES):
        mixed_ref[0, frame_rows(f), :] = out[f].T


def temporal_bwd_kernel(
    normed_ref,
    grad_ref,
    weight_ref,
    qkv_ref,
    mixed_ref,
    dweight_ref,
    dnormed_ref,
    dqkv,
    dmix,
    dcol,
):
    scale = HD ** (-0.5)
    for f in range(FRAMES):
        dmix[f] = low(dot(grad_ref[frame_rows(f), :], weight_ref[0, :, QKV:])).T
    for head in range(GROUP // HD):
        query, keys, values = (
            [qkv_ref[0, f, head_features(i, head), :].astype(SINGLE) for f in range(FRAMES)]
            for i in range(3)
        )
        d_keys = [jnp.zeros((HD, SLOTS), SINGLE) for _ in range(FRAMES)]
        d_values = [jnp.zeros((HD, SLOTS), SINGLE) for _ in range(FRAMES)]
        for f in range(FRAMES):
            d_mixed = dmix[f, head_features(0, head), :].astype(SINGLE)
            probs = frame_probs(query[f], keys)
            d_probs = [jnp.sum(d_mixed * value, axis=0, keepdims=True) for value in values]
            row = sum(prob * d_prob for prob, d_prob in zip(probs, d_probs))
            d_query = jnp.zeros((HD, SLOTS), SINGLE)
            for g in range(FRAMES):
                d_score = rounded(probs[g] * (d_probs[g] - row))
                d_query = d_query + d_score * keys[g]
                d_keys[g] = d_keys[g] + d_score * query[f]
                d_values[g] = d_values[g] + rounded(probs[g]) * d_mixed
            dcol[f, head_features(0, head), :] = low(d_query * scale)
        for g in range(FRAMES):
            dcol[g, head_features(1, head), :] = low(d_keys[g] * scale)
            dcol[g, head_features(2, head), :] = low(d_values[g])
    for f in range(FRAMES):
        dqkv[frame_rows(f), :] = dcol[f].T
    finish_backward(normed_ref, grad_ref, weight_ref, mixed_ref, dweight_ref, dnormed_ref, dqkv)


def finish_backward(
    normed_ref, grad_ref, weight_ref, mixed_ref, dweight_ref, dnormed_ref, dqkv
):
    dweight_ref[0, :, :QKV] = low(dot(normed_ref[...], dqkv[...], TN))
    dweight_ref[0, :, QKV:] = low(dot(grad_ref[...], mixed_ref[0], TN))
    d_normed = dot(dqkv[...], weight_ref[0, :, :QKV], NT)

    accumulate(dnormed_ref, d_normed)


def lane_pieces(pieces, rows):
    lane = lax.broadcasted_iota(jnp.int32, (rows, HD), 1)
    result = jnp.zeros((rows, HD), SINGLE)
    for number, piece in enumerate(pieces):
        result = jnp.where(lane == number, piece.astype(SINGLE), result)
    return low(result)


def spatial_fwd_kernel(
    normed_ref, weight_ref, key_extra_ref, qkv_ref, mixed_ref, extra_ref, branch_ref
):
    qkv_ref[0] = low(dot(normed_ref[...], weight_ref[0, :, :QKV]))
    one = jnp.ones((ROWS, 1), SINGLE)
    for head in range(GROUP // HD):
        at = HD * head
        query = qkv_ref[0, :, at : at + HD] * jnp.asarray(HD ** (-0.5), LOWER)
        query = jnp.concatenate([query, lane_pieces([one], ROWS)], axis=1)
        keys = jnp.concatenate(
            [qkv_ref[0, :, GROUP + at : GROUP + at + HD], key_extra_ref[...]], axis=1
        )
        values = jnp.concatenate(
            [qkv_ref[0, :, 2 * GROUP + at : 2 * GROUP + at + HD], lane_pieces([one], ROWS)], axis=1
        )
        score = dot(query, keys, NT)
        top = jnp.max(score, axis=1, keepdims=True)
        mixed = dot(low(jnp.exp(score - top)), values)
        total = mixed[:, HD : HD + 1]
        mixed_ref[0, :, at : at + HD] = low(mixed[:, :HD] / total)
        logsum = -(top + jnp.log(total))
        extra_ref[0, :, at : at + HD] = lane_pieces([one, *three_parts(logsum)], ROWS)
    branch = dot(mixed_ref[0], weight_ref[0, :, QKV:], NT)

    accumulate(branch_ref, branch)


def spatial_fwd_last_kernel(
    normed_ref,
    weight_ref,
    key_extra_ref,
    resid_ref,
    branch_ref,
    norms_ref,
    qkv_ref,
    mixed_ref,
    extra_ref,
    out_ref,
    out_normed_ref,
    branch,
):
    spatial_fwd_kernel(
        normed_ref, weight_ref, key_extra_ref, qkv_ref, mixed_ref, extra_ref, branch
    )

    @pl.when(pl.program_id(0) == 1)
    def _():
        for f in range(FRAMES):
            rows = frame_rows(f)
            value = resid_ref[rows, :] + (branch_ref[rows, :] + branch[rows, :])
            out_ref[rows, :] = value
            out_normed_ref[rows, :] = low(layer_norm(value, norms_ref[4:5, :], norms_ref[5:6, :]))


def spatial_bwd_kernel(
    normed_ref,
    grad_ref,
    weight_ref,
    qkv_ref,
    mixed_ref,
    extra_ref,
    key_extra_ref,
    dweight_ref,
    dnormed_ref,
    dqkv,
):
    scale = HD ** (-0.5)
    d_mixed_all = low(dot(grad_ref[...], weight_ref[0, :, QKV:]))
    one = jnp.ones((ROWS, 1), SINGLE)
    for head in range(GROUP // HD):
        at = HD * head
        query = qkv_ref[0, :, at : at + HD]
        query_long = jnp.concatenate(
            [query * jnp.asarray(scale, LOWER), extra_ref[0, :, at : at + HD]], axis=1
        )
        d_mixed = d_mixed_all[:, at : at + HD]
        delta = -jnp.sum(
            d_mixed.astype(SINGLE) * mixed_ref[0, :, at : at + HD].astype(SINGLE),
            axis=1,
            keepdims=True,
        )
        d_mixed_long = jnp.concatenate([d_mixed, lane_pieces(three_parts(delta), ROWS)], axis=1)
        d_query = jnp.zeros((ROWS, HD), SINGLE)
        for part in range(FRAMES):
            rows = slice(SLOTS * part, SLOTS * (part + 1))
            keys = qkv_ref[0, rows, GROUP + at : GROUP + at + HD]
            values = qkv_ref[0, rows, 2 * GROUP + at : 2 * GROUP + at + HD]
            keys_long = jnp.concatenate([keys, key_extra_ref[rows, :]], axis=1)
            values_long = jnp.concatenate(
                [values, lane_pieces([one[rows]] * 3, SLOTS)], axis=1
            )
            prob = jnp.exp(dot(keys_long, query_long, NT))
            d_score = low(prob * dot(values_long, d_mixed_long, NT))
            dqkv[rows, 2 * GROUP + at : 2 * GROUP + at + HD] = low(dot(low(prob), d_mixed))
            dqkv[rows, GROUP + at : GROUP + at + HD] = low(dot(d_score, query) * scale)
            d_query = d_query + dot(d_score, keys, TN)
        dqkv[:, at : at + HD] = low(d_query * scale)
    finish_backward(normed_ref, grad_ref, weight_ref, mixed_ref, dweight_ref, dnormed_ref, dqkv)


def spatial_bwd_last_kernel(
    normed_ref,
    grad_ref,
    weight_ref,
    qkv_ref,
    mixed_ref,
    extra_ref,
    key_extra_ref,
    resid_ref,
    dresid_ref,
    dother_ref,
    norms_ref,
    dweight_ref,
    drows_ref,
    dnorms_ref,
    dqkv,
    dnormed,
):
    spatial_bwd_kernel(
        normed_ref,
        grad_ref,
        weight_ref,
        qkv_ref,
        mixed_ref,
        extra_ref,
        key_extra_ref,
        dweight_ref,
        dnormed,
        dqkv,
    )

    @pl.when(pl.program_id(0) == 1)
    def _():
        norm_rows_back(
            resid_ref, norms_ref, 2, dother_ref, dnormed, dresid_ref, None, drows_ref, dnorms_ref
        )


def norm_back(value, gain, grad):
    center = value - jnp.mean(value, axis=-1, keepdims=True)
    inverse = lax.rsqrt(jnp.mean(center * center, axis=-1, keepdims=True) + 1e-06)
    hat = center * inverse
    scaled = grad * gain
    d_value = inverse * (
        scaled
        - jnp.mean(scaled, axis=-1, keepdims=True)
        - hat * jnp.mean(scaled * hat, axis=-1, keepdims=True)
    )
    return (
        d_value,
        jnp.sum(grad * hat, axis=0, keepdims=True),
        jnp.sum(grad, axis=0, keepdims=True),
    )


def norm_rows_back(
    resid_ref, norms_ref, at, dother_ref, dnormed_ref, dresid_ref, out_ref, rows_ref, dnorms_ref
):
    d_gain = jnp.zeros((1, resid_ref.shape[1]), SINGLE)
    d_bias = jnp.zeros((1, resid_ref.shape[1]), SINGLE)
    for f in range(FRAMES):
        rows = frame_rows(f)
        d_value, gain, bias = norm_back(
            resid_ref[rows, :],
            norms_ref[at : at + 1, :],
            dother_ref[rows, :] + dnormed_ref[rows, :],
        )
        d_value = d_value + dresid_ref[rows, :]
        if out_ref is not None:
            out_ref[rows, :] = d_value
        rows_ref[rows, :] = low(d_value)
        d_gain, d_bias = d_gain + gain, d_bias + bias
    dnorms_ref[0:1, :] = d_gain
    dnorms_ref[1:2, :] = d_bias


def accumulate(ref, value):
    first = pl.program_id(0) == 0
    ref[...] = jnp.where(first, value, ref[...] + value)


def feed_fwd_kernel(normed_ref, up_ref, down_ref, act_ref, slope_ref, branch_ref):
    hidden = dot(normed_ref[...], up_ref[0])
    root = 0.7978845608028654
    square = hidden * hidden
    bend = jnp.tanh(hidden * (root + root * 0.044715 * square))
    half = 0.5 + 0.5 * bend
    act_ref[0] = low(hidden * half)
    slope_ref[0] = low(
        half + hidden * (0.5 - 0.5 * bend * bend) * (root + 3.0 * root * 0.044715 * square)
    )
    accumulate(branch_ref, dot(act_ref[0], down_ref[0], NT))


def feed_fwd_last_kernel(
    normed_ref,
    up_ref,
    down_ref,
    resid_ref,
    branch_ref,
    norms_ref,
    valid_ref,
    act_ref,
    slope_ref,
    out_ref,
    sums_ref,
    branch,
):
    feed_fwd_kernel(normed_ref, up_ref, down_ref, act_ref, slope_ref, branch)

    @pl.when(pl.program_id(0) == 1)
    def _():
        sums = jnp.zeros(sums_ref.shape, SINGLE)
        for f in range(FRAMES):
            rows = frame_rows(f)
            value = resid_ref[rows, :] + (branch_ref[rows, :] + branch[rows, :])
            out_ref[rows, :] = value
            normed = layer_norm(value, norms_ref[6:7, :], norms_ref[7:8, :])
            sums = sums + jnp.sum(normed * valid_ref[rows, :], axis=0, keepdims=True)
        sums_ref[...] = sums


def feed_bwd_kernel(
    normed_ref, grad_ref, up_ref, down_ref, act_ref, slope_ref, dup_ref, ddown_ref, dnormed_ref, dhid
):
    dhid[...] = low(dot(grad_ref[...], down_ref[0]) * slope_ref[0].astype(SINGLE))
    ddown_ref[0] = low(dot(grad_ref[...], act_ref[0], TN))
    dup_ref[0] = low(dot(normed_ref[...], dhid[...], TN))
    accumulate(dnormed_ref, dot(dhid[...], up_ref[0], NT))


def feed_bwd_last_kernel(
    normed_ref,
    grad_ref,
    up_ref,
    down_ref,
    act_ref,
    slope_ref,
    resid_ref,
    dresid_ref,
    dother_ref,
    norms_ref,
    dup_ref,
    ddown_ref,
    out_ref,
    drows_ref,
    dnorms_ref,
    dhid,
    dnormed,
):
    feed_bwd_kernel(
        normed_ref, grad_ref, up_ref, down_ref, act_ref, slope_ref, dup_ref, ddown_ref, dnormed, dhid
    )

    @pl.when(pl.program_id(0) == 1)
    def _():
        norm_rows_back(
            resid_ref, norms_ref, 4, dother_ref, dnormed, dresid_ref, out_ref, drows_ref, dnorms_ref
        )


def embed_kernel(patches_ref, early_ref, valid_ref, start_ref, normed_ref, norms_ref):
    dim = start_ref.shape[1]
    norms = early_ref[:, dim : dim + 128].astype(SINGLE).T[:8]
    norms_ref[...] = norms
    for f in range(FRAMES):
        rows = frame_rows(f)
        start = dot(patches_ref[rows, :], early_ref[:, :dim]) * valid_ref[rows, :]
        start_ref[rows, :] = start
        normed_ref[rows, :] = low(layer_norm(start, norms[0:1], norms[1:2]))


def embed_bwd_kernel(
    patches_ref, start_ref, valid_ref, drows_ref, da_ref, db_ref, norms_ref, dnorms_ref, out_ref, dstart
):
    dim = start_ref.shape[1]
    d_gain, d_bias = jnp.zeros((1, dim), SINGLE), jnp.zeros((1, dim), SINGLE)
    for f in range(FRAMES):
        rows = frame_rows(f)
        d_value, gain, bias = norm_back(
            start_ref[rows, :], norms_ref[0:1, :], da_ref[rows, :] + db_ref[rows, :]
        )
        dstart[rows, :] = low((drows_ref[rows, :].astype(SINGLE) + d_value) * valid_ref[rows, :])
        d_gain, d_bias = d_gain + gain, d_bias + bias
    out_ref[:, :dim] = low(dot(patches_ref[...], dstart[...], TN))
    padded = jnp.concatenate(
        [d_gain, d_bias, dnorms_ref[...], jnp.zeros((120, dim), SINGLE)], axis=0
    )
    out_ref[:, dim : dim + 128] = low(padded.T)


def enter_frame_kernel(
    patches_ref, early_ref, valid_ref, mixed_ref, own_ref, other_ref, norms_ref, out_ref, normed_ref
):
    for f in range(FRAMES):
        rows = frame_rows(f)
        value = dot(patches_ref[rows, :], early_ref[:, : out_ref.shape[1]]) * valid_ref[rows, :]
        for place, (ref, at) in enumerate(
            ((own_ref, 0), (own_ref, 1), (other_ref, 0), (other_ref, 1))
        ):
            mixed = mixed_ref[rows, GROUP * place : GROUP * (place + 1)]
            value = value + dot(mixed, ref[at, :, QKV:], NT)
        out_ref[rows, :] = value
        normed_ref[rows, :] = low(layer_norm(value, norms_ref[2:3, :], norms_ref[3:4, :]))


def loss_kernel(
    dim,
    classes,
    proj,
    clip_ref,
    facts_ref,
    small_ref,
    resid_ref,
    valid_ref,
    norms_ref,
    loss_ref,
    dsmall_ref,
    pooled_ref,
    dresid_ref,
    drows_ref,
    dnorms_ref,
    dpool,
):
    facts = facts_ref[...]
    count = facts.shape[0]
    label, mate = (facts[:, dim + i : dim + i + 1].astype(jnp.int32) for i in range(2))
    pooled = low(facts[:, :dim] / facts[:, dim + 2 : dim + 3])
    pooled_ref[...] = pooled
    both = dot(pooled, small_ref[...])
    lane = lax.broadcasted_iota(jnp.int32, both.shape, 1)
    logits = jnp.where(lane < classes, both, -1e30)
    hot = (lane == label).astype(SINGLE)
    top = jnp.max(logits, axis=1, keepdims=True)
    raised = jnp.exp(logits - top)
    total = jnp.sum(raised, axis=1, keepdims=True)
    cross = top + jnp.log(total) - jnp.sum(both * hot, axis=1, keepdims=True)
    d_logits = raised / total - hot
    embedding = jnp.where((lane >= classes) & (lane < classes + proj), both, 0.0)
    inverse = lax.rsqrt(jnp.sum(embedding * embedding, axis=1, keepdims=True) + 1e-06)
    unit = embedding * inverse
    exact = functools.partial(
        lax.dot_general, precision=EXACT, preferred_element_type=SINGLE
    )
    similar = exact(unit, unit, NT) / TEMPER
    row = lax.broadcasted_iota(jnp.int32, (count, count), 0)
    col = lax.broadcasted_iota(jnp.int32, (count, count), 1)
    mate_hot = (col == mate).astype(SINGLE)
    masked = jnp.where(row == col, -1e30, similar)
    top = jnp.max(masked, axis=1, keepdims=True)
    raised = jnp.exp(masked - top)
    total = jnp.sum(raised, axis=1, keepdims=True)
    contrast = top + jnp.log(total) - jnp.sum(similar * mate_hot, axis=1, keepdims=True)
    loss_ref[...] = jnp.sum(cross + contrast, axis=0, keepdims=True)
    d_similar = (raised / total - mate_hot) / TEMPER
    d_unit = exact(d_similar, unit, NN) + exact(d_similar, unit, TN)
    d_embed = inverse * d_unit - embedding * (inverse * inverse * inverse) * jnp.sum(
        embedding * d_unit, axis=1, keepdims=True
    )
    dsmall_ref[...] = low(jnp.where(lane < classes, d_logits, d_embed))
    dpool[...] = dot(dsmall_ref[...], small_ref[...], NT) / facts[:, dim + 2 : dim + 3]
    d_pooled = dpool[pl.ds(clip_ref[0], 1), :]
    d_gain, d_bias = jnp.zeros((1, dim), SINGLE), jnp.zeros((1, dim), SINGLE)
    for f in range(FRAMES):
        rows = frame_rows(f)
        d_value, gain, bias = norm_back(
            resid_ref[rows, :], norms_ref[6:7, :], valid_ref[rows, :] * d_pooled
        )
        dresid_ref[rows, :] = d_value
        drows_ref[rows, :] = low(d_value)
        d_gain, d_bias = d_gain + gain, d_bias + bias
    dnorms_ref[0:1, :] = d_gain
    dnorms_ref[1:2, :] = d_bias


def adam_step(master, first, second, clipped, rate):
    first_new = BETA_ONE * first + (1.0 - BETA_ONE) * clipped
    second_new = BETA_TWO * second + (1.0 - BETA_TWO) * clipped * clipped
    first_hat = first_new / (1.0 - BETA_ONE**STEP)
    second_hat = second_new / (1.0 - BETA_TWO**STEP)
    master_new = master - rate * (first_hat / (jnp.sqrt(second_hat) + ADAM_EPS) + DECAY * master)
    return (master_new, first_new, second_new)


def adam_kernel(classes, proj, total_ref, *refs):
    masters, firsts, seconds, parts, outs = (
        refs[0:8], refs[8:16], refs[16:24], refs[24:30], refs[31:]
    )
    norm = jnp.sqrt(total_ref[...])
    refs[30][...] = norm
    factor = jnp.minimum(1.0, CLIP_AT / (norm + 1e-06))
    early, small, first, second, up, down = (ref[...] * factor for ref in parts)
    dim = masters[0].shape[1]
    columns = lambda k: slice(GROUP * k, GROUP * (k + 1))
    todo = [
        (0, ..., early[:, :dim]),
        (1, ..., early[:, dim : dim + 128].T[:8]),
        (2, ..., small[:, :classes]),
        (3, ..., small[:, classes : classes + proj]),
        (6, ..., up),
        (7, ..., down),
    ]
    for layer, grad in enumerate((first, second)):
        todo += [(4, (layer, k), grad[:, columns(k)]) for k in range(3)]
        todo.append((5, layer, grad[:, columns(3)].T))
    for i, at, grad in todo:
        results = adam_step(
            masters[i][at], firsts[i][at], seconds[i][at], grad, NORM_RATE if i == 1 else RATE
        )
        for j, result in enumerate(results):
            outs[3 * i + j][at] = result


def whole(shape):
    return pl.BlockSpec(shape, lambda g: (0,) * len(shape))


def per_group(rows, width):
    return pl.BlockSpec((1, rows, width), lambda g: (g, 0, 0))


def columns_of(width):
    return pl.BlockSpec((1, FRAMES, width, SLOTS), lambda g: (g, 0, 0, 0))


def shaped(*shape, dtype=SINGLE):
    return jax.ShapeDtypeStruct(shape, dtype)


def spec_of(value):
    shape = value.shape
    if len(shape) == 4:
        return columns_of(shape[2])
    return per_group(*shape[1:]) if len(shape) == 3 else whole(shape)


def call(kernel, name, inputs, outputs, scratch=(), gflops=1, steps=2, in_specs=None):
    return pl.pallas_call(
        kernel,
        grid=(steps,),
        in_specs=in_specs or [spec_of(value) for value in inputs],
        out_specs=[spec_of(value) for value in outputs],
        out_shape=list(outputs),
        scratch_shapes=[pltpu.VMEM(shape, dtype) for shape, dtype in scratch],
        compiler_params=pltpu.CompilerParams(vmem_limit_bytes=GRANT),
        cost_estimate=pl.CostEstimate(
            flops=gflops * 10**9, bytes_accessed=8 << 20, transcendentals=0
        ),
        name=name,
    )(*inputs)


def by_group(width, rows=ROWS):
    return shaped(2, rows, width, dtype=LOWER)


def temporal_forward(normed, weight):
    return call(
        temporal_fwd_kernel,
        "temporal_forward",
        (normed, weight),
        (shaped(2, FRAMES, QKV, SLOTS, dtype=LOWER), by_group(GROUP)),
        [((FRAMES, GROUP, SLOTS), LOWER)],
        5,
    )


def temporal_backward(normed, grad, weight, qkv, mixed):
    dim = normed.shape[1]
    return call(
        temporal_bwd_kernel,
        "temporal_backward",
        (normed, grad, weight, qkv, mixed),
        (by_group(dim, dim), shaped(ROWS, dim)),
        [((ROWS, QKV), LOWER), ((FRAMES, GROUP, SLOTS), LOWER), ((FRAMES, QKV, SLOTS), LOWER)],
        14,
    )


def spatial_forward(normed, weight, key_extra, last=None):
    dim = normed.shape[1]
    saved = (by_group(QKV), by_group(GROUP), by_group(GROUP))
    inputs = (normed, weight, key_extra)
    if last is None:
        return call(
            spatial_fwd_kernel, "spatial_forward", inputs, (*saved, shaped(ROWS, dim)), [], 15
        )
    return call(
        spatial_fwd_last_kernel,
        "spatial_forward",
        (*inputs, *last),
        (*saved, shaped(ROWS, dim), shaped(ROWS, dim, dtype=LOWER)),
        [((ROWS, dim), SINGLE)],
        15,
    )


def spatial_backward(normed, grad, weight, qkv, mixed, extra, key_extra, last=None):
    dim = normed.shape[1]
    inputs = (normed, grad, weight, qkv, mixed, extra, key_extra)
    scratch = [((ROWS, QKV), LOWER)]
    if last is None:
        outputs = (by_group(dim, dim), shaped(ROWS, dim))
        return call(spatial_bwd_kernel, "spatial_backward", inputs, outputs, scratch, 30)
    return call(
        spatial_bwd_last_kernel,
        "spatial_backward",
        (*inputs, *last),
        (by_group(dim, dim), shaped(ROWS, dim, dtype=LOWER), shaped(2, dim)),
        scratch + [((ROWS, dim), SINGLE)],
        30,
    )


def feed_forward(normed, up, down, last=None):
    dim, width = normed.shape[1], up.shape[2]
    inputs, saved = (normed, up, down), (by_group(width), by_group(width))
    if last is None:
        return call(feed_fwd_kernel, "feed_forward", inputs, (*saved, shaped(ROWS, dim)), [], 10)
    return call(
        feed_fwd_last_kernel,
        "feed_forward",
        (*inputs, *last),
        (*saved, shaped(ROWS, dim), shaped(1, dim)),
        [((ROWS, dim), SINGLE)],
        10,
    )


def feed_backward(normed, grad, up, down, act, slope, last=None):
    dim, width = normed.shape[1], up.shape[2]
    inputs = (normed, grad, up, down, act, slope)
    weights = (by_group(width, dim), by_group(width, dim))
    scratch = [((ROWS, width), LOWER)]
    if last is None:
        outputs = (*weights, shaped(ROWS, dim))
        return call(feed_bwd_kernel, "feed_backward", inputs, outputs, scratch, 15)
    return call(
        feed_bwd_last_kernel,
        "feed_backward",
        (*inputs, *last),
        (*weights, shaped(ROWS, dim), shaped(ROWS, dim, dtype=LOWER), shaped(2, dim)),
        scratch + [((ROWS, dim), SINGLE)],
        15,
    )


def embed(patches, early, valid):
    dim = patches.shape[1]
    outputs = (shaped(ROWS, dim), shaped(ROWS, dim, dtype=LOWER), shaped(8, dim))
    return call(embed_kernel, "embed", (patches, early, valid), outputs, steps=1)


def embed_backward(patches, start, valid, d_rows, d_a, d_b, norms, d_norms):
    dim = patches.shape[1]
    return call(
        embed_bwd_kernel,
        "embed_backward",
        (patches, start, valid, d_rows, d_a, d_b, norms, d_norms),
        (shaped(dim, dim + 128, dtype=LOWER),),
        [((ROWS, dim), LOWER)],
        2,
        1,
    )[0]


def enter_frame(patches, early, valid, mixed, own, other, norms):
    dim = patches.shape[1]
    inputs = (patches, early, valid, mixed, own, other, norms)
    return call(
        enter_frame_kernel,
        "enter_frame",
        inputs,
        (shaped(ROWS, dim), shaped(ROWS, dim, dtype=LOWER)),
        [],
        2,
        1,
        [whole(value.shape) for value in inputs],
    )


def all_losses(clip, facts, small, resid, valid, norms, classes, proj):
    count, dim = facts.shape[0], resid.shape[1]
    inputs = (facts, small, resid, valid, norms)
    return call(
        functools.partial(loss_kernel, dim, classes, proj),
        "losses",
        (clip, *inputs),
        (
            shaped(1, 1),
            shaped(count, dim, dtype=LOWER),
            shaped(count, dim, dtype=LOWER),
            shaped(ROWS, dim),
            shaped(ROWS, dim, dtype=LOWER),
            shaped(2, dim),
        ),
        [((count, dim), SINGLE)],
        1,
        1,
        [pl.BlockSpec(memory_space=pltpu.SMEM)] + [whole(value.shape) for value in inputs],
    )


def optimizer(total, masters, firsts, seconds, parts, classes, proj):
    inputs = (total, *masters, *firsts, *seconds, *parts)
    outputs = [shaped(1, 1)] + [shaped(*value.shape) for value in masters for _ in range(3)]
    return pl.pallas_call(
        functools.partial(adam_kernel, classes, proj),
        grid=(1,),
        in_specs=[whole(value.shape) for value in inputs],
        out_specs=[whole(value.shape) for value in outputs],
        out_shape=outputs,
        compiler_params=pltpu.CompilerParams(vmem_limit_bytes=GRANT),
        name="optimizer",
    )(*inputs)


def tick(*values):
    return lax.optimization_barrier(values)


def summed(terms):
    return functools.reduce(jnp.add, (term.astype(SINGLE) for term in terms))


class Cube:
    def __init__(self, sizes):
        self.count = sizes["batch"] * sizes["head"]
        self.mine = lax.axis_index(ALL)
        batch_bits = sizes["batch"].bit_length() - 1
        self.batch_masks = [4 << k for k in reversed(range(batch_bits))]

    def swap(self, value, mask):
        return lax.ppermute(value, ALL, [(i, i ^ mask) for i in range(self.count)])

    def has(self, mask):
        return (self.mine & mask) != 0

    def join(self, value, *masks):
        for mask in masks:
            other = self.swap(value, mask)
            has = self.has(mask)
            both = jnp.stack([jnp.where(has, other, value), jnp.where(has, value, other)], axis=-3)
            shape = value.shape
            value = both.reshape(*shape[:-3], 2 * shape[-3], *shape[-2:])
        return value

    def fork(self, value):
        return jnp.stack([value, self.swap(value, 2)])


    def shed(self, terms, *masks):
        for mask in masks:
            shape = terms[0].shape
            has = self.has(mask)
            send, keep = [], []
            for term in terms:
                pair = term.reshape(*shape[:-3], shape[-3] // 2, 2, *shape[-2:])
                send.append(jnp.where(has, pair[..., 0, :, :], pair[..., 1, :, :]))
                keep.append(jnp.where(has, pair[..., 1, :, :], pair[..., 0, :, :]))
            terms = keep + [self.swap(low(summed(send)), mask)]
        return terms

    def meet(self, terms):
        send = low(summed([term[1] for term in terms]))
        return [term[0] for term in terms] + [self.swap(send, 2)]

    def total(self, value):
        for mask in [1, 2] + self.batch_masks[::-1]:
            value = value + self.swap(value, mask)
        return value

    def swap_frames(self, parts):
        return [parts[0]] + [self.swap(parts[r], r) for r in range(1, FRAMES)]


def body(sizes, *args):
    patches, bucket, labels, partner = args[:4]
    views = [lambda v: v] * 4 + [
        lambda v: v.transpose(0, 2, 1, 3), lambda v: v, lambda v: v, lambda v: v.T
    ]
    masters, firsts, seconds = (
        [view(value) for view, value in zip(views, args[4 + 8 * i : 12 + 8 * i])] for i in range(3)
    )
    patch_weight, norm_params, head_weight, proj_weight, attn_in, attn_out, up, down = masters
    cube = Cube(sizes)
    dim = norm_params.shape[1] * cube.count
    classes, proj = head_weight.shape[1], proj_weight.shape[1]
    rows_wide, rows_small = attn_in.shape[2], patch_weight.shape[0]
    place = lax.axis_index("head")

    *first, near, last = cube.batch_masks
    middle = dim // 2
    flat = lambda value: value.reshape(2, dim, -1)
    blocked = lambda value: value.reshape(*value.shape[:-2], -1, rows_wide, value.shape[-1])
    pack = lambda w_in, w_out: jnp.concatenate(
        [low(w_in[0]), low(w_in[1]), low(w_in[2]), low(w_out).T], axis=1
    )[None]
    patch_count = jnp.where(bucket == 1, PMAX, PSMALL)
    offset = jnp.arange(SLOTS)[None, :]
    number = (place ^ jnp.arange(FRAMES))[:, None]
    frame_valid = ((number * SLOTS + offset) < patch_count).reshape(ROWS, 1).astype(SINGLE)
    slot_valid = (jnp.broadcast_to(place * SLOTS + offset, (FRAMES, SLOTS)) < patch_count).reshape(
        ROWS, 1
    ).astype(SINGLE)
    lane = jnp.arange(HD)[None, :]
    key_extra = low(
        jnp.where(lane == 0, jnp.where(frame_valid > 0, 0.0, -1e30), (lane < 4).astype(SINGLE))
    )

    first_w = pack(attn_in[0], attn_out[0])
    first_w, clip, w_patch, w_norms = tick(first_w, patches[0], patch_weight, norm_params)
    first_w = cube.join(first_w, *first)
    early = jnp.concatenate([low(w_patch), low(w_norms).T], axis=1)
    early = jnp.pad(early, ((0, 0), (0, 120)))[None]
    early = cube.join(early, *first)
    blocks = jnp.pad(clip, ((0, ROWS - PMAX), (0, 0))).reshape(FRAMES, SLOTS, -1)
    blocks = jnp.where((place & 1) != 0, blocks[jnp.array([1, 0, 3, 2])], blocks)
    blocks = jnp.where((place & 2) != 0, blocks[jnp.array([2, 3, 0, 1])], blocks)
    second_w = pack(attn_in[1], attn_out[1])
    first_w, early, blocks, second_w = tick(first_w, early, blocks, second_w)

    first_w = cube.join(first_w, near)
    early = cube.join(early, near)
    by_frame = blocks.reshape(ROWS, -1)
    by_slot = jnp.concatenate(cube.swap_frames(list(blocks)))
    up_w, down_w = low(up)[None], low(down)[None]
    first_w, early, by_slot, up_w, down_w = tick(first_w, early, by_slot, up_w, down_w)

    left = cube.join(first_w[..., :middle], last)
    right = cube.fork(first_w[..., middle:])
    early = cube.join(early, last)
    second_w, up_w = cube.join(second_w, *first), cube.join(up_w, *first)
    left, right, early, second_w, up_w = tick(left, right, early, second_w, up_w)

    left, right = cube.fork(left), cube.join(right, last)
    own_first = jnp.concatenate([flat(left), flat(right)], axis=-1)
    early = cube.join(early, 2)
    second_w, up_w = cube.join(second_w, near), cube.join(up_w, near)
    own_first, early, second_w, up_w = tick(own_first, early, second_w, up_w)

    early = cube.join(early, 1).reshape(dim, -1)
    other_first = cube.swap(own_first, 1)
    second_w, up_w, down_w = cube.fork(second_w), cube.join(up_w, last), cube.join(down_w, *first)
    start_slot, normed_t, norms = embed(by_slot, early, slot_valid)
    qkv_t, mixed_t = [None, None], [None, None]
    qkv_t[0], mixed_t[0] = temporal_forward(normed_t, own_first)
    mixed_t[0], normed_t, second_w, other_first, up_w, down_w = tick(
        mixed_t[0], normed_t, second_w, other_first, up_w, down_w
    )
    qkv_t[1], mixed_t[1] = temporal_forward(normed_t, other_first)
    own_second, down_w = flat(cube.join(second_w, last)), cube.join(down_w, near)
    small = jnp.concatenate([low(head_weight), low(proj_weight)], axis=1)
    small = cube.join(jnp.pad(small, ((0, 0), (0, dim - small.shape[1])))[None], *first)
    order = (0, 2, 1, 3)
    pieces = {m: mixed_t[m % 2][m // 2] for m in range(4)}
    parts = [
        jnp.concatenate([pieces[m ^ r][frame_rows(r)] for m in order], axis=1)
        for r in range(FRAMES)
    ]
    parts[0], parts[1], parts[2], parts[3], down_w, small = tick(*parts, down_w, small)

    mixed_frame = jnp.concatenate(cube.swap_frames(parts))
    small = cube.join(small, near)
    mixed_frame, own_second, small = tick(mixed_frame, own_second, small)

    resid_one, normed_s = enter_frame(
        by_frame, early, frame_valid, mixed_frame, own_first, other_first, norms
    )
    down_w, own_up = cube.fork(down_w), flat(cube.fork(up_w))
    other_second = cube.swap(own_second, 1)
    small = cube.join(small, last)
    qkv_s, mixed_s, extra_s = ([None, None] for _ in range(3))
    qkv_s[0], mixed_s[0], extra_s[0], branch = spatial_forward(normed_s, own_second, key_extra)
    branch, normed_s, other_second, down_w, small = tick(
        branch, normed_s, other_second, down_w, small
    )
    own_down = flat(cube.join(down_w, last))
    qkv_s[1], mixed_s[1], extra_s[1], resid_two, normed_m = spatial_forward(
        normed_s, other_second, key_extra, (resid_one, branch, norms)
    )
    normed_m, own_up, own_down = tick(normed_m, own_up, own_down)

    other_up, other_down = cube.swap(own_up, 1), cube.swap(own_down, 1)
    small = cube.join(small, 2)
    act, slope = ([None, None] for _ in range(2))
    act[0], slope[0], branch = feed_forward(normed_m, own_up, own_down)
    branch, normed_m, other_up, other_down, small = tick(
        branch, normed_m, other_up, other_down, small
    )
    act[1], slope[1], resid_three, sums = feed_forward(
        normed_m, other_up, other_down, (resid_two, branch, norms, frame_valid)
    )
    small = cube.join(small, 1).reshape(dim, -1)

    for mask in (1, 2):
        sums = sums + cube.swap(sums, mask)
    facts = jnp.stack([labels[0], partner[0], FRAMES * patch_count[0]]).astype(SINGLE)
    gathered = jnp.concatenate([sums, jnp.pad(facts, (0, 125))[None]], axis=1)[None]
    gathered = cube.join(gathered, *cube.batch_masks)[:, 0]
    clip = lax.axis_index("batch").reshape(1)
    loss_sum, d_small, pooled_low, d_resid, d_rows, d_norms_f = all_losses(
        clip, gathered, small, resid_three, frame_valid, norms, classes, proj
    )

    d_up, d_down = [None, None], [None, None]
    d_up[1], d_down[1], d_normed = feed_backward(
        normed_m, d_rows, other_up, other_down, act[1], slope[1]
    )
    up_other, down_other, d_normed, d_rows, normed_m = tick(
        d_up[1], d_down[1], d_normed, d_rows, normed_m
    )
    core_up, core_down = cube.swap(up_other, 1), cube.swap(down_other, 1)
    d_up[0], d_down[0], d_resid, d_rows, d_norms_m = feed_backward(
        normed_m,
        d_rows,
        own_up,
        own_down,
        act[0],
        slope[0],
        (resid_two, d_resid, d_normed, norms),
    )
    d_resid, d_rows, up_own, down_own, core_up, core_down = tick(
        d_resid, d_rows, d_up[0], d_down[0], core_up, core_down
    )

    sum_up = cube.meet([blocked(up_own), blocked(core_up)])
    sum_down = cube.shed([blocked(down_own), blocked(core_down)], last)
    d_second = [None, None]
    d_second[1], d_normed = spatial_backward(
        normed_s, d_rows, other_second, qkv_s[1], mixed_s[1], extra_s[1], key_extra
    )
    d_small = lax.dynamic_slice_in_dim(
        dot(pooled_low, d_small, TN), cube.mine * rows_small, rows_small, 0
    )
    second_other, d_normed, d_rows, normed_s, sum_up[-1], sum_down[-1], d_small = tick(
        d_second[1], d_normed, d_rows, normed_s, sum_up[-1], sum_down[-1], d_small
    )
    core_second = cube.swap(second_other, 1)
    sum_up, sum_down = cube.shed(sum_up, last), cube.meet(sum_down)
    d_second[0], d_rows, d_norms_s = spatial_backward(
        normed_s,
        d_rows,
        own_second,
        qkv_s[0],
        mixed_s[0],
        extra_s[0],
        key_extra,
        (resid_one, d_resid, d_normed, norms),
    )
    d_rows, second_own, sum_up[-1], sum_down[-1], core_second = tick(
        d_rows, d_second[0], sum_up[-1], sum_down[-1], core_second
    )

    d_rows = jnp.concatenate(cube.swap_frames(split_frames(d_rows)))
    sum_second = cube.shed([blocked(second_own), blocked(core_second)], last)
    d_rows, up_last, down_last = tick(d_rows, sum_up[-1], sum_down[-1])
    sum_up[-1], sum_down[-1] = up_last, down_last

    sum_up, sum_down = cube.shed(sum_up, near), cube.shed(sum_down, near)
    d_first, d_normed = [None, None], [None, None]
    d_first[1], d_normed[1] = temporal_backward(
        normed_t, d_rows, other_first, qkv_t[1], mixed_t[1]
    )
    first_other, d_normed[1], d_rows, normed_t, sum_up[-1], sum_down[-1], sum_second[-1] = tick(
        d_first[1], d_normed[1], d_rows, normed_t, sum_up[-1], sum_down[-1], sum_second[-1]
    )
    core_first = cube.swap(first_other, 1)
    sum_second = cube.meet(sum_second)
    sum_up, sum_down = cube.shed(sum_up, *first[::-1]), cube.shed(sum_down, *first[::-1])
    d_first[0], d_normed[0] = temporal_backward(
        normed_t, d_rows, own_first, qkv_t[0], mixed_t[0]
    )
    d_rows, first_own, d_normed[0], core_first, sum_second[-1], sum_up[-1], sum_down[-1] = tick(
        d_rows, d_first[0], d_normed[0], core_first, sum_second[-1], sum_up[-1], sum_down[-1]
    )

    sum_first = [blocked(first_own), blocked(core_first)]
    left = cube.meet([term[..., :middle] for term in sum_first])
    right = cube.shed([term[..., middle:] for term in sum_first], last)
    sum_second = cube.shed(sum_second, near)
    d_norms = jnp.concatenate([d_norms_s, d_norms_m, d_norms_f])
    d_early = embed_backward(
        by_slot, start_slot, slot_valid, d_rows, d_normed[0], d_normed[1], norms, d_norms
    )
    sum_early = cube.shed([d_early.reshape(-1, rows_small, dim + 128)], 1)
    d_up, d_down = summed(sum_up)[0], summed(sum_down)[0]
    square = lambda value: jnp.sum(value * value)
    squares = square(d_small) + square(d_up) + square(d_down)
    left[-1], right[-1], sum_early[-1], sum_second[-1], squares = tick(
        left[-1], right[-1], sum_early[-1], sum_second[-1], squares
    )
    left, right = cube.shed(left, last), cube.meet(right)
    sum_early = cube.shed(sum_early, 2)
    sum_second = cube.shed(sum_second, *first[::-1])
    left[-1], right[-1], sum_early[-1], sum_second[-1] = tick(
        left[-1], right[-1], sum_early[-1], sum_second[-1]
    )
    sum_first = [jnp.concatenate([summed(left), summed(right)], axis=-1)]
    sum_first = cube.shed(sum_first, near)
    sum_early = cube.shed(sum_early, last)
    d_second = summed(sum_second)[0]
    squares = squares + square(d_second)
    sum_first[-1], sum_early[-1], squares = tick(sum_first[-1], sum_early[-1], squares)
    sum_first = cube.shed(sum_first, *first[::-1])
    sum_early = cube.shed(sum_early, near)
    sum_first[-1], sum_early[-1] = tick(sum_first[-1], sum_early[-1])
    sum_early = cube.shed(sum_early, *first[::-1])
    d_first, d_early = summed(sum_first)[0], summed(sum_early)[0]

    total = cube.total((squares + square(d_first) + square(d_early)).reshape(1, 1))
    parts = (d_early, d_small, d_first, d_second, d_up, d_down)
    grad_norm, *updates = optimizer(total, masters, firsts, seconds, parts, classes, proj)
    updates = [views[i // 3](update) for i, update in enumerate(updates)]
    return (loss_sum[0, 0], grad_norm[0, 0], *updates)


def solution(mesh):
    placed = (
        P("batch", "head", None),
        P("batch"),
        P("batch"),
        P("batch"),
        P(("batch", "head"), None),
        P(None, ("batch", "head")),
        P(("batch", "head"), None),
        P(("batch", "head"), None),
        P(None, "batch", None, "head"),
        P(None, "head", "batch"),
        P("batch", "head"),
        P("head", "batch"),
        P(("batch", "head"), None),
        P(None, ("batch", "head")),
        P(("batch", "head"), None),
        P(("batch", "head"), None),
        P(None, "batch", None, "head"),
        P(None, "head", "batch"),
        P("batch", "head"),
        P("head", "batch"),
        P(("batch", "head"), None),
        P(None, ("batch", "head")),
        P(("batch", "head"), None),
        P(("batch", "head"), None),
        P(None, "batch", None, "head"),
        P(None, "head", "batch"),
        P("batch", "head"),
        P("head", "batch"),
    )
    return jax.shard_map(
        functools.partial(body, dict(mesh.shape)),
        mesh=mesh,
        in_specs=placed,
        out_specs=(
            P(),
            P(),
            P(("batch", "head"), None),
            P(("batch", "head"), None),
            P(("batch", "head"), None),
            P(None, ("batch", "head")),
            P(None, ("batch", "head")),
            P(None, ("batch", "head")),
            P(("batch", "head"), None),
            P(("batch", "head"), None),
            P(("batch", "head"), None),
            P(("batch", "head"), None),
            P(("batch", "head"), None),
            P(("batch", "head"), None),
            P(None, "batch", None, "head"),
            P(None, "batch", None, "head"),
            P(None, "batch", None, "head"),
            P(None, "head", "batch"),
            P(None, "head", "batch"),
            P(None, "head", "batch"),
            P("batch", "head"),
            P("batch", "head"),
            P("batch", "head"),
            P("head", "batch"),
            P("head", "batch"),
            P("head", "batch"),
        ),
        check_vma=False,
    )
```

time: 696 us -> 592 us (0.85)
  matrix products: 78.4 us -> 0.51 us
  Pallas kernels: 158 us -> 228 us
  waiting for transfers between devices: 203 us -> 158 us
  other arithmetic: 90.8 us -> 71.3 us
  local copies, waits for them, and re-layouts: 51.5 us -> 32.8 us
    dot_general x34 -> x1, matrix products: 77.9 us -> 0.51 us  [dot(): return lax.dot_general(left, right, dims, preferred_element_type=SINGLE)]
    pallas_call x8 -> x17, Pallas kernels: 158 us -> 228 us  [the longest x16 222 us: call(): pl.pallas_call(kernel, grid=(steps,), in_specs=in_specs or [spec_of(value...]
    ppermute x79 -> x78, waiting for transfers between devices: 203 us -> 158 us  [swap(): return lax.ppermute(value, ALL, [(i, i ^ mask) for i in range(self.count)])]
    reduce_sum x24 -> x6, other arithmetic: 29.8 us -> 8.96 us  [body(): square = lambda value: jnp.sum(value * value)]
    unnamed x316 -> x113, local copies, waits for them, and re-layouts: 28.8 us -> 10.1 us
    select_n x4 -> x32, other arithmetic: 0.89 us -> 14.7 us  [shed(): keep.append(jnp.where(has, pair[..., 1, :, :], pair[..., 0, :, :]))]
    convert_element_type x27 -> x23, other arithmetic: 11.1 us -> 21.5 us  [low(): return value.astype(LOWER)]
    sub x8 -> x0, other arithmetic: 8.96 us -> none  [adam_step(): master - rate * (first_hat / (jnp.sqrt(second_hat) + ADAM_EPS) + DECAY *...]
  transfers between devices with their start and end apart: 79 -> 78, of which waited for: 42 -> 43; matrix products, arithmetic and copies ran while one was open for 17% -> 9% of each run, Pallas kernels for 9% -> 31%
where the time goes in v2:
time: 592 us; the launch traced here: 585 us
  Pallas kernels  228 us (39%)
  waiting for transfers between devices  158 us (27%)
  starting transfers between devices  83.1 us (14%)
  other arithmetic  71.3 us (12%)
  local copies, waits for them, and re-layouts  32.8 us (6%)
  between operations  11.4 us (2%)
    pallas_call x16, Pallas kernels, call(): pl.pallas_call(kernel, grid=(steps,), in_specs=in_specs or [spec_of(value...  222 us
    ppermute x78, waiting for transfers between devices, swap(): return lax.ppermute(value, ALL, [(i, i ^ mask) for i in range(self.count)])  158 us
    ppermute x78, starting transfers between devices, swap(): return lax.ppermute(value, ALL, [(i, i ^ mask) for i in range(self.count)])  83.1 us
    convert_element_type x23, other arithmetic, low(): return value.astype(LOWER)  21.5 us
    select_n x32, other arithmetic, shed(): keep.append(jnp.where(has, pair[..., 1, :, :], pair[..., 0, :, :]))  14.7 us
  transfers between devices with their start and end apart: 78, of which 43 were waited for; matrix products, arithmetic and copies ran while one was open for 9% of the time, Pallas kernels for 31%

profile of v2, /device:TPU:0, one launch (start us, length us, event | category | flops | bytes accessed | tf_op | source)
XLA Modules:
  0.0 584.7 jit_solution(9520413707166755851)
XLA Ops:
  2.9 4.0 collective-permute-start.23
  9.6 2.9 collective-permute-start
  18.9 1.9 collective-permute-done
  20.9 2.3 collective-permute-start.10
  24.1 2.9 collective-permute-done.3
  28.6 5.5 collective-permute-done.2
  34.3 5.8 collective-permute-done.5
  41.3 2.6 collective-permute-start.11
  46.1 5.0 collective-permute-done.11
  51.2 5.2 collective-permute-done.7
  57.2 7.1 %collective-permute-done.8 = bf16[4,96,384]{2,1,0:T(8,128)(2,1)S(1)} collective-permute-done((bf16[4,96,384]{2,1,0:T(8,128)(2,1)S(1)}, bf16[4,96,384]{2,1,0:T(8,128)(2,1)S(1)}, u32[]{:S(2)}, u32[]{:S(2)}) %collective-permute-start.8) | collective-permute-done | bytes 294944 | tf_op jit(solution)/shard_map/ppermute | solution.py:794
  65.2 1.9 collective-permute-start.16
  69.7 4.7 collective-permute-done.15
  79.8 4.5 collective-permute-done.13
  84.7 3.2 collective-permute-done.12
  94.9 5.3 collective-permute-done.21
  101.2 4.5 collective-permute-done.20
  106.0 2.6 collective-permute-done.18
  111.4 5.0 embed.1
  116.5 6.4 %temporal_forward.2 = (bf16[2,4,576,208]{3,2,1,0:T(8,128)(2,1)}, bf16[2,832,192]{2,1,0:T(8,128)(2,1)}) custom-call(bf16[832,768]{1,0:T(8,128)(2,1)} %get-tuple-element.320.normed_ref, bf16[2,768,768]{2,1,0:T(8,128)(2,1)} %copy-done.3), custom_call_target="tpu_custom_call" | custom-call | flops 5000000000 | bytes 8388608 | tf_op jit(solution)/shard_map/temporal_forward/pallas_call | solution.py:598
  126.4 6.2 %temporal_forward.3 = (bf16[2,4,576,208]{3,2,1,0:T(8,128)(2,1)}, bf16[2,832,192]{2,1,0:T(8,128)(2,1)}) custom-call(bf16[832,768]{1,0:T(8,128)(2,1)} %get-tuple-element.320.normed_ref, bf16[2,768,768]{2,1,0:T(8,128)(2,1)} %collective-permute-done.19.weight_ref.other_ref), custom_call_target="tpu_custom_call" | custom-call | flops 5000000000 | bytes 8388608 | tf_op jit(solution)/shard_map/temporal_forward/pallas_call | solution.py:598
  142.2 4.9 collective-permute-done.25
  147.1 6.1 %collective-permute-done.26 = bf16[208,768]{1,0:T(8,128)(2,1)S(1)} collective-permute-done((bf16[208,768]{1,0:T(8,128)(2,1)S(1)}, bf16[208,768]{1,0:T(8,128)(2,1)S(1)}, u32[]{:S(2)}, u32[]{:S(2)}) %collective-permute-start.26) | collective-permute-done | bytes 319520 | tf_op jit(solution)/shard_map/ppermute | solution.py:794
  158.4 8.3 %collective-permute-done.30 = bf16[4,96,768]{2,1,0:T(8,128)(2,1)} collective-permute-done((bf16[4,96,768]{2,1,0:T(8,128)(2,1)}, bf16[4,96,768]{2,1,0:T(8,128)(2,1)}, u32[]{:S(2)}, u32[]{:S(2)}) %collective-permute-start.30) | collective-permute-done | bytes 589856 | tf_op jit(solution)/shard_map/ppermute | solution.py:794
  169.6 9.2 %enter_frame.1 = (f32[832,768]{1,0:T(8,128)}, bf16[832,768]{1,0:T(8,128)(2,1)}) custom-call(bf16[832,768]{1,0:T(8,128)(2,1)} %bitcast.812, bf16[768,896]{1,0:T(8,128)(2,1)} %bitcast.835, f32[832,1]{1,0:T(8,128)} %reshape.2400.valid_ref, bf16[832,768]{1,0:T(8,128)(2,1)} %pad_maximum_fusion.6.mixed_ref, bf16[2,768,768]{2,1,0:T(8,128)(2,1)} %copy-done.3, ...), custom_call_target="tpu_custom_call" | custom-call | flops 2000000000 | bytes 8388608 | tf_op jit(solution)/shard_map/enter_frame/pallas_call | solution.py:598
  178.8 15.3 %spatial_forward.2 = (bf16[2,832,576]{2,1,0:T(8,128)(2,1)}, bf16[2,832,192]{2,1,0:T(8,128)(2,1)}, bf16[2,832,192]{2,1,0:T(8,128)(2,1)}, f32[832,768]{1,0:T(8,128)}) custom-call(bf16[832,768]{1,0:T(8,128)(2,1)} %get-tuple-element.296.normed_ref, bf16[2,768,768]{2,1,0:T(8,128)(2,1)} %bitcast.881, bf16[832,64]{1,0:T(8,128)(2,1)} %select_convert_fusion.1.key_extra_ref), custom_call_target="tpu_custom_call" | custom-call | flops 15000000512 | bytes 8388608 | tf_op jit(solution)/shard_map/spatial_forward/pallas_call | solution.py:598
  196.5 18.8 %spatial_forward.3 = (bf16[2,832,576]{2,1,0:T(8,128)(2,1)}, bf16[2,832,192]{2,1,0:T(8,128)(2,1)}, bf16[2,832,192]{2,1,0:T(8,128)(2,1)}, f32[832,768]{1,0:T(8,128)}, bf16[832,768]{1,0:T(8,128)(2,1)}) custom-call(bf16[832,768]{1,0:T(8,128)(2,1)} %get-tuple-element.296.normed_ref, bf16[2,768,768]{2,1,0:T(8,128)(2,1)} %collective-permute-done.29.weight_ref, ...), custom_call_target="tpu_custom_call" | custom-call | flops 15000000512 | bytes 8388608 | tf_op jit(solution)/shard_map/spatial_forward/pallas_call | solution.py:598
  215.3 7.6 %collective-permute-done.33 = bf16[2,4,96,768]{3,2,1,0:T(8,128)(2,1)S(1)} collective-permute-done((bf16[2,4,96,768]{3,2,1,0:T(8,128)(2,1)S(1)}, bf16[2,4,96,768]{3,2,1,0:T(8,128)(2,1)S(1)}, u32[]{:S(2)}, u32[]{:S(2)}) %collective-permute-start.33) | collective-permute-done | bytes 1179680 | tf_op jit(solution)/shard_map/ppermute | solution.py:794
  227.1 6.0 %collective-permute-done.36 = bf16[8,24,768]{2,1,0:T(8,128)(2,1)S(1)} collective-permute-done((bf16[8,24,768]{2,1,0:T(8,128)(2,1)S(1)}, bf16[8,24,768]{2,1,0:T(8,128)(2,1)S(1)}, u32[]{:S(2)}, u32[]{:S(2)}) %collective-permute-start.36) | collective-permute-done | bytes 294944 | tf_op jit(solution)/shard_map/ppermute | solution.py:794
  233.2 9.7 %feed_forward.2 = (bf16[2,832,768]{2,1,0:T(8,128)(2,1)}, bf16[2,832,768]{2,1,0:T(8,128)(2,1)}, f32[832,768]{1,0:T(8,128)}) custom-call(bf16[832,768]{1,0:T(8,128)(2,1)} %get-tuple-element.272.normed_ref, bf16[2,768,768]{2,1,0:T(8,128)(2,1)} %pad_maximum_fusion.2.up_ref, bf16[2,768,768]{2,1,0:T(8,128)(2,1)} %bitcast.884), custom_call_target="tpu_custom_call" | custom-call | flops 10000000000 | bytes 8388608 | tf_op jit(solution)/shard_map/feed_forward/pallas_call | solution.py:598
  243.0 13.5 %feed_forward.3 = (bf16[2,832,768]{2,1,0:T(8,128)(2,1)}, bf16[2,832,768]{2,1,0:T(8,128)(2,1)}, f32[832,768]{1,0:T(8,128)}, f32[1,768]{1,0:T(1,128)}) custom-call(bf16[832,768]{1,0:T(8,128)(2,1)} %get-tuple-element.272.normed_ref, bf16[2,768,768]{2,1,0:T(8,128)(2,1)} %collective-permute-done.34.up_ref, bf16[2,768,768]{2,1,0:T(8,128)(2,1)} %collective-permute-done.35.down_ref, ...), custom_call_target="tpu_custom_call" | custom-call | flops 10000000000 | bytes 8388608 | tf_op jit(solution)/shard_map/feed_forward/pallas_call | solution.py:598
  262.2 2.7 collective-permute-start.39
  268.6 1.9 collective-permute-done.40
  271.2 3.2 collective-permute-done.41
  276.4 7.2 %losses.1 = (f32[1,1]{1,0:T(1,128)}, bf16[8,768]{1,0:T(8,128)(2,1)}, bf16[8,768]{1,0:T(8,128)(2,1)}, f32[832,768]{1,0:T(8,128)}, bf16[832,768]{1,0:T(8,128)(2,1)}, /*index=5*/f32[2,768]{1,0:T(2,128)}) custom-call(s32[1]{0:T(128)} %bitcast.clip_ref, f32[8,896]{1,0:T(8,128)} %squeeze_reshape.3.facts_ref, bf16[768,768]{1,0:T(8,128)(2,1)} %bitcast.858, ...), custom_call_target="tpu_custom_call" | custom-call | flops 1000000000 | bytes 8388608 | tf_op jit(solution)/shard_map/losses/pallas_call | solution.py:598
  283.6 14.6 %feed_backward.2 = (bf16[2,768,768]{2,1,0:T(8,128)(2,1)}, bf16[2,768,768]{2,1,0:T(8,128)(2,1)}, f32[832,768]{1,0:T(8,128)}) custom-call(bf16[832,768]{1,0:T(8,128)(2,1)} %get-tuple-element.272.normed_ref, bf16[832,768]{1,0:T(8,128)(2,1)} %get-tuple-element.273.grad_ref, bf16[2,768,768]{2,1,0:T(8,128)(2,1)} %collective-permute-done.34.up_ref, ...), custom_call_target="tpu_custom_call" | custom-call | flops 15000000512 | bytes 8388608 | tf_op jit(solution)/shard_map/feed_backward/pallas_call | solution.py:598
  299.9 19.8 %feed_backward.3 = (bf16[2,768,768]{2,1,0:T(8,128)(2,1)}, bf16[2,768,768]{2,1,0:T(8,128)(2,1)}, f32[832,768]{1,0:T(8,128)}, bf16[832,768]{1,0:T(8,128)(2,1)}, f32[2,768]{1,0:T(2,128)}) custom-call(bf16[832,768]{1,0:T(8,128)(2,1)} %get-tuple-element.272.normed_ref, bf16[832,768]{1,0:T(8,128)(2,1)} %get-tuple-element.273.grad_ref, ...), custom_call_target="tpu_custom_call" | custom-call | flops 15000000512 | bytes 8388608 | tf_op jit(solution)/shard_map/feed_backward/pallas_call | solution.py:598
  324.9 2.6 add_convert_fusion.2
  332.0 27.4 %spatial_backward.2 = (bf16[2,768,768]{2,1,0:T(8,128)(2,1)}, f32[832,768]{1,0:T(8,128)}) custom-call(bf16[832,768]{1,0:T(8,128)(2,1)} %get-tuple-element.296.normed_ref, bf16[832,768]{1,0:T(8,128)(2,1)} %get-tuple-element.297.grad_ref, bf16[2,768,768]{2,1,0:T(8,128)(2,1)} %collective-permute-done.29.weight_ref, ...), custom_call_target="tpu_custom_call" | custom-call | flops 30000001024 | bytes 8388608 | tf_op jit(solution)/shard_map/spatial_backward/pallas_call | solution.py:598
  363.1 2.1 fusion.10
  368.7 31.7 %spatial_backward.3 = (bf16[2,768,768]{2,1,0:T(8,128)(2,1)}, bf16[832,768]{1,0:T(8,128)(2,1)}, f32[2,768]{1,0:T(2,128)}) custom-call(bf16[832,768]{1,0:T(8,128)(2,1)} %get-tuple-element.296.normed_ref, bf16[832,768]{1,0:T(8,128)(2,1)} %get-tuple-element.297.grad_ref, bf16[2,768,768]{2,1,0:T(8,128)(2,1)} %bitcast.882, ...), custom_call_target="tpu_custom_call" | custom-call | flops 30000001024 | bytes 8388608 | tf_op jit(solution)/shard_map/spatial_backward/pallas_call | solution.py:598
  409.7 1.9 collective-permute-start.52
  414.1 5.4 collective-permute-done.52
  419.5 7.1 %collective-permute-done.51 = bf16[208,768]{1,0:T(8,128)(2,1)S(1)} collective-permute-done((bf16[208,768]{1,0:T(8,128)(2,1)S(1)}, bf16[208,768]{1,0:T(8,128)(2,1)S(1)}, u32[]{:S(2)}, u32[]{:S(2)}) %collective-permute-start.51) | collective-permute-done | bytes 319520 | tf_op jit(solution)/shard_map/ppermute | solution.py:794
  431.3 14.5 %temporal_backward.2 = (bf16[2,768,768]{2,1,0:T(8,128)(2,1)}, f32[832,768]{1,0:T(8,128)}) custom-call(bf16[832,768]{1,0:T(8,128)(2,1)} %get-tuple-element.320.normed_ref, bf16[832,768]{1,0:T(8,128)(2,1)} %pad_maximum_fusion.7.grad_ref.drows_ref, bf16[2,768,768]{2,1,0:T(8,128)(2,1)} %collective-permute-done.19.weight_ref.other_ref, ...), custom_call_target="tpu_custom_call" | custom-call | flops 14000000000 | bytes 8388608 | tf_op jit(solution)/shard_map/temporal_backward/pallas_call | solution.py:598
  447.3 2.7 collective-permute-start.59
  453.6 14.6 %temporal_backward.3 = (bf16[2,768,768]{2,1,0:T(8,128)(2,1)}, f32[832,768]{1,0:T(8,128)}) custom-call(bf16[832,768]{1,0:T(8,128)(2,1)} %get-tuple-element.320.normed_ref, bf16[832,768]{1,0:T(8,128)(2,1)} %pad_maximum_fusion.7.grad_ref.drows_ref, bf16[2,768,768]{2,1,0:T(8,128)(2,1)} %copy-done.3, bf16[2,4,576,208]{3,2,1,0:T(8,128)(2,1)} %get-tuple-element.321.qkv_ref, ...), custom_call_target="tpu_custom_call" | custom-call | flops 14000000000 | bytes 8388608 | tf_op jit(solution)/shard_map/temporal_backward/pallas_call | solution.py:598
  473.9 2.0 fusion.7
  480.0 8.3 %embed_backward.1 = bf16[768,896]{1,0:T(8,128)(2,1)} custom-call(bf16[832,768]{1,0:T(8,128)(2,1)} %pad_maximum_fusion.5.patches_ref, f32[832,768]{1,0:T(8,128)} %get-tuple-element.330.start_ref, f32[832,1]{1,0:T(8,128)} %convert_element_type.1202.valid_ref, bf16[832,768]{1,0:T(8,128)(2,1)} %pad_maximum_fusion.7.grad_ref.drows_ref, ...), custom_call_target="tpu_custom_call" | custom-call | flops 2000000000 | bytes 8388608 | tf_op jit(solution)/shard_map/embed_backward/pallas_call | solution.py:598
  488.3 2.3 broadcast_select_fusion.5
  499.1 9.0 %collective-permute-done.61 = bf16[2,4,96,384]{3,2,1,0:T(8,128)(2,1)} collective-permute-done((bf16[2,4,96,384]{3,2,1,0:T(8,128)(2,1)}, bf16[2,4,96,384]{3,2,1,0:T(8,128)(2,1)}, u32[]{:S(2)}, u32[]{:S(2)}) %collective-permute-start.61) | collective-permute-done | bytes 589856 | tf_op jit(solution)/shard_map/ppermute | solution.py:794
  519.8 4.5 collective-permute-done.65
  524.3 3.7 collective-permute-done.66
  530.6 2.5 multiply_reduce_fusion.1
  537.3 3.3 collective-permute-done.69
  542.2 2.1 collective-permute-start.71
  544.9 2.4 collective-permute-done.71
  547.3 4.3 collective-permute-done.70
  553.9 2.7 collective-permute-done.72
  560.5 2.2 collective-permute-start.74
  564.9 2.8 collective-permute-start.75
  570.6 2.3 collective-permute-done.76
  575.3 2.9 collective-permute-done.77
  578.8 5.7 optimizer.1
  (420 shorter events, 161.6 us)
Async XLA Ops:
  2.9 88.9 %collective-permute-start.23 = (bf16[1,24,768]{2,1,0:T(8,128)(2,1)}, bf16[1,24,768]{2,1,0:T(8,128)(2,1)}, u32[]{:S(2)}, u32[]{:S(2)}) collective-permute-start(bf16[1,24,768]{2,1,0:T(8,128)(2,1)} %fusion.39), channel_id=1, source_target_pairs={{0,16},{1,17},{2,18},{3,19},{4,20},{5,21},{6,22},{7,23},{8,24},{9,... | collective-permute-start | bytes 110600 | tf_op jit(solution)/shard_map/ppermute | solution.py:794
  9.5 9.3 %collective-permute-start.1 = (bf16[1,24,896]{2,1,0:T(8,128)(2,1)S(1)}, bf16[1,24,896]{2,1,0:T(8,128)(2,1)S(1)}, u32[]{:S(2)}, u32[]{:S(2)}) collective-permute-start(bf16[1,24,896]{2,1,0:T(8,128)(2,1)S(1)} %fusion.37), channel_id=1, source_target_pairs={{0,16},{1,17},{2,18},{3,19},{4,20},{5,21},{6,22},{7,23},{8,24},{9,... | collective-permute-start | bytes 129032 | tf_op jit(solution)/shard_map/ppermute | solution.py:794
  9.6 11.2 %collective-permute-start = (bf16[1,96,768]{2,1,0:T(8,128)(2,1)S(1)}, bf16[1,96,768]{2,1,0:T(8,128)(2,1)S(1)}, u32[]{:S(2)}, u32[]{:S(2)}) collective-permute-start(bf16[1,96,768]{2,1,0:T(8,128)(2,1)S(1)} %get-tuple-element.203), channel_id=1, source_target_pairs={{0,16},{1,17},{2,18},{3,19},{4,20},{5,21},{6,22},{7,23},{8,24},{9,... | collective-permute-start | bytes 442376 | tf_op jit(solution)/shard_map/ppermute | solution.py:794
  20.9 6.1 %collective-permute-start.3 = (bf16[2,24,896]{2,1,0:T(8,128)(2,1)S(1)}, bf16[2,24,896]{2,1,0:T(8,128)(2,1)S(1)}, u32[]{:S(2)}, u32[]{:S(2)}) collective-permute-start(bf16[2,24,896]{2,1,0:T(8,128)(2,1)S(1)} %maximum_bitcast_fusion.6), channel_id=1, source_target_pairs={{0,8},{1,9},{2,10},{3,11},{4,12},{5,13},{6,14},{7,15},{8,0},{9,1},... | collective-permute-start | bytes 258056 | tf_op jit(solution)/shard_map/ppermute | solution.py:794
  20.9 22.9 %collective-permute-start.10 = (bf16[1,96,768]{2,1,0:T(8,128)(2,1)S(1)}, bf16[1,96,768]{2,1,0:T(8,128)(2,1)S(1)}, u32[]{:S(2)}, u32[]{:S(2)}) collective-permute-start(bf16[1,96,768]{2,1,0:T(8,128)(2,1)S(1)} %get-tuple-element.212), channel_id=1, source_target_pairs={{0,16},{1,17},{2,18},{3,19},{4,20},{5,21},{6,22},{7,23},{8,24},{9,... | collective-permute-start | bytes 442376 | tf_op jit(solution)/shard_map/ppermute | solution.py:794
  23.2 11.0 %collective-permute-start.2 = (bf16[2,96,768]{2,1,0:T(8,128)(2,1)S(1)}, bf16[2,96,768]{2,1,0:T(8,128)(2,1)S(1)}, u32[]{:S(2)}, u32[]{:S(2)}) collective-permute-start(bf16[2,96,768]{2,1,0:T(8,128)(2,1)S(1)} %maximum_bitcast_fusion), channel_id=1, source_target_pairs={{0,8},{1,9},{2,10},{3,11},{4,12},{5,13},{6,14},{7,15},{8,0},{9,1},... | collective-permute-start | bytes 884744 | tf_op jit(solution)/shard_map/ppermute | solution.py:794
  23.4 11.0 %collective-permute-start.6 = (bf16[208,768]{1,0:T(8,128)(2,1)S(1)}, bf16[208,768]{1,0:T(8,128)(2,1)S(1)}, u32[]{:S(2)}, u32[]{:S(2)}) collective-permute-start(bf16[208,768]{1,0:T(8,128)(2,1)S(1)} %get-tuple-element.403), channel_id=1, source_target_pairs={{0,3},{1,2},{2,1},{3,0},{4,7},{5,6},{6,5},{7,4},{8,11},{9,10},{10,... | collective-permute-start | bytes 958472 | tf_op jit(solution)/shard_map/ppermute | solution.py:794
  27.0 13.1 %collective-permute-start.5 = (bf16[208,768]{1,0:T(8,128)(2,1)S(1)}, bf16[208,768]{1,0:T(8,128)(2,1)S(1)}, u32[]{:S(2)}, u32[]{:S(2)}) collective-permute-start(bf16[208,768]{1,0:T(8,128)(2,1)S(1)} %get-tuple-element.404), channel_id=1, source_target_pairs={{0,2},{1,3},{2,0},{3,1},{4,6},{5,7},{6,4},{7,5},{8,10},{9,11},{10,... | collective-permute-start | bytes 958472 | tf_op jit(solution)/shard_map/ppermute | solution.py:794
  34.2 6.0 %collective-permute-start.4 = (bf16[208,768]{1,0:T(8,128)(2,1)S(1)}, bf16[208,768]{1,0:T(8,128)(2,1)S(1)}, u32[]{:S(2)}, u32[]{:S(2)}) collective-permute-start(bf16[208,768]{1,0:T(8,128)(2,1)S(1)} %get-tuple-element.405), channel_id=1, source_target_pairs={{0,1},{1,0},{2,3},{3,2},{4,5},{5,4},{6,7},{7,6},{8,9},{9,8},{10,11... | collective-permute-start | bytes 958472 | tf_op jit(solution)/shard_map/ppermute | solution.py:794
  41.3 9.8 %collective-permute-start.11 = (bf16[1,96,768]{2,1,0:T(8,128)(2,1)S(1)}, bf16[1,96,768]{2,1,0:T(8,128)(2,1)S(1)}, u32[]{:S(2)}, u32[]{:S(2)}) collective-permute-start(bf16[1,96,768]{2,1,0:T(8,128)(2,1)S(1)} %convert_bitcast_fusion.1), channel_id=1, source_target_pairs={{0,16},{1,17},{2,18},{3,19},{4,20},{5,21},{6,22},{7,23},{8,24},{9,... | collective-permute-start | bytes 442376 | tf_op jit(solution)/shard_map/ppermute | solution.py:794
  43.9 13.0 %collective-permute-start.9 = (bf16[4,24,896]{2,1,0:T(8,128)(2,1)S(1)}, bf16[4,24,896]{2,1,0:T(8,128)(2,1)S(1)}, u32[]{:S(2)}, u32[]{:S(2)}) collective-permute-start(bf16[4,24,896]{2,1,0:T(8,128)(2,1)S(1)} %bitcast.915), channel_id=1, source_target_pairs={{0,4},{1,5},{2,6},{3,7},{4,0},{5,1},{6,2},{7,3},{8,12},{9,13},{10,... | collective-permute-start | bytes 516104 | tf_op jit(solution)/shard_map/ppermute | solution.py:794
  45.5 10.8 %collective-permute-start.7 = (bf16[4,96,384]{2,1,0:T(8,128)(2,1)S(1)}, bf16[4,96,384]{2,1,0:T(8,128)(2,1)S(1)}, u32[]{:S(2)}, u32[]{:S(2)}) collective-permute-start(bf16[4,96,384]{2,1,0:T(8,128)(2,1)S(1)} %slice.750), channel_id=1, source_target_pairs={{0,4},{1,5},{2,6},{3,7},{4,0},{5,1},{6,2},{7,3},{8,12},{9,13},{10,... | collective-permute-start | bytes 884744 | tf_op jit(solution)/shard_map/ppermute | solution.py:794
  56.5 7.9 %collective-permute-start.8 = (bf16[4,96,384]{2,1,0:T(8,128)(2,1)S(1)}, bf16[4,96,384]{2,1,0:T(8,128)(2,1)S(1)}, u32[]{:S(2)}, u32[]{:S(2)}) collective-permute-start(bf16[4,96,384]{2,1,0:T(8,128)(2,1)S(1)} %get-tuple-element.441), channel_id=1, source_target_pairs={{0,2},{1,3},{2,0},{3,1},{4,6},{5,7},{6,4},{7,5},{8,10},{9,11},{10,... | collective-permute-start | bytes 884744 | tf_op jit(solution)/shard_map/ppermute | solution.py:794
  64.4 10.0 %collective-permute-start.15 = (bf16[2,96,768]{2,1,0:T(8,128)(2,1)S(1)}, bf16[2,96,768]{2,1,0:T(8,128)(2,1)S(1)}, u32[]{:S(2)}, u32[]{:S(2)}) collective-permute-start(bf16[2,96,768]{2,1,0:T(8,128)(2,1)S(1)} %maximum_bitcast_fusion.1), channel_id=1, source_target_pairs={{0,8},{1,9},{2,10},{3,11},{4,12},{5,13},{6,14},{7,15},{8,0},{9,1},... | collective-permute-start | bytes 884744 | tf_op jit(solution)/shard_map/ppermute | solution.py:794
  65.2 12.5 %collective-permute-start.16 = (bf16[2,96,768]{2,1,0:T(8,128)(2,1)S(1)}, bf16[2,96,768]{2,1,0:T(8,128)(2,1)S(1)}, u32[]{:S(2)}, u32[]{:S(2)}) collective-permute-start(bf16[2,96,768]{2,1,0:T(8,128)(2,1)S(1)} %maximum_bitcast_fusion.2), channel_id=1, source_target_pairs={{0,8},{1,9},{2,10},{3,11},{4,12},{5,13},{6,14},{7,15},{8,0},{9,1},... | collective-permute-start | bytes 884744 | tf_op jit(solution)/shard_map/ppermute | solution.py:794
  67.7 11.1 %collective-permute-start.14 = (bf16[8,24,896]{2,1,0:T(8,128)(2,1)S(1)}, bf16[8,24,896]{2,1,0:T(8,128)(2,1)S(1)}, u32[]{:S(2)}, u32[]{:S(2)}) collective-permute-start(bf16[8,24,896]{2,1,0:T(8,128)(2,1)S(1)} %bitcast.900), channel_id=1, source_target_pairs={{0,2},{1,3},{2,0},{3,1},{4,6},{5,7},{6,4},{7,5},{8,10},{9,11},{10,... | collective-permute-start | bytes 1032200 | tf_op jit(solution)/shard_map/ppermute | solution.py:794
  68.9 19.1 %collective-permute-start.12 = (bf16[8,96,384]{2,1,0:T(8,128)(2,1)S(1)}, bf16[8,96,384]{2,1,0:T(8,128)(2,1)S(1)}, u32[]{:S(2)}, u32[]{:S(2)}) collective-permute-start(bf16[8,96,384]{2,1,0:T(8,128)(2,1)S(1)} %bitcast.871), channel_id=1, source_target_pairs={{0,2},{1,3},{2,0},{3,1},{4,6},{5,7},{6,4},{7,5},{8,10},{9,11},{10,... | collective-permute-start | bytes 1769480 | tf_op jit(solution)/shard_map/ppermute | solution.py:794
  74.4 9.9 %collective-permute-start.13 = (bf16[2,4,96,384]{3,2,1,0:T(8,128)(2,1)S(1)}, bf16[2,4,96,384]{3,2,1,0:T(8,128)(2,1)S(1)}, u32[]{:S(2)}, u32[]{:S(2)}) collective-permute-start(bf16[2,4,96,384]{3,2,1,0:T(8,128)(2,1)S(1)} %pad_maximum_fusion.17), channel_id=1, source_target_pairs={{0,4},{1,5},{2,6},{3,7},{4,0},{5,1},{6,2},{7,3},{8,12},{9,13},{10,... | collective-permute-start | bytes 1769480 | tf_op jit(solution)/shard_map/ppermute | solution.py:794
  88.2 34.7 %collective-permute-start.19 = (bf16[2,768,768]{2,1,0:T(8,128)(2,1)S(1)}, bf16[2,768,768]{2,1,0:T(8,128)(2,1)}, u32[]{:S(2)}, u32[]{:S(2)}) collective-permute-start(bf16[2,768,768]{2,1,0:T(8,128)(2,1)S(1)} %pad_maximum_fusion.weight_ref.own_ref), channel_id=1, source_target_pairs={{0,1},{1,0},{2,3},{3,2},{4,5},{5,4},{6,7},{7,6},{8,9},{9,8},{10,11... | collective-permute-start | bytes 7077896 | tf_op jit(solution)/shard_map/ppermute | solution.py:794
  90.0 10.2 %collective-permute-start.21 = (bf16[1,96,768]{2,1,0:T(8,128)(2,1)}, bf16[1,96,768]{2,1,0:T(8,128)(2,1)S(1)}, u32[]{:S(2)}, u32[]{:S(2)}) collective-permute-start(bf16[1,96,768]{2,1,0:T(8,128)(2,1)} %convert_bitcast_fusion), channel_id=1, source_target_pairs={{0,16},{1,17},{2,18},{3,19},{4,20},{5,21},{6,22},{7,23},{8,24},{9,... | collective-permute-start | bytes 442376 | tf_op jit(solution)/shard_map/ppermute | solution.py:794
  90.2 15.5 %collective-permute-start.20 = (bf16[4,96,768]{2,1,0:T(8,128)(2,1)S(1)}, bf16[4,96,768]{2,1,0:T(8,128)(2,1)S(1)}, u32[]{:S(2)}, u32[]{:S(2)}) collective-permute-start(bf16[4,96,768]{2,1,0:T(8,128)(2,1)S(1)} %bitcast.875), channel_id=1, source_target_pairs={{0,4},{1,5},{2,6},{3,7},{4,0},{5,1},{6,2},{7,3},{8,12},{9,13},{10,... | collective-permute-start | bytes 1769480 | tf_op jit(solution)/shard_map/ppermute | solution.py:794
  93.3 15.3 %collective-permute-start.18 = (bf16[4,96,768]{2,1,0:T(8,128)(2,1)}, bf16[4,96,768]{2,1,0:T(8,128)(2,1)S(1)}, u32[]{:S(2)}, u32[]{:S(2)}) collective-permute-start(bf16[4,96,768]{2,1,0:T(8,128)(2,1)} %bitcast.888), channel_id=1, source_target_pairs={{0,2},{1,3},{2,0},{3,1},{4,6},{5,7},{6,4},{7,5},{8,10},{9,11},{10,... | collective-permute-start | bytes 1769480 | tf_op jit(solution)/shard_map/ppermute | solution.py:794
  94.9 13.9 %collective-permute-start.17 = (bf16[16,24,896]{2,1,0:T(8,128)(2,1)}, bf16[16,24,896]{2,1,0:T(8,128)(2,1)S(1)}, u32[]{:S(2)}, u32[]{:S(2)}) collective-permute-start(bf16[16,24,896]{2,1,0:T(8,128)(2,1)} %bitcast.60), channel_id=1, source_target_pairs={{0,1},{1,0},{2,3},{3,2},{4,5},{5,4},{6,7},{7,6},{8,9},{9,8},{10,11... | collective-permute-start | bytes 2064392 | tf_op jit(solution)/shard_map/ppermute | solution.py:794
  122.9 11.6 %collective-permute-start.22 = (bf16[2,96,768]{2,1,0:T(8,128)(2,1)S(1)}, bf16[2,96,768]{2,1,0:T(8,128)(2,1)S(1)}, u32[]{:S(2)}, u32[]{:S(2)}) collective-permute-start(bf16[2,96,768]{2,1,0:T(8,128)(2,1)S(1)} %maximum_bitcast_fusion.3), channel_id=1, source_target_pairs={{0,8},{1,9},{2,10},{3,11},{4,12},{5,13},{6,14},{7,15},{8,0},{9,1},... | collective-permute-start | bytes 884744 | tf_op jit(solution)/shard_map/ppermute | solution.py:794
  125.9 28.5 %collective-permute-start.27 = (bf16[2,4,96,768]{3,2,1,0:T(8,128)(2,1)S(1)}, bf16[2,4,96,768]{3,2,1,0:T(8,128)(2,1)S(1)}, u32[]{:S(2)}, u32[]{:S(2)}) collective-permute-start(bf16[2,4,96,768]{3,2,1,0:T(8,128)(2,1)S(1)} %pad_maximum_fusion.9), channel_id=1, source_target_pairs={{0,4},{1,5},{2,6},{3,7},{4,0},{5,1},{6,2},{7,3},{8,12},{9,13},{10,... | collective-permute-start | bytes 3538952 | tf_op jit(solution)/shard_map/ppermute | solution.py:794
  136.8 10.3 %collective-permute-start.25 = (bf16[208,768]{1,0:T(8,128)(2,1)S(1)}, bf16[208,768]{1,0:T(8,128)(2,1)S(1)}, u32[]{:S(2)}, u32[]{:S(2)}) collective-permute-start(bf16[208,768]{1,0:T(8,128)(2,1)S(1)} %pad_maximum_fusion.25), channel_id=1, source_target_pairs={{0,2},{1,3},{2,0},{3,1},{4,6},{5,7},{6,4},{7,5},{8,10},{9,11},{10,... | collective-permute-start | bytes 958472 | tf_op jit(solution)/shard_map/ppermute | solution.py:794
  138.5 14.7 %collective-permute-start.26 = (bf16[208,768]{1,0:T(8,128)(2,1)S(1)}, bf16[208,768]{1,0:T(8,128)(2,1)S(1)}, u32[]{:S(2)}, u32[]{:S(2)}) collective-permute-start(bf16[208,768]{1,0:T(8,128)(2,1)S(1)} %pad_maximum_fusion.26), channel_id=1, source_target_pairs={{0,3},{1,2},{2,1},{3,0},{4,7},{5,6},{6,5},{7,4},{8,11},{9,10},{10,... | collective-permute-start | bytes 958472 | tf_op jit(solution)/shard_map/ppermute | solution.py:794
  139.8 26.9 %collective-permute-start.30 = (bf16[4,96,768]{2,1,0:T(8,128)(2,1)}, bf16[4,96,768]{2,1,0:T(8,128)(2,1)}, u32[]{:S(2)}, u32[]{:S(2)}) collective-permute-start(bf16[4,96,768]{2,1,0:T(8,128)(2,1)} %bitcast.97), channel_id=1, source_target_pairs={{0,2},{1,3},{2,0},{3,1},{4,6},{5,7},{6,4},{7,5},{8,10},{9,11},{10,... | collective-permute-start | bytes 1769480 | tf_op jit(solution)/shard_map/ppermute | solution.py:794
  154.9 41.0 %collective-permute-start.29 = (bf16[2,768,768]{2,1,0:T(8,128)(2,1)S(1)}, bf16[2,768,768]{2,1,0:T(8,128)(2,1)}, u32[]{:S(2)}, u32[]{:S(2)}) collective-permute-start(bf16[2,768,768]{2,1,0:T(8,128)(2,1)S(1)} %bitcast.880), channel_id=1, source_target_pairs={{0,1},{1,0},{2,3},{3,2},{4,5},{5,4},{6,7},{7,6},{8,9},{9,8},{10,11... | collective-permute-start | bytes 7077896 | tf_op jit(solution)/shard_map/ppermute | solution.py:794
  156.6 37.5 %collective-permute-start.32 = (bf16[8,96,768]{2,1,0:T(8,128)(2,1)S(1)}, bf16[8,96,768]{2,1,0:T(8,128)(2,1)S(1)}, u32[]{:S(2)}, u32[]{:S(2)}) collective-permute-start(bf16[8,96,768]{2,1,0:T(8,128)(2,1)S(1)} %bitcast.859), channel_id=1, source_target_pairs={{0,2},{1,3},{2,0},{3,1},{4,6},{5,7},{6,4},{7,5},{8,10},{9,11},{10,... | collective-permute-start | bytes 3538952 | tf_op jit(solution)/shard_map/ppermute | solution.py:794
  168.1 27.7 %collective-permute-start.31 = (bf16[4,24,768]{2,1,0:T(8,128)(2,1)S(1)}, bf16[4,24,768]{2,1,0:T(8,128)(2,1)S(1)}, u32[]{:S(2)}, u32[]{:S(2)}) collective-permute-start(bf16[4,24,768]{2,1,0:T(8,128)(2,1)S(1)} %bitcast.922), channel_id=1, source_target_pairs={{0,4},{1,5},{2,6},{3,7},{4,0},{5,1},{6,2},{7,3},{8,12},{9,13},{10,... | collective-permute-start | bytes 442376 | tf_op jit(solution)/shard_map/ppermute | solution.py:794
  195.9 27.0 %collective-permute-start.33 = (bf16[2,4,96,768]{3,2,1,0:T(8,128)(2,1)S(1)}, bf16[2,4,96,768]{3,2,1,0:T(8,128)(2,1)S(1)}, u32[]{:S(2)}, u32[]{:S(2)}) collective-permute-start(bf16[2,4,96,768]{3,2,1,0:T(8,128)(2,1)S(1)} %pad_maximum_fusion.11), channel_id=1, source_target_pairs={{0,4},{1,5},{2,6},{3,7},{4,0},{5,1},{6,2},{7,3},{8,12},{9,13},{10,... | collective-permute-start | bytes 3538952 | tf_op jit(solution)/shard_map/ppermute | solution.py:794
  223.5 19.5 %collective-permute-start.34 = (bf16[2,768,768]{2,1,0:T(8,128)(2,1)}, bf16[2,768,768]{2,1,0:T(8,128)(2,1)}, u32[]{:S(2)}, u32[]{:S(2)}) collective-permute-start(bf16[2,768,768]{2,1,0:T(8,128)(2,1)} %pad_maximum_fusion.2.up_ref), channel_id=1, source_target_pairs={{0,1},{1,0},{2,3},{3,2},{4,5},{5,4},{6,7},{7,6},{8,9},{9,8},{10,11... | collective-permute-start | bytes 7077896 | tf_op jit(solution)/shard_map/ppermute | solution.py:794
  223.5 19.4 %collective-permute-start.35 = (bf16[2,768,768]{2,1,0:T(8,128)(2,1)S(1)}, bf16[2,768,768]{2,1,0:T(8,128)(2,1)}, u32[]{:S(2)}, u32[]{:S(2)}) collective-permute-start(bf16[2,768,768]{2,1,0:T(8,128)(2,1)S(1)} %bitcast.883), channel_id=1, source_target_pairs={{0,1},{1,0},{2,3},{3,2},{4,5},{5,4},{6,7},{7,6},{8,9},{9,8},{10,11... | collective-permute-start | bytes 7077896 | tf_op jit(solution)/shard_map/ppermute | solution.py:794
  224.0 9.0 %collective-permute-start.36 = (bf16[8,24,768]{2,1,0:T(8,128)(2,1)S(1)}, bf16[8,24,768]{2,1,0:T(8,128)(2,1)S(1)}, u32[]{:S(2)}, u32[]{:S(2)}) collective-permute-start(bf16[8,24,768]{2,1,0:T(8,128)(2,1)S(1)} %bitcast.912), channel_id=1, source_target_pairs={{0,2},{1,3},{2,0},{3,1},{4,6},{5,7},{6,4},{7,5},{8,10},{9,11},{10,... | collective-permute-start | bytes 884744 | tf_op jit(solution)/shard_map/ppermute | solution.py:794
  268.6 6.4 %collective-permute-start.42 = (bf16[16,24,768]{2,1,0:T(8,128)(2,1)S(1)}, bf16[16,24,768]{2,1,0:T(8,128)(2,1)S(1)}, u32[]{:S(2)}, u32[]{:S(2)}) collective-permute-start(bf16[16,24,768]{2,1,0:T(8,128)(2,1)S(1)} %bitcast.873), channel_id=1, source_target_pairs={{0,1},{1,0},{2,3},{3,2},{4,5},{5,4},{6,7},{7,6},{8,9},{9,8},{10,11... | collective-permute-start | bytes 1769480 | tf_op jit(solution)/shard_map/ppermute | solution.py:794
  298.2 21.6 %collective-permute-start.43 = (bf16[2,768,768]{2,1,0:T(8,128)(2,1)}, bf16[2,768,768]{2,1,0:T(8,128)(2,1)}, u32[]{:S(2)}, u32[]{:S(2)}) collective-permute-start(bf16[2,768,768]{2,1,0:T(8,128)(2,1)} %get-tuple-element.282), channel_id=1, source_target_pairs={{0,1},{1,0},{2,3},{3,2},{4,5},{5,4},{6,7},{7,6},{8,9},{9,8},{10,11... | collective-permute-start | bytes 7077896 | tf_op jit(solution)/shard_map/ppermute | solution.py:794
  298.3 21.5 %collective-permute-start.44 = (bf16[2,768,768]{2,1,0:T(8,128)(2,1)}, bf16[2,768,768]{2,1,0:T(8,128)(2,1)S(1)}, u32[]{:S(2)}, u32[]{:S(2)}) collective-permute-start(bf16[2,768,768]{2,1,0:T(8,128)(2,1)} %get-tuple-element.283), channel_id=1, source_target_pairs={{0,1},{1,0},{2,3},{3,2},{4,5},{5,4},{6,7},{7,6},{8,9},{9,8},{10,11... | collective-permute-start | bytes 7077896 | tf_op jit(solution)/shard_map/ppermute | solution.py:794
  329.6 32.1 %collective-permute-start.45 = (bf16[8,96,768]{2,1,0:T(8,128)(2,1)}, bf16[8,96,768]{2,1,0:T(8,128)(2,1)S(1)}, u32[]{:S(2)}, u32[]{:S(2)}) collective-permute-start(bf16[8,96,768]{2,1,0:T(8,128)(2,1)} %bitcast.139), channel_id=1, source_target_pairs={{0,2},{1,3},{2,0},{3,1},{4,6},{5,7},{6,4},{7,5},{8,10},{9,11},{10,... | collective-permute-start | bytes 3538952 | tf_op jit(solution)/shard_map/ppermute | solution.py:794
  331.4 30.3 %collective-permute-start.46 = (bf16[2,4,96,768]{3,2,1,0:T(8,128)(2,1)}, bf16[2,4,96,768]{3,2,1,0:T(8,128)(2,1)}, u32[]{:S(2)}, u32[]{:S(2)}) collective-permute-start(bf16[2,4,96,768]{3,2,1,0:T(8,128)(2,1)} %fusion), channel_id=1, source_target_pairs={{0,4},{1,5},{2,6},{3,7},{4,0},{5,1},{6,2},{7,3},{8,12},{9,13},{10,... | collective-permute-start | bytes 3538952 | tf_op jit(solution)/shard_map/ppermute | solution.py:794
  367.0 36.3 %collective-permute-start.47 = (bf16[4,96,768]{2,1,0:T(8,128)(2,1)}, bf16[4,96,768]{2,1,0:T(8,128)(2,1)S(1)}, u32[]{:S(2)}, u32[]{:S(2)}) collective-permute-start(bf16[4,96,768]{2,1,0:T(8,128)(2,1)} %fusion.6), channel_id=1, source_target_pairs={{0,4},{1,5},{2,6},{3,7},{4,0},{5,1},{6,2},{7,3},{8,12},{9,13},{10,... | collective-permute-start | bytes 1769480 | tf_op jit(solution)/shard_map/ppermute | solution.py:794
  368.4 34.8 %collective-permute-start.48 = (bf16[4,96,768]{2,1,0:T(8,128)(2,1)}, bf16[4,96,768]{2,1,0:T(8,128)(2,1)S(1)}, u32[]{:S(2)}, u32[]{:S(2)}) collective-permute-start(bf16[4,96,768]{2,1,0:T(8,128)(2,1)} %fusion.10), channel_id=1, source_target_pairs={{0,2},{1,3},{2,0},{3,1},{4,6},{5,7},{6,4},{7,5},{8,10},{9,11},{10,... | collective-permute-start | bytes 1769480 | tf_op jit(solution)/shard_map/ppermute | solution.py:794
  368.7 34.5 %collective-permute-start.49 = (bf16[2,768,768]{2,1,0:T(8,128)(2,1)}, bf16[2,768,768]{2,1,0:T(8,128)(2,1)S(1)}, u32[]{:S(2)}, u32[]{:S(2)}) collective-permute-start(bf16[2,768,768]{2,1,0:T(8,128)(2,1)} %get-tuple-element.307), channel_id=1, source_target_pairs={{0,1},{1,0},{2,3},{3,2},{4,5},{5,4},{6,7},{7,6},{8,9},{9,8},{10,11... | collective-permute-start | bytes 7077896 | tf_op jit(solution)/shard_map/ppermute | solution.py:794
  409.7 9.8 %collective-permute-start.52 = (bf16[208,768]{1,0:T(8,128)(2,1)S(1)}, bf16[208,768]{1,0:T(8,128)(2,1)S(1)}, u32[]{:S(2)}, u32[]{:S(2)}) collective-permute-start(bf16[208,768]{1,0:T(8,128)(2,1)S(1)} %get-tuple-element.399), channel_id=1, source_target_pairs={{0,3},{1,2},{2,1},{3,0},{4,7},{5,6},{6,5},{7,4},{8,11},{9,10},{10,... | collective-permute-start | bytes 958472 | tf_op jit(solution)/shard_map/ppermute | solution.py:794
  411.6 14.9 %collective-permute-start.51 = (bf16[208,768]{1,0:T(8,128)(2,1)S(1)}, bf16[208,768]{1,0:T(8,128)(2,1)S(1)}, u32[]{:S(2)}, u32[]{:S(2)}) collective-permute-start(bf16[208,768]{1,0:T(8,128)(2,1)S(1)} %get-tuple-element.400), channel_id=1, source_target_pairs={{0,2},{1,3},{2,0},{3,1},{4,6},{5,7},{6,4},{7,5},{8,10},{9,11},{10,... | collective-permute-start | bytes 958472 | tf_op jit(solution)/shard_map/ppermute | solution.py:794
  411.9 14.7 %collective-permute-start.50 = (bf16[208,768]{1,0:T(8,128)(2,1)S(1)}, bf16[208,768]{1,0:T(8,128)(2,1)S(1)}, u32[]{:S(2)}, u32[]{:S(2)}) collective-permute-start(bf16[208,768]{1,0:T(8,128)(2,1)S(1)} %get-tuple-element.401), channel_id=1, source_target_pairs={{0,1},{1,0},{2,3},{3,2},{4,5},{5,4},{6,7},{7,6},{8,9},{9,8},{10,11... | collective-permute-start | bytes 958472 | tf_op jit(solution)/shard_map/ppermute | solution.py:794
  412.8 33.2 %collective-permute-start.55 = (bf16[2,4,96,768]{3,2,1,0:T(8,128)(2,1)}, bf16[2,4,96,768]{3,2,1,0:T(8,128)(2,1)}, u32[]{:S(2)}, u32[]{:S(2)}) collective-permute-start(bf16[2,4,96,768]{3,2,1,0:T(8,128)(2,1)} %fusion.1), channel_id=1, source_target_pairs={{0,4},{1,5},{2,6},{3,7},{4,0},{5,1},{6,2},{7,3},{8,12},{9,13},{10,... | collective-permute-start | bytes 3538952 | tf_op jit(solution)/shard_map/ppermute | solution.py:794
  429.2 16.7 %collective-permute-start.54 = (bf16[2,96,768]{2,1,0:T(8,128)(2,1)S(1)}, bf16[2,96,768]{2,1,0:T(8,128)(2,1)S(1)}, u32[]{:S(2)}, u32[]{:S(2)}) collective-permute-start(bf16[2,96,768]{2,1,0:T(8,128)(2,1)S(1)} %fusion.16), channel_id=1, source_target_pairs={{0,8},{1,9},{2,10},{3,11},{4,12},{5,13},{6,14},{7,15},{8,0},{9,1},... | collective-permute-start | bytes 884744 | tf_op jit(solution)/shard_map/ppermute | solution.py:794
  430.9 15.1 %collective-permute-start.53 = (bf16[2,96,768]{2,1,0:T(8,128)(2,1)}, bf16[2,96,768]{2,1,0:T(8,128)(2,1)S(1)}, u32[]{:S(2)}, u32[]{:S(2)}) collective-permute-start(bf16[2,96,768]{2,1,0:T(8,128)(2,1)} %fusion.15), channel_id=1, source_target_pairs={{0,8},{1,9},{2,10},{3,11},{4,12},{5,13},{6,14},{7,15},{8,0},{9,1},... | collective-permute-start | bytes 884744 | tf_op jit(solution)/shard_map/ppermute | solution.py:794
  446.0 24.1 %collective-permute-start.56 = (bf16[2,768,768]{2,1,0:T(8,128)(2,1)}, bf16[2,768,768]{2,1,0:T(8,128)(2,1)}, u32[]{:S(2)}, u32[]{:S(2)}) collective-permute-start(bf16[2,768,768]{2,1,0:T(8,128)(2,1)} %get-tuple-element.324), channel_id=1, source_target_pairs={{0,1},{1,0},{2,3},{3,2},{4,5},{5,4},{6,7},{7,6},{8,9},{9,8},{10,11... | collective-permute-start | bytes 7077896 | tf_op jit(solution)/shard_map/ppermute | solution.py:794
  447.3 22.7 %collective-permute-start.59 = (bf16[1,96,768]{2,1,0:T(8,128)(2,1)S(1)}, bf16[1,96,768]{2,1,0:T(8,128)(2,1)S(1)}, u32[]{:S(2)}, u32[]{:S(2)}) collective-permute-start(bf16[1,96,768]{2,1,0:T(8,128)(2,1)S(1)} %fusion.27), channel_id=1, source_target_pairs={{0,16},{1,17},{2,18},{3,19},{4,20},{5,21},{6,22},{7,23},{8,24},{9,... | collective-permute-start | bytes 442376 | tf_op jit(solution)/shard_map/ppermute | solution.py:794
  450.3 19.8 %collective-permute-start.58 = (bf16[1,96,768]{2,1,0:T(8,128)(2,1)S(1)}, bf16[1,96,768]{2,1,0:T(8,128)(2,1)S(1)}, u32[]{:S(2)}, u32[]{:S(2)}) collective-permute-start(bf16[1,96,768]{2,1,0:T(8,128)(2,1)S(1)} %fusion.26), channel_id=1, source_target_pairs={{0,16},{1,17},{2,18},{3,19},{4,20},{5,21},{6,22},{7,23},{8,24},{9,... | collective-permute-start | bytes 442376 | tf_op jit(solution)/shard_map/ppermute | solution.py:794
  451.9 18.2 %collective-permute-start.57 = (bf16[4,96,768]{2,1,0:T(8,128)(2,1)S(1)}, bf16[4,96,768]{2,1,0:T(8,128)(2,1)S(1)}, u32[]{:S(2)}, u32[]{:S(2)}) collective-permute-start(bf16[4,96,768]{2,1,0:T(8,128)(2,1)S(1)} %fusion.9), channel_id=1, source_target_pairs={{0,2},{1,3},{2,0},{3,1},{4,6},{5,7},{6,4},{7,5},{8,10},{9,11},{10,... | collective-permute-start | bytes 1769480 | tf_op jit(solution)/shard_map/ppermute | solution.py:794
  490.6 8.5 %collective-permute-start.63 = (bf16[2,96,768]{2,1,0:T(8,128)(2,1)}, bf16[2,96,768]{2,1,0:T(8,128)(2,1)}, u32[]{:S(2)}, u32[]{:S(2)}) collective-permute-start(bf16[2,96,768]{2,1,0:T(8,128)(2,1)} %fusion.17), channel_id=1, source_target_pairs={{0,8},{1,9},{2,10},{3,11},{4,12},{5,13},{6,14},{7,15},{8,0},{9,1},... | collective-permute-start | bytes 884744 | tf_op jit(solution)/shard_map/ppermute | solution.py:794
  494.2 13.9 %collective-permute-start.61 = (bf16[2,4,96,384]{3,2,1,0:T(8,128)(2,1)}, bf16[2,4,96,384]{3,2,1,0:T(8,128)(2,1)}, u32[]{:S(2)}, u32[]{:S(2)}) collective-permute-start(bf16[2,4,96,384]{3,2,1,0:T(8,128)(2,1)} %fusion.8), channel_id=1, source_target_pairs={{0,4},{1,5},{2,6},{3,7},{4,0},{5,1},{6,2},{7,3},{8,12},{9,13},{10,... | collective-permute-start | bytes 1769480 | tf_op jit(solution)/shard_map/ppermute | solution.py:794
  494.7 13.6 %collective-permute-start.60 = (bf16[8,96,384]{2,1,0:T(8,128)(2,1)}, bf16[8,96,384]{2,1,0:T(8,128)(2,1)}, u32[]{:S(2)}, u32[]{:S(2)}) collective-permute-start(bf16[8,96,384]{2,1,0:T(8,128)(2,1)} %fusion.7), channel_id=1, source_target_pairs={{0,2},{1,3},{2,0},{3,1},{4,6},{5,7},{6,4},{7,5},{8,10},{9,11},{10,... | collective-permute-start | bytes 1769480 | tf_op jit(solution)/shard_map/ppermute | solution.py:794
  495.1 13.2 %collective-permute-start.62 = (bf16[16,24,896]{2,1,0:T(8,128)(2,1)}, bf16[16,24,896]{2,1,0:T(8,128)(2,1)}, u32[]{:S(2)}, u32[]{:S(2)}) collective-permute-start(bf16[16,24,896]{2,1,0:T(8,128)(2,1)} %get-tuple-element.395), channel_id=1, source_target_pairs={{0,1},{1,0},{2,3},{3,2},{4,5},{5,4},{6,7},{7,6},{8,9},{9,8},{10,11... | collective-permute-start | bytes 2064392 | tf_op jit(solution)/shard_map/ppermute | solution.py:794
  512.2 7.6 %collective-permute-start.67 = (bf16[1,96,768]{2,1,0:T(8,128)(2,1)S(1)}, bf16[1,96,768]{2,1,0:T(8,128)(2,1)S(1)}, u32[]{:S(2)}, u32[]{:S(2)}) collective-permute-start(bf16[1,96,768]{2,1,0:T(8,128)(2,1)S(1)} %fusion.28), channel_id=1, source_target_pairs={{0,16},{1,17},{2,18},{3,19},{4,20},{5,21},{6,22},{7,23},{8,24},{9,... | collective-permute-start | bytes 442376 | tf_op jit(solution)/shard_map/ppermute | solution.py:794
  514.7 9.6 %collective-permute-start.65 = (bf16[4,96,384]{2,1,0:T(8,128)(2,1)S(1)}, bf16[4,96,384]{2,1,0:T(8,128)(2,1)S(1)}, u32[]{:S(2)}, u32[]{:S(2)}) collective-permute-start(bf16[4,96,384]{2,1,0:T(8,128)(2,1)S(1)} %fusion.18), channel_id=1, source_target_pairs={{0,2},{1,3},{2,0},{3,1},{4,6},{5,7},{6,4},{7,5},{8,10},{9,11},{10,... | collective-permute-start | bytes 884744 | tf_op jit(solution)/shard_map/ppermute | solution.py:794
  516.4 7.9 %collective-permute-start.64 = (bf16[4,96,384]{2,1,0:T(8,128)(2,1)S(1)}, bf16[4,96,384]{2,1,0:T(8,128)(2,1)S(1)}, u32[]{:S(2)}, u32[]{:S(2)}) collective-permute-start(bf16[4,96,384]{2,1,0:T(8,128)(2,1)S(1)} %fusion.19), channel_id=1, source_target_pairs={{0,4},{1,5},{2,6},{3,7},{4,0},{5,1},{6,2},{7,3},{8,12},{9,13},{10,... | collective-permute-start | bytes 884744 | tf_op jit(solution)/shard_map/ppermute | solution.py:794
  517.9 10.0 %collective-permute-start.66 = (bf16[8,24,896]{2,1,0:T(8,128)(2,1)S(1)}, bf16[8,24,896]{2,1,0:T(8,128)(2,1)S(1)}, u32[]{:S(2)}, u32[]{:S(2)}) collective-permute-start(bf16[8,24,896]{2,1,0:T(8,128)(2,1)S(1)} %fusion.13), channel_id=1, source_target_pairs={{0,2},{1,3},{2,0},{3,1},{4,6},{5,7},{6,4},{7,5},{8,10},{9,11},{10,... | collective-permute-start | bytes 1032200 | tf_op jit(solution)/shard_map/ppermute | solution.py:794
  533.2 8.9 %collective-permute-start.68 = (bf16[2,96,768]{2,1,0:T(8,128)(2,1)S(1)}, bf16[2,96,768]{2,1,0:T(8,128)(2,1)S(1)}, u32[]{:S(2)}, u32[]{:S(2)}) collective-permute-start(bf16[2,96,768]{2,1,0:T(8,128)(2,1)S(1)} %fusion.14), channel_id=1, source_target_pairs={{0,8},{1,9},{2,10},{3,11},{4,12},{5,13},{6,14},{7,15},{8,0},{9,1},... | collective-permute-start | bytes 884744 | tf_op jit(solution)/shard_map/ppermute | solution.py:794
  535.1 5.5 collective-permute-start.69
  544.4 7.1 %collective-permute-start.70 = (bf16[1,96,768]{2,1,0:T(8,128)(2,1)S(1)}, bf16[1,96,768]{2,1,0:T(8,128)(2,1)S(1)}, u32[]{:S(2)}, u32[]{:S(2)}) collective-permute-start(bf16[1,96,768]{2,1,0:T(8,128)(2,1)S(1)} %fusion.25), channel_id=1, source_target_pairs={{0,16},{1,17},{2,18},{3,19},{4,20},{5,21},{6,22},{7,23},{8,24},{9,... | collective-permute-start | bytes 442376 | tf_op jit(solution)/shard_map/ppermute | solution.py:794
  (70 other events, 398.4 us)

commit v3 on v2

--- a/solution.py
+++ b/solution.py
@@ -5,6 +5,7 @@
 from jax import lax
 from jax.experimental import pallas as pl
 from jax.experimental.pallas import tpu as pltpu
+from jax.sharding import Mesh
 from jax.sharding import PartitionSpec as P
 
 HD = 64
@@ -29,7 +30,8 @@
 CLIP_AT = 1.0
 LOWER = jnp.bfloat16
 SINGLE = jnp.float32
-ALL = ("batch", "head")
+ALL = ("batch", "row", "core")
+HEAD = ("row", "core")
 GRANT = 56 << 20
 
 NN = (((1,), (0,)), ((), ()))
@@ -339,8 +341,12 @@
     ref[...] = jnp.where(first, value, ref[...] + value)
 
 
+def wide(ref):
+    return ref[0].reshape(-1, ref.shape[-1])
+
+
 def feed_fwd_kernel(normed_ref, up_ref, down_ref, act_ref, slope_ref, branch_ref):
-    hidden = dot(normed_ref[...], up_ref[0])
+    hidden = dot(normed_ref[...], wide(up_ref))
     root = 0.7978845608028654
     square = hidden * hidden
     bend = jnp.tanh(hidden * (root + root * 0.044715 * square))
@@ -349,7 +355,7 @@
     slope_ref[0] = low(
         half + hidden * (0.5 - 0.5 * bend * bend) * (root + 3.0 * root * 0.044715 * square)
     )
-    accumulate(branch_ref, dot(act_ref[0], down_ref[0], NT))
+    accumulate(branch_ref, dot(act_ref[0], wide(down_ref), NT))
 
 
 def feed_fwd_last_kernel(
@@ -383,10 +389,10 @@
 def feed_bwd_kernel(
     normed_ref, grad_ref, up_ref, down_ref, act_ref, slope_ref, dup_ref, ddown_ref, dnormed_ref, dhid
 ):
-    dhid[...] = low(dot(grad_ref[...], down_ref[0]) * slope_ref[0].astype(SINGLE))
+    dhid[...] = low(dot(grad_ref[...], wide(down_ref)) * slope_ref[0].astype(SINGLE))
     ddown_ref[0] = low(dot(grad_ref[...], act_ref[0], TN))
     dup_ref[0] = low(dot(normed_ref[...], dhid[...], TN))
-    accumulate(dnormed_ref, dot(dhid[...], up_ref[0], NT))
+    accumulate(dnormed_ref, dot(dhid[...], wide(up_ref), NT))
 
 
 def feed_bwd_last_kernel(
@@ -419,15 +425,13 @@
         )
 
 
-def embed_kernel(patches_ref, early_ref, valid_ref, start_ref, normed_ref, norms_ref):
-    dim = start_ref.shape[1]
-    norms = early_ref[:, dim : dim + 128].astype(SINGLE).T[:8]
-    norms_ref[...] = norms
+def embed_kernel(patches_ref, weight_ref, valid_ref, norms_ref, start_ref, normed_ref):
+    start_ref[...] = dot(patches_ref[...], weight_ref[...]) * valid_ref[...]
     for f in range(FRAMES):
         rows = frame_rows(f)
-        start = dot(patches_ref[rows, :], early_ref[:, :dim]) * valid_ref[rows, :]
-        start_ref[rows, :] = start
-        normed_ref[rows, :] = low(layer_norm(start, norms[0:1], norms[1:2]))
+        normed_ref[rows, :] = low(
+            layer_norm(start_ref[rows, :], norms_ref[0:1, :], norms_ref[1:2, :])
+        )
 
 
 def embed_bwd_kernel(
@@ -449,19 +453,13 @@
     out_ref[:, dim : dim + 128] = low(padded.T)
 
 
-def enter_frame_kernel(
-    patches_ref, early_ref, valid_ref, mixed_ref, own_ref, other_ref, norms_ref, out_ref, normed_ref
-):
+def enter_frame_kernel(start_ref, mixed_ref, weight_ref, norms_ref, out_ref, normed_ref):
+    out_ref[...] = start_ref[...] + dot(mixed_ref[...], weight_ref[...], NT)
     for f in range(FRAMES):
         rows = frame_rows(f)
-        value = dot(patches_ref[rows, :], early_ref[:, : out_ref.shape[1]]) * valid_ref[rows, :]
-        for place, (ref, at) in enumerate(
-            ((own_ref, 0), (own_ref, 1), (other_ref, 0), (other_ref, 1))
-        ):
-            mixed = mixed_ref[rows, GROUP * place : GROUP * (place + 1)]
-            value = value + dot(mixed, ref[at, :, QKV:], NT)
-        out_ref[rows, :] = value
-        normed_ref[rows, :] = low(layer_norm(value, norms_ref[2:3, :], norms_ref[3:4, :]))
+        normed_ref[rows, :] = low(
+            layer_norm(out_ref[rows, :], norms_ref[2:3, :], norms_ref[3:4, :])
+        )
 
 
 def loss_kernel(
@@ -621,7 +619,7 @@
         (normed, weight),
         (shaped(2, FRAMES, QKV, SLOTS, dtype=LOWER), by_group(GROUP)),
         [((FRAMES, GROUP, SLOTS), LOWER)],
-        5,
+        15,
     )
 
 
@@ -672,11 +670,29 @@
     )
 
 
-def feed_forward(normed, up, down, last=None):
-    dim, width = normed.shape[1], up.shape[2]
-    inputs, saved = (normed, up, down), (by_group(width), by_group(width))
+def feed_specs(pair, rows):
+    if rows % 16 != 0:
+        pair = [value[:, :, :rows].reshape(2, 1, -1, value.shape[-1]) for value in pair]
+        rows = pair[0].shape[2]
+    block = (1, pair[0].shape[1], rows, pair[0].shape[3])
+    return pair, [pl.BlockSpec(block, lambda g: (g, 0, 0, 0)) for _ in pair]
+
+
+def feed_forward(normed, pair, rows, last=None):
+    dim, width = normed.shape[1], pair[0].shape[3]
+    pair, specs = feed_specs(pair, rows)
+    inputs, saved = (normed, *pair), (by_group(width), by_group(width))
+    specs = [spec_of(normed), *specs] + [spec_of(value) for value in last or ()]
     if last is None:
-        return call(feed_fwd_kernel, "feed_forward", inputs, (*saved, shaped(ROWS, dim)), [], 10)
+        return call(
+            feed_fwd_kernel,
+            "feed_forward",
+            inputs,
+            (*saved, shaped(ROWS, dim)),
+            [],
+            10,
+            in_specs=specs,
+        )
     return call(
         feed_fwd_last_kernel,
         "feed_forward",
@@ -684,17 +700,23 @@
         (*saved, shaped(ROWS, dim), shaped(1, dim)),
         [((ROWS, dim), SINGLE)],
         10,
-    )
-
-
-def feed_backward(normed, grad, up, down, act, slope, last=None):
-    dim, width = normed.shape[1], up.shape[2]
-    inputs = (normed, grad, up, down, act, slope)
+        in_specs=specs,
+    )
+
+
+def feed_backward(normed, grad, pair, rows, act, slope, last=None):
+    dim, width = normed.shape[1], pair[0].shape[3]
+    pair, specs = feed_specs(pair, rows)
+    inputs = (normed, grad, *pair, act, slope)
+    specs = [spec_of(normed), spec_of(grad), *specs, spec_of(act), spec_of(slope)]
+    specs += [spec_of(value) for value in last or ()]
     weights = (by_group(width, dim), by_group(width, dim))
     scratch = [((ROWS, width), LOWER)]
     if last is None:
         outputs = (*weights, shaped(ROWS, dim))
-        return call(feed_bwd_kernel, "feed_backward", inputs, outputs, scratch, 15)
+        return call(
+            feed_bwd_kernel, "feed_backward", inputs, outputs, scratch, 15, in_specs=specs
+        )
     return call(
         feed_bwd_last_kernel,
         "feed_backward",
@@ -702,13 +724,14 @@
         (*weights, shaped(ROWS, dim), shaped(ROWS, dim, dtype=LOWER), shaped(2, dim)),
         scratch + [((ROWS, dim), SINGLE)],
         15,
-    )
-
-
-def embed(patches, early, valid):
+        in_specs=specs,
+    )
+
+
+def embed(patches, weight, valid, norms):
     dim = patches.shape[1]
-    outputs = (shaped(ROWS, dim), shaped(ROWS, dim, dtype=LOWER), shaped(8, dim))
-    return call(embed_kernel, "embed", (patches, early, valid), outputs, steps=1)
+    outputs = (shaped(ROWS, dim), shaped(ROWS, dim, dtype=LOWER))
+    return call(embed_kernel, "embed", (patches, weight, valid, norms), outputs, (), 15, 1)
 
 
 def embed_backward(patches, start, valid, d_rows, d_a, d_b, norms, d_norms):
@@ -719,23 +742,21 @@
         (patches, start, valid, d_rows, d_a, d_b, norms, d_norms),
         (shaped(dim, dim + 128, dtype=LOWER),),
         [((ROWS, dim), LOWER)],
-        2,
+        30,
         1,
     )[0]
 
 
-def enter_frame(patches, early, valid, mixed, own, other, norms):
-    dim = patches.shape[1]
-    inputs = (patches, early, valid, mixed, own, other, norms)
+def enter_frame(start, mixed, weight, norms):
+    dim = start.shape[1]
     return call(
         enter_frame_kernel,
         "enter_frame",
-        inputs,
+        (start, mixed, weight, norms),
         (shaped(ROWS, dim), shaped(ROWS, dim, dtype=LOWER)),
         [],
         2,
         1,
-        [whole(value.shape) for value in inputs],
     )
 
 
@@ -775,6 +796,14 @@
     )(*inputs)
 
 
+def pace_kernel(token_ref, out_ref):
+    out_ref[...] = token_ref[...]
+
+
+def pace(token):
+    return call(pace_kernel, "pace", (token,), (shaped(*token.shape),), (), 30, 1)[0]
+
+
 def tick(*values):
     return lax.optimization_barrier(values)
 
@@ -798,32 +827,59 @@
 
     def join(self, value, *masks):
         for mask in masks:
-            other = self.swap(value, mask)
-            has = self.has(mask)
-            both = jnp.stack([jnp.where(has, other, value), jnp.where(has, value, other)], axis=-3)
-            shape = value.shape
-            value = both.reshape(*shape[:-3], 2 * shape[-3], *shape[-2:])
+            value = self.merge(value, self.swap(value, mask), mask)
         return value
 
     def fork(self, value):
-        return jnp.stack([value, self.swap(value, 2)])
-
+        return self.stack(value, self.swap(value, 2), 2)
+
+    def step(self, token, sends, late=()):
+        values = [value for value, _ in (*sends, *late)]
+        *values, token = tick(*values, token)
+        masks = [mask for _, mask in (*sends, *late)]
+        received = [self.swap(value, mask) for value, mask in zip(values, masks)]
+        count = len(sends)
+        *ended, token = tick(*received[:count], pace(token))
+        return token, *ended, *received[count:]
+
+    def merge(self, value, other, mask):
+        has = self.has(mask)
+        both = jnp.stack([jnp.where(has, other, value), jnp.where(has, value, other)], axis=-3)
+        shape = value.shape
+        return both.reshape(*shape[:-3], 2 * shape[-3], *shape[-2:])
+
+    def stack(self, value, other, mask):
+        has = self.has(mask)
+        return jnp.stack([jnp.where(has, other, value), jnp.where(has, value, other)])
+
+
+    def cut(self, terms, mask):
+        shape = terms[0].shape
+        mine = self.has(mask).astype(jnp.int32)
+        pairs = [
+            term.reshape(*shape[:-3], shape[-3] // 2, 2, *shape[-2:]) for term in terms
+        ]
+        half = lambda pair, which: lax.dynamic_index_in_dim(pair, which, pair.ndim - 3, False)
+        return low(summed([half(pair, 1 - mine) for pair in pairs])), [
+            half(pair, mine) for pair in pairs
+        ]
 
     def shed(self, terms, *masks):
         for mask in masks:
-            shape = terms[0].shape
-            has = self.has(mask)
-            send, keep = [], []
-            for term in terms:
-                pair = term.reshape(*shape[:-3], shape[-3] // 2, 2, *shape[-2:])
-                send.append(jnp.where(has, pair[..., 0, :, :], pair[..., 1, :, :]))
-                keep.append(jnp.where(has, pair[..., 1, :, :], pair[..., 0, :, :]))
-            terms = keep + [self.swap(low(summed(send)), mask)]
+            send, keep = self.cut(terms, mask)
+            terms = keep + [self.swap(send, mask)]
         return terms
 
+    def cut_row(self, terms):
+        mine = self.has(2).astype(jnp.int32)
+        half = lambda term, which: lax.dynamic_index_in_dim(term, which, 0, False)
+        return low(summed([half(term, 1 - mine) for term in terms])), [
+            half(term, mine) for term in terms
+        ]
+
     def meet(self, terms):
-        send = low(summed([term[1] for term in terms]))
-        return [term[0] for term in terms] + [self.swap(send, 2)]
+        send, keep = self.cut_row(terms)
+        return keep + [self.swap(send, 2)]
 
     def total(self, value):
         for mask in [1, 2] + self.batch_masks[::-1]:
@@ -847,7 +903,7 @@
     dim = norm_params.shape[1] * cube.count
     classes, proj = head_weight.shape[1], proj_weight.shape[1]
     rows_wide, rows_small = attn_in.shape[2], patch_weight.shape[0]
-    place = lax.axis_index("head")
+    place = lax.axis_index(HEAD)
 
     *first, near, last = cube.batch_masks
     middle = dim // 2
@@ -868,90 +924,126 @@
         jnp.where(lane == 0, jnp.where(frame_valid > 0, 0.0, -1e30), (lane < 4).astype(SINGLE))
     )
 
-    first_w = pack(attn_in[0], attn_out[0])
-    first_w, clip, w_patch, w_norms = tick(first_w, patches[0], patch_weight, norm_params)
-    first_w = cube.join(first_w, *first)
-    early = jnp.concatenate([low(w_patch), low(w_norms).T], axis=1)
-    early = jnp.pad(early, ((0, 0), (0, 120)))[None]
-    early = cube.join(early, *first)
+    extra = -(-(rows_small + 1) // 16) * 16
+    norm_row = low(norm_params).reshape(1, -1)
+    first_w = jnp.concatenate(
+        [
+            pack(attn_in[0], attn_out[0])[0],
+            low(patch_weight),
+            jnp.pad(norm_row, ((0, extra - rows_small - 1), (0, dim - norm_row.shape[1]))),
+        ]
+    )[None]
+    token = jnp.zeros((8, 128), SINGLE)
+    clip, w_in, w_out, w_up, w_down = patches[0], attn_in[1], attn_out[1], up, down
+    for mask in first:
+        first_w, clip, w_in, w_out, w_up, w_down = tick(first_w, clip, w_in, w_out, w_up, w_down)
+        token, other = cube.step(token, [(first_w, mask)])
+        first_w = cube.merge(first_w, other, mask)
     blocks = jnp.pad(clip, ((0, ROWS - PMAX), (0, 0))).reshape(FRAMES, SLOTS, -1)
     blocks = jnp.where((place & 1) != 0, blocks[jnp.array([1, 0, 3, 2])], blocks)
     blocks = jnp.where((place & 2) != 0, blocks[jnp.array([2, 3, 0, 1])], blocks)
-    second_w = pack(attn_in[1], attn_out[1])
-    first_w, early, blocks, second_w = tick(first_w, early, blocks, second_w)
-
-    first_w = cube.join(first_w, near)
-    early = cube.join(early, near)
+    second_w = jnp.concatenate([pack(w_in, w_out)[0], low(w_up)])[None]
+    small = jnp.concatenate([low(head_weight), low(proj_weight)], axis=1)
+    small = jnp.pad(small, ((0, -rows_small % 16), (0, dim - small.shape[1])))
+    down_w = jnp.concatenate([low(w_down), small])[None]
+
+    token, other, *slots = cube.step(
+        token, [(first_w, near)] + [(blocks[r], r) for r in range(1, FRAMES)]
+    )
+    first_w = cube.merge(first_w, other, near)
     by_frame = blocks.reshape(ROWS, -1)
-    by_slot = jnp.concatenate(cube.swap_frames(list(blocks)))
-    up_w, down_w = low(up)[None], low(down)[None]
-    first_w, early, by_slot, up_w, down_w = tick(first_w, early, by_slot, up_w, down_w)
-
-    left = cube.join(first_w[..., :middle], last)
-    right = cube.fork(first_w[..., middle:])
-    early = cube.join(early, last)
-    second_w, up_w = cube.join(second_w, *first), cube.join(up_w, *first)
-    left, right, early, second_w, up_w = tick(left, right, early, second_w, up_w)
-
-    left, right = cube.fork(left), cube.join(right, last)
-    own_first = jnp.concatenate([flat(left), flat(right)], axis=-1)
-    early = cube.join(early, 2)
-    second_w, up_w = cube.join(second_w, near), cube.join(up_w, near)
-    own_first, early, second_w, up_w = tick(own_first, early, second_w, up_w)
-
-    early = cube.join(early, 1).reshape(dim, -1)
-    other_first = cube.swap(own_first, 1)
-    second_w, up_w, down_w = cube.fork(second_w), cube.join(up_w, last), cube.join(down_w, *first)
-    start_slot, normed_t, norms = embed(by_slot, early, slot_valid)
+
+    left, right = first_w[..., :middle], first_w[..., middle:]
+    token, other_left, other_right, other = cube.step(
+        token, [(left, last), (right, 2), (second_w, first[0])]
+    )
+    left, right = cube.merge(left, other_left, last), cube.stack(right, other_right, 2)
+    second_w = cube.join(cube.merge(second_w, other, first[0]), *first[1:])
+
+    left, right, second_w, *slots = tick(left, right, second_w, *slots)
+    by_slot = jnp.concatenate([blocks[0], *slots])
+    token, other_left, other_right, other = cube.step(
+        token, [(left, 2), (right, last), (second_w, near)]
+    )
+    by_slot, slot_valid, token = tick(by_slot, slot_valid, token)
+    left, right = cube.stack(left, other_left, 2), cube.merge(right, other_right, last)
+    joined = lambda at: jnp.concatenate([left[:, :, at], right[:, :, at]], axis=-1)
+    own_first, early = flat(joined(slice(0, rows_wide))), joined(slice(rows_wide, None))
+
+    early, own_first, other = tick(early, own_first, other)
+    second_w = cube.merge(second_w, other, near)
+    second_w, up_w = second_w[..., :rows_wide, :], second_w[..., rows_wide:, :]
+    token, other, other_first, other_left, other_right, other_up = cube.step(
+        token,
+        [(early, 1)],
+        [
+            (own_first, 1),
+            (second_w[..., :middle], last),
+            (second_w[..., middle:], 2),
+            (up_w, 2),
+        ],
+    )
+    early = cube.stack(early, other, 1).transpose(2, 1, 0, 3, 4)
+    patch_copy = early[..., :rows_small, :].reshape(dim, dim)
+    norms = early[..., rows_small, : norm_row.shape[1]].reshape(-1, 8, rows_small)
+    norms = norms.transpose(1, 0, 2).reshape(8, dim).astype(SINGLE)
+    start_slot, normed_t = embed(by_slot, patch_copy, slot_valid, norms)
+    start_slot, normed_t, other_left, other_right, down_w = tick(
+        start_slot, normed_t, other_left, other_right, down_w
+    )
+    left = cube.fork(cube.merge(second_w[..., :middle], other_left, last))
+    right = cube.join(cube.stack(second_w[..., middle:], other_right, 2), last)
+    down_w = cube.join(down_w, *first)
     qkv_t, mixed_t = [None, None], [None, None]
     qkv_t[0], mixed_t[0] = temporal_forward(normed_t, own_first)
-    mixed_t[0], normed_t, second_w, other_first, up_w, down_w = tick(
-        mixed_t[0], normed_t, second_w, other_first, up_w, down_w
-    )
+    mixed_t[0], normed_t, other_first, patch_copy, other_up, down_w = tick(
+        mixed_t[0], normed_t, other_first, patch_copy, other_up, down_w
+    )
+    own_up = cube.join(cube.stack(up_w, other_up, 2), last)
+    down_w = cube.join(down_w, near)
+    pair = (own_first, other_first)
+    out_first = jnp.concatenate([pair[c][y][:, QKV:] for c in range(2) for y in range(2)], axis=1)
+    start_frame = dot(by_frame, patch_copy) * frame_valid
     qkv_t[1], mixed_t[1] = temporal_forward(normed_t, other_first)
-    own_second, down_w = flat(cube.join(second_w, last)), cube.join(down_w, near)
-    small = jnp.concatenate([low(head_weight), low(proj_weight)], axis=1)
-    small = cube.join(jnp.pad(small, ((0, 0), (0, dim - small.shape[1])))[None], *first)
-    order = (0, 2, 1, 3)
-    pieces = {m: mixed_t[m % 2][m // 2] for m in range(4)}
     parts = [
-        jnp.concatenate([pieces[m ^ r][frame_rows(r)] for m in order], axis=1)
+        jnp.concatenate(
+            [mixed_t[c ^ (r & 1)][y][frame_rows(r)] for c in range(2) for y in range(2)], axis=1
+        )
         for r in range(FRAMES)
     ]
-    parts[0], parts[1], parts[2], parts[3], down_w, small = tick(*parts, down_w, small)
-
-    mixed_frame = jnp.concatenate(cube.swap_frames(parts))
-    small = cube.join(small, near)
-    mixed_frame, own_second, small = tick(mixed_frame, own_second, small)
-
-    resid_one, normed_s = enter_frame(
-        by_frame, early, frame_valid, mixed_frame, own_first, other_first, norms
-    )
-    down_w, own_up = cube.fork(down_w), flat(cube.fork(up_w))
+    own_second = jnp.concatenate([flat(left), flat(right)], axis=-1)
+
+    parts[0], out_first, start_frame, token = tick(parts[0], out_first, start_frame, token)
+    token, *received = cube.step(token, [(parts[r], r) for r in range(1, FRAMES)])
+    mixed_frame = jnp.concatenate([parts[0], *received])
+    mixed_frame, own_second, key_extra, down_w = tick(mixed_frame, own_second, key_extra, down_w)
+
+    resid_one, normed_s = enter_frame(start_frame, mixed_frame, out_first, norms)
     other_second = cube.swap(own_second, 1)
-    small = cube.join(small, last)
+    left, right = cube.join(down_w[..., :middle], last), cube.fork(down_w[..., middle:])
     qkv_s, mixed_s, extra_s = ([None, None] for _ in range(3))
     qkv_s[0], mixed_s[0], extra_s[0], branch = spatial_forward(normed_s, own_second, key_extra)
-    branch, normed_s, other_second, down_w, small = tick(
-        branch, normed_s, other_second, down_w, small
-    )
-    own_down = flat(cube.join(down_w, last))
+    branch, normed_s, other_second, own_up, left, right = tick(
+        branch, normed_s, other_second, own_up, left, right
+    )
+    other_up = cube.swap(own_up, 1)
+    left, right = cube.fork(left), cube.join(right, last)
     qkv_s[1], mixed_s[1], extra_s[1], resid_two, normed_m = spatial_forward(
         normed_s, other_second, key_extra, (resid_one, branch, norms)
     )
-    normed_m, own_up, own_down = tick(normed_m, own_up, own_down)
-
-    other_up, other_down = cube.swap(own_up, 1), cube.swap(own_down, 1)
-    small = cube.join(small, 2)
+    own_down = jnp.concatenate([left, right], axis=-1)
+    normed_m, own_down, other_up = tick(normed_m, own_down, other_up)
+
+    other_down = cube.swap(own_down, 1)
+    own_pair, other_pair = (own_up, own_down), (other_up, other_down)
     act, slope = ([None, None] for _ in range(2))
-    act[0], slope[0], branch = feed_forward(normed_m, own_up, own_down)
-    branch, normed_m, other_up, other_down, small = tick(
-        branch, normed_m, other_up, other_down, small
-    )
+    act[0], slope[0], branch = feed_forward(normed_m, own_pair, rows_wide)
     act[1], slope[1], resid_three, sums = feed_forward(
-        normed_m, other_up, other_down, (resid_two, branch, norms, frame_valid)
-    )
-    small = cube.join(small, 1).reshape(dim, -1)
+        normed_m, other_pair, rows_wide, (resid_two, branch, norms, frame_valid)
+    )
+    small = slice(rows_wide, rows_wide + rows_small)
+    small = cube.stack(own_down[:, :, small], other_down[:, :, small], 1)
+    small = small.transpose(2, 1, 0, 3, 4).reshape(dim, dim)
 
     for mask in (1, 2):
         sums = sums + cube.swap(sums, mask)
@@ -965,7 +1057,7 @@
 
     d_up, d_down = [None, None], [None, None]
     d_up[1], d_down[1], d_normed = feed_backward(
-        normed_m, d_rows, other_up, other_down, act[1], slope[1]
+        normed_m, d_rows, other_pair, rows_wide, act[1], slope[1]
     )
     up_other, down_other, d_normed, d_rows, normed_m = tick(
         d_up[1], d_down[1], d_normed, d_rows, normed_m
@@ -974,8 +1066,8 @@
     d_up[0], d_down[0], d_resid, d_rows, d_norms_m = feed_backward(
         normed_m,
         d_rows,
-        own_up,
-        own_down,
+        own_pair,
+        rows_wide,
         act[0],
         slope[0],
         (resid_two, d_resid, d_normed, norms),
@@ -1012,10 +1104,13 @@
         d_rows, d_second[0], sum_up[-1], sum_down[-1], core_second
     )
 
-    d_rows = jnp.concatenate(cube.swap_frames(split_frames(d_rows)))
-    sum_second = cube.shed([blocked(second_own), blocked(core_second)], last)
-    d_rows, up_last, down_last = tick(d_rows, sum_up[-1], sum_down[-1])
-    sum_up[-1], sum_down[-1] = up_last, down_last
+    parts = split_frames(d_rows)
+    send, sum_second = cube.cut([blocked(second_own), blocked(core_second)], last)
+    token, *received, other = cube.step(
+        token, [(parts[r], r) for r in range(1, FRAMES)], [(send, last)]
+    )
+    d_rows = jnp.concatenate([parts[0], *received])
+    sum_second.append(other)
 
     sum_up, sum_down = cube.shed(sum_up, near), cube.shed(sum_down, near)
     d_first, d_normed = [None, None], [None, None]
@@ -1036,35 +1131,58 @@
     )
 
     sum_first = [blocked(first_own), blocked(core_first)]
-    left = cube.meet([term[..., :middle] for term in sum_first])
-    right = cube.shed([term[..., middle:] for term in sum_first], last)
-    sum_second = cube.shed(sum_second, near)
+    send_left, left = cube.cut_row([term[..., :middle] for term in sum_first])
+    send_right, right = cube.cut([term[..., middle:] for term in sum_first], last)
+    send_second, sum_second = cube.cut(sum_second, near)
+    send_left, send_right, send_second, d_normed[0] = tick(
+        send_left, send_right, send_second, d_normed[0]
+    )
+    other_left, other_right, other_second = (
+        cube.swap(send_left, 2), cube.swap(send_right, last), cube.swap(send_second, near)
+    )
     d_norms = jnp.concatenate([d_norms_s, d_norms_m, d_norms_f])
     d_early = embed_backward(
         by_slot, start_slot, slot_valid, d_rows, d_normed[0], d_normed[1], norms, d_norms
     )
-    sum_early = cube.shed([d_early.reshape(-1, rows_small, dim + 128)], 1)
+    send, sum_early = cube.cut([d_early.reshape(-1, rows_small, dim + 128)], 1)
+    other_left, other_right, other_second, send, token = tick(
+        other_left, other_right, other_second, send, token
+    )
+    other = cube.swap(send, 1)
+    left.append(other_left)
+    right.append(other_right)
+    sum_second.append(other_second)
+    sum_early.append(other)
+
+    send_left, left = cube.cut(left, last)
+    send_right, right = cube.cut_row(right)
+    send_second, sum_second = cube.cut(sum_second, first[-1])
+    send, sum_early = cube.cut(sum_early, 2)
+    token, other_left, other_right, other_second, other = cube.step(
+        token, [(send_left, last), (send_right, 2), (send_second, first[-1]), (send, 2)]
+    )
+    sum_first = [jnp.concatenate([summed(left + [other_left]), summed(right + [other_right])], -1)]
+    sum_second.append(other_second)
+    sum_early.append(other)
+
+    send_first, sum_first = cube.cut(sum_first, near)
+    send, sum_early = cube.cut(sum_early, last)
+    token, other_first, other = cube.step(token, [(send_first, near), (send, last)])
+    sum_first.append(other_first)
+    sum_early.append(other)
+
+    send_first, sum_first = cube.cut(sum_first, first[-1])
+    send, sum_early = cube.cut(sum_early, near)
+    ready, up_last, down_last = tick(send_first, sum_up[-1], sum_down[-1])
+    sum_up[-1], sum_down[-1] = up_last, down_last
+    square = lambda value: jnp.sum(value * value)
     d_up, d_down = summed(sum_up)[0], summed(sum_down)[0]
-    square = lambda value: jnp.sum(value * value)
-    squares = square(d_small) + square(d_up) + square(d_down)
-    left[-1], right[-1], sum_early[-1], sum_second[-1], squares = tick(
-        left[-1], right[-1], sum_early[-1], sum_second[-1], squares
-    )
-    left, right = cube.shed(left, last), cube.meet(right)
-    sum_early = cube.shed(sum_early, 2)
-    sum_second = cube.shed(sum_second, *first[::-1])
-    left[-1], right[-1], sum_early[-1], sum_second[-1] = tick(
-        left[-1], right[-1], sum_early[-1], sum_second[-1]
-    )
-    sum_first = [jnp.concatenate([summed(left), summed(right)], axis=-1)]
-    sum_first = cube.shed(sum_first, near)
-    sum_early = cube.shed(sum_early, last)
-    d_second = summed(sum_second)[0]
-    squares = squares + square(d_second)
-    sum_first[-1], sum_early[-1], squares = tick(sum_first[-1], sum_early[-1], squares)
-    sum_first = cube.shed(sum_first, *first[::-1])
-    sum_early = cube.shed(sum_early, near)
-    sum_first[-1], sum_early[-1] = tick(sum_first[-1], sum_early[-1])
+    d_second = summed(cube.shed(sum_second, *first[-2::-1]))[0]
+    squares = square(d_small) + square(d_up) + square(d_down) + square(d_second)
+    token, other_first, other = cube.step(token, [(ready, first[-1]), (send, near)])
+    sum_first.append(other_first)
+    sum_early.append(other)
+    sum_first = cube.shed(sum_first, *first[-2::-1])
     sum_early = cube.shed(sum_early, *first[::-1])
     d_first, d_early = summed(sum_first)[0], summed(sum_early)[0]
 
@@ -1076,67 +1194,69 @@
 
 
 def solution(mesh):
+    sizes = dict(mesh.shape)
+    split = Mesh(mesh.devices.reshape(sizes["batch"], 2, sizes["head"] // 2), ALL)
     placed = (
-        P("batch", "head", None),
+        P("batch", HEAD, None),
         P("batch"),
         P("batch"),
         P("batch"),
-        P(("batch", "head"), None),
-        P(None, ("batch", "head")),
-        P(("batch", "head"), None),
-        P(("batch", "head"), None),
-        P(None, "batch", None, "head"),
-        P(None, "head", "batch"),
-        P("batch", "head"),
-        P("head", "batch"),
-        P(("batch", "head"), None),
-        P(None, ("batch", "head")),
-        P(("batch", "head"), None),
-        P(("batch", "head"), None),
-        P(None, "batch", None, "head"),
-        P(None, "head", "batch"),
-        P("batch", "head"),
-        P("head", "batch"),
-        P(("batch", "head"), None),
-        P(None, ("batch", "head")),
-        P(("batch", "head"), None),
-        P(("batch", "head"), None),
-        P(None, "batch", None, "head"),
-        P(None, "head", "batch"),
-        P("batch", "head"),
-        P("head", "batch"),
+        P(ALL, None),
+        P(None, ALL),
+        P(ALL, None),
+        P(ALL, None),
+        P(None, "batch", None, HEAD),
+        P(None, HEAD, "batch"),
+        P("batch", HEAD),
+        P(HEAD, "batch"),
+        P(ALL, None),
+        P(None, ALL),
+        P(ALL, None),
+        P(ALL, None),
+        P(None, "batch", None, HEAD),
+        P(None, HEAD, "batch"),
+        P("batch", HEAD),
+        P(HEAD, "batch"),
+        P(ALL, None),
+        P(None, ALL),
+        P(ALL, None),
+        P(ALL, None),
+        P(None, "batch", None, HEAD),
+        P(None, HEAD, "batch"),
+        P("batch", HEAD),
+        P(HEAD, "batch"),
     )
     return jax.shard_map(
-        functools.partial(body, dict(mesh.shape)),
-        mesh=mesh,
+        functools.partial(body, sizes),
+        mesh=split,
         in_specs=placed,
         out_specs=(
             P(),
             P(),
-            P(("batch", "head"), None),
-            P(("batch", "head"), None),
-            P(("batch", "head"), None),
-            P(None, ("batch", "head")),
-            P(None, ("batch", "head")),
-            P(None, ("batch", "head")),
-            P(("batch", "head"), None),
-            P(("batch", "head"), None),
-            P(("batch", "head"), None),
-            P(("batch", "head"), None),
-            P(("batch", "head"), None),
-            P(("batch", "head"), None),
-            P(None, "batch", None, "head"),
-            P(None, "batch", None, "head"),
-            P(None, "batch", None, "head"),
-            P(None, "head", "batch"),
-            P(None, "head", "batch"),
-            P(None, "head", "batch"),
-            P("batch", "head"),
-            P("batch", "head"),
-            P("batch", "head"),
-            P("head", "batch"),
-            P("head", "batch"),
-            P("head", "batch"),
+            P(ALL, None),
+            P(ALL, None),
+            P(ALL, None),
+            P(None, ALL),
+            P(None, ALL),
+            P(None, ALL),
+            P(ALL, None),
+            P(ALL, None),
+            P(ALL, None),
+            P(ALL, None),
+            P(ALL, None),
+            P(ALL, None),
+            P(None, "batch", None, HEAD),
+            P(None, "batch", None, HEAD),
+            P(None, "batch", None, HEAD),
+            P(None, HEAD, "batch"),
+            P(None, HEAD, "batch"),
+            P(None, HEAD, "batch"),
+            P("batch", HEAD),
+            P("batch", HEAD),
+            P("batch", HEAD),
+            P(HEAD, "batch"),
+            P(HEAD, "batch"),
+            P(HEAD, "batch"),
         ),
         check_vma=False,
     )

time: 592 us -> 550 us (0.929)
  waiting for transfers between devices: 158 us -> 120 us
  local copies, waits for them, and re-layouts: 32.8 us -> 45.9 us
  starting transfers between devices: 83.1 us -> 70.6 us
    ppermute x78 -> x71, waiting for transfers between devices: 158 us -> 120 us  [swap(): return lax.ppermute(value, ALL, [(i, i ^ mask) for i in range(self.count)])]
    select_n x32 -> x1, other arithmetic: 14.7 us -> 0.17 us  [stack(): jnp.where(has, other, value)]
    ppermute x78 -> x71, starting transfers between devices: 83.1 us -> 70.6 us  [swap(): return lax.ppermute(value, ALL, [(i, i ^ mask) for i in range(self.count)])]
    dynamic_slice x0 -> x19, local copies, waits for them, and re-layouts: none -> 8.13 us  [the longest x10 6.46 us: cut_row(): half = lambda term, which: lax.dynamic_index_in_dim(term, which, 0, False)]
    another operation x50 -> x38, other arithmetic: 10.8 us -> 13.8 us  [the longest x26 6.97 us: merge(): jnp.stack([jnp.where(has, other, value), jnp.where(has, value, other)], a...]
    unnamed x113 -> x140, local copies, waits for them, and re-layouts: 10.1 us -> 12.8 us
    convert_element_type x23 -> x24, other arithmetic: 21.5 us -> 21.5 us  [low(): return value.astype(LOWER)]
  transfers between devices with their start and end apart: 78 -> 71, of which waited for: 43 -> 31; matrix products, arithmetic and copies ran while one was open for 9% -> 13% of each run, Pallas kernels for 31% -> 33%
where the time goes in v3:
time: 550 us; the launch traced here: 542 us
  Pallas kernels  224 us (41%)
  waiting for transfers between devices  120 us (22%)
  starting transfers between devices  70.6 us (13%)
  other arithmetic  66.9 us (12%)
  local copies, waits for them, and re-layouts  45.9 us (8%)
  between operations  11.6 us (2%)
    pallas_call x16, Pallas kernels, call(): pl.pallas_call(kernel, grid=(steps,), in_specs=in_specs or [spec_of(value...  218 us
    ppermute x71, waiting for transfers between devices, swap(): return lax.ppermute(value, ALL, [(i, i ^ mask) for i in range(self.count)])  120 us
    ppermute x71, starting transfers between devices, swap(): return lax.ppermute(value, ALL, [(i, i ^ mask) for i in range(self.count)])  70.6 us
    convert_element_type x24, other arithmetic, low(): return value.astype(LOWER)  21.5 us
    unnamed x140, local copies, waits for them, and re-layouts  12.8 us
    reduce_sum x6, other arithmetic, body(): square = lambda value: jnp.sum(value * value)  12.5 us
  transfers between devices with their start and end apart: 71, of which 31 were waited for; matrix products, arithmetic and copies ran while one was open for 13% of the time, Pallas kernels for 33%

profile of v3, /device:TPU:0, one launch (start us, length us, event | category | flops | bytes accessed | tf_op | source)
XLA Modules:
  0.0 541.6 jit_solution(1637484816807274255)
XLA Ops:
  5.9 4.1 collective-permute-start
  10.1 1.7 gather_fusion
  14.6 4.5 collective-permute-done
  22.7 7.9 %collective-permute-done.3 = bf16[208,768]{1,0:T(8,128)(2,1)S(1)} collective-permute-done((bf16[208,768]{1,0:T(8,128)(2,1)}, bf16[208,768]{1,0:T(8,128)(2,1)S(1)}, u32[]{:S(2)}, u32[]{:S(2)}) %collective-permute-start.3) | collective-permute-done | bytes 319520 | tf_op jit(solution)/shard_map/ppermute | solution.py:823
  30.7 5.9 %collective-permute-done.4 = bf16[208,768]{1,0:T(8,128)(2,1)S(1)} collective-permute-done((bf16[208,768]{1,0:T(8,128)(2,1)S(1)}, bf16[208,768]{1,0:T(8,128)(2,1)S(1)}, u32[]{:S(2)}, u32[]{:S(2)}) %collective-permute-start.4) | collective-permute-done | bytes 319520 | tf_op jit(solution)/shard_map/ppermute | solution.py:823
  41.3 3.4 collective-permute-start.7
  44.8 13.1 %collective-permute-done.7 = bf16[1,192,768]{2,1,0:T(8,128)(2,1)S(1)} collective-permute-done((bf16[1,192,768]{2,1,0:T(8,128)(2,1)S(1)}, bf16[1,192,768]{2,1,0:T(8,128)(2,1)S(1)}, u32[]{:S(2)}, u32[]{:S(2)}) %collective-permute-start.7) | collective-permute-done | bytes 294944 | tf_op jit(solution)/shard_map/ppermute | solution.py:823
  62.4 12.2 %collective-permute-done.10 = bf16[2,192,768]{2,1,0:T(8,128)(2,1)} collective-permute-done((bf16[2,192,768]{2,1,0:T(8,128)(2,1)S(1)}, bf16[2,192,768]{2,1,0:T(8,128)(2,1)}, u32[]{:S(2)}, u32[]{:S(2)}) %collective-permute-start.10) | collective-permute-done | bytes 589856 | tf_op jit(solution)/shard_map/ppermute | solution.py:823
  74.6 3.5 collective-permute-done.8
  80.6 1.6 fusion
  85.8 3.1 fusion.1
  99.2 5.1 embed.1
  107.2 6.7 %temporal_forward.2 = (bf16[2,4,576,208]{3,2,1,0:T(8,128)(2,1)}, bf16[2,832,192]{2,1,0:T(8,128)(2,1)}) custom-call(bf16[832,768]{1,0:T(8,128)(2,1)} %get-tuple-element.411.normed_ref, bf16[2,768,768]{2,1,0:T(8,128)(2,1)} %bitcast.478), custom_call_target="tpu_custom_call" | custom-call | flops 15000000512 | bytes 8388608 | tf_op jit(solution)/shard_map/temporal_forward/pallas_call | solution.py:596
  115.7 5.5 %collective-permute-done.21 = bf16[2,4,96,384]{3,2,1,0:T(8,128)(2,1)S(1)} collective-permute-done((bf16[2,4,96,384]{3,2,1,0:T(8,128)(2,1)S(1)}, bf16[2,4,96,384]{3,2,1,0:T(8,128)(2,1)S(1)}, u32[]{:S(2)}, u32[]{:S(2)}) %collective-permute-start.21) | collective-permute-done | bytes 589856 | tf_op jit(solution)/shard_map/ppermute | solution.py:823
  121.7 7.6 %collective-permute-done.20 = bf16[8,96,384]{2,1,0:T(8,128)(2,1)S(1)} collective-permute-done((bf16[8,96,384]{2,1,0:T(8,128)(2,1)S(1)}, bf16[8,96,384]{2,1,0:T(8,128)(2,1)S(1)}, u32[]{:S(2)}, u32[]{:S(2)}) %collective-permute-start.20) | collective-permute-done | bytes 589856 | tf_op jit(solution)/shard_map/ppermute | solution.py:823
  131.1 1.8 slice_bitcast_fusion.1
  132.9 6.2 %temporal_forward.3 = (bf16[2,4,576,208]{3,2,1,0:T(8,128)(2,1)}, bf16[2,832,192]{2,1,0:T(8,128)(2,1)}) custom-call(bf16[832,768]{1,0:T(8,128)(2,1)} %get-tuple-element.411.normed_ref, bf16[2,768,768]{2,1,0:T(8,128)(2,1)} %collective-permute-done.14.weight_ref), custom_call_target="tpu_custom_call" | custom-call | flops 15000000512 | bytes 8388608 | tf_op jit(solution)/shard_map/temporal_forward/pallas_call | solution.py:596
  144.4 2.7 convolution_multiply_fusion.start_ref
  152.7 5.0 collective-permute-done.19
  163.5 5.8 %enter_frame.1 = (f32[832,768]{1,0:T(8,128)}, bf16[832,768]{1,0:T(8,128)(2,1)}) custom-call(f32[832,768]{1,0:T(8,128)} %convolution_multiply_fusion.start_ref, bf16[832,768]{1,0:T(8,128)(2,1)} %pad_maximum_fusion.7.mixed_ref, bf16[768,768]{1,0:T(8,128)(2,1)} %pad_maximum_fusion.10.weight_ref, f32[8,768]{1,0:T(8,128)} %reshape.1247.norms_ref), custom_call_target="tpu_custom_call" | custom-call | flops 2000000000 | bytes 8388608 | tf_op jit(solution)/shard_map/enter_frame/pallas_call | solution.py:596
  169.2 15.2 %spatial_forward.2 = (bf16[2,832,576]{2,1,0:T(8,128)(2,1)}, bf16[2,832,192]{2,1,0:T(8,128)(2,1)}, bf16[2,832,192]{2,1,0:T(8,128)(2,1)}, f32[832,768]{1,0:T(8,128)}) custom-call(bf16[832,768]{1,0:T(8,128)(2,1)} %get-tuple-element.383.normed_ref, bf16[2,768,768]{2,1,0:T(8,128)(2,1)} %pad_maximum_fusion.2.weight_ref, ...), custom_call_target="tpu_custom_call" | custom-call | flops 15000000512 | bytes 8388608 | tf_op jit(solution)/shard_map/spatial_forward/pallas_call | solution.py:596
  184.4 4.3 collective-permute-done.25
  194.5 18.7 %spatial_forward.3 = (bf16[2,832,576]{2,1,0:T(8,128)(2,1)}, bf16[2,832,192]{2,1,0:T(8,128)(2,1)}, bf16[2,832,192]{2,1,0:T(8,128)(2,1)}, f32[832,768]{1,0:T(8,128)}, bf16[832,768]{1,0:T(8,128)(2,1)}) custom-call(bf16[832,768]{1,0:T(8,128)(2,1)} %get-tuple-element.383.normed_ref, bf16[2,768,768]{2,1,0:T(8,128)(2,1)} %collective-permute-done.23.weight_ref, ...), custom_call_target="tpu_custom_call" | custom-call | flops 15000000512 | bytes 8388608 | tf_op jit(solution)/shard_map/spatial_forward/pallas_call | solution.py:596
  217.4 9.7 %feed_forward.2 = (bf16[2,832,768]{2,1,0:T(8,128)(2,1)}, bf16[2,832,768]{2,1,0:T(8,128)(2,1)}, f32[832,768]{1,0:T(8,128)}) custom-call(bf16[832,768]{1,0:T(8,128)(2,1)} %get-tuple-element.357.normed_ref, bf16[2,8,96,768]{3,2,1,0:T(8,128)(2,1)} %bitcast.94.up_ref, bf16[2,8,128,768]{3,2,1,0:T(8,128)(2,1)} %copy-done.7), custom_call_target="tpu_custom_call" | custom-call | flops 10000000000 | bytes 8388608 | tf_op jit(solution)/shard_map/feed_forward/pallas_call | solution.py:596
  227.1 13.8 %feed_forward.3 = (bf16[2,832,768]{2,1,0:T(8,128)(2,1)}, bf16[2,832,768]{2,1,0:T(8,128)(2,1)}, f32[832,768]{1,0:T(8,128)}, f32[1,768]{1,0:T(1,128)}) custom-call(bf16[832,768]{1,0:T(8,128)(2,1)} %get-tuple-element.357.normed_ref, bf16[2,8,96,768]{3,2,1,0:T(8,128)(2,1)} %collective-permute-done.29.up_ref, ...), custom_call_target="tpu_custom_call" | custom-call | flops 10000000000 | bytes 8388608 | tf_op jit(solution)/shard_map/feed_forward/pallas_call | solution.py:596
  243.5 3.1 collective-permute-done.32
  246.6 1.7 collective-permute-start.33
  248.4 2.8 collective-permute-done.33
  259.5 7.2 %losses.1 = (f32[1,1]{1,0:T(1,128)}, bf16[8,768]{1,0:T(8,128)(2,1)}, bf16[8,768]{1,0:T(8,128)(2,1)}, f32[832,768]{1,0:T(8,128)}, bf16[832,768]{1,0:T(8,128)(2,1)}, /*index=5*/f32[2,768]{1,0:T(2,128)}) custom-call(s32[1]{0:T(128)} %bitcast.clip_ref, f32[8,896]{1,0:T(8,128)} %squeeze_reshape.3.facts_ref, bf16[768,768]{1,0:T(8,128)(2,1)} %bitcast.491, ...), custom_call_target="tpu_custom_call" | custom-call | flops 1000000000 | bytes 8388608 | tf_op jit(solution)/shard_map/losses/pallas_call | solution.py:596
  266.7 14.0 %feed_backward.2 = (bf16[2,768,768]{2,1,0:T(8,128)(2,1)}, bf16[2,768,768]{2,1,0:T(8,128)(2,1)}, f32[832,768]{1,0:T(8,128)}) custom-call(bf16[832,768]{1,0:T(8,128)(2,1)} %get-tuple-element.357.normed_ref, bf16[832,768]{1,0:T(8,128)(2,1)} %get-tuple-element.358.grad_ref, bf16[2,8,96,768]{3,2,1,0:T(8,128)(2,1)} %collective-permute-done.29.up_ref, ...), custom_call_target="tpu_custom_call" | custom-call | flops 15000000512 | bytes 8388608 | tf_op jit(solution)/shard_map/feed_backward/pallas_call | solution.py:596
  282.4 19.2 %feed_backward.3 = (bf16[2,768,768]{2,1,0:T(8,128)(2,1)}, bf16[2,768,768]{2,1,0:T(8,128)(2,1)}, f32[832,768]{1,0:T(8,128)}, bf16[832,768]{1,0:T(8,128)(2,1)}, f32[2,768]{1,0:T(2,128)}) custom-call(bf16[832,768]{1,0:T(8,128)(2,1)} %get-tuple-element.357.normed_ref, bf16[832,768]{1,0:T(8,128)(2,1)} %get-tuple-element.358.grad_ref, ...), custom_call_target="tpu_custom_call" | custom-call | flops 15000000512 | bytes 8388608 | tf_op jit(solution)/shard_map/feed_backward/pallas_call | solution.py:596
  301.6 2.8 fusion.2
  304.9 2.6 fusion.3
  309.0 27.2 %spatial_backward.2 = (bf16[2,768,768]{2,1,0:T(8,128)(2,1)}, f32[832,768]{1,0:T(8,128)}) custom-call(bf16[832,768]{1,0:T(8,128)(2,1)} %get-tuple-element.383.normed_ref, bf16[832,768]{1,0:T(8,128)(2,1)} %get-tuple-element.384.grad_ref, bf16[2,768,768]{2,1,0:T(8,128)(2,1)} %collective-permute-done.23.weight_ref, ...), custom_call_target="tpu_custom_call" | custom-call | flops 30000001024 | bytes 8388608 | tf_op jit(solution)/shard_map/spatial_backward/pallas_call | solution.py:596
  337.5 1.9 copy-done.9
  340.4 2.3 fusion.6
  344.2 31.8 %spatial_backward.3 = (bf16[2,768,768]{2,1,0:T(8,128)(2,1)}, bf16[832,768]{1,0:T(8,128)(2,1)}, f32[2,768]{1,0:T(2,128)}) custom-call(bf16[832,768]{1,0:T(8,128)(2,1)} %get-tuple-element.383.normed_ref, bf16[832,768]{1,0:T(8,128)(2,1)} %get-tuple-element.384.grad_ref, bf16[2,768,768]{2,1,0:T(8,128)(2,1)} %pad_maximum_fusion.2.weight_ref, ...), custom_call_target="tpu_custom_call" | custom-call | flops 30000001024 | bytes 8388608 | tf_op jit(solution)/shard_map/spatial_backward/pallas_call | solution.py:596
  376.1 2.0 fusion.59
  387.4 3.8 collective-permute-done.44
  391.3 5.1 collective-permute-done.45
  397.5 14.4 %temporal_backward.2 = (bf16[2,768,768]{2,1,0:T(8,128)(2,1)}, f32[832,768]{1,0:T(8,128)}) custom-call(bf16[832,768]{1,0:T(8,128)(2,1)} %get-tuple-element.411.normed_ref, bf16[832,768]{1,0:T(8,128)(2,1)} %pad_maximum_fusion.8.grad_ref.drows_ref, bf16[2,768,768]{2,1,0:T(8,128)(2,1)} %collective-permute-done.14.weight_ref, ...), custom_call_target="tpu_custom_call" | custom-call | flops 14000000000 | bytes 8388608 | tf_op jit(solution)/shard_map/temporal_backward/pallas_call | solution.py:596
  412.0 2.0 collective-permute-done.48
  418.0 1.9 constant_dynamic-slice_fusion.11
  419.9 1.9 constant_dynamic-slice_fusion.12
  425.0 2.1 collective-permute-start.51
  429.3 14.5 %temporal_backward.3 = (bf16[2,768,768]{2,1,0:T(8,128)(2,1)}, f32[832,768]{1,0:T(8,128)}) custom-call(bf16[832,768]{1,0:T(8,128)(2,1)} %get-tuple-element.411.normed_ref, bf16[832,768]{1,0:T(8,128)(2,1)} %pad_maximum_fusion.8.grad_ref.drows_ref, bf16[2,768,768]{2,1,0:T(8,128)(2,1)} %bitcast.479, bf16[2,4,576,208]{3,2,1,0:T(8,128)(2,1)} %get-tuple-element.412.qkv_ref, ...), custom_call_target="tpu_custom_call" | custom-call | flops 14000000000 | bytes 8388608 | tf_op jit(solution)/shard_map/temporal_backward/pallas_call | solution.py:596
  453.9 8.3 %embed_backward.1 = bf16[768,896]{1,0:T(8,128)(2,1)} custom-call(bf16[832,768]{1,0:T(8,128)(2,1)} %pad_maximum_fusion.6.patches_ref, f32[832,768]{1,0:T(8,128)} %get-tuple-element.425.start_ref, f32[832,1]{1,0:T(8,128)} %copy.176.valid_ref, bf16[832,768]{1,0:T(8,128)(2,1)} %pad_maximum_fusion.8.grad_ref.drows_ref, f32[832,768]{1,0:T(8,128)} %get-tuple-element.427.da_ref, ...), custom_call_target="tpu_custom_call" | custom-call | flops 30000001024 | bytes 8388608 | tf_op jit(solution)/shard_map/embed_backward/pallas_call | solution.py:596
  473.7 2.1 collective-permute-start.59
  475.8 6.6 %collective-permute-done.59 = bf16[1,96,768]{2,1,0:T(8,128)(2,1)S(1)} collective-permute-done((bf16[1,96,768]{2,1,0:T(8,128)(2,1)S(1)}, bf16[1,96,768]{2,1,0:T(8,128)(2,1)S(1)}, u32[]{:S(2)}, u32[]{:S(2)}) %collective-permute-start.59) | collective-permute-done | bytes 147488 | tf_op jit(solution)/shard_map/ppermute | solution.py:823
  482.4 4.9 collective-permute-done.60
  489.3 2.5 multiply_reduce_fusion.1
  491.8 2.3 collective-permute-done.62
  496.0 2.4 multiply_reduce_fusion.3
  498.5 2.1 collective-permute-start.63
  502.0 2.6 multiply_reduce_fusion.2
  510.4 3.0 collective-permute-done.65
  513.5 2.1 multiply_reduce_fusion.4
  518.0 1.8 collective-permute-start.67
  519.9 1.7 collective-permute-done.67
  522.2 1.9 collective-permute-start.68
  524.1 1.7 collective-permute-done.68
  528.0 1.9 collective-permute-done.69
  532.1 3.0 collective-permute-done.70
  535.7 5.7 %optimizer.1 = (f32[1,1]{1,0:T(1,128)}, f32[24,768]{1,0:T(8,128)}, f32[24,768]{1,0:T(8,128)}, f32[24,768]{1,0:T(8,128)}, f32[8,24]{1,0:T(8,128)}, /*index=5*/f32...) custom-call(f32[1,1]{1,0:T(1,128)S(6)} %add.1124.total_ref, ...), custom_call_target="tpu_custom_call" | custom-call | tf_op jit(solution)/shard_map/optimizer/pallas_call | solution.py:788
  (420 shorter events, 140.0 us)
Async XLA Ops:
  5.9 13.2 %collective-permute-start = (bf16[1,128,768]{2,1,0:T(8,128)(2,1)S(1)}, bf16[1,128,768]{2,1,0:T(8,128)(2,1)S(1)}, u32[]{:S(2)}, u32[]{:S(2)}) collective-permute-start(bf16[1,128,768]{2,1,0:T(8,128)(2,1)S(1)} %fusion.33), channel_id=1, source_target_pairs={{0,16},{1,17},{2,18},{3,19},{4,20},{5,21},{6,22},{7,23},{8,24},{9,... | collective-permute-start | bytes 589832 | tf_op jit(solution)/shard_map/ppermute | solution.py:823
  19.2 17.4 %collective-permute-start.1 = (bf16[2,128,768]{2,1,0:T(8,128)(2,1)S(1)}, bf16[2,128,768]{2,1,0:T(8,128)(2,1)S(1)}, u32[]{:S(2)}, u32[]{:S(2)}) collective-permute-start(bf16[2,128,768]{2,1,0:T(8,128)(2,1)S(1)} %maximum_bitcast_fusion.3), channel_id=1, source_target_pairs={{0,8},{1,9},{2,10},{3,11},{4,12},{5,13},{6,14},{7,15},{8,0},{9,1},... | collective-permute-start | bytes 1179656 | tf_op jit(solution)/shard_map/ppermute | solution.py:823
  20.0 10.6 %collective-permute-start.3 = (bf16[208,768]{1,0:T(8,128)(2,1)}, bf16[208,768]{1,0:T(8,128)(2,1)S(1)}, u32[]{:S(2)}, u32[]{:S(2)}) collective-permute-start(bf16[208,768]{1,0:T(8,128)(2,1)} %get-tuple-element.262), channel_id=1, source_target_pairs={{0,2},{1,3},{2,0},{3,1},{4,6},{5,7},{6,4},{7,5},{8,10},{9,11},{10,... | collective-permute-start | bytes 958472 | tf_op jit(solution)/shard_map/ppermute | solution.py:823
  21.6 15.0 %collective-permute-start.4 = (bf16[208,768]{1,0:T(8,128)(2,1)S(1)}, bf16[208,768]{1,0:T(8,128)(2,1)S(1)}, u32[]{:S(2)}, u32[]{:S(2)}) collective-permute-start(bf16[208,768]{1,0:T(8,128)(2,1)S(1)} %get-tuple-element.263), channel_id=1, source_target_pairs={{0,3},{1,2},{2,1},{3,0},{4,7},{5,6},{6,5},{7,4},{8,11},{9,10},{10,... | collective-permute-start | bytes 958472 | tf_op jit(solution)/shard_map/ppermute | solution.py:823
  37.5 20.5 %collective-permute-start.5 = (bf16[4,128,384]{2,1,0:T(8,128)(2,1)S(1)}, bf16[4,128,384]{2,1,0:T(8,128)(2,1)S(1)}, u32[]{:S(2)}, u32[]{:S(2)}) collective-permute-start(bf16[4,128,384]{2,1,0:T(8,128)(2,1)S(1)} %get-tuple-element.270), channel_id=1, source_target_pairs={{0,4},{1,5},{2,6},{3,7},{4,0},{5,1},{6,2},{7,3},{8,12},{9,13},{10,... | collective-permute-start | bytes 1179656 | tf_op jit(solution)/shard_map/ppermute | solution.py:823
  39.0 18.9 %collective-permute-start.6 = (bf16[4,128,384]{2,1,0:T(8,128)(2,1)S(1)}, bf16[4,128,384]{2,1,0:T(8,128)(2,1)S(1)}, u32[]{:S(2)}, u32[]{:S(2)}) collective-permute-start(bf16[4,128,384]{2,1,0:T(8,128)(2,1)S(1)} %get-tuple-element.271), channel_id=1, source_target_pairs={{0,2},{1,3},{2,0},{3,1},{4,6},{5,7},{6,4},{7,5},{8,10},{9,11},{10,... | collective-permute-start | bytes 1179656 | tf_op jit(solution)/shard_map/ppermute | solution.py:823
  41.3 16.7 %collective-permute-start.7 = (bf16[1,192,768]{2,1,0:T(8,128)(2,1)S(1)}, bf16[1,192,768]{2,1,0:T(8,128)(2,1)S(1)}, u32[]{:S(2)}, u32[]{:S(2)}) collective-permute-start(bf16[1,192,768]{2,1,0:T(8,128)(2,1)S(1)} %copy-done.49), channel_id=1, source_target_pairs={{0,16},{1,17},{2,18},{3,19},{4,20},{5,21},{6,22},{7,23},{8,24},{9,... | collective-permute-start | bytes 884744 | tf_op jit(solution)/shard_map/ppermute | solution.py:823
  58.6 19.5 %collective-permute-start.8 = (bf16[8,128,384]{2,1,0:T(8,128)(2,1)S(1)}, bf16[8,128,384]{2,1,0:T(8,128)(2,1)S(1)}, u32[]{:S(2)}, u32[]{:S(2)}) collective-permute-start(bf16[8,128,384]{2,1,0:T(8,128)(2,1)S(1)} %bitcast.506), channel_id=1, source_target_pairs={{0,2},{1,3},{2,0},{3,1},{4,6},{5,7},{6,4},{7,5},{8,10},{9,11},{10,... | collective-permute-start | bytes 2359304 | tf_op jit(solution)/shard_map/ppermute | solution.py:823
  59.2 19.2 %collective-permute-start.9 = (bf16[2,4,128,384]{3,2,1,0:T(8,128)(2,1)S(1)}, bf16[2,4,128,384]{3,2,1,0:T(8,128)(2,1)}, u32[]{:S(2)}, u32[]{:S(2)}) collective-permute-start(bf16[2,4,128,384]{3,2,1,0:T(8,128)(2,1)S(1)} %pad_maximum_fusion.17), channel_id=1, source_target_pairs={{0,4},{1,5},{2,6},{3,7},{4,0},{5,1},{6,2},{7,3},{8,12},{9,13},{10,... | collective-permute-start | bytes 2359304 | tf_op jit(solution)/shard_map/ppermute | solution.py:823
  59.8 14.8 %collective-permute-start.10 = (bf16[2,192,768]{2,1,0:T(8,128)(2,1)S(1)}, bf16[2,192,768]{2,1,0:T(8,128)(2,1)}, u32[]{:S(2)}, u32[]{:S(2)}) collective-permute-start(bf16[2,192,768]{2,1,0:T(8,128)(2,1)S(1)} %maximum_bitcast_fusion.2), channel_id=1, source_target_pairs={{0,8},{1,9},{2,10},{3,11},{4,12},{5,13},{6,14},{7,15},{8,0},{9,1},... | collective-permute-start | bytes 1769480 | tf_op jit(solution)/shard_map/ppermute | solution.py:823
  85.7 10.0 %collective-permute-start.11 = (bf16[2,8,32,768]{3,2,1,0:T(8,128)(2,1)S(1)}, bf16[2,8,32,768]{3,2,1,0:T(8,128)(2,1)}, u32[]{:S(2)}, u32[]{:S(2)}) collective-permute-start(bf16[2,8,32,768]{3,2,1,0:T(8,128)(2,1)S(1)} %fusion.7), channel_id=1, source_target_pairs={{0,1},{1,0},{2,3},{3,2},{4,5},{5,4},{6,7},{7,6},{8,9},{9,8},{10,11... | collective-permute-start | bytes 2359304 | tf_op jit(solution)/shard_map/ppermute | solution.py:823
  91.1 13.3 %collective-permute-start.12 = (bf16[4,96,384]{2,1,0:T(8,128)(2,1)}, bf16[4,96,384]{2,1,0:T(8,128)(2,1)}, u32[]{:S(2)}, u32[]{:S(2)}) collective-permute-start(bf16[4,96,384]{2,1,0:T(8,128)(2,1)} %get-tuple-element.303), channel_id=1, source_target_pairs={{0,4},{1,5},{2,6},{3,7},{4,0},{5,1},{6,2},{7,3},{8,12},{9,13},{10,... | collective-permute-start | bytes 884744 | tf_op jit(solution)/shard_map/ppermute | solution.py:823
  91.7 12.7 %collective-permute-start.13 = (bf16[4,96,384]{2,1,0:T(8,128)(2,1)}, bf16[4,96,384]{2,1,0:T(8,128)(2,1)}, u32[]{:S(2)}, u32[]{:S(2)}) collective-permute-start(bf16[4,96,384]{2,1,0:T(8,128)(2,1)} %get-tuple-element.304), channel_id=1, source_target_pairs={{0,2},{1,3},{2,0},{3,1},{4,6},{5,7},{6,4},{7,5},{8,10},{9,11},{10,... | collective-permute-start | bytes 884744 | tf_op jit(solution)/shard_map/ppermute | solution.py:823
  93.1 38.0 %collective-permute-start.14 = (bf16[2,768,768]{2,1,0:T(8,128)(2,1)S(1)}, bf16[2,768,768]{2,1,0:T(8,128)(2,1)}, u32[]{:S(2)}, u32[]{:S(2)}) collective-permute-start(bf16[2,768,768]{2,1,0:T(8,128)(2,1)S(1)} %bitcast.480), channel_id=1, source_target_pairs={{0,1},{1,0},{2,3},{3,2},{4,5},{5,4},{6,7},{7,6},{8,9},{9,8},{10,11... | collective-permute-start | bytes 7077896 | tf_op jit(solution)/shard_map/ppermute | solution.py:823
  93.1 38.0 %collective-permute-start.15 = (bf16[4,96,768]{2,1,0:T(8,128)(2,1)}, bf16[4,96,768]{2,1,0:T(8,128)(2,1)}, u32[]{:S(2)}, u32[]{:S(2)}) collective-permute-start(bf16[4,96,768]{2,1,0:T(8,128)(2,1)} %slice.378), channel_id=1, source_target_pairs={{0,2},{1,3},{2,0},{3,1},{4,6},{5,7},{6,4},{7,5},{8,10},{9,11},{10,... | collective-permute-start | bytes 1769480 | tf_op jit(solution)/shard_map/ppermute | solution.py:823
  104.4 11.2 %collective-permute-start.16 = (bf16[1,128,768]{2,1,0:T(8,128)(2,1)S(1)}, bf16[1,128,768]{2,1,0:T(8,128)(2,1)S(1)}, u32[]{:S(2)}, u32[]{:S(2)}) collective-permute-start(bf16[1,128,768]{2,1,0:T(8,128)(2,1)S(1)} %maximum_bitcast_fusion.6), channel_id=1, source_target_pairs={{0,16},{1,17},{2,18},{3,19},{4,20},{5,21},{6,22},{7,23},{8,24},{9,... | collective-permute-start | bytes 589832 | tf_op jit(solution)/shard_map/ppermute | solution.py:823
  105.7 15.5 %collective-permute-start.21 = (bf16[2,4,96,384]{3,2,1,0:T(8,128)(2,1)S(1)}, bf16[2,4,96,384]{3,2,1,0:T(8,128)(2,1)S(1)}, u32[]{:S(2)}, u32[]{:S(2)}) collective-permute-start(bf16[2,4,96,384]{3,2,1,0:T(8,128)(2,1)S(1)} %pad_maximum_fusion.22), channel_id=1, source_target_pairs={{0,4},{1,5},{2,6},{3,7},{4,0},{5,1},{6,2},{7,3},{8,12},{9,13},{10,... | collective-permute-start | bytes 1769480 | tf_op jit(solution)/shard_map/ppermute | solution.py:823
  114.0 15.2 %collective-permute-start.20 = (bf16[8,96,384]{2,1,0:T(8,128)(2,1)S(1)}, bf16[8,96,384]{2,1,0:T(8,128)(2,1)S(1)}, u32[]{:S(2)}, u32[]{:S(2)}) collective-permute-start(bf16[8,96,384]{2,1,0:T(8,128)(2,1)S(1)} %bitcast.516), channel_id=1, source_target_pairs={{0,2},{1,3},{2,0},{3,1},{4,6},{5,7},{6,4},{7,5},{8,10},{9,11},{10,... | collective-permute-start | bytes 1769480 | tf_op jit(solution)/shard_map/ppermute | solution.py:823
  141.2 11.5 %collective-permute-start.17 = (bf16[208,768]{1,0:T(8,128)(2,1)S(1)}, bf16[208,768]{1,0:T(8,128)(2,1)S(1)}, u32[]{:S(2)}, u32[]{:S(2)}) collective-permute-start(bf16[208,768]{1,0:T(8,128)(2,1)S(1)} %get-tuple-element.318), channel_id=1, source_target_pairs={{0,1},{1,0},{2,3},{3,2},{4,5},{5,4},{6,7},{7,6},{8,9},{9,8},{10,11... | collective-permute-start | bytes 958472 | tf_op jit(solution)/shard_map/ppermute | solution.py:823
  141.3 11.4 %collective-permute-start.18 = (bf16[208,768]{1,0:T(8,128)(2,1)S(1)}, bf16[208,768]{1,0:T(8,128)(2,1)S(1)}, u32[]{:S(2)}, u32[]{:S(2)}) collective-permute-start(bf16[208,768]{1,0:T(8,128)(2,1)S(1)} %get-tuple-element.319), channel_id=1, source_target_pairs={{0,2},{1,3},{2,0},{3,1},{4,6},{5,7},{6,4},{7,5},{8,10},{9,11},{10,... | collective-permute-start | bytes 958472 | tf_op jit(solution)/shard_map/ppermute | solution.py:823
  142.9 14.8 %collective-permute-start.19 = (bf16[208,768]{1,0:T(8,128)(2,1)S(1)}, bf16[208,768]{1,0:T(8,128)(2,1)S(1)}, u32[]{:S(2)}, u32[]{:S(2)}) collective-permute-start(bf16[208,768]{1,0:T(8,128)(2,1)S(1)} %get-tuple-element.320), channel_id=1, source_target_pairs={{0,3},{1,2},{2,1},{3,0},{4,7},{5,6},{6,5},{7,4},{8,11},{9,10},{10,... | collective-permute-start | bytes 958472 | tf_op jit(solution)/shard_map/ppermute | solution.py:823
  143.2 15.7 %collective-permute-start.22 = (bf16[2,128,768]{2,1,0:T(8,128)(2,1)S(1)}, bf16[2,128,768]{2,1,0:T(8,128)(2,1)S(1)}, u32[]{:S(2)}, u32[]{:S(2)}) collective-permute-start(bf16[2,128,768]{2,1,0:T(8,128)(2,1)S(1)} %maximum_bitcast_fusion.4), channel_id=1, source_target_pairs={{0,8},{1,9},{2,10},{3,11},{4,12},{5,13},{6,14},{7,15},{8,0},{9,1},... | collective-permute-start | bytes 1179656 | tf_op jit(solution)/shard_map/ppermute | solution.py:823
  152.2 37.0 %collective-permute-start.24 = (bf16[2,4,96,768]{3,2,1,0:T(8,128)(2,1)}, bf16[2,4,96,768]{3,2,1,0:T(8,128)(2,1)}, u32[]{:S(2)}, u32[]{:S(2)}) collective-permute-start(bf16[2,4,96,768]{3,2,1,0:T(8,128)(2,1)} %pad_maximum_fusion.12), channel_id=1, source_target_pairs={{0,4},{1,5},{2,6},{3,7},{4,0},{5,1},{6,2},{7,3},{8,12},{9,13},{10,... | collective-permute-start | bytes 3538952 | tf_op jit(solution)/shard_map/ppermute | solution.py:823
  160.6 31.9 %collective-permute-start.23 = (bf16[2,768,768]{2,1,0:T(8,128)(2,1)S(1)}, bf16[2,768,768]{2,1,0:T(8,128)(2,1)}, u32[]{:S(2)}, u32[]{:S(2)}) collective-permute-start(bf16[2,768,768]{2,1,0:T(8,128)(2,1)S(1)} %copy-done.8), channel_id=1, source_target_pairs={{0,1},{1,0},{2,3},{3,2},{4,5},{5,4},{6,7},{7,6},{8,9},{9,8},{10,11... | collective-permute-start | bytes 7077896 | tf_op jit(solution)/shard_map/ppermute | solution.py:823
  161.3 23.1 %collective-permute-start.26 = (bf16[4,128,384]{2,1,0:T(8,128)(2,1)S(1)}, bf16[4,128,384]{2,1,0:T(8,128)(2,1)S(1)}, u32[]{:S(2)}, u32[]{:S(2)}) collective-permute-start(bf16[4,128,384]{2,1,0:T(8,128)(2,1)S(1)} %get-tuple-element.566), channel_id=1, source_target_pairs={{0,2},{1,3},{2,0},{3,1},{4,6},{5,7},{6,4},{7,5},{8,10},{9,11},{10,... | collective-permute-start | bytes 1179656 | tf_op jit(solution)/shard_map/ppermute | solution.py:823
  162.9 25.8 %collective-permute-start.25 = (bf16[4,128,384]{2,1,0:T(8,128)(2,1)S(1)}, bf16[4,128,384]{2,1,0:T(8,128)(2,1)S(1)}, u32[]{:S(2)}, u32[]{:S(2)}) collective-permute-start(bf16[4,128,384]{2,1,0:T(8,128)(2,1)S(1)} %get-tuple-element.567), channel_id=1, source_target_pairs={{0,4},{1,5},{2,6},{3,7},{4,0},{5,1},{6,2},{7,3},{8,12},{9,13},{10,... | collective-permute-start | bytes 1179656 | tf_op jit(solution)/shard_map/ppermute | solution.py:823
  192.5 20.8 %collective-permute-start.28 = (bf16[2,4,128,384]{3,2,1,0:T(8,128)(2,1)S(1)}, bf16[2,4,128,384]{3,2,1,0:T(8,128)(2,1)S(1)}, u32[]{:S(2)}, u32[]{:S(2)}) collective-permute-start(bf16[2,4,128,384]{3,2,1,0:T(8,128)(2,1)S(1)} %pad_maximum_fusion.20), channel_id=1, source_target_pairs={{0,4},{1,5},{2,6},{3,7},{4,0},{5,1},{6,2},{7,3},{8,12},{9,13},{10,... | collective-permute-start | bytes 2359304 | tf_op jit(solution)/shard_map/ppermute | solution.py:823
  193.0 20.8 %collective-permute-start.27 = (bf16[8,128,384]{2,1,0:T(8,128)(2,1)S(1)}, bf16[8,128,384]{2,1,0:T(8,128)(2,1)S(1)}, u32[]{:S(2)}, u32[]{:S(2)}) collective-permute-start(bf16[8,128,384]{2,1,0:T(8,128)(2,1)S(1)} %bitcast.508), channel_id=1, source_target_pairs={{0,2},{1,3},{2,0},{3,1},{4,6},{5,7},{6,4},{7,5},{8,10},{9,11},{10,... | collective-permute-start | bytes 2359304 | tf_op jit(solution)/shard_map/ppermute | solution.py:823
  194.5 19.8 %collective-permute-start.29 = (bf16[2,8,96,768]{3,2,1,0:T(8,128)(2,1)}, bf16[2,8,96,768]{3,2,1,0:T(8,128)(2,1)}, u32[]{:S(2)}, u32[]{:S(2)}) collective-permute-start(bf16[2,8,96,768]{3,2,1,0:T(8,128)(2,1)} %bitcast.94.up_ref), channel_id=1, source_target_pairs={{0,1},{1,0},{2,3},{3,2},{4,5},{5,4},{6,7},{7,6},{8,9},{9,8},{10,11... | collective-permute-start | bytes 7077896 | tf_op jit(solution)/shard_map/ppermute | solution.py:823
  214.3 12.8 %collective-permute-start.30 = (bf16[2,8,128,768]{3,2,1,0:T(8,128)(2,1)S(1)}, bf16[2,8,128,768]{3,2,1,0:T(8,128)(2,1)}, u32[]{:S(2)}, u32[]{:S(2)}) collective-permute-start(bf16[2,8,128,768]{3,2,1,0:T(8,128)(2,1)S(1)} %pad_maximum_fusion.down_ref), channel_id=1, source_target_pairs={{0,1},{1,0},{2,3},{3,2},{4,5},{5,4},{6,7},{7,6},{8,9},{9,8},{10,11... | collective-permute-start | bytes 9437192 | tf_op jit(solution)/shard_map/ppermute | solution.py:823
  243.0 3.6 collective-permute-start.32
  246.6 4.6 collective-permute-start.33
  251.2 3.7 collective-permute-start.34
  255.0 3.8 collective-permute-start.35
  280.6 21.0 %collective-permute-start.36 = (bf16[2,768,768]{2,1,0:T(8,128)(2,1)}, bf16[2,768,768]{2,1,0:T(8,128)(2,1)S(1)}, u32[]{:S(2)}, u32[]{:S(2)}) collective-permute-start(bf16[2,768,768]{2,1,0:T(8,128)(2,1)} %get-tuple-element.367), channel_id=1, source_target_pairs={{0,1},{1,0},{2,3},{3,2},{4,5},{5,4},{6,7},{7,6},{8,9},{9,8},{10,11... | collective-permute-start | bytes 7077896 | tf_op jit(solution)/shard_map/ppermute | solution.py:823
  280.7 20.9 %collective-permute-start.37 = (bf16[2,768,768]{2,1,0:T(8,128)(2,1)}, bf16[2,768,768]{2,1,0:T(8,128)(2,1)}, u32[]{:S(2)}, u32[]{:S(2)}) collective-permute-start(bf16[2,768,768]{2,1,0:T(8,128)(2,1)} %get-tuple-element.368), channel_id=1, source_target_pairs={{0,1},{1,0},{2,3},{3,2},{4,5},{5,4},{6,7},{7,6},{8,9},{9,8},{10,11... | collective-permute-start | bytes 7077896 | tf_op jit(solution)/shard_map/ppermute | solution.py:823
  304.4 35.1 %collective-permute-start.38 = (bf16[8,96,768]{2,1,0:T(8,128)(2,1)}, bf16[8,96,768]{2,1,0:T(8,128)(2,1)S(1)}, u32[]{:S(2)}, u32[]{:S(2)}) collective-permute-start(bf16[8,96,768]{2,1,0:T(8,128)(2,1)} %fusion.2), channel_id=1, source_target_pairs={{0,2},{1,3},{2,0},{3,1},{4,6},{5,7},{6,4},{7,5},{8,10},{9,11},{10,... | collective-permute-start | bytes 3538952 | tf_op jit(solution)/shard_map/ppermute | solution.py:823
  307.5 32.1 %collective-permute-start.39 = (bf16[2,4,96,768]{3,2,1,0:T(8,128)(2,1)}, bf16[2,4,96,768]{3,2,1,0:T(8,128)(2,1)}, u32[]{:S(2)}, u32[]{:S(2)}) collective-permute-start(bf16[2,4,96,768]{3,2,1,0:T(8,128)(2,1)} %fusion.3), channel_id=1, source_target_pairs={{0,4},{1,5},{2,6},{3,7},{4,0},{5,1},{6,2},{7,3},{8,12},{9,13},{10,... | collective-permute-start | bytes 3538952 | tf_op jit(solution)/shard_map/ppermute | solution.py:823
  339.8 36.3 %collective-permute-start.40 = (bf16[4,96,768]{2,1,0:T(8,128)(2,1)S(1)}, bf16[4,96,768]{2,1,0:T(8,128)(2,1)S(1)}, u32[]{:S(2)}, u32[]{:S(2)}) collective-permute-start(bf16[4,96,768]{2,1,0:T(8,128)(2,1)S(1)} %fusion.8), channel_id=1, source_target_pairs={{0,4},{1,5},{2,6},{3,7},{4,0},{5,1},{6,2},{7,3},{8,12},{9,13},{10,... | collective-permute-start | bytes 1769480 | tf_op jit(solution)/shard_map/ppermute | solution.py:823
  342.7 33.4 %collective-permute-start.41 = (bf16[4,96,768]{2,1,0:T(8,128)(2,1)}, bf16[4,96,768]{2,1,0:T(8,128)(2,1)S(1)}, u32[]{:S(2)}, u32[]{:S(2)}) collective-permute-start(bf16[4,96,768]{2,1,0:T(8,128)(2,1)} %fusion.6), channel_id=1, source_target_pairs={{0,2},{1,3},{2,0},{3,1},{4,6},{5,7},{6,4},{7,5},{8,10},{9,11},{10,... | collective-permute-start | bytes 1769480 | tf_op jit(solution)/shard_map/ppermute | solution.py:823
  344.2 31.9 %collective-permute-start.42 = (bf16[2,768,768]{2,1,0:T(8,128)(2,1)}, bf16[2,768,768]{2,1,0:T(8,128)(2,1)}, u32[]{:S(2)}, u32[]{:S(2)}) collective-permute-start(bf16[2,768,768]{2,1,0:T(8,128)(2,1)} %get-tuple-element.393), channel_id=1, source_target_pairs={{0,1},{1,0},{2,3},{3,2},{4,5},{5,4},{6,7},{7,6},{8,9},{9,8},{10,11... | collective-permute-start | bytes 7077896 | tf_op jit(solution)/shard_map/ppermute | solution.py:823
  380.3 5.6 %collective-permute-start.43 = (bf16[208,768]{1,0:T(8,128)(2,1)S(1)}, bf16[208,768]{1,0:T(8,128)(2,1)S(1)}, u32[]{:S(2)}, u32[]{:S(2)}) collective-permute-start(bf16[208,768]{1,0:T(8,128)(2,1)S(1)} %get-tuple-element.398), channel_id=1, source_target_pairs={{0,1},{1,0},{2,3},{3,2},{4,5},{5,4},{6,7},{7,6},{8,9},{9,8},{10,11... | collective-permute-start | bytes 958472 | tf_op jit(solution)/shard_map/ppermute | solution.py:823
  380.9 10.4 %collective-permute-start.44 = (bf16[208,768]{1,0:T(8,128)(2,1)S(1)}, bf16[208,768]{1,0:T(8,128)(2,1)S(1)}, u32[]{:S(2)}, u32[]{:S(2)}) collective-permute-start(bf16[208,768]{1,0:T(8,128)(2,1)S(1)} %get-tuple-element.399), channel_id=1, source_target_pairs={{0,2},{1,3},{2,0},{3,1},{4,6},{5,7},{6,4},{7,5},{8,10},{9,11},{10,... | collective-permute-start | bytes 958472 | tf_op jit(solution)/shard_map/ppermute | solution.py:823
  381.4 15.0 %collective-permute-start.45 = (bf16[208,768]{1,0:T(8,128)(2,1)S(1)}, bf16[208,768]{1,0:T(8,128)(2,1)S(1)}, u32[]{:S(2)}, u32[]{:S(2)}) collective-permute-start(bf16[208,768]{1,0:T(8,128)(2,1)S(1)} %get-tuple-element.400), channel_id=1, source_target_pairs={{0,3},{1,2},{2,1},{3,0},{4,7},{5,6},{6,5},{7,4},{8,11},{9,10},{10,... | collective-permute-start | bytes 958472 | tf_op jit(solution)/shard_map/ppermute | solution.py:823
  383.6 28.3 %collective-permute-start.46 = (bf16[2,96,768]{2,1,0:T(8,128)(2,1)S(1)}, bf16[2,96,768]{2,1,0:T(8,128)(2,1)S(1)}, u32[]{:S(2)}, u32[]{:S(2)}) collective-permute-start(bf16[2,96,768]{2,1,0:T(8,128)(2,1)S(1)} %fusion.15), channel_id=1, source_target_pairs={{0,8},{1,9},{2,10},{3,11},{4,12},{5,13},{6,14},{7,15},{8,0},{9,1},... | collective-permute-start | bytes 884744 | tf_op jit(solution)/shard_map/ppermute | solution.py:823
  384.7 27.3 %collective-permute-start.47 = (bf16[2,96,768]{2,1,0:T(8,128)(2,1)S(1)}, bf16[2,96,768]{2,1,0:T(8,128)(2,1)S(1)}, u32[]{:S(2)}, u32[]{:S(2)}) collective-permute-start(bf16[2,96,768]{2,1,0:T(8,128)(2,1)S(1)} %fusion.16), channel_id=1, source_target_pairs={{0,8},{1,9},{2,10},{3,11},{4,12},{5,13},{6,14},{7,15},{8,0},{9,1},... | collective-permute-start | bytes 884744 | tf_op jit(solution)/shard_map/ppermute | solution.py:823
  386.0 28.0 %collective-permute-start.48 = (bf16[2,4,96,768]{3,2,1,0:T(8,128)(2,1)S(1)}, bf16[2,4,96,768]{3,2,1,0:T(8,128)(2,1)S(1)}, u32[]{:S(2)}, u32[]{:S(2)}) collective-permute-start(bf16[2,4,96,768]{3,2,1,0:T(8,128)(2,1)S(1)} %fusion.4), channel_id=1, source_target_pairs={{0,4},{1,5},{2,6},{3,7},{4,0},{5,1},{6,2},{7,3},{8,12},{9,13},{10,... | collective-permute-start | bytes 3538952 | tf_op jit(solution)/shard_map/ppermute | solution.py:823
  415.0 28.9 %collective-permute-start.49 = (bf16[2,768,768]{2,1,0:T(8,128)(2,1)}, bf16[2,768,768]{2,1,0:T(8,128)(2,1)S(1)}, u32[]{:S(2)}, u32[]{:S(2)}) collective-permute-start(bf16[2,768,768]{2,1,0:T(8,128)(2,1)} %get-tuple-element.415), channel_id=1, source_target_pairs={{0,1},{1,0},{2,3},{3,2},{4,5},{5,4},{6,7},{7,6},{8,9},{9,8},{10,11... | collective-permute-start | bytes 7077896 | tf_op jit(solution)/shard_map/ppermute | solution.py:823
  423.4 20.5 %collective-permute-start.50 = (bf16[4,96,768]{2,1,0:T(8,128)(2,1)S(1)}, bf16[4,96,768]{2,1,0:T(8,128)(2,1)S(1)}, u32[]{:S(2)}, u32[]{:S(2)}) collective-permute-start(bf16[4,96,768]{2,1,0:T(8,128)(2,1)S(1)} %fusion.5), channel_id=1, source_target_pairs={{0,2},{1,3},{2,0},{3,1},{4,6},{5,7},{6,4},{7,5},{8,10},{9,11},{10,... | collective-permute-start | bytes 1769480 | tf_op jit(solution)/shard_map/ppermute | solution.py:823
  425.0 18.9 %collective-permute-start.51 = (bf16[1,96,768]{2,1,0:T(8,128)(2,1)S(1)}, bf16[1,96,768]{2,1,0:T(8,128)(2,1)S(1)}, u32[]{:S(2)}, u32[]{:S(2)}) collective-permute-start(bf16[1,96,768]{2,1,0:T(8,128)(2,1)S(1)} %fusion.29), channel_id=1, source_target_pairs={{0,16},{1,17},{2,18},{3,19},{4,20},{5,21},{6,22},{7,23},{8,24},{9,... | collective-permute-start | bytes 442376 | tf_op jit(solution)/shard_map/ppermute | solution.py:823
  428.4 15.5 %collective-permute-start.52 = (bf16[1,96,768]{2,1,0:T(8,128)(2,1)S(1)}, bf16[1,96,768]{2,1,0:T(8,128)(2,1)S(1)}, u32[]{:S(2)}, u32[]{:S(2)}) collective-permute-start(bf16[1,96,768]{2,1,0:T(8,128)(2,1)S(1)} %fusion.28), channel_id=1, source_target_pairs={{0,16},{1,17},{2,18},{3,19},{4,20},{5,21},{6,22},{7,23},{8,24},{9,... | collective-permute-start | bytes 442376 | tf_op jit(solution)/shard_map/ppermute | solution.py:823
  450.1 15.1 %collective-permute-start.53 = (bf16[8,96,384]{2,1,0:T(8,128)(2,1)}, bf16[8,96,384]{2,1,0:T(8,128)(2,1)S(1)}, u32[]{:S(2)}, u32[]{:S(2)}) collective-permute-start(bf16[8,96,384]{2,1,0:T(8,128)(2,1)} %fusion.9), channel_id=1, source_target_pairs={{0,2},{1,3},{2,0},{3,1},{4,6},{5,7},{6,4},{7,5},{8,10},{9,11},{10,... | collective-permute-start | bytes 1769480 | tf_op jit(solution)/shard_map/ppermute | solution.py:823
  451.6 14.8 %collective-permute-start.54 = (bf16[2,4,96,384]{3,2,1,0:T(8,128)(2,1)}, bf16[2,4,96,384]{3,2,1,0:T(8,128)(2,1)S(1)}, u32[]{:S(2)}, u32[]{:S(2)}) collective-permute-start(bf16[2,4,96,384]{3,2,1,0:T(8,128)(2,1)} %fusion.10), channel_id=1, source_target_pairs={{0,4},{1,5},{2,6},{3,7},{4,0},{5,1},{6,2},{7,3},{8,12},{9,13},{10,... | collective-permute-start | bytes 1769480 | tf_op jit(solution)/shard_map/ppermute | solution.py:823
  453.1 10.5 %collective-permute-start.55 = (bf16[2,96,768]{2,1,0:T(8,128)(2,1)}, bf16[2,96,768]{2,1,0:T(8,128)(2,1)}, u32[]{:S(2)}, u32[]{:S(2)}) collective-permute-start(bf16[2,96,768]{2,1,0:T(8,128)(2,1)} %fusion.17), channel_id=1, source_target_pairs={{0,8},{1,9},{2,10},{3,11},{4,12},{5,13},{6,14},{7,15},{8,0},{9,1},... | collective-permute-start | bytes 884744 | tf_op jit(solution)/shard_map/ppermute | solution.py:823
  470.1 12.3 %collective-permute-start.57 = (bf16[4,96,384]{2,1,0:T(8,128)(2,1)S(1)}, bf16[4,96,384]{2,1,0:T(8,128)(2,1)S(1)}, u32[]{:S(2)}, u32[]{:S(2)}) collective-permute-start(bf16[4,96,384]{2,1,0:T(8,128)(2,1)S(1)} %fusion.18), channel_id=1, source_target_pairs={{0,4},{1,5},{2,6},{3,7},{4,0},{5,1},{6,2},{7,3},{8,12},{9,13},{10,... | collective-permute-start | bytes 884744 | tf_op jit(solution)/shard_map/ppermute | solution.py:823
  471.6 10.8 %collective-permute-start.58 = (bf16[4,96,384]{2,1,0:T(8,128)(2,1)S(1)}, bf16[4,96,384]{2,1,0:T(8,128)(2,1)S(1)}, u32[]{:S(2)}, u32[]{:S(2)}) collective-permute-start(bf16[4,96,384]{2,1,0:T(8,128)(2,1)S(1)} %fusion.12), channel_id=1, source_target_pairs={{0,2},{1,3},{2,0},{3,1},{4,6},{5,7},{6,4},{7,5},{8,10},{9,11},{10,... | collective-permute-start | bytes 884744 | tf_op jit(solution)/shard_map/ppermute | solution.py:823
  472.1 15.2 %collective-permute-start.60 = (bf16[8,24,896]{2,1,0:T(8,128)(2,1)S(1)}, bf16[8,24,896]{2,1,0:T(8,128)(2,1)S(1)}, u32[]{:S(2)}, u32[]{:S(2)}) collective-permute-start(bf16[8,24,896]{2,1,0:T(8,128)(2,1)S(1)} %fusion.14), channel_id=1, source_target_pairs={{0,2},{1,3},{2,0},{3,1},{4,6},{5,7},{6,4},{7,5},{8,10},{9,11},{10,... | collective-permute-start | bytes 1032200 | tf_op jit(solution)/shard_map/ppermute | solution.py:823
  473.7 8.7 %collective-permute-start.59 = (bf16[1,96,768]{2,1,0:T(8,128)(2,1)S(1)}, bf16[1,96,768]{2,1,0:T(8,128)(2,1)S(1)}, u32[]{:S(2)}, u32[]{:S(2)}) collective-permute-start(bf16[1,96,768]{2,1,0:T(8,128)(2,1)S(1)} %fusion.27), channel_id=1, source_target_pairs={{0,16},{1,17},{2,18},{3,19},{4,20},{5,21},{6,22},{7,23},{8,24},{9,... | collective-permute-start | bytes 442376 | tf_op jit(solution)/shard_map/ppermute | solution.py:823
  487.8 7.4 %collective-permute-start.61 = (bf16[2,96,768]{2,1,0:T(8,128)(2,1)S(1)}, bf16[2,96,768]{2,1,0:T(8,128)(2,1)S(1)}, u32[]{:S(2)}, u32[]{:S(2)}) collective-permute-start(bf16[2,96,768]{2,1,0:T(8,128)(2,1)S(1)} %fusion.19), channel_id=1, source_target_pairs={{0,8},{1,9},{2,10},{3,11},{4,12},{5,13},{6,14},{7,15},{8,0},{9,1},... | collective-permute-start | bytes 884744 | tf_op jit(solution)/shard_map/ppermute | solution.py:823
  488.7 5.4 collective-permute-start.62
  498.5 8.7 %collective-permute-start.63 = (bf16[1,96,768]{2,1,0:T(8,128)(2,1)}, bf16[1,96,768]{2,1,0:T(8,128)(2,1)S(1)}, u32[]{:S(2)}, u32[]{:S(2)}) collective-permute-start(bf16[1,96,768]{2,1,0:T(8,128)(2,1)} %fusion.26), channel_id=1, source_target_pairs={{0,16},{1,17},{2,18},{3,19},{4,20},{5,21},{6,22},{7,23},{8,24},{9,... | collective-permute-start | bytes 442376 | tf_op jit(solution)/shard_map/ppermute | solution.py:823
  500.5 6.6 %collective-permute-start.64 = (bf16[2,24,896]{2,1,0:T(8,128)(2,1)S(1)}, bf16[2,24,896]{2,1,0:T(8,128)(2,1)S(1)}, u32[]{:S(2)}, u32[]{:S(2)}) collective-permute-start(bf16[2,24,896]{2,1,0:T(8,128)(2,1)S(1)} %fusion.38), channel_id=1, source_target_pairs={{0,8},{1,9},{2,10},{3,11},{4,12},{5,13},{6,14},{7,15},{8,0},{9,1},... | collective-permute-start | bytes 258056 | tf_op jit(solution)/shard_map/ppermute | solution.py:823
  508.0 5.4 %collective-permute-start.65 = (bf16[1,24,896]{2,1,0:T(8,128)(2,1)S(1)}, bf16[1,24,896]{2,1,0:T(8,128)(2,1)S(1)}, u32[]{:S(2)}, u32[]{:S(2)}) collective-permute-start(bf16[1,24,896]{2,1,0:T(8,128)(2,1)S(1)} %fusion.39), channel_id=1, source_target_pairs={{0,16},{1,17},{2,18},{3,19},{4,20},{5,21},{6,22},{7,23},{8,24},{9,... | collective-permute-start | bytes 129032 | tf_op jit(solution)/shard_map/ppermute | solution.py:823
  530.6 4.5 collective-permute-start.70
  (76 other events, 455.7 us)

commit v4 on v3

--- a/solution.py
+++ b/solution.py
@@ -53,6 +53,10 @@
     return center * lax.rsqrt(spread + 1e-06) * gain + bias
 
 
+def wide(*refs):
+    return jnp.concatenate([ref[0].reshape(-1, ref.shape[-1]) for ref in refs], axis=1)
+
+
 def three_parts(value):
     high = low(value)
     rest = value - high.astype(SINGLE)
@@ -84,9 +88,22 @@
     return slice(GROUP * which + HD * head, GROUP * which + HD * (head + 1))
 
 
-def temporal_fwd_kernel(normed_ref, weight_ref, qkv_ref, mixed_ref, out):
+def temporal_fwd_kernel(
+    normed_ref, own_left, own_right, other_left, other_right, qkv_ref, mixed_ref, out, left, right
+):
+    for chosen, parts in (
+        (pl.program_id(0) < 2, (own_left, own_right)),
+        (pl.program_id(0) >= 2, (other_left, other_right)),
+    ):
+
+        @pl.when(chosen)
+        def _(parts=parts):
+            left[...], right[...] = wide(parts[0]), wide(parts[1])
+
     for f in range(FRAMES):
-        qkv_ref[0, f] = low(dot(normed_ref[frame_rows(f), :], weight_ref[0, :, :QKV])).T
+        rows = normed_ref[frame_rows(f), :]
+        qkv_ref[0, f, : 2 * GROUP, :] = low(dot(rows, left[...])).T
+        qkv_ref[0, f, 2 * GROUP :, :] = low(dot(rows, right[:, :GROUP])).T
     for head in range(GROUP // HD):
         query, keys, values = (
             [qkv_ref[0, f, head_features(i, head), :].astype(SINGLE) for f in range(FRAMES)]
@@ -103,7 +120,8 @@
 def temporal_bwd_kernel(
     normed_ref,
     grad_ref,
-    weight_ref,
+    left_ref,
+    right_ref,
     qkv_ref,
     mixed_ref,
     dweight_ref,
@@ -114,7 +132,7 @@
 ):
     scale = HD ** (-0.5)
     for f in range(FRAMES):
-        dmix[f] = low(dot(grad_ref[frame_rows(f), :], weight_ref[0, :, QKV:])).T
+        dmix[f] = low(dot(grad_ref[frame_rows(f), :], wide(right_ref)[:, GROUP:])).T
     for head in range(GROUP // HD):
         query, keys, values = (
             [qkv_ref[0, f, head_features(i, head), :].astype(SINGLE) for f in range(FRAMES)]
@@ -139,15 +157,17 @@
             dcol[g, head_features(2, head), :] = low(d_values[g])
     for f in range(FRAMES):
         dqkv[frame_rows(f), :] = dcol[f].T
-    finish_backward(normed_ref, grad_ref, weight_ref, mixed_ref, dweight_ref, dnormed_ref, dqkv)
+    finish_backward(normed_ref, grad_ref, left_ref, right_ref, mixed_ref, dweight_ref, dnormed_ref, dqkv)
 
 
 def finish_backward(
-    normed_ref, grad_ref, weight_ref, mixed_ref, dweight_ref, dnormed_ref, dqkv
+    normed_ref, grad_ref, left_ref, right_ref, mixed_ref, dweight_ref, dnormed_ref, dqkv
 ):
     dweight_ref[0, :, :QKV] = low(dot(normed_ref[...], dqkv[...], TN))
     dweight_ref[0, :, QKV:] = low(dot(grad_ref[...], mixed_ref[0], TN))
-    d_normed = dot(dqkv[...], weight_ref[0, :, :QKV], NT)
+    d_normed = dot(dqkv[:, : 2 * GROUP], wide(left_ref), NT) + dot(
+        dqkv[:, 2 * GROUP :], wide(right_ref)[:, :GROUP], NT
+    )
 
     accumulate(dnormed_ref, d_normed)
 
@@ -161,9 +181,10 @@
 
 
 def spatial_fwd_kernel(
-    normed_ref, weight_ref, key_extra_ref, qkv_ref, mixed_ref, extra_ref, branch_ref
+    normed_ref, left_ref, right_ref, key_extra_ref, qkv_ref, mixed_ref, extra_ref, branch_ref
 ):
-    qkv_ref[0] = low(dot(normed_ref[...], weight_ref[0, :, :QKV]))
+    qkv_ref[0, :, : 2 * GROUP] = low(dot(normed_ref[...], wide(left_ref)))
+    qkv_ref[0, :, 2 * GROUP :] = low(dot(normed_ref[...], wide(right_ref)[:, :GROUP]))
     one = jnp.ones((ROWS, 1), SINGLE)
     for head in range(GROUP // HD):
         at = HD * head
@@ -182,14 +203,15 @@
         mixed_ref[0, :, at : at + HD] = low(mixed[:, :HD] / total)
         logsum = -(top + jnp.log(total))
         extra_ref[0, :, at : at + HD] = lane_pieces([one, *three_parts(logsum)], ROWS)
-    branch = dot(mixed_ref[0], weight_ref[0, :, QKV:], NT)
+    branch = dot(mixed_ref[0], wide(right_ref)[:, GROUP:], NT)
 
     accumulate(branch_ref, branch)
 
 
 def spatial_fwd_last_kernel(
     normed_ref,
-    weight_ref,
+    left_ref,
+    right_ref,
     key_extra_ref,
     resid_ref,
     branch_ref,
@@ -202,7 +224,7 @@
     branch,
 ):
     spatial_fwd_kernel(
-        normed_ref, weight_ref, key_extra_ref, qkv_ref, mixed_ref, extra_ref, branch
+        normed_ref, left_ref, right_ref, key_extra_ref, qkv_ref, mixed_ref, extra_ref, branch
     )
 
     @pl.when(pl.program_id(0) == 1)
@@ -217,7 +239,8 @@
 def spatial_bwd_kernel(
     normed_ref,
     grad_ref,
-    weight_ref,
+    left_ref,
+    right_ref,
     qkv_ref,
     mixed_ref,
     extra_ref,
@@ -227,7 +250,7 @@
     dqkv,
 ):
     scale = HD ** (-0.5)
-    d_mixed_all = low(dot(grad_ref[...], weight_ref[0, :, QKV:]))
+    d_mixed_all = low(dot(grad_ref[...], wide(right_ref)[:, GROUP:]))
     one = jnp.ones((ROWS, 1), SINGLE)
     for head in range(GROUP // HD):
         at = HD * head
@@ -257,13 +280,14 @@
             dqkv[rows, GROUP + at : GROUP + at + HD] = low(dot(d_score, query) * scale)
             d_query = d_query + dot(d_score, keys, TN)
         dqkv[:, at : at + HD] = low(d_query * scale)
-    finish_backward(normed_ref, grad_ref, weight_ref, mixed_ref, dweight_ref, dnormed_ref, dqkv)
+    finish_backward(normed_ref, grad_ref, left_ref, right_ref, mixed_ref, dweight_ref, dnormed_ref, dqkv)
 
 
 def spatial_bwd_last_kernel(
     normed_ref,
     grad_ref,
-    weight_ref,
+    left_ref,
+    right_ref,
     qkv_ref,
     mixed_ref,
     extra_ref,
@@ -281,7 +305,8 @@
     spatial_bwd_kernel(
         normed_ref,
         grad_ref,
-        weight_ref,
+        left_ref,
+    right_ref,
         qkv_ref,
         mixed_ref,
         extra_ref,
@@ -341,12 +366,10 @@
     ref[...] = jnp.where(first, value, ref[...] + value)
 
 
-def wide(ref):
-    return ref[0].reshape(-1, ref.shape[-1])
-
-
-def feed_fwd_kernel(normed_ref, up_ref, down_ref, act_ref, slope_ref, branch_ref):
-    hidden = dot(normed_ref[...], wide(up_ref))
+def feed_fwd_kernel(normed_ref, *refs):
+    up_refs, down_refs = refs[:2], refs[2:4]
+    act_ref, slope_ref, branch_ref = refs[4:]
+    hidden = dot(normed_ref[...], wide(*up_refs))
     root = 0.7978845608028654
     square = hidden * hidden
     bend = jnp.tanh(hidden * (root + root * 0.044715 * square))
@@ -355,24 +378,13 @@
     slope_ref[0] = low(
         half + hidden * (0.5 - 0.5 * bend * bend) * (root + 3.0 * root * 0.044715 * square)
     )
-    accumulate(branch_ref, dot(act_ref[0], wide(down_ref), NT))
-
-
-def feed_fwd_last_kernel(
-    normed_ref,
-    up_ref,
-    down_ref,
-    resid_ref,
-    branch_ref,
-    norms_ref,
-    valid_ref,
-    act_ref,
-    slope_ref,
-    out_ref,
-    sums_ref,
-    branch,
-):
-    feed_fwd_kernel(normed_ref, up_ref, down_ref, act_ref, slope_ref, branch)
+    accumulate(branch_ref, dot(act_ref[0], wide(*down_refs), NT))
+
+
+def feed_fwd_last_kernel(normed_ref, *refs):
+    resid_ref, branch_ref, norms_ref, valid_ref = refs[4:8]
+    act_ref, slope_ref, out_ref, sums_ref, branch = refs[8:]
+    feed_fwd_kernel(normed_ref, *refs[:4], act_ref, slope_ref, branch)
 
     @pl.when(pl.program_id(0) == 1)
     def _():
@@ -386,36 +398,20 @@
         sums_ref[...] = sums
 
 
-def feed_bwd_kernel(
-    normed_ref, grad_ref, up_ref, down_ref, act_ref, slope_ref, dup_ref, ddown_ref, dnormed_ref, dhid
-):
-    dhid[...] = low(dot(grad_ref[...], wide(down_ref)) * slope_ref[0].astype(SINGLE))
+def feed_bwd_kernel(normed_ref, grad_ref, *refs):
+    up_refs, down_refs = refs[:2], refs[2:4]
+    act_ref, slope_ref, dup_ref, ddown_ref, dnormed_ref, dhid = refs[4:]
+    dhid[...] = low(dot(grad_ref[...], wide(*down_refs)) * slope_ref[0].astype(SINGLE))
     ddown_ref[0] = low(dot(grad_ref[...], act_ref[0], TN))
     dup_ref[0] = low(dot(normed_ref[...], dhid[...], TN))
-    accumulate(dnormed_ref, dot(dhid[...], wide(up_ref), NT))
-
-
-def feed_bwd_last_kernel(
-    normed_ref,
-    grad_ref,
-    up_ref,
-    down_ref,
-    act_ref,
-    slope_ref,
-    resid_ref,
-    dresid_ref,
-    dother_ref,
-    norms_ref,
-    dup_ref,
-    ddown_ref,
-    out_ref,
-    drows_ref,
-    dnorms_ref,
-    dhid,
-    dnormed,
-):
+    accumulate(dnormed_ref, dot(dhid[...], wide(*up_refs), NT))
+
+
+def feed_bwd_last_kernel(normed_ref, grad_ref, *refs):
+    act_ref, slope_ref, resid_ref, dresid_ref, dother_ref, norms_ref = refs[4:10]
+    dup_ref, ddown_ref, out_ref, drows_ref, dnorms_ref, dhid, dnormed = refs[10:]
     feed_bwd_kernel(
-        normed_ref, grad_ref, up_ref, down_ref, act_ref, slope_ref, dup_ref, ddown_ref, dnormed, dhid
+        normed_ref, grad_ref, *refs[:4], act_ref, slope_ref, dup_ref, ddown_ref, dnormed, dhid
     )
 
     @pl.when(pl.program_id(0) == 1)
@@ -612,119 +608,118 @@
     return shaped(2, rows, width, dtype=LOWER)
 
 
-def temporal_forward(normed, weight):
+def weight_specs(parts, rows):
+    inputs, specs = [], []
+    for value, half in parts:
+        taken = rows
+        if rows % 16 != 0:
+            value = value[:, :, :rows].reshape(2, 1, -1, value.shape[-1])
+            taken = value.shape[2]
+        width = value.shape[3] if half is None else value.shape[3] // 2
+        inputs.append(value)
+        specs.append(
+            pl.BlockSpec((1, value.shape[1], taken, width), lambda g, h=half or 0: (g, 0, 0, h))
+        )
+    return inputs, specs
+
+
+def block_call(kernel, name, before, parts, rows, rest, outputs, scratch, gflops):
+    parts, specs = weight_specs(parts, rows)
+    specs = [spec_of(v) for v in before] + specs + [spec_of(v) for v in rest]
+    return call(
+        kernel, name, (*before, *parts, *rest), outputs, scratch, gflops, in_specs=specs
+    )
+
+
+def temporal_forward(normed, own, other, rows):
+    dim = normed.shape[1]
+    parts, specs = weight_specs([*own, *other], rows)
+    place = [lambda g: jnp.minimum(g, 1)] * 2 + [lambda g: jnp.maximum(g - 2, 0)] * 2
+    specs = [
+        pl.BlockSpec(spec.block_shape, lambda g, at=at: (at(g), 0, 0, 0))
+        for spec, at in zip(specs, place)
+    ]
+    width = parts[0].shape[3]
     return call(
         temporal_fwd_kernel,
         "temporal_forward",
-        (normed, weight),
-        (shaped(2, FRAMES, QKV, SLOTS, dtype=LOWER), by_group(GROUP)),
-        [((FRAMES, GROUP, SLOTS), LOWER)],
-        15,
-    )
-
-
-def temporal_backward(normed, grad, weight, qkv, mixed):
+        (normed, *parts),
+        (shaped(4, FRAMES, QKV, SLOTS, dtype=LOWER), shaped(4, ROWS, GROUP, dtype=LOWER)),
+        [((FRAMES, GROUP, SLOTS), LOWER), ((dim, width), LOWER), ((dim, width), LOWER)],
+        40,
+        4,
+        [spec_of(normed), *specs],
+    )
+
+
+def temporal_backward(normed, grad, parts, rows, qkv, mixed, skip):
     dim = normed.shape[1]
+    parts, specs = weight_specs(parts, rows)
+    specs = [spec_of(normed), spec_of(grad), *specs]
+    specs += [
+        pl.BlockSpec((1, FRAMES, QKV, SLOTS), lambda g: (g + skip, 0, 0, 0)),
+        pl.BlockSpec((1, ROWS, GROUP), lambda g: (g + skip, 0, 0)),
+    ]
     return call(
         temporal_bwd_kernel,
         "temporal_backward",
-        (normed, grad, weight, qkv, mixed),
+        (normed, grad, *parts, qkv, mixed),
         (by_group(dim, dim), shaped(ROWS, dim)),
         [((ROWS, QKV), LOWER), ((FRAMES, GROUP, SLOTS), LOWER), ((FRAMES, QKV, SLOTS), LOWER)],
         14,
-    )
-
-
-def spatial_forward(normed, weight, key_extra, last=None):
+        2,
+        specs,
+    )
+
+
+def spatial_forward(normed, parts, rows, key_extra, last=None):
     dim = normed.shape[1]
-    saved = (by_group(QKV), by_group(GROUP), by_group(GROUP))
-    inputs = (normed, weight, key_extra)
-    if last is None:
-        return call(
-            spatial_fwd_kernel, "spatial_forward", inputs, (*saved, shaped(ROWS, dim)), [], 15
-        )
-    return call(
-        spatial_fwd_last_kernel,
-        "spatial_forward",
-        (*inputs, *last),
-        (*saved, shaped(ROWS, dim), shaped(ROWS, dim, dtype=LOWER)),
-        [((ROWS, dim), SINGLE)],
-        15,
-    )
-
-
-def spatial_backward(normed, grad, weight, qkv, mixed, extra, key_extra, last=None):
+    outputs = (by_group(QKV), by_group(GROUP), by_group(GROUP), shaped(ROWS, dim))
+    kernel, scratch = spatial_fwd_kernel, []
+    if last is not None:
+        kernel, scratch = spatial_fwd_last_kernel, [((ROWS, dim), SINGLE)]
+        outputs += (shaped(ROWS, dim, dtype=LOWER),)
+    rest = (key_extra, *(last or ()))
+    return block_call(
+        kernel, "spatial_forward", (normed,), parts, rows, rest, outputs, scratch, 15
+    )
+
+
+def spatial_backward(normed, grad, parts, rows, qkv, mixed, extra, key_extra, last=None):
     dim = normed.shape[1]
-    inputs = (normed, grad, weight, qkv, mixed, extra, key_extra)
-    scratch = [((ROWS, QKV), LOWER)]
-    if last is None:
-        outputs = (by_group(dim, dim), shaped(ROWS, dim))
-        return call(spatial_bwd_kernel, "spatial_backward", inputs, outputs, scratch, 30)
-    return call(
-        spatial_bwd_last_kernel,
-        "spatial_backward",
-        (*inputs, *last),
-        (by_group(dim, dim), shaped(ROWS, dim, dtype=LOWER), shaped(2, dim)),
-        scratch + [((ROWS, dim), SINGLE)],
-        30,
-    )
-
-
-def feed_specs(pair, rows):
-    if rows % 16 != 0:
-        pair = [value[:, :, :rows].reshape(2, 1, -1, value.shape[-1]) for value in pair]
-        rows = pair[0].shape[2]
-    block = (1, pair[0].shape[1], rows, pair[0].shape[3])
-    return pair, [pl.BlockSpec(block, lambda g: (g, 0, 0, 0)) for _ in pair]
-
-
-def feed_forward(normed, pair, rows, last=None):
-    dim, width = normed.shape[1], pair[0].shape[3]
-    pair, specs = feed_specs(pair, rows)
-    inputs, saved = (normed, *pair), (by_group(width), by_group(width))
-    specs = [spec_of(normed), *specs] + [spec_of(value) for value in last or ()]
-    if last is None:
-        return call(
-            feed_fwd_kernel,
-            "feed_forward",
-            inputs,
-            (*saved, shaped(ROWS, dim)),
-            [],
-            10,
-            in_specs=specs,
-        )
-    return call(
-        feed_fwd_last_kernel,
-        "feed_forward",
-        (*inputs, *last),
-        (*saved, shaped(ROWS, dim), shaped(1, dim)),
-        [((ROWS, dim), SINGLE)],
-        10,
-        in_specs=specs,
-    )
-
-
-def feed_backward(normed, grad, pair, rows, act, slope, last=None):
-    dim, width = normed.shape[1], pair[0].shape[3]
-    pair, specs = feed_specs(pair, rows)
-    inputs = (normed, grad, *pair, act, slope)
-    specs = [spec_of(normed), spec_of(grad), *specs, spec_of(act), spec_of(slope)]
-    specs += [spec_of(value) for value in last or ()]
-    weights = (by_group(width, dim), by_group(width, dim))
-    scratch = [((ROWS, width), LOWER)]
-    if last is None:
-        outputs = (*weights, shaped(ROWS, dim))
-        return call(
-            feed_bwd_kernel, "feed_backward", inputs, outputs, scratch, 15, in_specs=specs
-        )
-    return call(
-        feed_bwd_last_kernel,
-        "feed_backward",
-        (*inputs, *last),
-        (*weights, shaped(ROWS, dim), shaped(ROWS, dim, dtype=LOWER), shaped(2, dim)),
-        scratch + [((ROWS, dim), SINGLE)],
-        15,
-        in_specs=specs,
+    kernel, scratch = spatial_bwd_kernel, [((ROWS, QKV), LOWER)]
+    outputs = (by_group(dim, dim), shaped(ROWS, dim))
+    if last is not None:
+        kernel, scratch = spatial_bwd_last_kernel, scratch + [((ROWS, dim), SINGLE)]
+        outputs = (by_group(dim, dim), shaped(ROWS, dim, dtype=LOWER), shaped(2, dim))
+    rest = (qkv, mixed, extra, key_extra, *(last or ()))
+    return block_call(
+        kernel, "spatial_backward", (normed, grad), parts, rows, rest, outputs, scratch, 30
+    )
+
+
+def feed_forward(normed, parts, rows, last=None):
+    dim, width = normed.shape[1], 2 * parts[0][0].shape[3]
+    outputs = (by_group(width), by_group(width), shaped(ROWS, dim))
+    kernel, scratch = feed_fwd_kernel, []
+    if last is not None:
+        kernel, scratch = feed_fwd_last_kernel, [((ROWS, dim), SINGLE)]
+        outputs += (shaped(1, dim),)
+    return block_call(
+        kernel, "feed_forward", (normed,), parts, rows, last or (), outputs, scratch, 10
+    )
+
+
+def feed_backward(normed, grad, parts, rows, act, slope, last=None):
+    dim, width = normed.shape[1], 2 * parts[0][0].shape[3]
+    kernel, scratch = feed_bwd_kernel, [((ROWS, width), LOWER)]
+    outputs = (by_group(width, dim), by_group(width, dim), shaped(ROWS, dim))
+    if last is not None:
+        kernel, scratch = feed_bwd_last_kernel, scratch + [((ROWS, dim), SINGLE)]
+        outputs += (shaped(ROWS, dim, dtype=LOWER), shaped(2, dim))
+    rest = (act, slope, *(last or ()))
+    return block_call(
+        kernel, "feed_backward", (normed, grad), parts, rows, rest, outputs, scratch, 15
     )
 
 
@@ -796,6 +791,38 @@
     )(*inputs)
 
 
+def finish_kernel(count, token_ref, *refs):
+    squares = jnp.zeros((1, 1), SINGLE)
+    ins, outs = list(refs[: -count - 2]), refs[-count - 2 :]
+    per = len(ins) // count
+    for i in range(count):
+        value = functools.reduce(
+            jnp.add, (ref[...].astype(SINGLE) for ref in ins[per * i : per * (i + 1)])
+        )
+        outs[i][...] = value
+        squares = squares + jnp.sum(
+            jnp.sum(value * value, axis=1, keepdims=True), axis=0, keepdims=True
+        )
+    outs[count][...] = squares
+    outs[count + 1][...] = token_ref[...]
+
+
+def finish(token, lists):
+    inputs = (token, *(term for terms in lists for term in terms))
+    outputs = [shaped(*terms[0].shape) for terms in lists]
+    outputs += [shaped(1, 1), shaped(*token.shape)]
+    return call(
+        functools.partial(finish_kernel, len(lists)),
+        "finish",
+        inputs,
+        outputs,
+        (),
+        30,
+        1,
+        [whole(value.shape) for value in inputs],
+    )
+
+
 def pace_kernel(token_ref, out_ref):
     out_ref[...] = token_ref[...]
 
@@ -833,14 +860,42 @@
     def fork(self, value):
         return self.stack(value, self.swap(value, 2), 2)
 
-    def step(self, token, sends, late=()):
+    def step(self, token, sends, late=(), work=None):
         values = [value for value, _ in (*sends, *late)]
         *values, token = tick(*values, token)
         masks = [mask for _, mask in (*sends, *late)]
         received = [self.swap(value, mask) for value, mask in zip(values, masks)]
         count = len(sends)
+        if work is not None:
+            *done, paced = finish(token, work)
+            *ended, token = tick(*received[:count], paced)
+            return token, done, *ended, *received[count:]
         *ended, token = tick(*received[:count], pace(token))
         return token, *ended, *received[count:]
+
+
+    def quads(self):
+        *_, high, near, _ = self.batch_masks
+        return [near, high, near | high]
+
+    def gathered(self, value, others):
+        near, high, _ = (self.has(mask) for mask in self.quads())
+        p = [value, *others]
+        p = [jnp.where(near, p[i ^ 1], p[i]) for i in range(4)]
+        p = [jnp.where(high, p[i ^ 2], p[i]) for i in range(4)]
+        shape = value.shape
+        return jnp.stack(p, axis=-3).reshape(*shape[:-3], 4 * shape[-3], *shape[-2:])
+
+    def quarter(self, terms):
+        near, high, _ = (self.has(mask).astype(jnp.int32) for mask in self.quads())
+        place = near + 2 * high
+        views = [term.reshape(-1, 4, *term.shape[-2:]) for term in terms]
+        part = lambda view, r: lax.dynamic_index_in_dim(view, place ^ r, 1, False)
+        sends = [low(summed([part(view, r) for view in views])) for r in range(1, 4)]
+        return sends, [part(view, 0) for view in views]
+
+    def fourfold(self, sends):
+        return list(zip(sends, self.quads()))
 
     def merge(self, value, other, mask):
         has = self.has(mask)
@@ -882,7 +937,7 @@
         return keep + [self.swap(send, 2)]
 
     def total(self, value):
-        for mask in [1, 2] + self.batch_masks[::-1]:
+        for mask in [1, 2, *self.batch_masks[::-1]]:
             value = value + self.swap(value, mask)
         return value
 
@@ -907,7 +962,6 @@
 
     *first, near, last = cube.batch_masks
     middle = dim // 2
-    flat = lambda value: value.reshape(2, dim, -1)
     blocked = lambda value: value.reshape(*value.shape[:-2], -1, rows_wide, value.shape[-1])
     pack = lambda w_in, w_out: jnp.concatenate(
         [low(w_in[0]), low(w_in[1]), low(w_in[2]), low(w_out).T], axis=1
@@ -942,6 +996,7 @@
     blocks = jnp.pad(clip, ((0, ROWS - PMAX), (0, 0))).reshape(FRAMES, SLOTS, -1)
     blocks = jnp.where((place & 1) != 0, blocks[jnp.array([1, 0, 3, 2])], blocks)
     blocks = jnp.where((place & 2) != 0, blocks[jnp.array([2, 3, 0, 1])], blocks)
+    blocks, token = tick(blocks, token)
     second_w = jnp.concatenate([pack(w_in, w_out)[0], low(w_up)])[None]
     small = jnp.concatenate([low(head_weight), low(proj_weight)], axis=1)
     small = jnp.pad(small, ((0, -rows_small % 16), (0, dim - small.shape[1])))
@@ -954,102 +1009,120 @@
     by_frame = blocks.reshape(ROWS, -1)
 
     left, right = first_w[..., :middle], first_w[..., middle:]
-    token, other_left, other_right, other = cube.step(
-        token, [(left, last), (right, 2), (second_w, first[0])]
+    second_w = cube.join(second_w, *first[:-1])
+    token, other_left, other_right, *others = cube.step(
+        token, [(left, last), (right, 2)], cube.fourfold([second_w] * 3)
     )
     left, right = cube.merge(left, other_left, last), cube.stack(right, other_right, 2)
-    second_w = cube.join(cube.merge(second_w, other, first[0]), *first[1:])
-
-    left, right, second_w, *slots = tick(left, right, second_w, *slots)
+
+    left, right, *slots = tick(left, right, *slots)
     by_slot = jnp.concatenate([blocks[0], *slots])
-    token, other_left, other_right, other = cube.step(
-        token, [(left, 2), (right, last), (second_w, near)]
-    )
-    by_slot, slot_valid, token = tick(by_slot, slot_valid, token)
-    left, right = cube.stack(left, other_left, 2), cube.merge(right, other_right, last)
-    joined = lambda at: jnp.concatenate([left[:, :, at], right[:, :, at]], axis=-1)
-    own_first, early = flat(joined(slice(0, rows_wide))), joined(slice(rows_wide, None))
-
-    early, own_first, other = tick(early, own_first, other)
-    second_w = cube.merge(second_w, other, near)
-    second_w, up_w = second_w[..., :rows_wide, :], second_w[..., rows_wide:, :]
-    token, other, other_first, other_left, other_right, other_up = cube.step(
+    token, other_left, other_right = cube.step(token, [(left, 2), (right, last)])
+    by_slot, slot_valid, token, *others = tick(by_slot, slot_valid, token, *others)
+    own_first = (cube.stack(left, other_left, 2), cube.merge(right, other_right, last))
+
+    second_w = cube.gathered(second_w, others)
+    token, *other_first, other_left, other_right, other = cube.step(
         token,
-        [(early, 1)],
-        [
-            (own_first, 1),
-            (second_w[..., :middle], last),
-            (second_w[..., middle:], 2),
-            (up_w, 2),
-        ],
-    )
-    early = cube.stack(early, other, 1).transpose(2, 1, 0, 3, 4)
+        [(own_first[0], 1), (own_first[1], 1)],
+        [(second_w[..., :middle], last), (second_w[..., middle:], 2)]
+        + [(down_w, mask) for mask in first[:1]],
+    )
+    other_down = other
+    joined = lambda parts, at: jnp.concatenate([part[:, :, at] for part in parts], axis=-1)
+    early = [joined(parts, slice(rows_wide, None)) for parts in (own_first, other_first)]
+    early = cube.stack(*early, 1).transpose(2, 1, 0, 3, 4)
     patch_copy = early[..., :rows_small, :].reshape(dim, dim)
     norms = early[..., rows_small, : norm_row.shape[1]].reshape(-1, 8, rows_small)
     norms = norms.transpose(1, 0, 2).reshape(8, dim).astype(SINGLE)
     start_slot, normed_t = embed(by_slot, patch_copy, slot_valid, norms)
-    start_slot, normed_t, other_left, other_right, down_w = tick(
-        start_slot, normed_t, other_left, other_right, down_w
-    )
-    left = cube.fork(cube.merge(second_w[..., :middle], other_left, last))
-    right = cube.join(cube.stack(second_w[..., middle:], other_right, 2), last)
-    down_w = cube.join(down_w, *first)
-    qkv_t, mixed_t = [None, None], [None, None]
-    qkv_t[0], mixed_t[0] = temporal_forward(normed_t, own_first)
-    mixed_t[0], normed_t, other_first, patch_copy, other_up, down_w = tick(
-        mixed_t[0], normed_t, other_first, patch_copy, other_up, down_w
-    )
-    own_up = cube.join(cube.stack(up_w, other_up, 2), last)
-    down_w = cube.join(down_w, near)
-    pair = (own_first, other_first)
-    out_first = jnp.concatenate([pair[c][y][:, QKV:] for c in range(2) for y in range(2)], axis=1)
-    start_frame = dot(by_frame, patch_copy) * frame_valid
-    qkv_t[1], mixed_t[1] = temporal_forward(normed_t, other_first)
+    normed_t, other_left, other_right = tick(normed_t, other_left, other_right)
+    left = cube.merge(second_w[..., :middle], other_left, last)
+    right = cube.stack(second_w[..., middle:], other_right, 2)
+    ours, theirs = slice(0, rows_wide), slice(rows_wide, None)
+    other_left, other_right = (
+        cube.swap(left[..., ours, :], 2), cube.swap(right[..., ours, :], last)
+    )
+    first_w = tuple([(part, None) for part in parts] for parts in (own_first, other_first))
+    qkv_t, mixed_t = temporal_forward(normed_t, *first_w, rows_wide)
+    mixed_t, other_left, other_right = tick(mixed_t, other_left, other_right)
     parts = [
         jnp.concatenate(
-            [mixed_t[c ^ (r & 1)][y][frame_rows(r)] for c in range(2) for y in range(2)], axis=1
+            [mixed_t[2 * (c ^ (r & 1)) + y][frame_rows(r)] for c in range(2) for y in range(2)],
+            axis=1,
         )
         for r in range(FRAMES)
     ]
-    own_second = jnp.concatenate([flat(left), flat(right)], axis=-1)
-
-    parts[0], out_first, start_frame, token = tick(parts[0], out_first, start_frame, token)
-    token, *received = cube.step(token, [(parts[r], r) for r in range(1, FRAMES)])
+    parts[0], other_down, patch_copy, token = tick(parts[0], other_down, patch_copy, token)
+    outs = [
+        part[y, :, :rows_wide, GROUP:].reshape(dim, GROUP)
+        for part in (own_first[1], other_first[1])
+        for y in range(2)
+    ]
+    out_first = jnp.concatenate(outs, axis=1)
+    start_frame = dot(by_frame, patch_copy) * frame_valid
+    own_second = jnp.concatenate(
+        [
+            cube.stack(left[..., ours, :], other_left, 2),
+            cube.merge(right[..., ours, :], other_right, last),
+        ],
+        axis=-1,
+    )
+    down_w = cube.join(cube.merge(down_w, other_down, first[0]), *first[1:])
+
+    token, *received, other = cube.step(
+        token, [(parts[r], r) for r in range(1, FRAMES)] + [(down_w, near)]
+    )
+    down_w = cube.merge(down_w, other, near)
     mixed_frame = jnp.concatenate([parts[0], *received])
-    mixed_frame, own_second, key_extra, down_w = tick(mixed_frame, own_second, key_extra, down_w)
+    mixed_frame, key_extra, own_second, down_w, out_first, start_frame = tick(
+        mixed_frame, key_extra, own_second, down_w, out_first, start_frame
+    )
 
     resid_one, normed_s = enter_frame(start_frame, mixed_frame, out_first, norms)
     other_second = cube.swap(own_second, 1)
-    left, right = cube.join(down_w[..., :middle], last), cube.fork(down_w[..., middle:])
+    other_left = cube.swap(left[..., theirs, :], 2)
+    other_right = cube.swap(right[..., theirs, :], last)
+    left_down, right_down = cube.join(down_w[..., :middle], last), cube.fork(down_w[..., middle:])
     qkv_s, mixed_s, extra_s = ([None, None] for _ in range(3))
-    qkv_s[0], mixed_s[0], extra_s[0], branch = spatial_forward(normed_s, own_second, key_extra)
-    branch, normed_s, other_second, own_up, left, right = tick(
-        branch, normed_s, other_second, own_up, left, right
-    )
-    other_up = cube.swap(own_up, 1)
-    left, right = cube.fork(left), cube.join(right, last)
+    halves = lambda value: [(value, 0), (value, 1)]
+    qkv_s[0], mixed_s[0], extra_s[0], branch = spatial_forward(
+        normed_s, halves(own_second), rows_wide, key_extra
+    )
+    branch, normed_s, other_second, other_left, other_right, left_down, right_down = tick(
+        branch, normed_s, other_second, other_left, other_right, left_down, right_down
+    )
+    own_up = (
+        cube.stack(left[..., theirs, :], other_left, 2),
+        cube.merge(right[..., theirs, :], other_right, last),
+    )
+    other_up = [cube.swap(part, 1) for part in own_up]
+    left, right = cube.fork(left_down), cube.join(right_down, last)
     qkv_s[1], mixed_s[1], extra_s[1], resid_two, normed_m = spatial_forward(
-        normed_s, other_second, key_extra, (resid_one, branch, norms)
-    )
-    own_down = jnp.concatenate([left, right], axis=-1)
-    normed_m, own_down, other_up = tick(normed_m, own_down, other_up)
-
-    other_down = cube.swap(own_down, 1)
-    own_pair, other_pair = (own_up, own_down), (other_up, other_down)
+        normed_s, halves(other_second), rows_wide, key_extra, (resid_one, branch, norms)
+    )
+    normed_m, left, right, *other_up = tick(normed_m, left, right, *other_up)
+
+    own_down, other_down = (left, right), (cube.swap(left, 1), cube.swap(right, 1))
+    own_feed = [(part, None) for part in (*own_up, *own_down)]
+    other_feed = [(part, None) for part in (*other_up, *other_down)]
     act, slope = ([None, None] for _ in range(2))
-    act[0], slope[0], branch = feed_forward(normed_m, own_pair, rows_wide)
+    act[0], slope[0], branch = feed_forward(normed_m, own_feed, rows_wide)
     act[1], slope[1], resid_three, sums = feed_forward(
-        normed_m, other_pair, rows_wide, (resid_two, branch, norms, frame_valid)
-    )
-    small = slice(rows_wide, rows_wide + rows_small)
-    small = cube.stack(own_down[:, :, small], other_down[:, :, small], 1)
-    small = small.transpose(2, 1, 0, 3, 4).reshape(dim, dim)
+        normed_m, other_feed, rows_wide, (resid_two, branch, norms, frame_valid)
+    )
+    small = [
+        joined(parts, slice(rows_wide, rows_wide + rows_small)) for parts in (own_down, other_down)
+    ]
+    small = cube.stack(*small, 1).transpose(2, 1, 0, 3, 4).reshape(dim, dim)
 
     for mask in (1, 2):
         sums = sums + cube.swap(sums, mask)
     facts = jnp.stack([labels[0], partner[0], FRAMES * patch_count[0]]).astype(SINGLE)
     gathered = jnp.concatenate([sums, jnp.pad(facts, (0, 125))[None]], axis=1)[None]
-    gathered = cube.join(gathered, *cube.batch_masks)[:, 0]
+    gathered = cube.join(gathered, *first[:-1])
+    others = [cube.swap(gathered, mask) for mask in cube.quads()]
+    gathered = cube.join(cube.gathered(gathered, others), last)[:, 0]
     clip = lax.axis_index("batch").reshape(1)
     loss_sum, d_small, pooled_low, d_resid, d_rows, d_norms_f = all_losses(
         clip, gathered, small, resid_three, frame_valid, norms, classes, proj
@@ -1057,7 +1130,7 @@
 
     d_up, d_down = [None, None], [None, None]
     d_up[1], d_down[1], d_normed = feed_backward(
-        normed_m, d_rows, other_pair, rows_wide, act[1], slope[1]
+        normed_m, d_rows, other_feed, rows_wide, act[1], slope[1]
     )
     up_other, down_other, d_normed, d_rows, normed_m = tick(
         d_up[1], d_down[1], d_normed, d_rows, normed_m
@@ -1066,7 +1139,7 @@
     d_up[0], d_down[0], d_resid, d_rows, d_norms_m = feed_backward(
         normed_m,
         d_rows,
-        own_pair,
+        own_feed,
         rows_wide,
         act[0],
         slope[0],
@@ -1080,7 +1153,7 @@
     sum_down = cube.shed([blocked(down_own), blocked(core_down)], last)
     d_second = [None, None]
     d_second[1], d_normed = spatial_backward(
-        normed_s, d_rows, other_second, qkv_s[1], mixed_s[1], extra_s[1], key_extra
+        normed_s, d_rows, halves(other_second), rows_wide, qkv_s[1], mixed_s[1], extra_s[1], key_extra
     )
     d_small = lax.dynamic_slice_in_dim(
         dot(pooled_low, d_small, TN), cube.mine * rows_small, rows_small, 0
@@ -1093,7 +1166,8 @@
     d_second[0], d_rows, d_norms_s = spatial_backward(
         normed_s,
         d_rows,
-        own_second,
+        halves(own_second),
+        rows_wide,
         qkv_s[0],
         mixed_s[0],
         extra_s[0],
@@ -1112,81 +1186,81 @@
     d_rows = jnp.concatenate([parts[0], *received])
     sum_second.append(other)
 
-    sum_up, sum_down = cube.shed(sum_up, near), cube.shed(sum_down, near)
+    sum_up, sum_down = cube.shed(sum_up, *first[-2::-1]), cube.shed(sum_down, *first[-2::-1])
+    (sends_up, sum_up), (sends_down, sum_down) = cube.quarter(sum_up), cube.quarter(sum_down)
+    sends = [jnp.concatenate(pair, axis=-2) for pair in zip(sends_up, sends_down)]
+    others = [cube.swap(send, mask) for send, mask in cube.fourfold(sends)]
     d_first, d_normed = [None, None], [None, None]
     d_first[1], d_normed[1] = temporal_backward(
-        normed_t, d_rows, other_first, qkv_t[1], mixed_t[1]
-    )
-    first_other, d_normed[1], d_rows, normed_t, sum_up[-1], sum_down[-1], sum_second[-1] = tick(
-        d_first[1], d_normed[1], d_rows, normed_t, sum_up[-1], sum_down[-1], sum_second[-1]
+        normed_t, d_rows, first_w[1], rows_wide, qkv_t, mixed_t, 2
+    )
+    first_other, d_normed[1], d_rows, normed_t, sum_second[-1] = tick(
+        d_first[1], d_normed[1], d_rows, normed_t, sum_second[-1]
     )
     core_first = cube.swap(first_other, 1)
     sum_second = cube.meet(sum_second)
-    sum_up, sum_down = cube.shed(sum_up, *first[::-1]), cube.shed(sum_down, *first[::-1])
     d_first[0], d_normed[0] = temporal_backward(
-        normed_t, d_rows, own_first, qkv_t[0], mixed_t[0]
-    )
-    d_rows, first_own, d_normed[0], core_first, sum_second[-1], sum_up[-1], sum_down[-1] = tick(
-        d_rows, d_first[0], d_normed[0], core_first, sum_second[-1], sum_up[-1], sum_down[-1]
-    )
+        normed_t, d_rows, first_w[0], rows_wide, qkv_t, mixed_t, 0
+    )
+    d_rows, first_own, d_normed[0], core_first, sum_second[-1], *others = tick(
+        d_rows, d_first[0], d_normed[0], core_first, sum_second[-1], *others
+    )
+    sum_up += [other[..., :rows_wide, :] for other in others]
+    sum_down += [other[..., rows_wide:, :] for other in others]
 
     sum_first = [blocked(first_own), blocked(core_first)]
     send_left, left = cube.cut_row([term[..., :middle] for term in sum_first])
     send_right, right = cube.cut([term[..., middle:] for term in sum_first], last)
-    send_second, sum_second = cube.cut(sum_second, near)
-    send_left, send_right, send_second, d_normed[0] = tick(
-        send_left, send_right, send_second, d_normed[0]
-    )
-    other_left, other_right, other_second = (
-        cube.swap(send_left, 2), cube.swap(send_right, last), cube.swap(send_second, near)
-    )
+    sum_second = cube.shed(sum_second, *first[-2::-1])
+    send_left, send_right, d_normed[0], d_norms_f, d_small, sum_second[-1] = tick(
+        send_left, send_right, d_normed[0], d_norms_f, d_small, sum_second[-1]
+    )
+    other_left, other_right = cube.swap(send_left, 2), cube.swap(send_right, last)
+    sends, sum_second = cube.quarter(sum_second)
+    others = [cube.swap(send, mask) for send, mask in cube.fourfold(sends)]
     d_norms = jnp.concatenate([d_norms_s, d_norms_m, d_norms_f])
     d_early = embed_backward(
         by_slot, start_slot, slot_valid, d_rows, d_normed[0], d_normed[1], norms, d_norms
     )
     send, sum_early = cube.cut([d_early.reshape(-1, rows_small, dim + 128)], 1)
-    other_left, other_right, other_second, send, token = tick(
-        other_left, other_right, other_second, send, token
-    )
+    other_left, other_right, send, token = tick(other_left, other_right, send, token)
     other = cube.swap(send, 1)
     left.append(other_left)
     right.append(other_right)
-    sum_second.append(other_second)
     sum_early.append(other)
 
     send_left, left = cube.cut(left, last)
     send_right, right = cube.cut_row(right)
-    send_second, sum_second = cube.cut(sum_second, first[-1])
     send, sum_early = cube.cut(sum_early, 2)
-    token, other_left, other_right, other_second, other = cube.step(
-        token, [(send_left, last), (send_right, 2), (send_second, first[-1]), (send, 2)]
-    )
+    flat = lambda terms: [summed(terms)[0]]
+    token, other_left, other_right, other = cube.step(
+        token, [(send_left, last), (send_right, 2), (send, 2)]
+    )
+    *others, token = tick(*others, token)
+    sum_second += others
     sum_first = [jnp.concatenate([summed(left + [other_left]), summed(right + [other_right])], -1)]
-    sum_second.append(other_second)
     sum_early.append(other)
 
-    send_first, sum_first = cube.cut(sum_first, near)
+    sum_first = cube.shed(sum_first, *first[-2::-1])
+    sends, sum_first = cube.quarter(sum_first)
     send, sum_early = cube.cut(sum_early, last)
-    token, other_first, other = cube.step(token, [(send_first, near), (send, last)])
-    sum_first.append(other_first)
+    token, (d_second, d_up, d_down, squares), *others, other = cube.step(
+        token,
+        [*cube.fourfold(sends), (send, last)],
+        work=[flat(terms) for terms in (sum_second, sum_up, sum_down)],
+    )
+    sum_first += others
     sum_early.append(other)
 
-    send_first, sum_first = cube.cut(sum_first, first[-1])
-    send, sum_early = cube.cut(sum_early, near)
-    ready, up_last, down_last = tick(send_first, sum_up[-1], sum_down[-1])
-    sum_up[-1], sum_down[-1] = up_last, down_last
+    sum_early = cube.shed(sum_early, *first[-2::-1])
+    sends, sum_early = cube.quarter(sum_early)
     square = lambda value: jnp.sum(value * value)
-    d_up, d_down = summed(sum_up)[0], summed(sum_down)[0]
-    d_second = summed(cube.shed(sum_second, *first[-2::-1]))[0]
-    squares = square(d_small) + square(d_up) + square(d_down) + square(d_second)
-    token, other_first, other = cube.step(token, [(ready, first[-1]), (send, near)])
-    sum_first.append(other_first)
-    sum_early.append(other)
-    sum_first = cube.shed(sum_first, *first[-2::-1])
-    sum_early = cube.shed(sum_early, *first[::-1])
-    d_first, d_early = summed(sum_first)[0], summed(sum_early)[0]
-
-    total = cube.total((squares + square(d_first) + square(d_early)).reshape(1, 1))
+    d_first = summed(sum_first)[0]
+    token, *others = cube.step(token, cube.fourfold(sends))
+    d_early = summed(sum_early + others)[0]
+    squares = squares[0, 0] + square(d_small) + square(d_first)
+
+    total = cube.total((squares + square(d_early)).reshape(1, 1))
     parts = (d_early, d_small, d_first, d_second, d_up, d_down)
     grad_norm, *updates = optimizer(total, masters, firsts, seconds, parts, classes, proj)
     updates = [views[i // 3](update) for i, update in enumerate(updates)]

time: 550 us -> 529 us (0.962)
  waiting for transfers between devices: 120 us -> 86.1 us
  starting transfers between devices: 70.6 us -> 87.7 us
  Pallas kernels: 224 us -> 234 us
  local copies, waits for them, and re-layouts: 45.9 us -> 39.1 us
  other arithmetic: 66.9 us -> 60.3 us
    ppermute x71 -> x77, waiting for transfers between devices: 120 us -> 86.1 us  [swap(): return lax.ppermute(value, ALL, [(i, i ^ mask) for i in range(self.count)])]
    ppermute x71 -> x77, starting transfers between devices: 70.6 us -> 87.7 us  [swap(): return lax.ppermute(value, ALL, [(i, i ^ mask) for i in range(self.count)])]
    pallas_call x16 -> x24, Pallas kernels: 218 us -> 228 us  [call(): pl.pallas_call(kernel, grid=(steps,), in_specs=in_specs or [spec_of(value...]
    reduce_sum x6 -> x3, other arithmetic: 12.5 us -> 3.27 us  [body(): square = lambda value: jnp.sum(value * value)]
    dynamic_slice x10 -> x4, local copies, waits for them, and re-layouts: 6.46 us -> 0.29 us  [cut_row(): half = lambda term, which: lax.dynamic_index_in_dim(term, which, 0, False)]
    unnamed x140 -> x134, local copies, waits for them, and re-layouts: 12.8 us -> 11.3 us
  transfers between devices with their start and end apart: 71 -> 77, of which waited for: 31 -> 28; matrix products, arithmetic and copies ran while one was open for 13% -> 13% of each run, Pallas kernels for 33% -> 37%
where the time goes in v4:
time: 529 us; the launch traced here: 521 us
  Pallas kernels  234 us (44%)
  starting transfers between devices  87.7 us (17%)
  waiting for transfers between devices  86.1 us (16%)
  other arithmetic  60.3 us (11%)
  local copies, waits for them, and re-layouts  39.1 us (7%)
  between operations  10.5 us (2%)
    pallas_call x24, Pallas kernels, call(): pl.pallas_call(kernel, grid=(steps,), in_specs=in_specs or [spec_of(value...  228 us
    ppermute x77, starting transfers between devices, swap(): return lax.ppermute(value, ALL, [(i, i ^ mask) for i in range(self.count)])  87.7 us
    ppermute x77, waiting for transfers between devices, swap(): return lax.ppermute(value, ALL, [(i, i ^ mask) for i in range(self.count)])  86.1 us
    convert_element_type x24, other arithmetic, low(): return value.astype(LOWER)  22.7 us
    unnamed x134, local copies, waits for them, and re-layouts  11.3 us
  transfers between devices with their start and end apart: 77, of which 28 were waited for; matrix products, arithmetic and copies ran while one was open for 13% of the time, Pallas kernels for 37%

profile of v4, /device:TPU:0, one launch (start us, length us, event | category | flops | bytes accessed | tf_op | source)
XLA Modules:
  0.0 520.6 jit_solution(1606509614790757367)
XLA Ops:
  5.7 4.1 collective-permute-start
  15.3 1.7 gather_fusion
  20.8 1.6 collective-permute-start.1
  25.8 7.6 %collective-permute-done.3 = bf16[208,768]{1,0:T(8,128)(2,1)S(1)} collective-permute-done((bf16[208,768]{1,0:T(8,128)(2,1)S(1)}, bf16[208,768]{1,0:T(8,128)(2,1)S(1)}, u32[]{:S(2)}, u32[]{:S(2)}) %collective-permute-start.3) | collective-permute-done | bytes 319520 | tf_op jit(solution)/shard_map/ppermute | solution.py:850
  33.4 4.9 collective-permute-done.4
  38.6 1.6 collective-permute-start.5
  44.4 3.0 collective-permute-start.11
  47.4 3.1 collective-permute-done.5
  52.1 1.6 collective-permute-start.7
  56.6 14.7 %collective-permute-done.7 = bf16[8,128,384]{2,1,0:T(8,128)(2,1)S(1)} collective-permute-done((bf16[8,128,384]{2,1,0:T(8,128)(2,1)S(1)}, bf16[8,128,384]{2,1,0:T(8,128)(2,1)S(1)}, u32[]{:S(2)}, u32[]{:S(2)}) %collective-permute-start.7) | collective-permute-done | bytes 786464 | tf_op jit(solution)/shard_map/ppermute | solution.py:850
  83.4 1.8 collective-permute-done.12.other_left.left_ref
  89.1 5.1 embed.1
  94.2 2.1 collective-permute-done.14
  99.1 1.6 collective-permute-start.17
  100.7 10.7 %temporal_forward.1 = (bf16[4,4,576,208]{3,2,1,0:T(8,128)(2,1)}, bf16[4,832,192]{2,1,0:T(8,128)(2,1)}) custom-call(bf16[832,768]{1,0:T(8,128)(2,1)} %get-tuple-element.440.normed_ref, bf16[2,8,128,384]{3,2,1,0:T(8,128)(2,1)} %pad_maximum_fusion.1.own_left.left_ref, bf16[2,8,128,384]{3,2,1,0:T(8,128)(2,1)} %bitcast.466, ...), custom_call_target="tpu_custom_call" | custom-call | flops 40000000000 | bytes 8388608 | tf_op jit(solution)/shard_map/temporal_forward/pallas_call | solution.py:592
  126.2 2.6 convolution_multiply_fusion.start_ref
  130.3 5.9 %collective-permute-done.21 = bf16[208,768]{1,0:T(8,128)(2,1)} collective-permute-done((bf16[208,768]{1,0:T(8,128)(2,1)}, bf16[208,768]{1,0:T(8,128)(2,1)}, u32[]{:S(2)}, u32[]{:S(2)}) %collective-permute-start.21) | collective-permute-done | bytes 319520 | tf_op jit(solution)/shard_map/ppermute | solution.py:850
  137.4 2.2 pad_maximum_fusion.6.mixed_ref
  140.3 1.6 collective-permute-start.27
  143.4 5.7 %enter_frame.1 = (f32[832,768]{1,0:T(8,128)}, bf16[832,768]{1,0:T(8,128)(2,1)}) custom-call(f32[832,768]{1,0:T(8,128)} %convolution_multiply_fusion.start_ref, bf16[832,768]{1,0:T(8,128)(2,1)} %pad_maximum_fusion.6.mixed_ref, bf16[768,768]{1,0:T(8,128)(2,1)} %pad_maximum_fusion.10.weight_ref, f32[8,768]{1,0:T(8,128)} %reshape.1629.norms_ref.refs_6_.refs_9_), custom_call_target="tpu_custom_call" | custom-call | flops 2000000000 | bytes 8388608 | tf_op jit(solution)/shard_map/enter_frame/pallas_call | solution.py:592
  149.1 15.4 %spatial_forward.2 = (bf16[2,832,576]{2,1,0:T(8,128)(2,1)}, bf16[2,832,192]{2,1,0:T(8,128)(2,1)}, bf16[2,832,192]{2,1,0:T(8,128)(2,1)}, f32[832,768]{1,0:T(8,128)}) custom-call(bf16[832,768]{1,0:T(8,128)(2,1)} %get-tuple-element.412.normed_ref, bf16[2,8,96,768]{3,2,1,0:T(8,128)(2,1)} %copy-done.3, bf16[2,8,96,768]{3,2,1,0:T(8,128)(2,1)} %copy-done.3, ...), custom_call_target="tpu_custom_call" | custom-call | flops 15000000512 | bytes 8388608 | tf_op jit(solution)/shard_map/spatial_forward/pallas_call | solution.py:592
  172.7 18.9 %spatial_forward.3 = (bf16[2,832,576]{2,1,0:T(8,128)(2,1)}, bf16[2,832,192]{2,1,0:T(8,128)(2,1)}, bf16[2,832,192]{2,1,0:T(8,128)(2,1)}, f32[832,768]{1,0:T(8,128)}, bf16[832,768]{1,0:T(8,128)(2,1)}) custom-call(bf16[832,768]{1,0:T(8,128)(2,1)} %get-tuple-element.412.normed_ref, bf16[2,8,96,768]{3,2,1,0:T(8,128)(2,1)} %collective-permute-done.23.left_ref.right_ref, ...), custom_call_target="tpu_custom_call" | custom-call | flops 15000000512 | bytes 8388608 | tf_op jit(solution)/shard_map/spatial_forward/pallas_call | solution.py:592
  194.3 9.9 %feed_forward.2 = (bf16[2,832,768]{2,1,0:T(8,128)(2,1)}, bf16[2,832,768]{2,1,0:T(8,128)(2,1)}, f32[832,768]{1,0:T(8,128)}) custom-call(bf16[832,768]{1,0:T(8,128)(2,1)} %get-tuple-element.388.normed_ref, bf16[2,8,96,384]{3,2,1,0:T(8,128)(2,1)} %copy-done.21, bf16[2,8,96,384]{3,2,1,0:T(8,128)(2,1)} %bitcast.103.refs_1_, bf16[2,8,128,384]{3,2,1,0:T(8,128)(2,1)} %copy-done.10, ...), custom_call_target="tpu_custom_call" | custom-call | flops 10000000000 | bytes 8388608 | tf_op jit(solution)/shard_map/feed_forward/pallas_call | solution.py:592
  204.2 13.5 %feed_forward.3 = (bf16[2,832,768]{2,1,0:T(8,128)(2,1)}, bf16[2,832,768]{2,1,0:T(8,128)(2,1)}, f32[832,768]{1,0:T(8,128)}, f32[1,768]{1,0:T(1,128)}) custom-call(bf16[832,768]{1,0:T(8,128)(2,1)} %get-tuple-element.388.normed_ref, bf16[2,8,96,384]{3,2,1,0:T(8,128)(2,1)} %collective-permute-done.30.refs_0_, ...), custom_call_target="tpu_custom_call" | custom-call | flops 10000000000 | bytes 8388608 | tf_op jit(solution)/shard_map/feed_forward/pallas_call | solution.py:592
  223.8 1.8 collective-permute-start.37
  225.5 2.5 collective-permute-start.38
  229.6 1.6 collective-permute-start.39
  234.1 7.3 %losses.1 = (f32[1,1]{1,0:T(1,128)}, bf16[8,768]{1,0:T(8,128)(2,1)}, bf16[8,768]{1,0:T(8,128)(2,1)}, f32[832,768]{1,0:T(8,128)}, bf16[832,768]{1,0:T(8,128)(2,1)}, /*index=5*/f32[2,768]{1,0:T(2,128)}) custom-call(s32[1]{0:T(128)} %bitcast.clip_ref, f32[8,896]{1,0:T(8,128)} %squeeze_reshape.3.facts_ref, bf16[768,768]{1,0:T(8,128)(2,1)} %bitcast.474, ...), custom_call_target="tpu_custom_call" | custom-call | flops 1000000000 | bytes 8388608 | tf_op jit(solution)/shard_map/losses/pallas_call | solution.py:592
  241.4 14.2 %feed_backward.2 = (bf16[2,768,768]{2,1,0:T(8,128)(2,1)}, bf16[2,768,768]{2,1,0:T(8,128)(2,1)}, f32[832,768]{1,0:T(8,128)}) custom-call(bf16[832,768]{1,0:T(8,128)(2,1)} %get-tuple-element.388.normed_ref, bf16[832,768]{1,0:T(8,128)(2,1)} %get-tuple-element.389.grad_ref, bf16[2,8,96,384]{3,2,1,0:T(8,128)(2,1)} %collective-permute-done.30.refs_0_, ...), custom_call_target="tpu_custom_call" | custom-call | flops 15000000512 | bytes 8388608 | tf_op jit(solution)/shard_map/feed_backward/pallas_call | solution.py:592
  257.4 19.2 %feed_backward.3 = (bf16[2,768,768]{2,1,0:T(8,128)(2,1)}, bf16[2,768,768]{2,1,0:T(8,128)(2,1)}, f32[832,768]{1,0:T(8,128)}, bf16[832,768]{1,0:T(8,128)(2,1)}, f32[2,768]{1,0:T(2,128)}) custom-call(bf16[832,768]{1,0:T(8,128)(2,1)} %get-tuple-element.388.normed_ref, bf16[832,768]{1,0:T(8,128)(2,1)} %get-tuple-element.389.grad_ref, ...), custom_call_target="tpu_custom_call" | custom-call | flops 15000000512 | bytes 8388608 | tf_op jit(solution)/shard_map/feed_backward/pallas_call | solution.py:592
  276.7 2.7 fusion
  280.9 2.6 fusion.1
  285.0 27.4 %spatial_backward.2 = (bf16[2,768,768]{2,1,0:T(8,128)(2,1)}, f32[832,768]{1,0:T(8,128)}) custom-call(bf16[832,768]{1,0:T(8,128)(2,1)} %get-tuple-element.412.normed_ref, bf16[832,768]{1,0:T(8,128)(2,1)} %get-tuple-element.413.grad_ref, bf16[2,8,96,768]{3,2,1,0:T(8,128)(2,1)} %collective-permute-done.23.left_ref.right_ref, ...), custom_call_target="tpu_custom_call" | custom-call | flops 30000001024 | bytes 8388608 | tf_op jit(solution)/shard_map/spatial_backward/pallas_call | solution.py:592
  312.5 1.6 copy-done.4
  318.1 31.5 %spatial_backward.3 = (bf16[2,768,768]{2,1,0:T(8,128)(2,1)}, bf16[832,768]{1,0:T(8,128)(2,1)}, f32[2,768]{1,0:T(2,128)}) custom-call(bf16[832,768]{1,0:T(8,128)(2,1)} %get-tuple-element.412.normed_ref, bf16[832,768]{1,0:T(8,128)(2,1)} %get-tuple-element.413.grad_ref, bf16[2,8,96,768]{3,2,1,0:T(8,128)(2,1)} %copy-done.3, bf16[2,8,96,768]{3,2,1,0:T(8,128)(2,1)} %copy-done.3, ...), custom_call_target="tpu_custom_call" | custom-call | flops 30000001024 | bytes 8388608 | tf_op jit(solution)/shard_map/spatial_backward/pallas_call | solution.py:592
  349.7 3.3 fusion.85
  358.2 6.3 %collective-permute-done.48 = bf16[208,768]{1,0:T(8,128)(2,1)S(1)} collective-permute-done((bf16[208,768]{1,0:T(8,128)(2,1)}, bf16[208,768]{1,0:T(8,128)(2,1)S(1)}, u32[]{:S(2)}, u32[]{:S(2)}) %collective-permute-start.48) | collective-permute-done | bytes 319520 | tf_op jit(solution)/shard_map/ppermute | solution.py:850
  364.5 5.1 collective-permute-done.49
  370.8 14.1 %temporal_backward.2 = (bf16[2,768,768]{2,1,0:T(8,128)(2,1)}, f32[832,768]{1,0:T(8,128)}) custom-call(bf16[832,768]{1,0:T(8,128)(2,1)} %get-tuple-element.440.normed_ref, bf16[832,768]{1,0:T(8,128)(2,1)} %pad_maximum_fusion.7.grad_ref.drows_ref, bf16[2,8,128,384]{3,2,1,0:T(8,128)(2,1)} %collective-permute-done.12.other_left.left_ref, ...), custom_call_target="tpu_custom_call" | custom-call | flops 14000000000 | bytes 8388608 | tf_op jit(solution)/shard_map/temporal_backward/pallas_call | solution.py:592
  387.5 1.6 fusion.44
  389.1 2.1 collective-permute-start.53
  395.2 1.6 collective-permute-start.52
  396.8 14.3 %temporal_backward.3 = (bf16[2,768,768]{2,1,0:T(8,128)(2,1)}, f32[832,768]{1,0:T(8,128)}) custom-call(bf16[832,768]{1,0:T(8,128)(2,1)} %get-tuple-element.440.normed_ref, bf16[832,768]{1,0:T(8,128)(2,1)} %pad_maximum_fusion.7.grad_ref.drows_ref, bf16[2,8,128,384]{3,2,1,0:T(8,128)(2,1)} %pad_maximum_fusion.1.own_left.left_ref, ...), custom_call_target="tpu_custom_call" | custom-call | flops 14000000000 | bytes 8388608 | tf_op jit(solution)/shard_map/temporal_backward/pallas_call | solution.py:592
  411.1 3.6 collective-permute-done.54
  415.7 2.1 fusion.82
  420.3 1.6 collective-permute-start.56
  423.3 2.2 fusion.38
  425.5 6.0 %collective-permute-start.62 = (bf16[1,96,768]{2,1,0:T(8,128)(2,1)}, bf16[1,96,768]{2,1,0:T(8,128)(2,1)S(1)}, u32[]{:S(2)}, u32[]{:S(2)}) collective-permute-start(bf16[1,96,768]{2,1,0:T(8,128)(2,1)} %get-tuple-element.534), channel_id=1, source_target_pairs={{0,8},{1,9},{2,10},{3,11},{4,12},{5,13},{6,14},{7,15},{8,0},{9,1},... | collective-permute-start | bytes 442376 | tf_op jit(solution)/shard_map/ppermute | solution.py:850
  432.1 8.3 %embed_backward.1 = bf16[768,896]{1,0:T(8,128)(2,1)} custom-call(bf16[832,768]{1,0:T(8,128)(2,1)} %pad_maximum_fusion.5.patches_ref, f32[832,768]{1,0:T(8,128)} %get-tuple-element.455.start_ref, f32[832,1]{1,0:T(8,128)} %copy.104.valid_ref, bf16[832,768]{1,0:T(8,128)(2,1)} %pad_maximum_fusion.7.grad_ref.drows_ref, f32[832,768]{1,0:T(8,128)} %get-tuple-element.457.da_ref, ...), custom_call_target="tpu_custom_call" | custom-call | flops 30000001024 | bytes 8388608 | tf_op jit(solution)/shard_map/embed_backward/pallas_call | solution.py:592
  443.4 2.3 fusion.31
  452.6 4.9 collective-permute-done.59
  457.5 2.4 collective-permute-start.64
  459.9 5.3 %collective-permute-done.61 = bf16[8,24,896]{2,1,0:T(8,128)(2,1)S(1)} collective-permute-done((bf16[8,24,896]{2,1,0:T(8,128)(2,1)S(1)}, bf16[8,24,896]{2,1,0:T(8,128)(2,1)S(1)}, u32[]{:S(2)}, u32[]{:S(2)}) %collective-permute-start.61) | collective-permute-done | bytes 344096 | tf_op jit(solution)/shard_map/ppermute | solution.py:850
  469.5 1.8 collective-permute-start.66
  474.2 2.0 fusion.36.refs_0_
  476.2 2.1 finish.1
  479.6 3.2 collective-permute-done.66
  483.0 2.2 collective-permute-start.69
  496.1 1.9 collective-permute-start.73
  498.0 1.9 collective-permute-done.73
  500.4 2.8 collective-permute-start.74
  506.3 2.2 collective-permute-done.75
  510.5 3.2 collective-permute-done.76
  514.4 5.7 %optimizer.1 = (f32[1,1]{1,0:T(1,128)}, f32[24,768]{1,0:T(8,128)}, f32[24,768]{1,0:T(8,128)}, f32[24,768]{1,0:T(8,128)}, f32[8,24]{1,0:T(8,128)}, /*index=5*/f32...) custom-call(f32[1,1]{1,0:T(1,128)S(6)} %add.1305.total_ref, ...), custom_call_target="tpu_custom_call" | custom-call | tf_op jit(solution)/shard_map/optimizer/pallas_call | solution.py:783
  (413 shorter events, 140.8 us)
Async XLA Ops:
  5.7 14.8 %collective-permute-start = (bf16[1,128,768]{2,1,0:T(8,128)(2,1)S(1)}, bf16[1,128,768]{2,1,0:T(8,128)(2,1)S(1)}, u32[]{:S(2)}, u32[]{:S(2)}) collective-permute-start(bf16[1,128,768]{2,1,0:T(8,128)(2,1)S(1)} %fusion.57), channel_id=1, source_target_pairs={{0,16},{1,17},{2,18},{3,19},{4,20},{5,21},{6,22},{7,23},{8,24},{9,... | collective-permute-start | bytes 589832 | tf_op jit(solution)/shard_map/ppermute | solution.py:850
  20.8 17.5 %collective-permute-start.1 = (bf16[2,128,768]{2,1,0:T(8,128)(2,1)S(1)}, bf16[2,128,768]{2,1,0:T(8,128)(2,1)S(1)}, u32[]{:S(2)}, u32[]{:S(2)}) collective-permute-start(bf16[2,128,768]{2,1,0:T(8,128)(2,1)S(1)} %maximum_bitcast_fusion.3), channel_id=1, source_target_pairs={{0,8},{1,9},{2,10},{3,11},{4,12},{5,13},{6,14},{7,15},{8,0},{9,1},... | collective-permute-start | bytes 1179656 | tf_op jit(solution)/shard_map/ppermute | solution.py:850
  23.0 10.4 %collective-permute-start.3 = (bf16[208,768]{1,0:T(8,128)(2,1)S(1)}, bf16[208,768]{1,0:T(8,128)(2,1)S(1)}, u32[]{:S(2)}, u32[]{:S(2)}) collective-permute-start(bf16[208,768]{1,0:T(8,128)(2,1)S(1)} %get-tuple-element.287), channel_id=1, source_target_pairs={{0,2},{1,3},{2,0},{3,1},{4,6},{5,7},{6,4},{7,5},{8,10},{9,11},{10,... | collective-permute-start | bytes 958472 | tf_op jit(solution)/shard_map/ppermute | solution.py:850
  24.5 13.8 %collective-permute-start.4 = (bf16[208,768]{1,0:T(8,128)(2,1)S(1)}, bf16[208,768]{1,0:T(8,128)(2,1)S(1)}, u32[]{:S(2)}, u32[]{:S(2)}) collective-permute-start(bf16[208,768]{1,0:T(8,128)(2,1)S(1)} %get-tuple-element.288), channel_id=1, source_target_pairs={{0,3},{1,2},{2,1},{3,0},{4,7},{5,6},{6,5},{7,4},{8,11},{9,10},{10,... | collective-permute-start | bytes 958472 | tf_op jit(solution)/shard_map/ppermute | solution.py:850
  38.6 11.9 %collective-permute-start.5 = (bf16[4,128,384]{2,1,0:T(8,128)(2,1)S(1)}, bf16[4,128,384]{2,1,0:T(8,128)(2,1)S(1)}, u32[]{:S(2)}, u32[]{:S(2)}) collective-permute-start(bf16[4,128,384]{2,1,0:T(8,128)(2,1)S(1)} %get-tuple-element.295), channel_id=1, source_target_pairs={{0,4},{1,5},{2,6},{3,7},{4,0},{5,1},{6,2},{7,3},{8,12},{9,13},{10,... | collective-permute-start | bytes 1179656 | tf_op jit(solution)/shard_map/ppermute | solution.py:850
  40.2 11.5 %collective-permute-start.6 = (bf16[4,128,384]{2,1,0:T(8,128)(2,1)S(1)}, bf16[4,128,384]{2,1,0:T(8,128)(2,1)S(1)}, u32[]{:S(2)}, u32[]{:S(2)}) collective-permute-start(bf16[4,128,384]{2,1,0:T(8,128)(2,1)S(1)} %get-tuple-element.296), channel_id=1, source_target_pairs={{0,2},{1,3},{2,0},{3,1},{4,6},{5,7},{6,4},{7,5},{8,10},{9,11},{10,... | collective-permute-start | bytes 1179656 | tf_op jit(solution)/shard_map/ppermute | solution.py:850
  43.0 33.1 %collective-permute-start.9 = (bf16[1,192,768]{2,1,0:T(8,128)(2,1)}, bf16[1,192,768]{2,1,0:T(8,128)(2,1)S(1)}, u32[]{:S(2)}, u32[]{:S(2)}) collective-permute-start(bf16[1,192,768]{2,1,0:T(8,128)(2,1)} %maximum_bitcast_fusion.5), channel_id=1, source_target_pairs={{0,8},{1,9},{2,10},{3,11},{4,12},{5,13},{6,14},{7,15},{8,0},{9,1},... | collective-permute-start | bytes 884744 | tf_op jit(solution)/shard_map/ppermute | solution.py:850
  43.4 32.7 %collective-permute-start.10 = (bf16[1,192,768]{2,1,0:T(8,128)(2,1)}, bf16[1,192,768]{2,1,0:T(8,128)(2,1)S(1)}, u32[]{:S(2)}, u32[]{:S(2)}) collective-permute-start(bf16[1,192,768]{2,1,0:T(8,128)(2,1)} %maximum_bitcast_fusion.5), channel_id=1, source_target_pairs={{0,16},{1,17},{2,18},{3,19},{4,20},{5,21},{6,22},{7,23},{8,24},{9,... | collective-permute-start | bytes 884744 | tf_op jit(solution)/shard_map/ppermute | solution.py:850
  44.4 31.7 %collective-permute-start.11 = (bf16[1,192,768]{2,1,0:T(8,128)(2,1)}, bf16[1,192,768]{2,1,0:T(8,128)(2,1)}, u32[]{:S(2)}, u32[]{:S(2)}) collective-permute-start(bf16[1,192,768]{2,1,0:T(8,128)(2,1)} %maximum_bitcast_fusion.5), channel_id=1, source_target_pairs={{0,24},{1,25},{2,26},{3,27},{4,28},{5,29},{6,30},{7,31},{8,16},{9,... | collective-permute-start | bytes 884744 | tf_op jit(solution)/shard_map/ppermute | solution.py:850
  52.1 19.2 %collective-permute-start.7 = (bf16[8,128,384]{2,1,0:T(8,128)(2,1)S(1)}, bf16[8,128,384]{2,1,0:T(8,128)(2,1)S(1)}, u32[]{:S(2)}, u32[]{:S(2)}) collective-permute-start(bf16[8,128,384]{2,1,0:T(8,128)(2,1)S(1)} %bitcast.484), channel_id=1, source_target_pairs={{0,2},{1,3},{2,0},{3,1},{4,6},{5,7},{6,4},{7,5},{8,10},{9,11},{10,... | collective-permute-start | bytes 2359304 | tf_op jit(solution)/shard_map/ppermute | solution.py:850
  53.7 18.9 %collective-permute-start.8 = (bf16[2,4,128,384]{3,2,1,0:T(8,128)(2,1)S(1)}, bf16[2,4,128,384]{3,2,1,0:T(8,128)(2,1)S(1)}, u32[]{:S(2)}, u32[]{:S(2)}) collective-permute-start(bf16[2,4,128,384]{3,2,1,0:T(8,128)(2,1)S(1)} %pad_maximum_fusion.15), channel_id=1, source_target_pairs={{0,4},{1,5},{2,6},{3,7},{4,0},{5,1},{6,2},{7,3},{8,12},{9,13},{10,... | collective-permute-start | bytes 2359304 | tf_op jit(solution)/shard_map/ppermute | solution.py:850
  79.3 5.9 %collective-permute-start.12 = (bf16[2,8,128,384]{3,2,1,0:T(8,128)(2,1)}, bf16[2,8,128,384]{3,2,1,0:T(8,128)(2,1)}, u32[]{:S(2)}, u32[]{:S(2)}) collective-permute-start(bf16[2,8,128,384]{3,2,1,0:T(8,128)(2,1)} %pad_maximum_fusion.1.own_left.left_ref), channel_id=1, source_target_pairs={{0,1},{1,0},{2,3},{3,2},{4,5},{5,4},{6,7},{7,6},{8,9},{9,8},{10,11... | collective-permute-start | bytes 4718600 | tf_op jit(solution)/shard_map/ppermute | solution.py:850
  79.3 5.9 %collective-permute-start.13 = (bf16[2,8,128,384]{3,2,1,0:T(8,128)(2,1)S(1)}, bf16[2,8,128,384]{3,2,1,0:T(8,128)(2,1)}, u32[]{:S(2)}, u32[]{:S(2)}) collective-permute-start(bf16[2,8,128,384]{3,2,1,0:T(8,128)(2,1)S(1)} %bitcast.465), channel_id=1, source_target_pairs={{0,1},{1,0},{2,3},{3,2},{4,5},{5,4},{6,7},{7,6},{8,9},{9,8},{10,11... | collective-permute-start | bytes 4718600 | tf_op jit(solution)/shard_map/ppermute | solution.py:850
  80.8 15.6 %collective-permute-start.14 = (bf16[4,192,384]{2,1,0:T(8,128)(2,1)}, bf16[4,192,384]{2,1,0:T(8,128)(2,1)}, u32[]{:S(2)}, u32[]{:S(2)}) collective-permute-start(bf16[4,192,384]{2,1,0:T(8,128)(2,1)} %get-tuple-element.331), channel_id=1, source_target_pairs={{0,4},{1,5},{2,6},{3,7},{4,0},{5,1},{6,2},{7,3},{8,12},{9,13},{10,... | collective-permute-start | bytes 1769480 | tf_op jit(solution)/shard_map/ppermute | solution.py:850
  81.3 15.3 %collective-permute-start.15 = (bf16[4,192,384]{2,1,0:T(8,128)(2,1)}, bf16[4,192,384]{2,1,0:T(8,128)(2,1)}, u32[]{:S(2)}, u32[]{:S(2)}) collective-permute-start(bf16[4,192,384]{2,1,0:T(8,128)(2,1)} %get-tuple-element.332), channel_id=1, source_target_pairs={{0,2},{1,3},{2,0},{3,1},{4,6},{5,7},{6,4},{7,5},{8,10},{9,11},{10,... | collective-permute-start | bytes 1769480 | tf_op jit(solution)/shard_map/ppermute | solution.py:850
  81.8 33.4 %collective-permute-start.18 = (bf16[1,128,768]{2,1,0:T(8,128)(2,1)}, bf16[1,128,768]{2,1,0:T(8,128)(2,1)}, u32[]{:S(2)}, u32[]{:S(2)}) collective-permute-start(bf16[1,128,768]{2,1,0:T(8,128)(2,1)} %maximum_bitcast_fusion.6), channel_id=1, source_target_pairs={{0,16},{1,17},{2,18},{3,19},{4,20},{5,21},{6,22},{7,23},{8,24},{9,... | collective-permute-start | bytes 589832 | tf_op jit(solution)/shard_map/ppermute | solution.py:850
  98.4 16.5 %collective-permute-start.16 = (bf16[8,96,384]{2,1,0:T(8,128)(2,1)S(1)}, bf16[8,96,384]{2,1,0:T(8,128)(2,1)S(1)}, u32[]{:S(2)}, u32[]{:S(2)}) collective-permute-start(bf16[8,96,384]{2,1,0:T(8,128)(2,1)S(1)} %slice.406), channel_id=1, source_target_pairs={{0,2},{1,3},{2,0},{3,1},{4,6},{5,7},{6,4},{7,5},{8,10},{9,11},{10,... | collective-permute-start | bytes 1769480 | tf_op jit(solution)/shard_map/ppermute | solution.py:850
  99.1 15.8 %collective-permute-start.17 = (bf16[2,4,96,384]{3,2,1,0:T(8,128)(2,1)S(1)}, bf16[2,4,96,384]{3,2,1,0:T(8,128)(2,1)S(1)}, u32[]{:S(2)}, u32[]{:S(2)}) collective-permute-start(bf16[2,4,96,384]{3,2,1,0:T(8,128)(2,1)S(1)} %get-tuple-element.608), channel_id=1, source_target_pairs={{0,4},{1,5},{2,6},{3,7},{4,0},{5,1},{6,2},{7,3},{8,12},{9,13},{10,... | collective-permute-start | bytes 1769480 | tf_op jit(solution)/shard_map/ppermute | solution.py:850
  111.4 55.5 %collective-permute-start.25 = (bf16[2,4,96,384]{3,2,1,0:T(8,128)(2,1)S(1)}, bf16[2,4,96,384]{3,2,1,0:T(8,128)(2,1)S(1)}, u32[]{:S(2)}, u32[]{:S(2)}) collective-permute-start(bf16[2,4,96,384]{3,2,1,0:T(8,128)(2,1)S(1)} %get-tuple-element.607), channel_id=1, source_target_pairs={{0,4},{1,5},{2,6},{3,7},{4,0},{5,1},{6,2},{7,3},{8,12},{9,13},{10,... | collective-permute-start | bytes 1769480 | tf_op jit(solution)/shard_map/ppermute | solution.py:850
  119.5 9.3 %collective-permute-start.19 = (bf16[208,768]{1,0:T(8,128)(2,1)S(1)}, bf16[208,768]{1,0:T(8,128)(2,1)S(1)}, u32[]{:S(2)}, u32[]{:S(2)}) collective-permute-start(bf16[208,768]{1,0:T(8,128)(2,1)S(1)} %pad_maximum_fusion.25), channel_id=1, source_target_pairs={{0,1},{1,0},{2,3},{3,2},{4,5},{5,4},{6,7},{7,6},{8,9},{9,8},{10,11... | collective-permute-start | bytes 958472 | tf_op jit(solution)/shard_map/ppermute | solution.py:850
  119.5 10.8 %collective-permute-start.20 = (bf16[208,768]{1,0:T(8,128)(2,1)}, bf16[208,768]{1,0:T(8,128)(2,1)}, u32[]{:S(2)}, u32[]{:S(2)}) collective-permute-start(bf16[208,768]{1,0:T(8,128)(2,1)} %pad_maximum_fusion.26), channel_id=1, source_target_pairs={{0,2},{1,3},{2,0},{3,1},{4,6},{5,7},{6,4},{7,5},{8,10},{9,11},{10,... | collective-permute-start | bytes 958472 | tf_op jit(solution)/shard_map/ppermute | solution.py:850
  121.0 15.2 %collective-permute-start.21 = (bf16[208,768]{1,0:T(8,128)(2,1)}, bf16[208,768]{1,0:T(8,128)(2,1)}, u32[]{:S(2)}, u32[]{:S(2)}) collective-permute-start(bf16[208,768]{1,0:T(8,128)(2,1)} %pad_maximum_fusion.27), channel_id=1, source_target_pairs={{0,3},{1,2},{2,1},{3,0},{4,7},{5,6},{6,5},{7,4},{8,11},{9,10},{10,... | collective-permute-start | bytes 958472 | tf_op jit(solution)/shard_map/ppermute | solution.py:850
  121.3 14.9 %collective-permute-start.22 = (bf16[2,128,768]{2,1,0:T(8,128)(2,1)}, bf16[2,128,768]{2,1,0:T(8,128)(2,1)}, u32[]{:S(2)}, u32[]{:S(2)}) collective-permute-start(bf16[2,128,768]{2,1,0:T(8,128)(2,1)} %maximum_bitcast_fusion.4), channel_id=1, source_target_pairs={{0,8},{1,9},{2,10},{3,11},{4,12},{5,13},{6,14},{7,15},{8,0},{9,1},... | collective-permute-start | bytes 1179656 | tf_op jit(solution)/shard_map/ppermute | solution.py:850
  128.8 38.1 %collective-permute-start.24 = (bf16[8,96,384]{2,1,0:T(8,128)(2,1)S(1)}, bf16[8,96,384]{2,1,0:T(8,128)(2,1)S(1)}, u32[]{:S(2)}, u32[]{:S(2)}) collective-permute-start(bf16[8,96,384]{2,1,0:T(8,128)(2,1)S(1)} %get-tuple-element.609), channel_id=1, source_target_pairs={{0,2},{1,3},{2,0},{3,1},{4,6},{5,7},{6,4},{7,5},{8,10},{9,11},{10,... | collective-permute-start | bytes 1769480 | tf_op jit(solution)/shard_map/ppermute | solution.py:850
  139.6 27.3 %collective-permute-start.23 = (bf16[2,8,96,768]{3,2,1,0:T(8,128)(2,1)S(1)}, bf16[2,8,96,768]{3,2,1,0:T(8,128)(2,1)}, u32[]{:S(2)}, u32[]{:S(2)}) collective-permute-start(bf16[2,8,96,768]{3,2,1,0:T(8,128)(2,1)S(1)} %pad_maximum_fusion.left_ref.right_ref), channel_id=1, source_target_pairs={{0,1},{1,0},{2,3},{3,2},{4,5},{5,4},{6,7},{7,6},{8,9},{9,8},{10,11... | collective-permute-start | bytes 7077896 | tf_op jit(solution)/shard_map/ppermute | solution.py:850
  140.3 24.3 %collective-permute-start.27 = (bf16[4,128,384]{2,1,0:T(8,128)(2,1)S(1)}, bf16[4,128,384]{2,1,0:T(8,128)(2,1)S(1)}, u32[]{:S(2)}, u32[]{:S(2)}) collective-permute-start(bf16[4,128,384]{2,1,0:T(8,128)(2,1)S(1)} %get-tuple-element.628), channel_id=1, source_target_pairs={{0,2},{1,3},{2,0},{3,1},{4,6},{5,7},{6,4},{7,5},{8,10},{9,11},{10,... | collective-permute-start | bytes 1179656 | tf_op jit(solution)/shard_map/ppermute | solution.py:850
  141.9 23.4 %collective-permute-start.26 = (bf16[4,128,384]{2,1,0:T(8,128)(2,1)S(1)}, bf16[4,128,384]{2,1,0:T(8,128)(2,1)}, u32[]{:S(2)}, u32[]{:S(2)}) collective-permute-start(bf16[4,128,384]{2,1,0:T(8,128)(2,1)S(1)} %get-tuple-element.629), channel_id=1, source_target_pairs={{0,4},{1,5},{2,6},{3,7},{4,0},{5,1},{6,2},{7,3},{8,12},{9,13},{10,... | collective-permute-start | bytes 1179656 | tf_op jit(solution)/shard_map/ppermute | solution.py:850
  167.9 24.2 %collective-permute-start.28 = (bf16[8,128,384]{2,1,0:T(8,128)(2,1)S(1)}, bf16[8,128,384]{2,1,0:T(8,128)(2,1)S(1)}, u32[]{:S(2)}, u32[]{:S(2)}) collective-permute-start(bf16[8,128,384]{2,1,0:T(8,128)(2,1)S(1)} %bitcast.482), channel_id=1, source_target_pairs={{0,2},{1,3},{2,0},{3,1},{4,6},{5,7},{6,4},{7,5},{8,10},{9,11},{10,... | collective-permute-start | bytes 2359304 | tf_op jit(solution)/shard_map/ppermute | solution.py:850
  168.4 23.1 %collective-permute-start.29 = (bf16[2,4,128,384]{3,2,1,0:T(8,128)(2,1)S(1)}, bf16[2,4,128,384]{3,2,1,0:T(8,128)(2,1)S(1)}, u32[]{:S(2)}, u32[]{:S(2)}) collective-permute-start(bf16[2,4,128,384]{3,2,1,0:T(8,128)(2,1)S(1)} %pad_maximum_fusion.20), channel_id=1, source_target_pairs={{0,4},{1,5},{2,6},{3,7},{4,0},{5,1},{6,2},{7,3},{8,12},{9,13},{10,... | collective-permute-start | bytes 2359304 | tf_op jit(solution)/shard_map/ppermute | solution.py:850
  170.3 22.2 %collective-permute-start.30 = (bf16[2,8,96,384]{3,2,1,0:T(8,128)(2,1)S(1)}, bf16[2,8,96,384]{3,2,1,0:T(8,128)(2,1)}, u32[]{:S(2)}, u32[]{:S(2)}) collective-permute-start(bf16[2,8,96,384]{3,2,1,0:T(8,128)(2,1)S(1)} %pad_maximum_fusion.11.refs_0_), channel_id=1, source_target_pairs={{0,1},{1,0},{2,3},{3,2},{4,5},{5,4},{6,7},{7,6},{8,9},{9,8},{10,11... | collective-permute-start | bytes 3538952 | tf_op jit(solution)/shard_map/ppermute | solution.py:850
  172.7 19.8 %collective-permute-start.31 = (bf16[2,8,96,384]{3,2,1,0:T(8,128)(2,1)}, bf16[2,8,96,384]{3,2,1,0:T(8,128)(2,1)}, u32[]{:S(2)}, u32[]{:S(2)}) collective-permute-start(bf16[2,8,96,384]{3,2,1,0:T(8,128)(2,1)} %bitcast.103.refs_1_), channel_id=1, source_target_pairs={{0,1},{1,0},{2,3},{3,2},{4,5},{5,4},{6,7},{7,6},{8,9},{9,8},{10,11... | collective-permute-start | bytes 3538952 | tf_op jit(solution)/shard_map/ppermute | solution.py:850
  192.5 11.6 %collective-permute-start.32 = (bf16[2,8,128,384]{3,2,1,0:T(8,128)(2,1)S(1)}, bf16[2,8,128,384]{3,2,1,0:T(8,128)(2,1)}, u32[]{:S(2)}, u32[]{:S(2)}) collective-permute-start(bf16[2,8,128,384]{3,2,1,0:T(8,128)(2,1)S(1)} %pad_maximum_fusion.3.refs_2_), channel_id=1, source_target_pairs={{0,1},{1,0},{2,3},{3,2},{4,5},{5,4},{6,7},{7,6},{8,9},{9,8},{10,11... | collective-permute-start | bytes 4718600 | tf_op jit(solution)/shard_map/ppermute | solution.py:850
  193.1 11.1 %collective-permute-start.33 = (bf16[2,8,128,384]{3,2,1,0:T(8,128)(2,1)S(1)}, bf16[2,8,128,384]{3,2,1,0:T(8,128)(2,1)}, u32[]{:S(2)}, u32[]{:S(2)}) collective-permute-start(bf16[2,8,128,384]{3,2,1,0:T(8,128)(2,1)S(1)} %bitcast.511), channel_id=1, source_target_pairs={{0,1},{1,0},{2,3},{3,2},{4,5},{5,4},{6,7},{7,6},{8,9},{9,8},{10,11... | collective-permute-start | bytes 4718600 | tf_op jit(solution)/shard_map/ppermute | solution.py:850
  255.6 21.0 %collective-permute-start.40 = (bf16[2,768,768]{2,1,0:T(8,128)(2,1)}, bf16[2,768,768]{2,1,0:T(8,128)(2,1)S(1)}, u32[]{:S(2)}, u32[]{:S(2)}) collective-permute-start(bf16[2,768,768]{2,1,0:T(8,128)(2,1)} %get-tuple-element.398), channel_id=1, source_target_pairs={{0,1},{1,0},{2,3},{3,2},{4,5},{5,4},{6,7},{7,6},{8,9},{9,8},{10,11... | collective-permute-start | bytes 7077896 | tf_op jit(solution)/shard_map/ppermute | solution.py:850
  255.7 20.9 %collective-permute-start.41 = (bf16[2,768,768]{2,1,0:T(8,128)(2,1)}, bf16[2,768,768]{2,1,0:T(8,128)(2,1)}, u32[]{:S(2)}, u32[]{:S(2)}) collective-permute-start(bf16[2,768,768]{2,1,0:T(8,128)(2,1)} %get-tuple-element.399), channel_id=1, source_target_pairs={{0,1},{1,0},{2,3},{3,2},{4,5},{5,4},{6,7},{7,6},{8,9},{9,8},{10,11... | collective-permute-start | bytes 7077896 | tf_op jit(solution)/shard_map/ppermute | solution.py:850
  279.4 34.8 %collective-permute-start.42 = (bf16[8,96,768]{2,1,0:T(8,128)(2,1)}, bf16[8,96,768]{2,1,0:T(8,128)(2,1)}, u32[]{:S(2)}, u32[]{:S(2)}) collective-permute-start(bf16[8,96,768]{2,1,0:T(8,128)(2,1)} %fusion), channel_id=1, source_target_pairs={{0,2},{1,3},{2,0},{3,1},{4,6},{5,7},{6,4},{7,5},{8,10},{9,11},{10,... | collective-permute-start | bytes 3538952 | tf_op jit(solution)/shard_map/ppermute | solution.py:850
  283.5 30.7 %collective-permute-start.43 = (bf16[2,4,96,768]{3,2,1,0:T(8,128)(2,1)}, bf16[2,4,96,768]{3,2,1,0:T(8,128)(2,1)}, u32[]{:S(2)}, u32[]{:S(2)}) collective-permute-start(bf16[2,4,96,768]{3,2,1,0:T(8,128)(2,1)} %fusion.1), channel_id=1, source_target_pairs={{0,4},{1,5},{2,6},{3,7},{4,0},{5,1},{6,2},{7,3},{8,12},{9,13},{10,... | collective-permute-start | bytes 3538952 | tf_op jit(solution)/shard_map/ppermute | solution.py:850
  315.5 34.2 %collective-permute-start.44 = (bf16[4,96,768]{2,1,0:T(8,128)(2,1)S(1)}, bf16[4,96,768]{2,1,0:T(8,128)(2,1)S(1)}, u32[]{:S(2)}, u32[]{:S(2)}) collective-permute-start(bf16[4,96,768]{2,1,0:T(8,128)(2,1)S(1)} %fusion.5), channel_id=1, source_target_pairs={{0,4},{1,5},{2,6},{3,7},{4,0},{5,1},{6,2},{7,3},{8,12},{9,13},{10,... | collective-permute-start | bytes 1769480 | tf_op jit(solution)/shard_map/ppermute | solution.py:850
  317.5 32.1 %collective-permute-start.45 = (bf16[4,96,768]{2,1,0:T(8,128)(2,1)S(1)}, bf16[4,96,768]{2,1,0:T(8,128)(2,1)S(1)}, u32[]{:S(2)}, u32[]{:S(2)}) collective-permute-start(bf16[4,96,768]{2,1,0:T(8,128)(2,1)S(1)} %fusion.4), channel_id=1, source_target_pairs={{0,2},{1,3},{2,0},{3,1},{4,6},{5,7},{6,4},{7,5},{8,10},{9,11},{10,... | collective-permute-start | bytes 1769480 | tf_op jit(solution)/shard_map/ppermute | solution.py:850
  318.1 31.6 %collective-permute-start.46 = (bf16[2,768,768]{2,1,0:T(8,128)(2,1)}, bf16[2,768,768]{2,1,0:T(8,128)(2,1)S(1)}, u32[]{:S(2)}, u32[]{:S(2)}) collective-permute-start(bf16[2,768,768]{2,1,0:T(8,128)(2,1)} %get-tuple-element.423), channel_id=1, source_target_pairs={{0,1},{1,0},{2,3},{3,2},{4,5},{5,4},{6,7},{7,6},{8,9},{9,8},{10,11... | collective-permute-start | bytes 7077896 | tf_op jit(solution)/shard_map/ppermute | solution.py:850
  353.9 10.6 %collective-permute-start.48 = (bf16[208,768]{1,0:T(8,128)(2,1)}, bf16[208,768]{1,0:T(8,128)(2,1)S(1)}, u32[]{:S(2)}, u32[]{:S(2)}) collective-permute-start(bf16[208,768]{1,0:T(8,128)(2,1)} %get-tuple-element.429), channel_id=1, source_target_pairs={{0,2},{1,3},{2,0},{3,1},{4,6},{5,7},{6,4},{7,5},{8,10},{9,11},{10,... | collective-permute-start | bytes 958472 | tf_op jit(solution)/shard_map/ppermute | solution.py:850
  355.4 14.2 %collective-permute-start.49 = (bf16[208,768]{1,0:T(8,128)(2,1)S(1)}, bf16[208,768]{1,0:T(8,128)(2,1)S(1)}, u32[]{:S(2)}, u32[]{:S(2)}) collective-permute-start(bf16[208,768]{1,0:T(8,128)(2,1)S(1)} %get-tuple-element.430), channel_id=1, source_target_pairs={{0,3},{1,2},{2,1},{3,0},{4,7},{5,6},{6,5},{7,4},{8,11},{9,10},{10,... | collective-permute-start | bytes 958472 | tf_op jit(solution)/shard_map/ppermute | solution.py:850
  356.7 28.5 %collective-permute-start.50 = (bf16[2,4,96,768]{3,2,1,0:T(8,128)(2,1)S(1)}, bf16[2,4,96,768]{3,2,1,0:T(8,128)(2,1)S(1)}, u32[]{:S(2)}, u32[]{:S(2)}) collective-permute-start(bf16[2,4,96,768]{3,2,1,0:T(8,128)(2,1)S(1)} %fusion.2), channel_id=1, source_target_pairs={{0,4},{1,5},{2,6},{3,7},{4,0},{5,1},{6,2},{7,3},{8,12},{9,13},{10,... | collective-permute-start | bytes 3538952 | tf_op jit(solution)/shard_map/ppermute | solution.py:850
  385.2 29.6 %collective-permute-start.51 = (bf16[2,768,768]{2,1,0:T(8,128)(2,1)}, bf16[2,768,768]{2,1,0:T(8,128)(2,1)}, u32[]{:S(2)}, u32[]{:S(2)}) collective-permute-start(bf16[2,768,768]{2,1,0:T(8,128)(2,1)} %get-tuple-element.443), channel_id=1, source_target_pairs={{0,1},{1,0},{2,3},{3,2},{4,5},{5,4},{6,7},{7,6},{8,9},{9,8},{10,11... | collective-permute-start | bytes 7077896 | tf_op jit(solution)/shard_map/ppermute | solution.py:850
  389.1 22.0 %collective-permute-start.53 = (bf16[1,192,768]{2,1,0:T(8,128)(2,1)S(1)}, bf16[1,192,768]{2,1,0:T(8,128)(2,1)S(1)}, u32[]{:S(2)}, u32[]{:S(2)}) collective-permute-start(bf16[1,192,768]{2,1,0:T(8,128)(2,1)S(1)} %pad_maximum_fusion.28), channel_id=1, source_target_pairs={{0,8},{1,9},{2,10},{3,11},{4,12},{5,13},{6,14},{7,15},{8,0},{9,1},... | collective-permute-start | bytes 884744 | tf_op jit(solution)/shard_map/ppermute | solution.py:850
  391.2 23.5 %collective-permute-start.54 = (bf16[1,192,768]{2,1,0:T(8,128)(2,1)S(1)}, bf16[1,192,768]{2,1,0:T(8,128)(2,1)S(1)}, u32[]{:S(2)}, u32[]{:S(2)}) collective-permute-start(bf16[1,192,768]{2,1,0:T(8,128)(2,1)S(1)} %pad_maximum_fusion.29), channel_id=1, source_target_pairs={{0,16},{1,17},{2,18},{3,19},{4,20},{5,21},{6,22},{7,23},{8,24},{9,... | collective-permute-start | bytes 884744 | tf_op jit(solution)/shard_map/ppermute | solution.py:850
  392.2 22.5 %collective-permute-start.55 = (bf16[1,192,768]{2,1,0:T(8,128)(2,1)S(1)}, bf16[1,192,768]{2,1,0:T(8,128)(2,1)S(1)}, u32[]{:S(2)}, u32[]{:S(2)}) collective-permute-start(bf16[1,192,768]{2,1,0:T(8,128)(2,1)S(1)} %pad_maximum_fusion.30), channel_id=1, source_target_pairs={{0,24},{1,25},{2,26},{3,27},{4,28},{5,29},{6,30},{7,31},{8,16},{9,... | collective-permute-start | bytes 884744 | tf_op jit(solution)/shard_map/ppermute | solution.py:850
  395.2 19.5 %collective-permute-start.52 = (bf16[4,96,768]{2,1,0:T(8,128)(2,1)S(1)}, bf16[4,96,768]{2,1,0:T(8,128)(2,1)S(1)}, u32[]{:S(2)}, u32[]{:S(2)}) collective-permute-start(bf16[4,96,768]{2,1,0:T(8,128)(2,1)S(1)} %fusion.3), channel_id=1, source_target_pairs={{0,2},{1,3},{2,0},{3,1},{4,6},{5,7},{6,4},{7,5},{8,10},{9,11},{10,... | collective-permute-start | bytes 1769480 | tf_op jit(solution)/shard_map/ppermute | solution.py:850
  420.3 21.7 %collective-permute-start.56 = (bf16[8,96,384]{2,1,0:T(8,128)(2,1)}, bf16[8,96,384]{2,1,0:T(8,128)(2,1)}, u32[]{:S(2)}, u32[]{:S(2)}) collective-permute-start(bf16[8,96,384]{2,1,0:T(8,128)(2,1)} %fusion.6), channel_id=1, source_target_pairs={{0,2},{1,3},{2,0},{3,1},{4,6},{5,7},{6,4},{7,5},{8,10},{9,11},{10,... | collective-permute-start | bytes 1769480 | tf_op jit(solution)/shard_map/ppermute | solution.py:850
  421.9 20.1 %collective-permute-start.57 = (bf16[2,4,96,384]{3,2,1,0:T(8,128)(2,1)}, bf16[2,4,96,384]{3,2,1,0:T(8,128)(2,1)}, u32[]{:S(2)}, u32[]{:S(2)}) collective-permute-start(bf16[2,4,96,384]{3,2,1,0:T(8,128)(2,1)} %fusion.7), channel_id=1, source_target_pairs={{0,4},{1,5},{2,6},{3,7},{4,0},{5,1},{6,2},{7,3},{8,12},{9,13},{10,... | collective-permute-start | bytes 1769480 | tf_op jit(solution)/shard_map/ppermute | solution.py:850
  425.5 41.9 %collective-permute-start.62 = (bf16[1,96,768]{2,1,0:T(8,128)(2,1)}, bf16[1,96,768]{2,1,0:T(8,128)(2,1)S(1)}, u32[]{:S(2)}, u32[]{:S(2)}) collective-permute-start(bf16[1,96,768]{2,1,0:T(8,128)(2,1)} %get-tuple-element.534), channel_id=1, source_target_pairs={{0,8},{1,9},{2,10},{3,11},{4,12},{5,13},{6,14},{7,15},{8,0},{9,1},... | collective-permute-start | bytes 442376 | tf_op jit(solution)/shard_map/ppermute | solution.py:850
  431.5 35.9 %collective-permute-start.63 = (bf16[1,96,768]{2,1,0:T(8,128)(2,1)}, bf16[1,96,768]{2,1,0:T(8,128)(2,1)}, u32[]{:S(2)}, u32[]{:S(2)}) collective-permute-start(bf16[1,96,768]{2,1,0:T(8,128)(2,1)} %get-tuple-element.533), channel_id=1, source_target_pairs={{0,16},{1,17},{2,18},{3,19},{4,20},{5,21},{6,22},{7,23},{8,24},{9,... | collective-permute-start | bytes 442376 | tf_op jit(solution)/shard_map/ppermute | solution.py:850
  442.0 5.9 %collective-permute-start.58 = (bf16[16,24,896]{2,1,0:T(8,128)(2,1)S(1)}, bf16[16,24,896]{2,1,0:T(8,128)(2,1)S(1)}, u32[]{:S(2)}, u32[]{:S(2)}) collective-permute-start(bf16[16,24,896]{2,1,0:T(8,128)(2,1)S(1)} %get-tuple-element.465), channel_id=1, source_target_pairs={{0,1},{1,0},{2,3},{3,2},{4,5},{5,4},{6,7},{7,6},{8,9},{9,8},{10,11... | collective-permute-start | bytes 2064392 | tf_op jit(solution)/shard_map/ppermute | solution.py:850
  448.8 8.8 %collective-permute-start.59 = (bf16[4,96,384]{2,1,0:T(8,128)(2,1)S(1)}, bf16[4,96,384]{2,1,0:T(8,128)(2,1)S(1)}, u32[]{:S(2)}, u32[]{:S(2)}) collective-permute-start(bf16[4,96,384]{2,1,0:T(8,128)(2,1)S(1)} %fusion.15), channel_id=1, source_target_pairs={{0,4},{1,5},{2,6},{3,7},{4,0},{5,1},{6,2},{7,3},{8,12},{9,13},{10,... | collective-permute-start | bytes 884744 | tf_op jit(solution)/shard_map/ppermute | solution.py:850
  449.3 10.6 %collective-permute-start.60 = (bf16[4,96,384]{2,1,0:T(8,128)(2,1)S(1)}, bf16[4,96,384]{2,1,0:T(8,128)(2,1)S(1)}, u32[]{:S(2)}, u32[]{:S(2)}) collective-permute-start(bf16[4,96,384]{2,1,0:T(8,128)(2,1)S(1)} %fusion.10), channel_id=1, source_target_pairs={{0,2},{1,3},{2,0},{3,1},{4,6},{5,7},{6,4},{7,5},{8,10},{9,11},{10,... | collective-permute-start | bytes 884744 | tf_op jit(solution)/shard_map/ppermute | solution.py:850
  449.8 15.4 %collective-permute-start.61 = (bf16[8,24,896]{2,1,0:T(8,128)(2,1)S(1)}, bf16[8,24,896]{2,1,0:T(8,128)(2,1)S(1)}, u32[]{:S(2)}, u32[]{:S(2)}) collective-permute-start(bf16[8,24,896]{2,1,0:T(8,128)(2,1)S(1)} %fusion.14), channel_id=1, source_target_pairs={{0,2},{1,3},{2,0},{3,1},{4,6},{5,7},{6,4},{7,5},{8,10},{9,11},{10,... | collective-permute-start | bytes 1032200 | tf_op jit(solution)/shard_map/ppermute | solution.py:850
  457.5 9.9 %collective-permute-start.64 = (bf16[1,96,768]{2,1,0:T(8,128)(2,1)S(1)}, bf16[1,96,768]{2,1,0:T(8,128)(2,1)S(1)}, u32[]{:S(2)}, u32[]{:S(2)}) collective-permute-start(bf16[1,96,768]{2,1,0:T(8,128)(2,1)S(1)} %copy-done.53), channel_id=1, source_target_pairs={{0,24},{1,25},{2,26},{3,27},{4,28},{5,29},{6,30},{7,31},{8,16},{9,... | collective-permute-start | bytes 442376 | tf_op jit(solution)/shard_map/ppermute | solution.py:850
  468.2 11.4 %collective-permute-start.65 = (bf16[1,96,768]{2,1,0:T(8,128)(2,1)}, bf16[1,96,768]{2,1,0:T(8,128)(2,1)S(1)}, u32[]{:S(2)}, u32[]{:S(2)}) collective-permute-start(bf16[1,96,768]{2,1,0:T(8,128)(2,1)} %get-tuple-element.486), channel_id=1, source_target_pairs={{0,8},{1,9},{2,10},{3,11},{4,12},{5,13},{6,14},{7,15},{8,0},{9,1},... | collective-permute-start | bytes 442376 | tf_op jit(solution)/shard_map/ppermute | solution.py:850
  469.5 13.4 %collective-permute-start.66 = (bf16[1,96,768]{2,1,0:T(8,128)(2,1)S(1)}, bf16[1,96,768]{2,1,0:T(8,128)(2,1)S(1)}, u32[]{:S(2)}, u32[]{:S(2)}) collective-permute-start(bf16[1,96,768]{2,1,0:T(8,128)(2,1)S(1)} %get-tuple-element.487), channel_id=1, source_target_pairs={{0,16},{1,17},{2,18},{3,19},{4,20},{5,21},{6,22},{7,23},{8,24},{9,... | collective-permute-start | bytes 442376 | tf_op jit(solution)/shard_map/ppermute | solution.py:850
  471.3 11.6 %collective-permute-start.67 = (bf16[1,96,768]{2,1,0:T(8,128)(2,1)S(1)}, bf16[1,96,768]{2,1,0:T(8,128)(2,1)S(1)}, u32[]{:S(2)}, u32[]{:S(2)}) collective-permute-start(bf16[1,96,768]{2,1,0:T(8,128)(2,1)S(1)} %get-tuple-element.488), channel_id=1, source_target_pairs={{0,24},{1,25},{2,26},{3,27},{4,28},{5,29},{6,30},{7,31},{8,16},{9,... | collective-permute-start | bytes 442376 | tf_op jit(solution)/shard_map/ppermute | solution.py:850
  472.7 10.2 %collective-permute-start.68 = (bf16[4,24,896]{2,1,0:T(8,128)(2,1)S(1)}, bf16[4,24,896]{2,1,0:T(8,128)(2,1)S(1)}, u32[]{:S(2)}, u32[]{:S(2)}) collective-permute-start(bf16[4,24,896]{2,1,0:T(8,128)(2,1)S(1)} %fusion.58), channel_id=1, source_target_pairs={{0,4},{1,5},{2,6},{3,7},{4,0},{5,1},{6,2},{7,3},{8,12},{9,13},{10,... | collective-permute-start | bytes 516104 | tf_op jit(solution)/shard_map/ppermute | solution.py:850
  483.0 6.8 %collective-permute-start.69 = (bf16[1,24,896]{2,1,0:T(8,128)(2,1)S(1)}, bf16[1,24,896]{2,1,0:T(8,128)(2,1)S(1)}, u32[]{:S(2)}, u32[]{:S(2)}) collective-permute-start(bf16[1,24,896]{2,1,0:T(8,128)(2,1)S(1)} %get-tuple-element.494), channel_id=1, source_target_pairs={{0,8},{1,9},{2,10},{3,11},{4,12},{5,13},{6,14},{7,15},{8,0},{9,1},... | collective-permute-start | bytes 129032 | tf_op jit(solution)/shard_map/ppermute | solution.py:850
  485.2 5.8 %collective-permute-start.70 = (bf16[1,24,896]{2,1,0:T(8,128)(2,1)S(1)}, bf16[1,24,896]{2,1,0:T(8,128)(2,1)S(1)}, u32[]{:S(2)}, u32[]{:S(2)}) collective-permute-start(bf16[1,24,896]{2,1,0:T(8,128)(2,1)S(1)} %get-tuple-element.495), channel_id=1, source_target_pairs={{0,16},{1,17},{2,18},{3,19},{4,20},{5,21},{6,22},{7,23},{8,24},{9,... | collective-permute-start | bytes 129032 | tf_op jit(solution)/shard_map/ppermute | solution.py:850
  486.4 5.9 %collective-permute-start.71 = (bf16[1,24,896]{2,1,0:T(8,128)(2,1)S(1)}, bf16[1,24,896]{2,1,0:T(8,128)(2,1)S(1)}, u32[]{:S(2)}, u32[]{:S(2)}) collective-permute-start(bf16[1,24,896]{2,1,0:T(8,128)(2,1)S(1)} %get-tuple-element.496), channel_id=1, source_target_pairs={{0,24},{1,25},{2,26},{3,27},{4,28},{5,29},{6,30},{7,31},{8,16},{9,... | collective-permute-start | bytes 129032 | tf_op jit(solution)/shard_map/ppermute | solution.py:850
  (79 other events, 320.1 us)

commit v5 on v4

--- a/solution.py
+++ b/solution.py
@@ -449,8 +449,11 @@
     out_ref[:, dim : dim + 128] = low(padded.T)
 
 
-def enter_frame_kernel(start_ref, mixed_ref, weight_ref, norms_ref, out_ref, normed_ref):
-    out_ref[...] = start_ref[...] + dot(mixed_ref[...], weight_ref[...], NT)
+def enter_frame_kernel(start_ref, *refs):
+    parts, (weight_ref, norms_ref, out_ref, normed_ref, mixed) = refs[:FRAMES], refs[FRAMES:]
+    for f in range(FRAMES):
+        mixed[frame_rows(f), :] = parts[f][...]
+    out_ref[...] = start_ref[...] + dot(mixed[...], weight_ref[...], NT)
     for f in range(FRAMES):
         rows = frame_rows(f)
         normed_ref[rows, :] = low(
@@ -623,12 +626,61 @@
     return inputs, specs
 
 
-def block_call(kernel, name, before, parts, rows, rest, outputs, scratch, gflops):
+def with_fetches(kernel, places):
+    def wrapped(*refs):
+        *refs, sems = refs
+        buffers = refs[len(refs) - len(places) :]
+        refs = list(refs[: len(refs) - len(places)])
+        copies = [
+            pltpu.make_async_copy(refs[at], buffer, sems.at[i])
+            for i, (at, buffer) in enumerate(zip(places, buffers))
+        ]
+
+        @pl.when(pl.program_id(0) == 0)
+        def _():
+            for copy in copies:
+                copy.start()
+
+        @pl.when(pl.program_id(0) == 1)
+        def _():
+            for copy in copies:
+                copy.wait()
+
+        for at, buffer in zip(places, buffers):
+            refs[at] = buffer
+        kernel(*refs)
+
+    return wrapped
+
+
+def block_call(kernel, name, before, parts, rows, rest, outputs, scratch, gflops, later=False):
     parts, specs = weight_specs(parts, rows)
     specs = [spec_of(v) for v in before] + specs + [spec_of(v) for v in rest]
-    return call(
-        kernel, name, (*before, *parts, *rest), outputs, scratch, gflops, in_specs=specs
-    )
+    inputs = (*before, *parts, *rest)
+    if not later:
+        return call(kernel, name, inputs, outputs, scratch, gflops, in_specs=specs)
+    places = [
+        i
+        for i, value in enumerate(inputs)
+        if value.dtype == SINGLE and value.shape == (ROWS, inputs[0].shape[1])
+    ]
+    for at in places:
+        specs[at] = pl.BlockSpec(memory_space=pl.ANY)
+    scratch = [pltpu.VMEM(shape, dtype) for shape, dtype in scratch]
+    scratch += [pltpu.VMEM(inputs[at].shape, SINGLE) for at in places]
+    return pl.pallas_call(
+        with_fetches(kernel, places),
+        grid=(2,),
+        in_specs=specs,
+        out_specs=[spec_of(value) for value in outputs],
+        out_shape=list(outputs),
+        scratch_shapes=scratch + [pltpu.SemaphoreType.DMA((len(places),))],
+        compiler_params=pltpu.CompilerParams(vmem_limit_bytes=GRANT),
+        cost_estimate=pl.CostEstimate(
+            flops=gflops * 10**9, bytes_accessed=8 << 20, transcendentals=0
+        ),
+        name=name,
+    )(*inputs)
 
 
 def temporal_forward(normed, own, other, rows):
@@ -681,7 +733,7 @@
         outputs += (shaped(ROWS, dim, dtype=LOWER),)
     rest = (key_extra, *(last or ()))
     return block_call(
-        kernel, "spatial_forward", (normed,), parts, rows, rest, outputs, scratch, 15
+        kernel, "spatial_forward", (normed,), parts, rows, rest, outputs, scratch, 15, last is not None
     )
 
 
@@ -694,7 +746,7 @@
         outputs = (by_group(dim, dim), shaped(ROWS, dim, dtype=LOWER), shaped(2, dim))
     rest = (qkv, mixed, extra, key_extra, *(last or ()))
     return block_call(
-        kernel, "spatial_backward", (normed, grad), parts, rows, rest, outputs, scratch, 30
+        kernel, "spatial_backward", (normed, grad), parts, rows, rest, outputs, scratch, 30, last is not None
     )
 
 
@@ -706,7 +758,7 @@
         kernel, scratch = feed_fwd_last_kernel, [((ROWS, dim), SINGLE)]
         outputs += (shaped(1, dim),)
     return block_call(
-        kernel, "feed_forward", (normed,), parts, rows, last or (), outputs, scratch, 10
+        kernel, "feed_forward", (normed,), parts, rows, last or (), outputs, scratch, 10, last is not None
     )
 
 
@@ -719,7 +771,7 @@
         outputs += (shaped(ROWS, dim, dtype=LOWER), shaped(2, dim))
     rest = (act, slope, *(last or ()))
     return block_call(
-        kernel, "feed_backward", (normed, grad), parts, rows, rest, outputs, scratch, 15
+        kernel, "feed_backward", (normed, grad), parts, rows, rest, outputs, scratch, 15, last is not None
     )
 
 
@@ -742,14 +794,14 @@
     )[0]
 
 
-def enter_frame(start, mixed, weight, norms):
+def enter_frame(start, parts, weight, norms):
     dim = start.shape[1]
     return call(
         enter_frame_kernel,
         "enter_frame",
-        (start, mixed, weight, norms),
+        (start, *parts, weight, norms),
         (shaped(ROWS, dim), shaped(ROWS, dim, dtype=LOWER)),
-        [],
+        [((ROWS, dim), LOWER)],
         2,
         1,
     )
@@ -860,9 +912,14 @@
     def fork(self, value):
         return self.stack(value, self.swap(value, 2), 2)
 
-    def step(self, token, sends, late=(), work=None):
+    def step(self, token, sends, late=(), work=None, hold=None, beside=None):
         values = [value for value, _ in (*sends, *late)]
-        *values, token = tick(*values, token)
+        count = len(values)
+        *values, token = tick(*values, *(hold or ()), token)
+        if hold is not None:
+            hold[:] = values[count:]
+        values = values[:count]
+        extra = beside(*hold) if beside is not None else []
         masks = [mask for _, mask in (*sends, *late)]
         received = [self.swap(value, mask) for value, mask in zip(values, masks)]
         count = len(sends)
@@ -870,8 +927,10 @@
             *done, paced = finish(token, work)
             *ended, token = tick(*received[:count], paced)
             return token, done, *ended, *received[count:]
-        *ended, token = tick(*received[:count], pace(token))
-        return token, *ended, *received[count:]
+        results = tick(*received[:count], *extra, pace(token))
+        if extra:
+            hold[:] = results[count:-1]
+        return results[-1], *results[:count], *received[count:]
 
 
     def quads(self):
@@ -1045,7 +1104,9 @@
     )
     first_w = tuple([(part, None) for part in parts] for parts in (own_first, other_first))
     qkv_t, mixed_t = temporal_forward(normed_t, *first_w, rows_wide)
-    mixed_t, other_left, other_right = tick(mixed_t, other_left, other_right)
+    mixed_t, other_left, other_right, other_down = tick(
+        mixed_t, other_left, other_right, other_down
+    )
     parts = [
         jnp.concatenate(
             [mixed_t[2 * (c ^ (r & 1)) + y][frame_rows(r)] for c in range(2) for y in range(2)],
@@ -1053,7 +1114,13 @@
         )
         for r in range(FRAMES)
     ]
-    parts[0], other_down, patch_copy, token = tick(parts[0], other_down, patch_copy, token)
+    down_w = cube.join(cube.merge(down_w, other_down, first[0]), *first[1:])
+
+    hold = [other_left, other_right, patch_copy]
+    token, *received, other = cube.step(
+        token, [(parts[r], r) for r in range(1, FRAMES)] + [(down_w, near)], hold=hold
+    )
+    other_left, other_right, patch_copy = hold
     outs = [
         part[y, :, :rows_wide, GROUP:].reshape(dim, GROUP)
         for part in (own_first[1], other_first[1])
@@ -1068,18 +1135,12 @@
         ],
         axis=-1,
     )
-    down_w = cube.join(cube.merge(down_w, other_down, first[0]), *first[1:])
-
-    token, *received, other = cube.step(
-        token, [(parts[r], r) for r in range(1, FRAMES)] + [(down_w, near)]
-    )
     down_w = cube.merge(down_w, other, near)
-    mixed_frame = jnp.concatenate([parts[0], *received])
-    mixed_frame, key_extra, own_second, down_w, out_first, start_frame = tick(
-        mixed_frame, key_extra, own_second, down_w, out_first, start_frame
-    )
-
-    resid_one, normed_s = enter_frame(start_frame, mixed_frame, out_first, norms)
+    key_extra, own_second, down_w, out_first, start_frame = tick(
+        key_extra, own_second, down_w, out_first, start_frame
+    )
+
+    resid_one, normed_s = enter_frame(start_frame, [parts[0], *received], out_first, norms)
     other_second = cube.swap(own_second, 1)
     other_left = cube.swap(left[..., theirs, :], 2)
     other_right = cube.swap(right[..., theirs, :], last)
@@ -1180,15 +1241,25 @@
 
     parts = split_frames(d_rows)
     send, sum_second = cube.cut([blocked(second_own), blocked(core_second)], last)
+    def to_quarters(up_last, down_last):
+        up, down = sum_up[:-1] + [up_last], sum_down[:-1] + [down_last]
+        up, down = cube.shed(up, *first[-2::-1]), cube.shed(down, *first[-2::-1])
+        kept.extend([cube.quarter(up)[1], cube.quarter(down)[1]])
+        pairs = zip(cube.quarter(up)[0], cube.quarter(down)[0])
+        return [jnp.concatenate(pair, axis=-2) for pair in pairs]
+
+    kept, hold = [], [sum_up[-1], sum_down[-1]]
     token, *received, other = cube.step(
-        token, [(parts[r], r) for r in range(1, FRAMES)], [(send, last)]
-    )
+        token,
+        [(parts[r], r) for r in range(1, FRAMES)],
+        [(send, last)],
+        hold=hold,
+        beside=to_quarters,
+    )
+    sends, (sum_up, sum_down) = hold, kept
     d_rows = jnp.concatenate([parts[0], *received])
     sum_second.append(other)
 
-    sum_up, sum_down = cube.shed(sum_up, *first[-2::-1]), cube.shed(sum_down, *first[-2::-1])
-    (sends_up, sum_up), (sends_down, sum_down) = cube.quarter(sum_up), cube.quarter(sum_down)
-    sends = [jnp.concatenate(pair, axis=-2) for pair in zip(sends_up, sends_down)]
     others = [cube.swap(send, mask) for send, mask in cube.fourfold(sends)]
     d_first, d_normed = [None, None], [None, None]
     d_first[1], d_normed[1] = temporal_backward(

time: 529 us -> 518 us (0.979)
  Pallas kernels: 234 us -> 226 us
    pallas_call x24 -> x20, Pallas kernels: 228 us -> 145 us  [call(): pl.pallas_call(kernel, grid=(steps,), in_specs=in_specs or [spec_of(value...]
    pallas_call x0 -> x4, Pallas kernels: none -> 75.6 us  [block_call(): pl.pallas_call(with_fetches(kernel, places), grid=(2,), in_specs=specs, o...]
    unnamed x134 -> x138, local copies, waits for them, and re-layouts: 11.3 us -> 12.4 us
where the time goes in v5:
time: 518 us; the launch traced here: 510 us
  Pallas kernels  226 us (44%)
  starting transfers between devices  86.9 us (17%)
  waiting for transfers between devices  81.9 us (16%)
  other arithmetic  61.9 us (12%)
  local copies, waits for them, and re-layouts  39.2 us (8%)
  between operations  10.6 us (2%)
    pallas_call x20, Pallas kernels, call(): pl.pallas_call(kernel, grid=(steps,), in_specs=in_specs or [spec_of(value...  145 us
    ppermute x77, starting transfers between devices, swap(): return lax.ppermute(value, ALL, [(i, i ^ mask) for i in range(self.count)])  86.9 us
    ppermute x77, waiting for transfers between devices, swap(): return lax.ppermute(value, ALL, [(i, i ^ mask) for i in range(self.count)])  81.9 us
    pallas_call x4, Pallas kernels, block_call(): pl.pallas_call(with_fetches(kernel, places), grid=(2,), in_specs=specs, o...  75.6 us
    convert_element_type x24, other arithmetic, low(): return value.astype(LOWER)  24 us
    unnamed x138, local copies, waits for them, and re-layouts  12.4 us
  transfers between devices with their start and end apart: 77, of which 28 were waited for; matrix products, arithmetic and copies ran while one was open for 13% of the time, Pallas kernels for 37%

profile of v5, /device:TPU:0, one launch (start us, length us, event | category | flops | bytes accessed | tf_op | source)
XLA Modules:
  0.0 509.7 jit_solution(15947136277975511362)
XLA Ops:
  5.7 4.1 collective-permute-start
  15.4 1.7 gather_fusion
  20.9 1.6 collective-permute-start.1
  25.9 7.6 %collective-permute-done.3 = bf16[208,768]{1,0:T(8,128)(2,1)S(1)} collective-permute-done((bf16[208,768]{1,0:T(8,128)(2,1)S(1)}, bf16[208,768]{1,0:T(8,128)(2,1)S(1)}, u32[]{:S(2)}, u32[]{:S(2)}) %collective-permute-start.3) | collective-permute-done | bytes 319520 | tf_op jit(solution)/shard_map/ppermute | solution.py:902
  33.5 4.9 collective-permute-done.4
  38.7 1.6 collective-permute-start.5
  44.3 3.1 collective-permute-start.11
  47.5 3.1 collective-permute-done.5
  52.3 1.6 collective-permute-start.7
  56.8 14.8 %collective-permute-done.7 = bf16[8,128,384]{2,1,0:T(8,128)(2,1)S(1)} collective-permute-done((bf16[8,128,384]{2,1,0:T(8,128)(2,1)S(1)}, bf16[8,128,384]{2,1,0:T(8,128)(2,1)S(1)}, u32[]{:S(2)}, u32[]{:S(2)}) %collective-permute-start.7) | collective-permute-done | bytes 786464 | tf_op jit(solution)/shard_map/ppermute | solution.py:902
  83.8 1.8 collective-permute-done.12.other_left.left_ref
  89.5 5.1 %embed.1 = (f32[832,768]{1,0:T(8,128)}, bf16[832,768]{1,0:T(8,128)(2,1)}) custom-call(bf16[832,768]{1,0:T(8,128)(2,1)} %pad_maximum_fusion.5.patches_ref, bf16[768,768]{1,0:T(8,128)(2,1)} %bitcast.532, f32[832,1]{1,0:T(8,128)} %copy.104.valid_ref, f32[8,768]{1,0:T(8,128)} %reshape.1638.norms_ref.refs_5_.refs_6_.refs_7_.refs_11_), custom_call_target="tpu_custom_call" | custom-call | flops 15000000512 | bytes 8388608 | tf_op jit(solution)/shard_map/embed/pallas_call | solution.py:595
  94.6 2.1 collective-permute-done.14
  99.5 1.6 collective-permute-start.17
  101.1 10.7 %temporal_forward.1 = (bf16[4,4,576,208]{3,2,1,0:T(8,128)(2,1)}, bf16[4,832,192]{2,1,0:T(8,128)(2,1)}) custom-call(bf16[832,768]{1,0:T(8,128)(2,1)} %get-tuple-element.447.normed_ref, bf16[2,8,128,384]{3,2,1,0:T(8,128)(2,1)} %pad_maximum_fusion.1.own_left.left_ref, bf16[2,8,128,384]{3,2,1,0:T(8,128)(2,1)} %bitcast.466, ...), custom_call_target="tpu_custom_call" | custom-call | flops 40000000000 | bytes 8388608 | tf_op jit(solution)/shard_map/temporal_forward/pallas_call | solution.py:595
  128.7 2.6 convolution_multiply_fusion.start_ref
  133.1 6.1 %collective-permute-done.21.refs_3_ = bf16[208,768]{1,0:T(8,128)(2,1)} collective-permute-done((bf16[208,768]{1,0:T(8,128)(2,1)}, bf16[208,768]{1,0:T(8,128)(2,1)}, u32[]{:S(2)}, u32[]{:S(2)}) %collective-permute-start.21) | collective-permute-done | bytes 319520 | tf_op jit(solution)/shard_map/ppermute | solution.py:902
  141.1 1.6 collective-permute-start.27
  144.2 5.7 %enter_frame.1 = (f32[832,768]{1,0:T(8,128)}, bf16[832,768]{1,0:T(8,128)(2,1)}) custom-call(f32[832,768]{1,0:T(8,128)} %convolution_multiply_fusion.start_ref, bf16[208,768]{1,0:T(8,128)(2,1)} %pad_maximum_fusion.26.refs_0_, bf16[208,768]{1,0:T(8,128)(2,1)} %collective-permute-done.19.refs_1_, bf16[208,768]{1,0:T(8,128)(2,1)} %collective-permute-done.20.refs_2_, ...), custom_call_target="tpu_custom_call" | custom-call | flops 2000000000 | bytes 8388608 | tf_op jit(solution)/shard_map/enter_frame/pallas_call | solution.py:595
  149.9 15.4 %spatial_forward.2 = (bf16[2,832,576]{2,1,0:T(8,128)(2,1)}, bf16[2,832,192]{2,1,0:T(8,128)(2,1)}, bf16[2,832,192]{2,1,0:T(8,128)(2,1)}, f32[832,768]{1,0:T(8,128)}) custom-call(bf16[832,768]{1,0:T(8,128)(2,1)} %get-tuple-element.415.normed_ref.refs_0_, bf16[2,8,96,768]{3,2,1,0:T(8,128)(2,1)} %copy-done.3, bf16[2,8,96,768]{3,2,1,0:T(8,128)(2,1)} %copy-done.3, ...), custom_call_target="tpu_custom_call" | custom-call | flops 15000000512 | bytes 8388608 | tf_op jit(solution)/shard_map/spatial_forward/pallas_call | solution.py:595
  170.4 17.2 %spatial_forward.3 = (bf16[2,832,576]{2,1,0:T(8,128)(2,1)}, bf16[2,832,192]{2,1,0:T(8,128)(2,1)}, bf16[2,832,192]{2,1,0:T(8,128)(2,1)}, f32[832,768]{1,0:T(8,128)}, bf16[832,768]{1,0:T(8,128)(2,1)}) custom-call(bf16[832,768]{1,0:T(8,128)(2,1)} %get-tuple-element.415.normed_ref.refs_0_, ...), custom_call_target="tpu_custom_call" | custom-call | flops 15000000512 | bytes 8388608 | tf_op jit(solution)/shard_map/spatial_forward/pallas_call | solution.py:671
  190.9 9.9 %feed_forward.2 = (bf16[2,832,768]{2,1,0:T(8,128)(2,1)}, bf16[2,832,768]{2,1,0:T(8,128)(2,1)}, f32[832,768]{1,0:T(8,128)}) custom-call(bf16[832,768]{1,0:T(8,128)(2,1)} %get-tuple-element.391.normed_ref.refs_0_, bf16[2,8,96,384]{3,2,1,0:T(8,128)(2,1)} %copy-done.21, bf16[2,8,96,384]{3,2,1,0:T(8,128)(2,1)} %bitcast.530, bf16[2,8,128,384]{3,2,1,0:T(8,128)(2,1)} %copy-done.10, ...), custom_call_target="tpu_custom_call" | custom-call | flops 10000000000 | bytes 8388608 | tf_op jit(solution)/shard_map/feed_forward/pallas_call | solution.py:595
  200.8 12.0 %feed_forward.3 = (bf16[2,832,768]{2,1,0:T(8,128)(2,1)}, bf16[2,832,768]{2,1,0:T(8,128)(2,1)}, f32[832,768]{1,0:T(8,128)}, f32[1,768]{1,0:T(1,128)}) custom-call(bf16[832,768]{1,0:T(8,128)(2,1)} %get-tuple-element.391.normed_ref.refs_0_, bf16[2,8,96,384]{3,2,1,0:T(8,128)(2,1)} %collective-permute-done.30.refs_1_.refs_0_, bf16[2,8,96,384]{3,2,1,0:T(8,128)(2,1)} %copy-done.67, ...), custom_call_target="tpu_custom_call" | custom-call | flops 10000000000 | bytes 8388608 | tf_op jit(solution)/shard_map/feed_forward/pallas_call | solution.py:671
  219.0 1.7 collective-permute-start.37
  220.7 2.5 collective-permute-start.38
  229.3 7.3 %losses.1 = (f32[1,1]{1,0:T(1,128)}, bf16[8,768]{1,0:T(8,128)(2,1)}, bf16[8,768]{1,0:T(8,128)(2,1)}, f32[832,768]{1,0:T(8,128)}, bf16[832,768]{1,0:T(8,128)(2,1)}, /*index=5*/f32[2,768]{1,0:T(2,128)}) custom-call(s32[1]{0:T(128)} %bitcast.clip_ref, f32[8,896]{1,0:T(8,128)} %squeeze_reshape.3.facts_ref, bf16[768,768]{1,0:T(8,128)(2,1)} %bitcast.474, ...), custom_call_target="tpu_custom_call" | custom-call | flops 1000000000 | bytes 8388608 | tf_op jit(solution)/shard_map/losses/pallas_call | solution.py:595
  236.6 14.2 %feed_backward.2 = (bf16[2,768,768]{2,1,0:T(8,128)(2,1)}, bf16[2,768,768]{2,1,0:T(8,128)(2,1)}, f32[832,768]{1,0:T(8,128)}) custom-call(bf16[832,768]{1,0:T(8,128)(2,1)} %get-tuple-element.391.normed_ref.refs_0_, bf16[832,768]{1,0:T(8,128)(2,1)} %get-tuple-element.392.grad_ref.refs_1_, bf16[2,8,96,384]{3,2,1,0:T(8,128)(2,1)} %collective-permute-done.30.refs_1_.refs_0_, ...), custom_call_target="tpu_custom_call" | custom-call | flops 15000000512 | bytes 8388608 | tf_op jit(solution)/shard_map/feed_backward/pallas_call | solution.py:595
  252.5 17.0 %feed_backward.3 = (bf16[2,768,768]{2,1,0:T(8,128)(2,1)}, bf16[2,768,768]{2,1,0:T(8,128)(2,1)}, f32[832,768]{1,0:T(8,128)}, bf16[832,768]{1,0:T(8,128)(2,1)}, f32[2,768]{1,0:T(2,128)}) custom-call(bf16[832,768]{1,0:T(8,128)(2,1)} %get-tuple-element.391.normed_ref.refs_0_, bf16[832,768]{1,0:T(8,128)(2,1)} %get-tuple-element.392.grad_ref.refs_1_, ...), custom_call_target="tpu_custom_call" | custom-call | flops 15000000512 | bytes 8388608 | tf_op jit(solution)/shard_map/feed_backward/pallas_call | solution.py:671
  269.6 2.7 fusion
  273.9 2.6 fusion.1
  277.9 27.4 %spatial_backward.2 = (bf16[2,768,768]{2,1,0:T(8,128)(2,1)}, f32[832,768]{1,0:T(8,128)}) custom-call(bf16[832,768]{1,0:T(8,128)(2,1)} %get-tuple-element.415.normed_ref.refs_0_, bf16[832,768]{1,0:T(8,128)(2,1)} %get-tuple-element.416.grad_ref.refs_1_, bf16[2,8,96,768]{3,2,1,0:T(8,128)(2,1)} %collective-permute-done.23.refs_1_.refs_2_.left_ref.right_ref, ...), custom_call_target="tpu_custom_call" | custom-call | flops 30000001024 | bytes 8388608 | tf_op jit(solution)/shard_map/spatial_backward/pallas_call | solution.py:595
  305.4 1.6 copy-done.4
  309.0 2.3 fusion.4
  311.8 29.3 %spatial_backward.3 = (bf16[2,768,768]{2,1,0:T(8,128)(2,1)}, bf16[832,768]{1,0:T(8,128)(2,1)}, f32[2,768]{1,0:T(2,128)}) custom-call(bf16[832,768]{1,0:T(8,128)(2,1)} %get-tuple-element.415.normed_ref.refs_0_, bf16[832,768]{1,0:T(8,128)(2,1)} %get-tuple-element.416.grad_ref.refs_1_, bf16[2,8,96,768]{3,2,1,0:T(8,128)(2,1)} %copy-done.3, ...), custom_call_target="tpu_custom_call" | custom-call | flops 30000001024 | bytes 8388608 | tf_op jit(solution)/shard_map/spatial_backward/pallas_call | solution.py:671
  341.1 3.3 fusion.85
  351.8 1.6 fusion.44
  354.2 2.7 collective-permute-done.48
  357.0 5.0 collective-permute-done.49
  361.9 2.4 pad_maximum_fusion.6.grad_ref.drows_ref
  364.3 14.1 %temporal_backward.2 = (bf16[2,768,768]{2,1,0:T(8,128)(2,1)}, f32[832,768]{1,0:T(8,128)}) custom-call(bf16[832,768]{1,0:T(8,128)(2,1)} %get-tuple-element.447.normed_ref, bf16[832,768]{1,0:T(8,128)(2,1)} %pad_maximum_fusion.6.grad_ref.drows_ref, bf16[2,8,128,384]{3,2,1,0:T(8,128)(2,1)} %collective-permute-done.12.other_left.left_ref, ...), custom_call_target="tpu_custom_call" | custom-call | flops 14000000000 | bytes 8388608 | tf_op jit(solution)/shard_map/temporal_backward/pallas_call | solution.py:595
  380.4 2.0 collective-permute-start.53
  384.8 1.6 fusion.3
  386.4 1.6 collective-permute-start.52
  388.0 14.3 %temporal_backward.3 = (bf16[2,768,768]{2,1,0:T(8,128)(2,1)}, f32[832,768]{1,0:T(8,128)}) custom-call(bf16[832,768]{1,0:T(8,128)(2,1)} %get-tuple-element.447.normed_ref, bf16[832,768]{1,0:T(8,128)(2,1)} %pad_maximum_fusion.6.grad_ref.drows_ref, bf16[2,8,128,384]{3,2,1,0:T(8,128)(2,1)} %pad_maximum_fusion.1.own_left.left_ref, ...), custom_call_target="tpu_custom_call" | custom-call | flops 14000000000 | bytes 8388608 | tf_op jit(solution)/shard_map/temporal_backward/pallas_call | solution.py:595
  402.3 3.5 collective-permute-done.54
  406.6 2.1 fusion.82
  414.3 2.3 fusion.38
  416.6 5.3 %collective-permute-start.62 = (bf16[1,96,768]{2,1,0:T(8,128)(2,1)}, bf16[1,96,768]{2,1,0:T(8,128)(2,1)}, u32[]{:S(2)}, u32[]{:S(2)}) collective-permute-start(bf16[1,96,768]{2,1,0:T(8,128)(2,1)} %get-tuple-element.542), channel_id=1, source_target_pairs={{0,8},{1,9},{2,10},{3,11},{4,12},{5,13},{6,14},{7,15},{8,0},{9,1},... | collective-permute-start | bytes 442376 | tf_op jit(solution)/shard_map/ppermute | solution.py:902
  422.5 8.2 %embed_backward.1 = bf16[768,896]{1,0:T(8,128)(2,1)} custom-call(bf16[832,768]{1,0:T(8,128)(2,1)} %pad_maximum_fusion.5.patches_ref, f32[832,768]{1,0:T(8,128)} %get-tuple-element.463.start_ref, f32[832,1]{1,0:T(8,128)} %copy.104.valid_ref, bf16[832,768]{1,0:T(8,128)(2,1)} %pad_maximum_fusion.6.grad_ref.drows_ref, f32[832,768]{1,0:T(8,128)} %get-tuple-element.465.da_ref, ...), custom_call_target="tpu_custom_call" | custom-call | flops 30000001024 | bytes 8388608 | tf_op jit(solution)/shard_map/embed_backward/pallas_call | solution.py:595
  433.8 2.3 fusion.31
  443.0 4.9 collective-permute-done.59
  447.9 2.3 collective-permute-start.64
  450.2 5.3 %collective-permute-done.61 = bf16[8,24,896]{2,1,0:T(8,128)(2,1)S(1)} collective-permute-done((bf16[8,24,896]{2,1,0:T(8,128)(2,1)S(1)}, bf16[8,24,896]{2,1,0:T(8,128)(2,1)S(1)}, u32[]{:S(2)}, u32[]{:S(2)}) %collective-permute-start.61) | collective-permute-done | bytes 344096 | tf_op jit(solution)/shard_map/ppermute | solution.py:902
  459.3 1.8 collective-permute-start.66
  464.0 2.1 fusion.36.refs_0_
  466.1 2.2 finish.1
  469.6 3.1 collective-permute-done.66
  472.8 2.2 collective-permute-start.69
  485.8 1.9 collective-permute-start.73
  487.6 1.7 collective-permute-done.73
  490.0 2.8 collective-permute-start.74
  495.7 2.1 collective-permute-done.75
  499.7 3.1 collective-permute-done.76
  503.5 5.7 %optimizer.1 = (f32[1,1]{1,0:T(1,128)}, f32[24,768]{1,0:T(8,128)}, f32[24,768]{1,0:T(8,128)}, f32[24,768]{1,0:T(8,128)}, f32[8,24]{1,0:T(8,128)}, /*index=5*/f32...) custom-call(f32[1,1]{1,0:T(1,128)S(6)} %add.1307.total_ref, ...), custom_call_target="tpu_custom_call" | custom-call | tf_op jit(solution)/shard_map/optimizer/pallas_call | solution.py:835
  (416 shorter events, 140.9 us)
Async XLA Ops:
  5.7 14.9 %collective-permute-start = (bf16[1,128,768]{2,1,0:T(8,128)(2,1)S(1)}, bf16[1,128,768]{2,1,0:T(8,128)(2,1)S(1)}, u32[]{:S(2)}, u32[]{:S(2)}) collective-permute-start(bf16[1,128,768]{2,1,0:T(8,128)(2,1)S(1)} %fusion.57), channel_id=1, source_target_pairs={{0,16},{1,17},{2,18},{3,19},{4,20},{5,21},{6,22},{7,23},{8,24},{9,... | collective-permute-start | bytes 589832 | tf_op jit(solution)/shard_map/ppermute | solution.py:902
  20.9 17.5 %collective-permute-start.1 = (bf16[2,128,768]{2,1,0:T(8,128)(2,1)S(1)}, bf16[2,128,768]{2,1,0:T(8,128)(2,1)S(1)}, u32[]{:S(2)}, u32[]{:S(2)}) collective-permute-start(bf16[2,128,768]{2,1,0:T(8,128)(2,1)S(1)} %maximum_bitcast_fusion.3), channel_id=1, source_target_pairs={{0,8},{1,9},{2,10},{3,11},{4,12},{5,13},{6,14},{7,15},{8,0},{9,1},... | collective-permute-start | bytes 1179656 | tf_op jit(solution)/shard_map/ppermute | solution.py:902
  23.1 10.4 %collective-permute-start.3 = (bf16[208,768]{1,0:T(8,128)(2,1)S(1)}, bf16[208,768]{1,0:T(8,128)(2,1)S(1)}, u32[]{:S(2)}, u32[]{:S(2)}) collective-permute-start(bf16[208,768]{1,0:T(8,128)(2,1)S(1)} %get-tuple-element.291), channel_id=1, source_target_pairs={{0,2},{1,3},{2,0},{3,1},{4,6},{5,7},{6,4},{7,5},{8,10},{9,11},{10,... | collective-permute-start | bytes 958472 | tf_op jit(solution)/shard_map/ppermute | solution.py:902
  24.6 13.8 %collective-permute-start.4 = (bf16[208,768]{1,0:T(8,128)(2,1)S(1)}, bf16[208,768]{1,0:T(8,128)(2,1)S(1)}, u32[]{:S(2)}, u32[]{:S(2)}) collective-permute-start(bf16[208,768]{1,0:T(8,128)(2,1)S(1)} %get-tuple-element.292), channel_id=1, source_target_pairs={{0,3},{1,2},{2,1},{3,0},{4,7},{5,6},{6,5},{7,4},{8,11},{9,10},{10,... | collective-permute-start | bytes 958472 | tf_op jit(solution)/shard_map/ppermute | solution.py:902
  38.7 11.9 %collective-permute-start.5 = (bf16[4,128,384]{2,1,0:T(8,128)(2,1)S(1)}, bf16[4,128,384]{2,1,0:T(8,128)(2,1)S(1)}, u32[]{:S(2)}, u32[]{:S(2)}) collective-permute-start(bf16[4,128,384]{2,1,0:T(8,128)(2,1)S(1)} %get-tuple-element.299), channel_id=1, source_target_pairs={{0,4},{1,5},{2,6},{3,7},{4,0},{5,1},{6,2},{7,3},{8,12},{9,13},{10,... | collective-permute-start | bytes 1179656 | tf_op jit(solution)/shard_map/ppermute | solution.py:902
  40.3 11.5 %collective-permute-start.6 = (bf16[4,128,384]{2,1,0:T(8,128)(2,1)S(1)}, bf16[4,128,384]{2,1,0:T(8,128)(2,1)S(1)}, u32[]{:S(2)}, u32[]{:S(2)}) collective-permute-start(bf16[4,128,384]{2,1,0:T(8,128)(2,1)S(1)} %get-tuple-element.300), channel_id=1, source_target_pairs={{0,2},{1,3},{2,0},{3,1},{4,6},{5,7},{6,4},{7,5},{8,10},{9,11},{10,... | collective-permute-start | bytes 1179656 | tf_op jit(solution)/shard_map/ppermute | solution.py:902
  43.1 33.3 %collective-permute-start.9 = (bf16[1,192,768]{2,1,0:T(8,128)(2,1)}, bf16[1,192,768]{2,1,0:T(8,128)(2,1)}, u32[]{:S(2)}, u32[]{:S(2)}) collective-permute-start(bf16[1,192,768]{2,1,0:T(8,128)(2,1)} %maximum_bitcast_fusion.5), channel_id=1, source_target_pairs={{0,8},{1,9},{2,10},{3,11},{4,12},{5,13},{6,14},{7,15},{8,0},{9,1},... | collective-permute-start | bytes 884744 | tf_op jit(solution)/shard_map/ppermute | solution.py:902
  43.5 32.8 %collective-permute-start.10 = (bf16[1,192,768]{2,1,0:T(8,128)(2,1)}, bf16[1,192,768]{2,1,0:T(8,128)(2,1)}, u32[]{:S(2)}, u32[]{:S(2)}) collective-permute-start(bf16[1,192,768]{2,1,0:T(8,128)(2,1)} %maximum_bitcast_fusion.5), channel_id=1, source_target_pairs={{0,16},{1,17},{2,18},{3,19},{4,20},{5,21},{6,22},{7,23},{8,24},{9,... | collective-permute-start | bytes 884744 | tf_op jit(solution)/shard_map/ppermute | solution.py:902
  44.3 32.0 %collective-permute-start.11 = (bf16[1,192,768]{2,1,0:T(8,128)(2,1)}, bf16[1,192,768]{2,1,0:T(8,128)(2,1)}, u32[]{:S(2)}, u32[]{:S(2)}) collective-permute-start(bf16[1,192,768]{2,1,0:T(8,128)(2,1)} %maximum_bitcast_fusion.5), channel_id=1, source_target_pairs={{0,24},{1,25},{2,26},{3,27},{4,28},{5,29},{6,30},{7,31},{8,16},{9,... | collective-permute-start | bytes 884744 | tf_op jit(solution)/shard_map/ppermute | solution.py:902
  52.3 19.3 %collective-permute-start.7 = (bf16[8,128,384]{2,1,0:T(8,128)(2,1)S(1)}, bf16[8,128,384]{2,1,0:T(8,128)(2,1)S(1)}, u32[]{:S(2)}, u32[]{:S(2)}) collective-permute-start(bf16[8,128,384]{2,1,0:T(8,128)(2,1)S(1)} %bitcast.484), channel_id=1, source_target_pairs={{0,2},{1,3},{2,0},{3,1},{4,6},{5,7},{6,4},{7,5},{8,10},{9,11},{10,... | collective-permute-start | bytes 2359304 | tf_op jit(solution)/shard_map/ppermute | solution.py:902
  53.8 19.0 %collective-permute-start.8 = (bf16[2,4,128,384]{3,2,1,0:T(8,128)(2,1)S(1)}, bf16[2,4,128,384]{3,2,1,0:T(8,128)(2,1)S(1)}, u32[]{:S(2)}, u32[]{:S(2)}) collective-permute-start(bf16[2,4,128,384]{3,2,1,0:T(8,128)(2,1)S(1)} %pad_maximum_fusion.14), channel_id=1, source_target_pairs={{0,4},{1,5},{2,6},{3,7},{4,0},{5,1},{6,2},{7,3},{8,12},{9,13},{10,... | collective-permute-start | bytes 2359304 | tf_op jit(solution)/shard_map/ppermute | solution.py:902
  79.7 5.9 %collective-permute-start.12 = (bf16[2,8,128,384]{3,2,1,0:T(8,128)(2,1)}, bf16[2,8,128,384]{3,2,1,0:T(8,128)(2,1)}, u32[]{:S(2)}, u32[]{:S(2)}) collective-permute-start(bf16[2,8,128,384]{3,2,1,0:T(8,128)(2,1)} %pad_maximum_fusion.1.own_left.left_ref), channel_id=1, source_target_pairs={{0,1},{1,0},{2,3},{3,2},{4,5},{5,4},{6,7},{7,6},{8,9},{9,8},{10,11... | collective-permute-start | bytes 4718600 | tf_op jit(solution)/shard_map/ppermute | solution.py:902
  79.7 5.9 %collective-permute-start.13 = (bf16[2,8,128,384]{3,2,1,0:T(8,128)(2,1)S(1)}, bf16[2,8,128,384]{3,2,1,0:T(8,128)(2,1)}, u32[]{:S(2)}, u32[]{:S(2)}) collective-permute-start(bf16[2,8,128,384]{3,2,1,0:T(8,128)(2,1)S(1)} %bitcast.465), channel_id=1, source_target_pairs={{0,1},{1,0},{2,3},{3,2},{4,5},{5,4},{6,7},{7,6},{8,9},{9,8},{10,11... | collective-permute-start | bytes 4718600 | tf_op jit(solution)/shard_map/ppermute | solution.py:902
  81.2 15.6 %collective-permute-start.14 = (bf16[4,192,384]{2,1,0:T(8,128)(2,1)}, bf16[4,192,384]{2,1,0:T(8,128)(2,1)}, u32[]{:S(2)}, u32[]{:S(2)}) collective-permute-start(bf16[4,192,384]{2,1,0:T(8,128)(2,1)} %get-tuple-element.335), channel_id=1, source_target_pairs={{0,4},{1,5},{2,6},{3,7},{4,0},{5,1},{6,2},{7,3},{8,12},{9,13},{10,... | collective-permute-start | bytes 1769480 | tf_op jit(solution)/shard_map/ppermute | solution.py:902
  81.7 15.3 %collective-permute-start.15 = (bf16[4,192,384]{2,1,0:T(8,128)(2,1)}, bf16[4,192,384]{2,1,0:T(8,128)(2,1)}, u32[]{:S(2)}, u32[]{:S(2)}) collective-permute-start(bf16[4,192,384]{2,1,0:T(8,128)(2,1)} %get-tuple-element.336), channel_id=1, source_target_pairs={{0,2},{1,3},{2,0},{3,1},{4,6},{5,7},{6,4},{7,5},{8,10},{9,11},{10,... | collective-permute-start | bytes 1769480 | tf_op jit(solution)/shard_map/ppermute | solution.py:902
  82.2 33.1 %collective-permute-start.18 = (bf16[1,128,768]{2,1,0:T(8,128)(2,1)}, bf16[1,128,768]{2,1,0:T(8,128)(2,1)}, u32[]{:S(2)}, u32[]{:S(2)}) collective-permute-start(bf16[1,128,768]{2,1,0:T(8,128)(2,1)} %maximum_bitcast_fusion.6), channel_id=1, source_target_pairs={{0,16},{1,17},{2,18},{3,19},{4,20},{5,21},{6,22},{7,23},{8,24},{9,... | collective-permute-start | bytes 589832 | tf_op jit(solution)/shard_map/ppermute | solution.py:902
  98.8 16.5 %collective-permute-start.16 = (bf16[8,96,384]{2,1,0:T(8,128)(2,1)S(1)}, bf16[8,96,384]{2,1,0:T(8,128)(2,1)S(1)}, u32[]{:S(2)}, u32[]{:S(2)}) collective-permute-start(bf16[8,96,384]{2,1,0:T(8,128)(2,1)S(1)} %slice.406), channel_id=1, source_target_pairs={{0,2},{1,3},{2,0},{3,1},{4,6},{5,7},{6,4},{7,5},{8,10},{9,11},{10,... | collective-permute-start | bytes 1769480 | tf_op jit(solution)/shard_map/ppermute | solution.py:902
  99.5 15.8 %collective-permute-start.17 = (bf16[2,4,96,384]{3,2,1,0:T(8,128)(2,1)S(1)}, bf16[2,4,96,384]{3,2,1,0:T(8,128)(2,1)S(1)}, u32[]{:S(2)}, u32[]{:S(2)}) collective-permute-start(bf16[2,4,96,384]{3,2,1,0:T(8,128)(2,1)S(1)} %get-tuple-element.616), channel_id=1, source_target_pairs={{0,4},{1,5},{2,6},{3,7},{4,0},{5,1},{6,2},{7,3},{8,12},{9,13},{10,... | collective-permute-start | bytes 1769480 | tf_op jit(solution)/shard_map/ppermute | solution.py:902
  113.2 53.6 %collective-permute-start.25 = (bf16[2,4,96,384]{3,2,1,0:T(8,128)(2,1)S(1)}, bf16[2,4,96,384]{3,2,1,0:T(8,128)(2,1)S(1)}, u32[]{:S(2)}, u32[]{:S(2)}) collective-permute-start(bf16[2,4,96,384]{3,2,1,0:T(8,128)(2,1)S(1)} %get-tuple-element.615), channel_id=1, source_target_pairs={{0,4},{1,5},{2,6},{3,7},{4,0},{5,1},{6,2},{7,3},{8,12},{9,13},{10,... | collective-permute-start | bytes 1769480 | tf_op jit(solution)/shard_map/ppermute | solution.py:902
  122.5 8.8 %collective-permute-start.19 = (bf16[208,768]{1,0:T(8,128)(2,1)S(1)}, bf16[208,768]{1,0:T(8,128)(2,1)}, u32[]{:S(2)}, u32[]{:S(2)}) collective-permute-start(bf16[208,768]{1,0:T(8,128)(2,1)S(1)} %pad_maximum_fusion.23), channel_id=1, source_target_pairs={{0,1},{1,0},{2,3},{3,2},{4,5},{5,4},{6,7},{7,6},{8,9},{9,8},{10,11... | collective-permute-start | bytes 958472 | tf_op jit(solution)/shard_map/ppermute | solution.py:902
  122.5 10.6 %collective-permute-start.20 = (bf16[208,768]{1,0:T(8,128)(2,1)}, bf16[208,768]{1,0:T(8,128)(2,1)}, u32[]{:S(2)}, u32[]{:S(2)}) collective-permute-start(bf16[208,768]{1,0:T(8,128)(2,1)} %pad_maximum_fusion.24), channel_id=1, source_target_pairs={{0,2},{1,3},{2,0},{3,1},{4,6},{5,7},{6,4},{7,5},{8,10},{9,11},{10,... | collective-permute-start | bytes 958472 | tf_op jit(solution)/shard_map/ppermute | solution.py:902
  124.0 15.2 %collective-permute-start.21 = (bf16[208,768]{1,0:T(8,128)(2,1)}, bf16[208,768]{1,0:T(8,128)(2,1)}, u32[]{:S(2)}, u32[]{:S(2)}) collective-permute-start(bf16[208,768]{1,0:T(8,128)(2,1)} %pad_maximum_fusion.25), channel_id=1, source_target_pairs={{0,3},{1,2},{2,1},{3,0},{4,7},{5,6},{6,5},{7,4},{8,11},{9,10},{10,... | collective-permute-start | bytes 958472 | tf_op jit(solution)/shard_map/ppermute | solution.py:902
  124.3 14.9 %collective-permute-start.22 = (bf16[2,128,768]{2,1,0:T(8,128)(2,1)}, bf16[2,128,768]{2,1,0:T(8,128)(2,1)}, u32[]{:S(2)}, u32[]{:S(2)}) collective-permute-start(bf16[2,128,768]{2,1,0:T(8,128)(2,1)} %maximum_bitcast_fusion.4), channel_id=1, source_target_pairs={{0,8},{1,9},{2,10},{3,11},{4,12},{5,13},{6,14},{7,15},{8,0},{9,1},... | collective-permute-start | bytes 1179656 | tf_op jit(solution)/shard_map/ppermute | solution.py:902
  131.3 35.5 %collective-permute-start.24 = (bf16[8,96,384]{2,1,0:T(8,128)(2,1)S(1)}, bf16[8,96,384]{2,1,0:T(8,128)(2,1)S(1)}, u32[]{:S(2)}, u32[]{:S(2)}) collective-permute-start(bf16[8,96,384]{2,1,0:T(8,128)(2,1)S(1)} %copy-done.33), channel_id=1, source_target_pairs={{0,2},{1,3},{2,0},{3,1},{4,6},{5,7},{6,4},{7,5},{8,10},{9,11},{10,... | collective-permute-start | bytes 1769480 | tf_op jit(solution)/shard_map/ppermute | solution.py:902
  140.4 26.5 %collective-permute-start.23 = (bf16[2,8,96,768]{3,2,1,0:T(8,128)(2,1)S(1)}, bf16[2,8,96,768]{3,2,1,0:T(8,128)(2,1)}, u32[]{:S(2)}, u32[]{:S(2)}) collective-permute-start(bf16[2,8,96,768]{3,2,1,0:T(8,128)(2,1)S(1)} %pad_maximum_fusion.left_ref.right_ref.refs_2_.refs_3_), channel_id=1, source_target_pairs={{0,1},{1,0},{2,3},{3,2},{4,5},{5,4},{6,7},{7,6},{8,9},{9,8},{10,11... | collective-permute-start | bytes 7077896 | tf_op jit(solution)/shard_map/ppermute | solution.py:902
  141.1 24.2 %collective-permute-start.27 = (bf16[4,128,384]{2,1,0:T(8,128)(2,1)S(1)}, bf16[4,128,384]{2,1,0:T(8,128)(2,1)S(1)}, u32[]{:S(2)}, u32[]{:S(2)}) collective-permute-start(bf16[4,128,384]{2,1,0:T(8,128)(2,1)S(1)} %get-tuple-element.636), channel_id=1, source_target_pairs={{0,2},{1,3},{2,0},{3,1},{4,6},{5,7},{6,4},{7,5},{8,10},{9,11},{10,... | collective-permute-start | bytes 1179656 | tf_op jit(solution)/shard_map/ppermute | solution.py:902
  142.7 22.6 %collective-permute-start.26 = (bf16[4,128,384]{2,1,0:T(8,128)(2,1)S(1)}, bf16[4,128,384]{2,1,0:T(8,128)(2,1)}, u32[]{:S(2)}, u32[]{:S(2)}) collective-permute-start(bf16[4,128,384]{2,1,0:T(8,128)(2,1)S(1)} %get-tuple-element.637), channel_id=1, source_target_pairs={{0,4},{1,5},{2,6},{3,7},{4,0},{5,1},{6,2},{7,3},{8,12},{9,13},{10,... | collective-permute-start | bytes 1179656 | tf_op jit(solution)/shard_map/ppermute | solution.py:902
  167.6 20.5 %collective-permute-start.28 = (bf16[8,128,384]{2,1,0:T(8,128)(2,1)S(1)}, bf16[8,128,384]{2,1,0:T(8,128)(2,1)S(1)}, u32[]{:S(2)}, u32[]{:S(2)}) collective-permute-start(bf16[8,128,384]{2,1,0:T(8,128)(2,1)S(1)} %bitcast.482), channel_id=1, source_target_pairs={{0,2},{1,3},{2,0},{3,1},{4,6},{5,7},{6,4},{7,5},{8,10},{9,11},{10,... | collective-permute-start | bytes 2359304 | tf_op jit(solution)/shard_map/ppermute | solution.py:902
  168.2 19.5 %collective-permute-start.29 = (bf16[2,4,128,384]{3,2,1,0:T(8,128)(2,1)S(1)}, bf16[2,4,128,384]{3,2,1,0:T(8,128)(2,1)S(1)}, u32[]{:S(2)}, u32[]{:S(2)}) collective-permute-start(bf16[2,4,128,384]{3,2,1,0:T(8,128)(2,1)S(1)} %pad_maximum_fusion.19), channel_id=1, source_target_pairs={{0,4},{1,5},{2,6},{3,7},{4,0},{5,1},{6,2},{7,3},{8,12},{9,13},{10,... | collective-permute-start | bytes 2359304 | tf_op jit(solution)/shard_map/ppermute | solution.py:902
  169.0 19.6 %collective-permute-start.30 = (bf16[2,8,96,384]{3,2,1,0:T(8,128)(2,1)S(1)}, bf16[2,8,96,384]{3,2,1,0:T(8,128)(2,1)}, u32[]{:S(2)}, u32[]{:S(2)}) collective-permute-start(bf16[2,8,96,384]{3,2,1,0:T(8,128)(2,1)S(1)} %pad_maximum_fusion.10.refs_0_.refs_2_), channel_id=1, source_target_pairs={{0,1},{1,0},{2,3},{3,2},{4,5},{5,4},{6,7},{7,6},{8,9},{9,8},{10,11... | collective-permute-start | bytes 3538952 | tf_op jit(solution)/shard_map/ppermute | solution.py:902
  170.3 18.2 %collective-permute-start.31 = (bf16[2,8,96,384]{3,2,1,0:T(8,128)(2,1)S(1)}, bf16[2,8,96,384]{3,2,1,0:T(8,128)(2,1)S(1)}, u32[]{:S(2)}, u32[]{:S(2)}) collective-permute-start(bf16[2,8,96,384]{3,2,1,0:T(8,128)(2,1)S(1)} %bitcast.529), channel_id=1, source_target_pairs={{0,1},{1,0},{2,3},{3,2},{4,5},{5,4},{6,7},{7,6},{8,9},{9,8},{10,11... | collective-permute-start | bytes 3538952 | tf_op jit(solution)/shard_map/ppermute | solution.py:902
  188.6 12.2 %collective-permute-start.32 = (bf16[2,8,128,384]{3,2,1,0:T(8,128)(2,1)S(1)}, bf16[2,8,128,384]{3,2,1,0:T(8,128)(2,1)}, u32[]{:S(2)}, u32[]{:S(2)}) collective-permute-start(bf16[2,8,128,384]{3,2,1,0:T(8,128)(2,1)S(1)} %pad_maximum_fusion.3.refs_2_.refs_4_), channel_id=1, source_target_pairs={{0,1},{1,0},{2,3},{3,2},{4,5},{5,4},{6,7},{7,6},{8,9},{9,8},{10,11... | collective-permute-start | bytes 4718600 | tf_op jit(solution)/shard_map/ppermute | solution.py:902
  189.1 11.7 %collective-permute-start.33 = (bf16[2,8,128,384]{3,2,1,0:T(8,128)(2,1)S(1)}, bf16[2,8,128,384]{3,2,1,0:T(8,128)(2,1)}, u32[]{:S(2)}, u32[]{:S(2)}) collective-permute-start(bf16[2,8,128,384]{3,2,1,0:T(8,128)(2,1)S(1)} %bitcast.511), channel_id=1, source_target_pairs={{0,1},{1,0},{2,3},{3,2},{4,5},{5,4},{6,7},{7,6},{8,9},{9,8},{10,11... | collective-permute-start | bytes 4718600 | tf_op jit(solution)/shard_map/ppermute | solution.py:902
  250.8 18.8 %collective-permute-start.40 = (bf16[2,768,768]{2,1,0:T(8,128)(2,1)}, bf16[2,768,768]{2,1,0:T(8,128)(2,1)S(1)}, u32[]{:S(2)}, u32[]{:S(2)}) collective-permute-start(bf16[2,768,768]{2,1,0:T(8,128)(2,1)} %get-tuple-element.401), channel_id=1, source_target_pairs={{0,1},{1,0},{2,3},{3,2},{4,5},{5,4},{6,7},{7,6},{8,9},{9,8},{10,11... | collective-permute-start | bytes 7077896 | tf_op jit(solution)/shard_map/ppermute | solution.py:902
  250.9 18.7 %collective-permute-start.41 = (bf16[2,768,768]{2,1,0:T(8,128)(2,1)}, bf16[2,768,768]{2,1,0:T(8,128)(2,1)}, u32[]{:S(2)}, u32[]{:S(2)}) collective-permute-start(bf16[2,768,768]{2,1,0:T(8,128)(2,1)} %get-tuple-element.402), channel_id=1, source_target_pairs={{0,1},{1,0},{2,3},{3,2},{4,5},{5,4},{6,7},{7,6},{8,9},{9,8},{10,11... | collective-permute-start | bytes 7077896 | tf_op jit(solution)/shard_map/ppermute | solution.py:902
  272.3 34.7 %collective-permute-start.42 = (bf16[8,96,768]{2,1,0:T(8,128)(2,1)}, bf16[8,96,768]{2,1,0:T(8,128)(2,1)}, u32[]{:S(2)}, u32[]{:S(2)}) collective-permute-start(bf16[8,96,768]{2,1,0:T(8,128)(2,1)} %fusion), channel_id=1, source_target_pairs={{0,2},{1,3},{2,0},{3,1},{4,6},{5,7},{6,4},{7,5},{8,10},{9,11},{10,... | collective-permute-start | bytes 3538952 | tf_op jit(solution)/shard_map/ppermute | solution.py:902
  276.4 30.6 %collective-permute-start.43 = (bf16[2,4,96,768]{3,2,1,0:T(8,128)(2,1)}, bf16[2,4,96,768]{3,2,1,0:T(8,128)(2,1)}, u32[]{:S(2)}, u32[]{:S(2)}) collective-permute-start(bf16[2,4,96,768]{3,2,1,0:T(8,128)(2,1)} %fusion.1), channel_id=1, source_target_pairs={{0,4},{1,5},{2,6},{3,7},{4,0},{5,1},{6,2},{7,3},{8,12},{9,13},{10,... | collective-permute-start | bytes 3538952 | tf_op jit(solution)/shard_map/ppermute | solution.py:902
  308.4 32.7 %collective-permute-start.44 = (bf16[4,96,768]{2,1,0:T(8,128)(2,1)S(1)}, bf16[4,96,768]{2,1,0:T(8,128)(2,1)S(1)}, u32[]{:S(2)}, u32[]{:S(2)}) collective-permute-start(bf16[4,96,768]{2,1,0:T(8,128)(2,1)S(1)} %fusion.5), channel_id=1, source_target_pairs={{0,4},{1,5},{2,6},{3,7},{4,0},{5,1},{6,2},{7,3},{8,12},{9,13},{10,... | collective-permute-start | bytes 1769480 | tf_op jit(solution)/shard_map/ppermute | solution.py:902
  311.3 29.8 %collective-permute-start.45 = (bf16[4,96,768]{2,1,0:T(8,128)(2,1)}, bf16[4,96,768]{2,1,0:T(8,128)(2,1)}, u32[]{:S(2)}, u32[]{:S(2)}) collective-permute-start(bf16[4,96,768]{2,1,0:T(8,128)(2,1)} %fusion.4), channel_id=1, source_target_pairs={{0,2},{1,3},{2,0},{3,1},{4,6},{5,7},{6,4},{7,5},{8,10},{9,11},{10,... | collective-permute-start | bytes 1769480 | tf_op jit(solution)/shard_map/ppermute | solution.py:902
  311.8 29.3 %collective-permute-start.46 = (bf16[2,768,768]{2,1,0:T(8,128)(2,1)}, bf16[2,768,768]{2,1,0:T(8,128)(2,1)S(1)}, u32[]{:S(2)}, u32[]{:S(2)}) collective-permute-start(bf16[2,768,768]{2,1,0:T(8,128)(2,1)} %get-tuple-element.426), channel_id=1, source_target_pairs={{0,1},{1,0},{2,3},{3,2},{4,5},{5,4},{6,7},{7,6},{8,9},{9,8},{10,11... | collective-permute-start | bytes 7077896 | tf_op jit(solution)/shard_map/ppermute | solution.py:902
  345.8 8.5 %collective-permute-start.47 = (bf16[208,768]{1,0:T(8,128)(2,1)}, bf16[208,768]{1,0:T(8,128)(2,1)}, u32[]{:S(2)}, u32[]{:S(2)}) collective-permute-start(bf16[208,768]{1,0:T(8,128)(2,1)} %get-tuple-element.433), channel_id=1, source_target_pairs={{0,1},{1,0},{2,3},{3,2},{4,5},{5,4},{6,7},{7,6},{8,9},{9,8},{10,11... | collective-permute-start | bytes 958472 | tf_op jit(solution)/shard_map/ppermute | solution.py:902
  346.2 10.7 %collective-permute-start.48 = (bf16[208,768]{1,0:T(8,128)(2,1)}, bf16[208,768]{1,0:T(8,128)(2,1)}, u32[]{:S(2)}, u32[]{:S(2)}) collective-permute-start(bf16[208,768]{1,0:T(8,128)(2,1)} %get-tuple-element.434), channel_id=1, source_target_pairs={{0,2},{1,3},{2,0},{3,1},{4,6},{5,7},{6,4},{7,5},{8,10},{9,11},{10,... | collective-permute-start | bytes 958472 | tf_op jit(solution)/shard_map/ppermute | solution.py:902
  347.8 14.2 %collective-permute-start.49 = (bf16[208,768]{1,0:T(8,128)(2,1)}, bf16[208,768]{1,0:T(8,128)(2,1)}, u32[]{:S(2)}, u32[]{:S(2)}) collective-permute-start(bf16[208,768]{1,0:T(8,128)(2,1)} %get-tuple-element.435), channel_id=1, source_target_pairs={{0,3},{1,2},{2,1},{3,0},{4,7},{5,6},{6,5},{7,4},{8,11},{9,10},{10,... | collective-permute-start | bytes 958472 | tf_op jit(solution)/shard_map/ppermute | solution.py:902
  349.1 29.4 %collective-permute-start.50 = (bf16[2,4,96,768]{3,2,1,0:T(8,128)(2,1)S(1)}, bf16[2,4,96,768]{3,2,1,0:T(8,128)(2,1)S(1)}, u32[]{:S(2)}, u32[]{:S(2)}) collective-permute-start(bf16[2,4,96,768]{3,2,1,0:T(8,128)(2,1)S(1)} %copy-done.24), channel_id=1, source_target_pairs={{0,4},{1,5},{2,6},{3,7},{4,0},{5,1},{6,2},{7,3},{8,12},{9,13},{10,... | collective-permute-start | bytes 3538952 | tf_op jit(solution)/shard_map/ppermute | solution.py:902
  379.5 26.5 %collective-permute-start.51 = (bf16[2,768,768]{2,1,0:T(8,128)(2,1)}, bf16[2,768,768]{2,1,0:T(8,128)(2,1)}, u32[]{:S(2)}, u32[]{:S(2)}) collective-permute-start(bf16[2,768,768]{2,1,0:T(8,128)(2,1)} %get-tuple-element.450), channel_id=1, source_target_pairs={{0,1},{1,0},{2,3},{3,2},{4,5},{5,4},{6,7},{7,6},{8,9},{9,8},{10,11... | collective-permute-start | bytes 7077896 | tf_op jit(solution)/shard_map/ppermute | solution.py:902
  380.4 21.9 %collective-permute-start.53 = (bf16[1,192,768]{2,1,0:T(8,128)(2,1)S(1)}, bf16[1,192,768]{2,1,0:T(8,128)(2,1)S(1)}, u32[]{:S(2)}, u32[]{:S(2)}) collective-permute-start(bf16[1,192,768]{2,1,0:T(8,128)(2,1)S(1)} %pad_maximum_fusion.27), channel_id=1, source_target_pairs={{0,8},{1,9},{2,10},{3,11},{4,12},{5,13},{6,14},{7,15},{8,0},{9,1},... | collective-permute-start | bytes 884744 | tf_op jit(solution)/shard_map/ppermute | solution.py:902
  382.4 23.5 %collective-permute-start.54 = (bf16[1,192,768]{2,1,0:T(8,128)(2,1)S(1)}, bf16[1,192,768]{2,1,0:T(8,128)(2,1)S(1)}, u32[]{:S(2)}, u32[]{:S(2)}) collective-permute-start(bf16[1,192,768]{2,1,0:T(8,128)(2,1)S(1)} %pad_maximum_fusion.28), channel_id=1, source_target_pairs={{0,16},{1,17},{2,18},{3,19},{4,20},{5,21},{6,22},{7,23},{8,24},{9,... | collective-permute-start | bytes 884744 | tf_op jit(solution)/shard_map/ppermute | solution.py:902
  383.3 22.6 %collective-permute-start.55 = (bf16[1,192,768]{2,1,0:T(8,128)(2,1)}, bf16[1,192,768]{2,1,0:T(8,128)(2,1)S(1)}, u32[]{:S(2)}, u32[]{:S(2)}) collective-permute-start(bf16[1,192,768]{2,1,0:T(8,128)(2,1)} %pad_maximum_fusion.29), channel_id=1, source_target_pairs={{0,24},{1,25},{2,26},{3,27},{4,28},{5,29},{6,30},{7,31},{8,16},{9,... | collective-permute-start | bytes 884744 | tf_op jit(solution)/shard_map/ppermute | solution.py:902
  386.4 19.5 %collective-permute-start.52 = (bf16[4,96,768]{2,1,0:T(8,128)(2,1)S(1)}, bf16[4,96,768]{2,1,0:T(8,128)(2,1)S(1)}, u32[]{:S(2)}, u32[]{:S(2)}) collective-permute-start(bf16[4,96,768]{2,1,0:T(8,128)(2,1)S(1)} %fusion.3), channel_id=1, source_target_pairs={{0,2},{1,3},{2,0},{3,1},{4,6},{5,7},{6,4},{7,5},{8,10},{9,11},{10,... | collective-permute-start | bytes 1769480 | tf_op jit(solution)/shard_map/ppermute | solution.py:902
  411.2 21.1 %collective-permute-start.56 = (bf16[8,96,384]{2,1,0:T(8,128)(2,1)}, bf16[8,96,384]{2,1,0:T(8,128)(2,1)}, u32[]{:S(2)}, u32[]{:S(2)}) collective-permute-start(bf16[8,96,384]{2,1,0:T(8,128)(2,1)} %fusion.6), channel_id=1, source_target_pairs={{0,2},{1,3},{2,0},{3,1},{4,6},{5,7},{6,4},{7,5},{8,10},{9,11},{10,... | collective-permute-start | bytes 1769480 | tf_op jit(solution)/shard_map/ppermute | solution.py:902
  412.8 19.6 %collective-permute-start.57 = (bf16[2,4,96,384]{3,2,1,0:T(8,128)(2,1)}, bf16[2,4,96,384]{3,2,1,0:T(8,128)(2,1)}, u32[]{:S(2)}, u32[]{:S(2)}) collective-permute-start(bf16[2,4,96,384]{3,2,1,0:T(8,128)(2,1)} %fusion.7), channel_id=1, source_target_pairs={{0,4},{1,5},{2,6},{3,7},{4,0},{5,1},{6,2},{7,3},{8,12},{9,13},{10,... | collective-permute-start | bytes 1769480 | tf_op jit(solution)/shard_map/ppermute | solution.py:902
  416.6 41.3 %collective-permute-start.62 = (bf16[1,96,768]{2,1,0:T(8,128)(2,1)}, bf16[1,96,768]{2,1,0:T(8,128)(2,1)}, u32[]{:S(2)}, u32[]{:S(2)}) collective-permute-start(bf16[1,96,768]{2,1,0:T(8,128)(2,1)} %get-tuple-element.542), channel_id=1, source_target_pairs={{0,8},{1,9},{2,10},{3,11},{4,12},{5,13},{6,14},{7,15},{8,0},{9,1},... | collective-permute-start | bytes 442376 | tf_op jit(solution)/shard_map/ppermute | solution.py:902
  421.8 36.1 %collective-permute-start.63 = (bf16[1,96,768]{2,1,0:T(8,128)(2,1)}, bf16[1,96,768]{2,1,0:T(8,128)(2,1)}, u32[]{:S(2)}, u32[]{:S(2)}) collective-permute-start(bf16[1,96,768]{2,1,0:T(8,128)(2,1)} %get-tuple-element.541), channel_id=1, source_target_pairs={{0,16},{1,17},{2,18},{3,19},{4,20},{5,21},{6,22},{7,23},{8,24},{9,... | collective-permute-start | bytes 442376 | tf_op jit(solution)/shard_map/ppermute | solution.py:902
  432.3 5.9 %collective-permute-start.58 = (bf16[16,24,896]{2,1,0:T(8,128)(2,1)S(1)}, bf16[16,24,896]{2,1,0:T(8,128)(2,1)S(1)}, u32[]{:S(2)}, u32[]{:S(2)}) collective-permute-start(bf16[16,24,896]{2,1,0:T(8,128)(2,1)S(1)} %get-tuple-element.473), channel_id=1, source_target_pairs={{0,1},{1,0},{2,3},{3,2},{4,5},{5,4},{6,7},{7,6},{8,9},{9,8},{10,11... | collective-permute-start | bytes 2064392 | tf_op jit(solution)/shard_map/ppermute | solution.py:902
  439.1 8.8 %collective-permute-start.59 = (bf16[4,96,384]{2,1,0:T(8,128)(2,1)S(1)}, bf16[4,96,384]{2,1,0:T(8,128)(2,1)S(1)}, u32[]{:S(2)}, u32[]{:S(2)}) collective-permute-start(bf16[4,96,384]{2,1,0:T(8,128)(2,1)S(1)} %fusion.15), channel_id=1, source_target_pairs={{0,4},{1,5},{2,6},{3,7},{4,0},{5,1},{6,2},{7,3},{8,12},{9,13},{10,... | collective-permute-start | bytes 884744 | tf_op jit(solution)/shard_map/ppermute | solution.py:902
  439.6 10.6 %collective-permute-start.60 = (bf16[4,96,384]{2,1,0:T(8,128)(2,1)S(1)}, bf16[4,96,384]{2,1,0:T(8,128)(2,1)S(1)}, u32[]{:S(2)}, u32[]{:S(2)}) collective-permute-start(bf16[4,96,384]{2,1,0:T(8,128)(2,1)S(1)} %fusion.10), channel_id=1, source_target_pairs={{0,2},{1,3},{2,0},{3,1},{4,6},{5,7},{6,4},{7,5},{8,10},{9,11},{10,... | collective-permute-start | bytes 884744 | tf_op jit(solution)/shard_map/ppermute | solution.py:902
  440.1 15.4 %collective-permute-start.61 = (bf16[8,24,896]{2,1,0:T(8,128)(2,1)S(1)}, bf16[8,24,896]{2,1,0:T(8,128)(2,1)S(1)}, u32[]{:S(2)}, u32[]{:S(2)}) collective-permute-start(bf16[8,24,896]{2,1,0:T(8,128)(2,1)S(1)} %fusion.14), channel_id=1, source_target_pairs={{0,2},{1,3},{2,0},{3,1},{4,6},{5,7},{6,4},{7,5},{8,10},{9,11},{10,... | collective-permute-start | bytes 1032200 | tf_op jit(solution)/shard_map/ppermute | solution.py:902
  447.9 10.0 %collective-permute-start.64 = (bf16[1,96,768]{2,1,0:T(8,128)(2,1)S(1)}, bf16[1,96,768]{2,1,0:T(8,128)(2,1)S(1)}, u32[]{:S(2)}, u32[]{:S(2)}) collective-permute-start(bf16[1,96,768]{2,1,0:T(8,128)(2,1)S(1)} %get-tuple-element.540), channel_id=1, source_target_pairs={{0,24},{1,25},{2,26},{3,27},{4,28},{5,29},{6,30},{7,31},{8,16},{9,... | collective-permute-start | bytes 442376 | tf_op jit(solution)/shard_map/ppermute | solution.py:902
  458.1 11.5 %collective-permute-start.65 = (bf16[1,96,768]{2,1,0:T(8,128)(2,1)S(1)}, bf16[1,96,768]{2,1,0:T(8,128)(2,1)S(1)}, u32[]{:S(2)}, u32[]{:S(2)}) collective-permute-start(bf16[1,96,768]{2,1,0:T(8,128)(2,1)S(1)} %get-tuple-element.494), channel_id=1, source_target_pairs={{0,8},{1,9},{2,10},{3,11},{4,12},{5,13},{6,14},{7,15},{8,0},{9,1},... | collective-permute-start | bytes 442376 | tf_op jit(solution)/shard_map/ppermute | solution.py:902
  459.3 13.4 %collective-permute-start.66 = (bf16[1,96,768]{2,1,0:T(8,128)(2,1)S(1)}, bf16[1,96,768]{2,1,0:T(8,128)(2,1)S(1)}, u32[]{:S(2)}, u32[]{:S(2)}) collective-permute-start(bf16[1,96,768]{2,1,0:T(8,128)(2,1)S(1)} %get-tuple-element.495), channel_id=1, source_target_pairs={{0,16},{1,17},{2,18},{3,19},{4,20},{5,21},{6,22},{7,23},{8,24},{9,... | collective-permute-start | bytes 442376 | tf_op jit(solution)/shard_map/ppermute | solution.py:902
  461.1 11.6 %collective-permute-start.67 = (bf16[1,96,768]{2,1,0:T(8,128)(2,1)S(1)}, bf16[1,96,768]{2,1,0:T(8,128)(2,1)S(1)}, u32[]{:S(2)}, u32[]{:S(2)}) collective-permute-start(bf16[1,96,768]{2,1,0:T(8,128)(2,1)S(1)} %get-tuple-element.496), channel_id=1, source_target_pairs={{0,24},{1,25},{2,26},{3,27},{4,28},{5,29},{6,30},{7,31},{8,16},{9,... | collective-permute-start | bytes 442376 | tf_op jit(solution)/shard_map/ppermute | solution.py:902
  462.5 10.2 %collective-permute-start.68 = (bf16[4,24,896]{2,1,0:T(8,128)(2,1)S(1)}, bf16[4,24,896]{2,1,0:T(8,128)(2,1)S(1)}, u32[]{:S(2)}, u32[]{:S(2)}) collective-permute-start(bf16[4,24,896]{2,1,0:T(8,128)(2,1)S(1)} %fusion.58), channel_id=1, source_target_pairs={{0,4},{1,5},{2,6},{3,7},{4,0},{5,1},{6,2},{7,3},{8,12},{9,13},{10,... | collective-permute-start | bytes 516104 | tf_op jit(solution)/shard_map/ppermute | solution.py:902
  472.8 6.8 %collective-permute-start.69 = (bf16[1,24,896]{2,1,0:T(8,128)(2,1)S(1)}, bf16[1,24,896]{2,1,0:T(8,128)(2,1)S(1)}, u32[]{:S(2)}, u32[]{:S(2)}) collective-permute-start(bf16[1,24,896]{2,1,0:T(8,128)(2,1)S(1)} %get-tuple-element.502), channel_id=1, source_target_pairs={{0,8},{1,9},{2,10},{3,11},{4,12},{5,13},{6,14},{7,15},{8,0},{9,1},... | collective-permute-start | bytes 129032 | tf_op jit(solution)/shard_map/ppermute | solution.py:902
  476.2 5.9 %collective-permute-start.71 = (bf16[1,24,896]{2,1,0:T(8,128)(2,1)S(1)}, bf16[1,24,896]{2,1,0:T(8,128)(2,1)S(1)}, u32[]{:S(2)}, u32[]{:S(2)}) collective-permute-start(bf16[1,24,896]{2,1,0:T(8,128)(2,1)S(1)} %get-tuple-element.504), channel_id=1, source_target_pairs={{0,24},{1,25},{2,26},{3,27},{4,28},{5,29},{6,30},{7,31},{8,16},{9,... | collective-permute-start | bytes 129032 | tf_op jit(solution)/shard_map/ppermute | solution.py:902
  (81 other events, 301.4 us)

commit v6 on v5

--- a/solution.py
+++ b/solution.py
@@ -265,21 +265,15 @@
             keepdims=True,
         )
         d_mixed_long = jnp.concatenate([d_mixed, lane_pieces(three_parts(delta), ROWS)], axis=1)
-        d_query = jnp.zeros((ROWS, HD), SINGLE)
-        for part in range(FRAMES):
-            rows = slice(SLOTS * part, SLOTS * (part + 1))
-            keys = qkv_ref[0, rows, GROUP + at : GROUP + at + HD]
-            values = qkv_ref[0, rows, 2 * GROUP + at : 2 * GROUP + at + HD]
-            keys_long = jnp.concatenate([keys, key_extra_ref[rows, :]], axis=1)
-            values_long = jnp.concatenate(
-                [values, lane_pieces([one[rows]] * 3, SLOTS)], axis=1
-            )
-            prob = jnp.exp(dot(keys_long, query_long, NT))
-            d_score = low(prob * dot(values_long, d_mixed_long, NT))
-            dqkv[rows, 2 * GROUP + at : 2 * GROUP + at + HD] = low(dot(low(prob), d_mixed))
-            dqkv[rows, GROUP + at : GROUP + at + HD] = low(dot(d_score, query) * scale)
-            d_query = d_query + dot(d_score, keys, TN)
-        dqkv[:, at : at + HD] = low(d_query * scale)
+        keys = qkv_ref[0, :, GROUP + at : GROUP + at + HD]
+        values = qkv_ref[0, :, 2 * GROUP + at : 2 * GROUP + at + HD]
+        keys_long = jnp.concatenate([keys, key_extra_ref[...]], axis=1)
+        values_long = jnp.concatenate([values, lane_pieces([one] * 3, ROWS)], axis=1)
+        prob = jnp.exp(dot(keys_long, query_long, NT))
+        d_score = low(prob * dot(values_long, d_mixed_long, NT))
+        dqkv[:, 2 * GROUP + at : 2 * GROUP + at + HD] = low(dot(low(prob), d_mixed))
+        dqkv[:, GROUP + at : GROUP + at + HD] = low(dot(d_score, query) * scale)
+        dqkv[:, at : at + HD] = low(dot(d_score, keys, TN) * scale)
     finish_backward(normed_ref, grad_ref, left_ref, right_ref, mixed_ref, dweight_ref, dnormed_ref, dqkv)
 
 

time: 518 us -> 514 us (level)
  transfers between devices with their start and end apart: 77 -> 77, of which waited for: 28 -> 30; matrix products, arithmetic and copies ran while one was open for 13% -> 13% of each run, Pallas kernels for 37% -> 36%
where the time goes in v6:
time: 514 us; the launch traced here: 505 us
  Pallas kernels  221 us (43%)
  starting transfers between devices  85 us (17%)
  waiting for transfers between devices  84.9 us (17%)
  other arithmetic  61.9 us (12%)
  local copies, waits for them, and re-layouts  39.2 us (8%)
  between operations  10.6 us (2%)
    pallas_call x20, Pallas kernels, call(): pl.pallas_call(kernel, grid=(steps,), in_specs=in_specs or [spec_of(value...  142 us
    ppermute x77, starting transfers between devices, swap(): return lax.ppermute(value, ALL, [(i, i ^ mask) for i in range(self.count)])  85 us
    ppermute x77, waiting for transfers between devices, swap(): return lax.ppermute(value, ALL, [(i, i ^ mask) for i in range(self.count)])  84.9 us
    pallas_call x4, Pallas kernels, block_call(): pl.pallas_call(with_fetches(kernel, places), grid=(2,), in_specs=specs, o...  73.1 us
    convert_element_type x24, other arithmetic, low(): return value.astype(LOWER)  24 us
    unnamed x138, local copies, waits for them, and re-layouts  12.4 us
  transfers between devices with their start and end apart: 77, of which 30 were waited for; matrix products, arithmetic and copies ran while one was open for 13% of the time, Pallas kernels for 36%

profile of v6, /device:TPU:0, one launch (start us, length us, event | category | flops | bytes accessed | tf_op | source)
XLA Modules:
  0.0 505.5 jit_solution(8548098740037040538)
XLA Ops:
  5.7 4.1 collective-permute-start
  15.4 1.7 gather_fusion
  20.9 1.6 collective-permute-start.1
  25.9 7.6 %collective-permute-done.3 = bf16[208,768]{1,0:T(8,128)(2,1)S(1)} collective-permute-done((bf16[208,768]{1,0:T(8,128)(2,1)S(1)}, bf16[208,768]{1,0:T(8,128)(2,1)S(1)}, u32[]{:S(2)}, u32[]{:S(2)}) %collective-permute-start.3) | collective-permute-done | bytes 319520 | tf_op jit(solution)/shard_map/ppermute | solution.py:896
  33.5 4.9 collective-permute-done.4
  38.7 1.6 collective-permute-start.5
  44.3 3.1 collective-permute-start.11
  47.5 3.1 collective-permute-done.5
  52.3 1.6 collective-permute-start.7
  56.8 14.8 %collective-permute-done.7 = bf16[8,128,384]{2,1,0:T(8,128)(2,1)S(1)} collective-permute-done((bf16[8,128,384]{2,1,0:T(8,128)(2,1)S(1)}, bf16[8,128,384]{2,1,0:T(8,128)(2,1)S(1)}, u32[]{:S(2)}, u32[]{:S(2)}) %collective-permute-start.7) | collective-permute-done | bytes 786464 | tf_op jit(solution)/shard_map/ppermute | solution.py:896
  83.8 1.8 collective-permute-done.12.other_left.left_ref
  89.5 5.1 %embed.1 = (f32[832,768]{1,0:T(8,128)}, bf16[832,768]{1,0:T(8,128)(2,1)}) custom-call(bf16[832,768]{1,0:T(8,128)(2,1)} %pad_maximum_fusion.5.patches_ref, bf16[768,768]{1,0:T(8,128)(2,1)} %bitcast.532, f32[832,1]{1,0:T(8,128)} %copy.104.valid_ref, f32[8,768]{1,0:T(8,128)} %reshape.1638.norms_ref.refs_5_.refs_6_.refs_7_.refs_11_), custom_call_target="tpu_custom_call" | custom-call | flops 15000000512 | bytes 8388608 | tf_op jit(solution)/shard_map/embed/pallas_call | solution.py:589
  94.6 2.1 collective-permute-done.14
  101.1 10.7 %temporal_forward.1 = (bf16[4,4,576,208]{3,2,1,0:T(8,128)(2,1)}, bf16[4,832,192]{2,1,0:T(8,128)(2,1)}) custom-call(bf16[832,768]{1,0:T(8,128)(2,1)} %get-tuple-element.447.normed_ref, bf16[2,8,128,384]{3,2,1,0:T(8,128)(2,1)} %pad_maximum_fusion.1.own_left.left_ref, bf16[2,8,128,384]{3,2,1,0:T(8,128)(2,1)} %bitcast.466, ...), custom_call_target="tpu_custom_call" | custom-call | flops 40000000000 | bytes 8388608 | tf_op jit(solution)/shard_map/temporal_forward/pallas_call | solution.py:589
  128.7 2.6 convolution_multiply_fusion.start_ref
  133.1 6.1 %collective-permute-done.21.refs_3_ = bf16[208,768]{1,0:T(8,128)(2,1)} collective-permute-done((bf16[208,768]{1,0:T(8,128)(2,1)}, bf16[208,768]{1,0:T(8,128)(2,1)}, u32[]{:S(2)}, u32[]{:S(2)}) %collective-permute-start.21) | collective-permute-done | bytes 319520 | tf_op jit(solution)/shard_map/ppermute | solution.py:896
  141.1 1.6 collective-permute-start.27
  144.2 5.7 %enter_frame.1 = (f32[832,768]{1,0:T(8,128)}, bf16[832,768]{1,0:T(8,128)(2,1)}) custom-call(f32[832,768]{1,0:T(8,128)} %convolution_multiply_fusion.start_ref, bf16[208,768]{1,0:T(8,128)(2,1)} %pad_maximum_fusion.26.refs_0_, bf16[208,768]{1,0:T(8,128)(2,1)} %collective-permute-done.19.refs_1_, bf16[208,768]{1,0:T(8,128)(2,1)} %collective-permute-done.20.refs_2_, ...), custom_call_target="tpu_custom_call" | custom-call | flops 2000000000 | bytes 8388608 | tf_op jit(solution)/shard_map/enter_frame/pallas_call | solution.py:589
  149.9 15.4 %spatial_forward.2 = (bf16[2,832,576]{2,1,0:T(8,128)(2,1)}, bf16[2,832,192]{2,1,0:T(8,128)(2,1)}, bf16[2,832,192]{2,1,0:T(8,128)(2,1)}, f32[832,768]{1,0:T(8,128)}) custom-call(bf16[832,768]{1,0:T(8,128)(2,1)} %get-tuple-element.415.normed_ref.refs_0_, bf16[2,8,96,768]{3,2,1,0:T(8,128)(2,1)} %copy-done.3, bf16[2,8,96,768]{3,2,1,0:T(8,128)(2,1)} %copy-done.3, ...), custom_call_target="tpu_custom_call" | custom-call | flops 15000000512 | bytes 8388608 | tf_op jit(solution)/shard_map/spatial_forward/pallas_call | solution.py:589
  170.4 17.2 %spatial_forward.3 = (bf16[2,832,576]{2,1,0:T(8,128)(2,1)}, bf16[2,832,192]{2,1,0:T(8,128)(2,1)}, bf16[2,832,192]{2,1,0:T(8,128)(2,1)}, f32[832,768]{1,0:T(8,128)}, bf16[832,768]{1,0:T(8,128)(2,1)}) custom-call(bf16[832,768]{1,0:T(8,128)(2,1)} %get-tuple-element.415.normed_ref.refs_0_, ...), custom_call_target="tpu_custom_call" | custom-call | flops 15000000512 | bytes 8388608 | tf_op jit(solution)/shard_map/spatial_forward/pallas_call | solution.py:665
  190.9 9.9 %feed_forward.2 = (bf16[2,832,768]{2,1,0:T(8,128)(2,1)}, bf16[2,832,768]{2,1,0:T(8,128)(2,1)}, f32[832,768]{1,0:T(8,128)}) custom-call(bf16[832,768]{1,0:T(8,128)(2,1)} %get-tuple-element.391.normed_ref.refs_0_, bf16[2,8,96,384]{3,2,1,0:T(8,128)(2,1)} %copy-done.21, bf16[2,8,96,384]{3,2,1,0:T(8,128)(2,1)} %bitcast.530, bf16[2,8,128,384]{3,2,1,0:T(8,128)(2,1)} %copy-done.10, ...), custom_call_target="tpu_custom_call" | custom-call | flops 10000000000 | bytes 8388608 | tf_op jit(solution)/shard_map/feed_forward/pallas_call | solution.py:589
  200.8 12.0 %feed_forward.3 = (bf16[2,832,768]{2,1,0:T(8,128)(2,1)}, bf16[2,832,768]{2,1,0:T(8,128)(2,1)}, f32[832,768]{1,0:T(8,128)}, f32[1,768]{1,0:T(1,128)}) custom-call(bf16[832,768]{1,0:T(8,128)(2,1)} %get-tuple-element.391.normed_ref.refs_0_, bf16[2,8,96,384]{3,2,1,0:T(8,128)(2,1)} %collective-permute-done.30.refs_1_.refs_0_, bf16[2,8,96,384]{3,2,1,0:T(8,128)(2,1)} %copy-done.67, ...), custom_call_target="tpu_custom_call" | custom-call | flops 10000000000 | bytes 8388608 | tf_op jit(solution)/shard_map/feed_forward/pallas_call | solution.py:665
  219.0 1.7 collective-permute-start.37
  220.7 2.5 collective-permute-start.38
  229.3 7.3 %losses.1 = (f32[1,1]{1,0:T(1,128)}, bf16[8,768]{1,0:T(8,128)(2,1)}, bf16[8,768]{1,0:T(8,128)(2,1)}, f32[832,768]{1,0:T(8,128)}, bf16[832,768]{1,0:T(8,128)(2,1)}, /*index=5*/f32[2,768]{1,0:T(2,128)}) custom-call(s32[1]{0:T(128)} %bitcast.clip_ref, f32[8,896]{1,0:T(8,128)} %squeeze_reshape.3.facts_ref, bf16[768,768]{1,0:T(8,128)(2,1)} %bitcast.474, ...), custom_call_target="tpu_custom_call" | custom-call | flops 1000000000 | bytes 8388608 | tf_op jit(solution)/shard_map/losses/pallas_call | solution.py:589
  236.6 14.2 %feed_backward.2 = (bf16[2,768,768]{2,1,0:T(8,128)(2,1)}, bf16[2,768,768]{2,1,0:T(8,128)(2,1)}, f32[832,768]{1,0:T(8,128)}) custom-call(bf16[832,768]{1,0:T(8,128)(2,1)} %get-tuple-element.391.normed_ref.refs_0_, bf16[832,768]{1,0:T(8,128)(2,1)} %get-tuple-element.392.grad_ref.refs_1_, bf16[2,8,96,384]{3,2,1,0:T(8,128)(2,1)} %collective-permute-done.30.refs_1_.refs_0_, ...), custom_call_target="tpu_custom_call" | custom-call | flops 15000000512 | bytes 8388608 | tf_op jit(solution)/shard_map/feed_backward/pallas_call | solution.py:589
  252.5 17.4 %feed_backward.3 = (bf16[2,768,768]{2,1,0:T(8,128)(2,1)}, bf16[2,768,768]{2,1,0:T(8,128)(2,1)}, f32[832,768]{1,0:T(8,128)}, bf16[832,768]{1,0:T(8,128)(2,1)}, f32[2,768]{1,0:T(2,128)}) custom-call(bf16[832,768]{1,0:T(8,128)(2,1)} %get-tuple-element.391.normed_ref.refs_0_, bf16[832,768]{1,0:T(8,128)(2,1)} %get-tuple-element.392.grad_ref.refs_1_, ...), custom_call_target="tpu_custom_call" | custom-call | flops 15000000512 | bytes 8388608 | tf_op jit(solution)/shard_map/feed_backward/pallas_call | solution.py:665
  270.0 2.7 fusion
  274.3 2.6 fusion.1
  278.3 24.6 %spatial_backward.2 = (bf16[2,768,768]{2,1,0:T(8,128)(2,1)}, f32[832,768]{1,0:T(8,128)}) custom-call(bf16[832,768]{1,0:T(8,128)(2,1)} %get-tuple-element.415.normed_ref.refs_0_, bf16[832,768]{1,0:T(8,128)(2,1)} %get-tuple-element.416.grad_ref.refs_1_, bf16[2,8,96,768]{3,2,1,0:T(8,128)(2,1)} %collective-permute-done.23.refs_1_.refs_2_.left_ref.right_ref, ...), custom_call_target="tpu_custom_call" | custom-call | flops 30000001024 | bytes 8388608 | tf_op jit(solution)/shard_map/spatial_backward/pallas_call | solution.py:589
  303.0 1.6 copy-done.4
  307.7 2.3 fusion.4
  310.4 26.5 %spatial_backward.3 = (bf16[2,768,768]{2,1,0:T(8,128)(2,1)}, bf16[832,768]{1,0:T(8,128)(2,1)}, f32[2,768]{1,0:T(2,128)}) custom-call(bf16[832,768]{1,0:T(8,128)(2,1)} %get-tuple-element.415.normed_ref.refs_0_, bf16[832,768]{1,0:T(8,128)(2,1)} %get-tuple-element.416.grad_ref.refs_1_, bf16[2,8,96,768]{3,2,1,0:T(8,128)(2,1)} %copy-done.3, ...), custom_call_target="tpu_custom_call" | custom-call | flops 30000001024 | bytes 8388608 | tf_op jit(solution)/shard_map/spatial_backward/pallas_call | solution.py:665
  337.0 3.3 fusion.85
  346.7 1.6 fusion.44
  349.2 3.7 collective-permute-done.48
  352.8 5.0 collective-permute-done.49
  357.8 2.4 pad_maximum_fusion.6.grad_ref.drows_ref
  360.2 14.1 %temporal_backward.2 = (bf16[2,768,768]{2,1,0:T(8,128)(2,1)}, f32[832,768]{1,0:T(8,128)}) custom-call(bf16[832,768]{1,0:T(8,128)(2,1)} %get-tuple-element.447.normed_ref, bf16[832,768]{1,0:T(8,128)(2,1)} %pad_maximum_fusion.6.grad_ref.drows_ref, bf16[2,8,128,384]{3,2,1,0:T(8,128)(2,1)} %collective-permute-done.12.other_left.left_ref, ...), custom_call_target="tpu_custom_call" | custom-call | flops 14000000000 | bytes 8388608 | tf_op jit(solution)/shard_map/temporal_backward/pallas_call | solution.py:589
  376.3 2.0 collective-permute-start.53
  380.7 1.6 fusion.3
  382.3 1.6 collective-permute-start.52
  383.9 14.3 %temporal_backward.3 = (bf16[2,768,768]{2,1,0:T(8,128)(2,1)}, f32[832,768]{1,0:T(8,128)}) custom-call(bf16[832,768]{1,0:T(8,128)(2,1)} %get-tuple-element.447.normed_ref, bf16[832,768]{1,0:T(8,128)(2,1)} %pad_maximum_fusion.6.grad_ref.drows_ref, bf16[2,8,128,384]{3,2,1,0:T(8,128)(2,1)} %pad_maximum_fusion.1.own_left.left_ref, ...), custom_call_target="tpu_custom_call" | custom-call | flops 14000000000 | bytes 8388608 | tf_op jit(solution)/shard_map/temporal_backward/pallas_call | solution.py:589
  398.2 3.6 collective-permute-done.54
  402.5 2.1 fusion.82
  409.2 2.3 fusion.38
  411.5 5.3 %collective-permute-start.62 = (bf16[1,96,768]{2,1,0:T(8,128)(2,1)}, bf16[1,96,768]{2,1,0:T(8,128)(2,1)}, u32[]{:S(2)}, u32[]{:S(2)}) collective-permute-start(bf16[1,96,768]{2,1,0:T(8,128)(2,1)} %get-tuple-element.542), channel_id=1, source_target_pairs={{0,8},{1,9},{2,10},{3,11},{4,12},{5,13},{6,14},{7,15},{8,0},{9,1},... | collective-permute-start | bytes 442376 | tf_op jit(solution)/shard_map/ppermute | solution.py:896
  417.4 8.2 %embed_backward.1 = bf16[768,896]{1,0:T(8,128)(2,1)} custom-call(bf16[832,768]{1,0:T(8,128)(2,1)} %pad_maximum_fusion.5.patches_ref, f32[832,768]{1,0:T(8,128)} %get-tuple-element.463.start_ref, f32[832,1]{1,0:T(8,128)} %copy.104.valid_ref, bf16[832,768]{1,0:T(8,128)(2,1)} %pad_maximum_fusion.6.grad_ref.drows_ref, f32[832,768]{1,0:T(8,128)} %get-tuple-element.465.da_ref, ...), custom_call_target="tpu_custom_call" | custom-call | flops 30000001024 | bytes 8388608 | tf_op jit(solution)/shard_map/embed_backward/pallas_call | solution.py:589
  428.6 2.3 fusion.31
  438.8 4.0 collective-permute-done.59
  442.8 2.4 collective-permute-start.64
  445.4 6.0 %collective-permute-done.61 = bf16[8,24,896]{2,1,0:T(8,128)(2,1)S(1)} collective-permute-done((bf16[8,24,896]{2,1,0:T(8,128)(2,1)S(1)}, bf16[8,24,896]{2,1,0:T(8,128)(2,1)S(1)}, u32[]{:S(2)}, u32[]{:S(2)}) %collective-permute-start.61) | collective-permute-done | bytes 344096 | tf_op jit(solution)/shard_map/ppermute | solution.py:896
  455.1 1.8 collective-permute-start.66
  458.9 2.1 fusion.36.refs_0_
  461.0 2.2 finish.1
  464.5 4.1 collective-permute-done.66
  468.7 2.2 collective-permute-start.69
  481.6 1.9 collective-permute-start.73
  483.5 1.7 collective-permute-done.73
  485.8 1.9 collective-permute-start.74
  487.7 1.6 collective-permute-done.74
  491.5 2.1 collective-permute-done.75
  495.6 3.1 collective-permute-done.76
  499.3 5.7 %optimizer.1 = (f32[1,1]{1,0:T(1,128)}, f32[24,768]{1,0:T(8,128)}, f32[24,768]{1,0:T(8,128)}, f32[24,768]{1,0:T(8,128)}, f32[8,24]{1,0:T(8,128)}, /*index=5*/f32...) custom-call(f32[1,1]{1,0:T(1,128)S(6)} %add.1307.total_ref, ...), custom_call_target="tpu_custom_call" | custom-call | tf_op jit(solution)/shard_map/optimizer/pallas_call | solution.py:829
  (416 shorter events, 141.2 us)
Async XLA Ops:
  5.7 14.9 %collective-permute-start = (bf16[1,128,768]{2,1,0:T(8,128)(2,1)S(1)}, bf16[1,128,768]{2,1,0:T(8,128)(2,1)S(1)}, u32[]{:S(2)}, u32[]{:S(2)}) collective-permute-start(bf16[1,128,768]{2,1,0:T(8,128)(2,1)S(1)} %fusion.57), channel_id=1, source_target_pairs={{0,16},{1,17},{2,18},{3,19},{4,20},{5,21},{6,22},{7,23},{8,24},{9,... | collective-permute-start | bytes 589832 | tf_op jit(solution)/shard_map/ppermute | solution.py:896
  20.9 17.5 %collective-permute-start.1 = (bf16[2,128,768]{2,1,0:T(8,128)(2,1)S(1)}, bf16[2,128,768]{2,1,0:T(8,128)(2,1)S(1)}, u32[]{:S(2)}, u32[]{:S(2)}) collective-permute-start(bf16[2,128,768]{2,1,0:T(8,128)(2,1)S(1)} %maximum_bitcast_fusion.3), channel_id=1, source_target_pairs={{0,8},{1,9},{2,10},{3,11},{4,12},{5,13},{6,14},{7,15},{8,0},{9,1},... | collective-permute-start | bytes 1179656 | tf_op jit(solution)/shard_map/ppermute | solution.py:896
  23.1 10.4 %collective-permute-start.3 = (bf16[208,768]{1,0:T(8,128)(2,1)S(1)}, bf16[208,768]{1,0:T(8,128)(2,1)S(1)}, u32[]{:S(2)}, u32[]{:S(2)}) collective-permute-start(bf16[208,768]{1,0:T(8,128)(2,1)S(1)} %get-tuple-element.291), channel_id=1, source_target_pairs={{0,2},{1,3},{2,0},{3,1},{4,6},{5,7},{6,4},{7,5},{8,10},{9,11},{10,... | collective-permute-start | bytes 958472 | tf_op jit(solution)/shard_map/ppermute | solution.py:896
  24.6 13.8 %collective-permute-start.4 = (bf16[208,768]{1,0:T(8,128)(2,1)S(1)}, bf16[208,768]{1,0:T(8,128)(2,1)S(1)}, u32[]{:S(2)}, u32[]{:S(2)}) collective-permute-start(bf16[208,768]{1,0:T(8,128)(2,1)S(1)} %get-tuple-element.292), channel_id=1, source_target_pairs={{0,3},{1,2},{2,1},{3,0},{4,7},{5,6},{6,5},{7,4},{8,11},{9,10},{10,... | collective-permute-start | bytes 958472 | tf_op jit(solution)/shard_map/ppermute | solution.py:896
  38.7 11.9 %collective-permute-start.5 = (bf16[4,128,384]{2,1,0:T(8,128)(2,1)S(1)}, bf16[4,128,384]{2,1,0:T(8,128)(2,1)S(1)}, u32[]{:S(2)}, u32[]{:S(2)}) collective-permute-start(bf16[4,128,384]{2,1,0:T(8,128)(2,1)S(1)} %get-tuple-element.299), channel_id=1, source_target_pairs={{0,4},{1,5},{2,6},{3,7},{4,0},{5,1},{6,2},{7,3},{8,12},{9,13},{10,... | collective-permute-start | bytes 1179656 | tf_op jit(solution)/shard_map/ppermute | solution.py:896
  40.3 11.5 %collective-permute-start.6 = (bf16[4,128,384]{2,1,0:T(8,128)(2,1)S(1)}, bf16[4,128,384]{2,1,0:T(8,128)(2,1)S(1)}, u32[]{:S(2)}, u32[]{:S(2)}) collective-permute-start(bf16[4,128,384]{2,1,0:T(8,128)(2,1)S(1)} %get-tuple-element.300), channel_id=1, source_target_pairs={{0,2},{1,3},{2,0},{3,1},{4,6},{5,7},{6,4},{7,5},{8,10},{9,11},{10,... | collective-permute-start | bytes 1179656 | tf_op jit(solution)/shard_map/ppermute | solution.py:896
  43.1 33.3 %collective-permute-start.9 = (bf16[1,192,768]{2,1,0:T(8,128)(2,1)}, bf16[1,192,768]{2,1,0:T(8,128)(2,1)}, u32[]{:S(2)}, u32[]{:S(2)}) collective-permute-start(bf16[1,192,768]{2,1,0:T(8,128)(2,1)} %maximum_bitcast_fusion.5), channel_id=1, source_target_pairs={{0,8},{1,9},{2,10},{3,11},{4,12},{5,13},{6,14},{7,15},{8,0},{9,1},... | collective-permute-start | bytes 884744 | tf_op jit(solution)/shard_map/ppermute | solution.py:896
  43.5 32.8 %collective-permute-start.10 = (bf16[1,192,768]{2,1,0:T(8,128)(2,1)}, bf16[1,192,768]{2,1,0:T(8,128)(2,1)}, u32[]{:S(2)}, u32[]{:S(2)}) collective-permute-start(bf16[1,192,768]{2,1,0:T(8,128)(2,1)} %maximum_bitcast_fusion.5), channel_id=1, source_target_pairs={{0,16},{1,17},{2,18},{3,19},{4,20},{5,21},{6,22},{7,23},{8,24},{9,... | collective-permute-start | bytes 884744 | tf_op jit(solution)/shard_map/ppermute | solution.py:896
  44.3 32.0 %collective-permute-start.11 = (bf16[1,192,768]{2,1,0:T(8,128)(2,1)}, bf16[1,192,768]{2,1,0:T(8,128)(2,1)}, u32[]{:S(2)}, u32[]{:S(2)}) collective-permute-start(bf16[1,192,768]{2,1,0:T(8,128)(2,1)} %maximum_bitcast_fusion.5), channel_id=1, source_target_pairs={{0,24},{1,25},{2,26},{3,27},{4,28},{5,29},{6,30},{7,31},{8,16},{9,... | collective-permute-start | bytes 884744 | tf_op jit(solution)/shard_map/ppermute | solution.py:896
  52.3 19.3 %collective-permute-start.7 = (bf16[8,128,384]{2,1,0:T(8,128)(2,1)S(1)}, bf16[8,128,384]{2,1,0:T(8,128)(2,1)S(1)}, u32[]{:S(2)}, u32[]{:S(2)}) collective-permute-start(bf16[8,128,384]{2,1,0:T(8,128)(2,1)S(1)} %bitcast.484), channel_id=1, source_target_pairs={{0,2},{1,3},{2,0},{3,1},{4,6},{5,7},{6,4},{7,5},{8,10},{9,11},{10,... | collective-permute-start | bytes 2359304 | tf_op jit(solution)/shard_map/ppermute | solution.py:896
  53.8 19.0 %collective-permute-start.8 = (bf16[2,4,128,384]{3,2,1,0:T(8,128)(2,1)S(1)}, bf16[2,4,128,384]{3,2,1,0:T(8,128)(2,1)S(1)}, u32[]{:S(2)}, u32[]{:S(2)}) collective-permute-start(bf16[2,4,128,384]{3,2,1,0:T(8,128)(2,1)S(1)} %pad_maximum_fusion.14), channel_id=1, source_target_pairs={{0,4},{1,5},{2,6},{3,7},{4,0},{5,1},{6,2},{7,3},{8,12},{9,13},{10,... | collective-permute-start | bytes 2359304 | tf_op jit(solution)/shard_map/ppermute | solution.py:896
  79.7 5.9 %collective-permute-start.12 = (bf16[2,8,128,384]{3,2,1,0:T(8,128)(2,1)}, bf16[2,8,128,384]{3,2,1,0:T(8,128)(2,1)}, u32[]{:S(2)}, u32[]{:S(2)}) collective-permute-start(bf16[2,8,128,384]{3,2,1,0:T(8,128)(2,1)} %pad_maximum_fusion.1.own_left.left_ref), channel_id=1, source_target_pairs={{0,1},{1,0},{2,3},{3,2},{4,5},{5,4},{6,7},{7,6},{8,9},{9,8},{10,11... | collective-permute-start | bytes 4718600 | tf_op jit(solution)/shard_map/ppermute | solution.py:896
  79.7 5.9 %collective-permute-start.13 = (bf16[2,8,128,384]{3,2,1,0:T(8,128)(2,1)S(1)}, bf16[2,8,128,384]{3,2,1,0:T(8,128)(2,1)}, u32[]{:S(2)}, u32[]{:S(2)}) collective-permute-start(bf16[2,8,128,384]{3,2,1,0:T(8,128)(2,1)S(1)} %bitcast.465), channel_id=1, source_target_pairs={{0,1},{1,0},{2,3},{3,2},{4,5},{5,4},{6,7},{7,6},{8,9},{9,8},{10,11... | collective-permute-start | bytes 4718600 | tf_op jit(solution)/shard_map/ppermute | solution.py:896
  81.2 15.6 %collective-permute-start.14 = (bf16[4,192,384]{2,1,0:T(8,128)(2,1)}, bf16[4,192,384]{2,1,0:T(8,128)(2,1)}, u32[]{:S(2)}, u32[]{:S(2)}) collective-permute-start(bf16[4,192,384]{2,1,0:T(8,128)(2,1)} %get-tuple-element.335), channel_id=1, source_target_pairs={{0,4},{1,5},{2,6},{3,7},{4,0},{5,1},{6,2},{7,3},{8,12},{9,13},{10,... | collective-permute-start | bytes 1769480 | tf_op jit(solution)/shard_map/ppermute | solution.py:896
  81.7 15.3 %collective-permute-start.15 = (bf16[4,192,384]{2,1,0:T(8,128)(2,1)}, bf16[4,192,384]{2,1,0:T(8,128)(2,1)}, u32[]{:S(2)}, u32[]{:S(2)}) collective-permute-start(bf16[4,192,384]{2,1,0:T(8,128)(2,1)} %get-tuple-element.336), channel_id=1, source_target_pairs={{0,2},{1,3},{2,0},{3,1},{4,6},{5,7},{6,4},{7,5},{8,10},{9,11},{10,... | collective-permute-start | bytes 1769480 | tf_op jit(solution)/shard_map/ppermute | solution.py:896
  82.2 33.1 %collective-permute-start.18 = (bf16[1,128,768]{2,1,0:T(8,128)(2,1)}, bf16[1,128,768]{2,1,0:T(8,128)(2,1)}, u32[]{:S(2)}, u32[]{:S(2)}) collective-permute-start(bf16[1,128,768]{2,1,0:T(8,128)(2,1)} %maximum_bitcast_fusion.6), channel_id=1, source_target_pairs={{0,16},{1,17},{2,18},{3,19},{4,20},{5,21},{6,22},{7,23},{8,24},{9,... | collective-permute-start | bytes 589832 | tf_op jit(solution)/shard_map/ppermute | solution.py:896
  98.8 16.5 %collective-permute-start.16 = (bf16[8,96,384]{2,1,0:T(8,128)(2,1)S(1)}, bf16[8,96,384]{2,1,0:T(8,128)(2,1)S(1)}, u32[]{:S(2)}, u32[]{:S(2)}) collective-permute-start(bf16[8,96,384]{2,1,0:T(8,128)(2,1)S(1)} %slice.406), channel_id=1, source_target_pairs={{0,2},{1,3},{2,0},{3,1},{4,6},{5,7},{6,4},{7,5},{8,10},{9,11},{10,... | collective-permute-start | bytes 1769480 | tf_op jit(solution)/shard_map/ppermute | solution.py:896
  99.5 15.8 %collective-permute-start.17 = (bf16[2,4,96,384]{3,2,1,0:T(8,128)(2,1)S(1)}, bf16[2,4,96,384]{3,2,1,0:T(8,128)(2,1)S(1)}, u32[]{:S(2)}, u32[]{:S(2)}) collective-permute-start(bf16[2,4,96,384]{3,2,1,0:T(8,128)(2,1)S(1)} %get-tuple-element.616), channel_id=1, source_target_pairs={{0,4},{1,5},{2,6},{3,7},{4,0},{5,1},{6,2},{7,3},{8,12},{9,13},{10,... | collective-permute-start | bytes 1769480 | tf_op jit(solution)/shard_map/ppermute | solution.py:896
  113.2 53.6 %collective-permute-start.25 = (bf16[2,4,96,384]{3,2,1,0:T(8,128)(2,1)S(1)}, bf16[2,4,96,384]{3,2,1,0:T(8,128)(2,1)S(1)}, u32[]{:S(2)}, u32[]{:S(2)}) collective-permute-start(bf16[2,4,96,384]{3,2,1,0:T(8,128)(2,1)S(1)} %get-tuple-element.615), channel_id=1, source_target_pairs={{0,4},{1,5},{2,6},{3,7},{4,0},{5,1},{6,2},{7,3},{8,12},{9,13},{10,... | collective-permute-start | bytes 1769480 | tf_op jit(solution)/shard_map/ppermute | solution.py:896
  122.5 8.8 %collective-permute-start.19 = (bf16[208,768]{1,0:T(8,128)(2,1)S(1)}, bf16[208,768]{1,0:T(8,128)(2,1)}, u32[]{:S(2)}, u32[]{:S(2)}) collective-permute-start(bf16[208,768]{1,0:T(8,128)(2,1)S(1)} %pad_maximum_fusion.23), channel_id=1, source_target_pairs={{0,1},{1,0},{2,3},{3,2},{4,5},{5,4},{6,7},{7,6},{8,9},{9,8},{10,11... | collective-permute-start | bytes 958472 | tf_op jit(solution)/shard_map/ppermute | solution.py:896
  122.5 10.6 %collective-permute-start.20 = (bf16[208,768]{1,0:T(8,128)(2,1)}, bf16[208,768]{1,0:T(8,128)(2,1)}, u32[]{:S(2)}, u32[]{:S(2)}) collective-permute-start(bf16[208,768]{1,0:T(8,128)(2,1)} %pad_maximum_fusion.24), channel_id=1, source_target_pairs={{0,2},{1,3},{2,0},{3,1},{4,6},{5,7},{6,4},{7,5},{8,10},{9,11},{10,... | collective-permute-start | bytes 958472 | tf_op jit(solution)/shard_map/ppermute | solution.py:896
  124.0 15.2 %collective-permute-start.21 = (bf16[208,768]{1,0:T(8,128)(2,1)}, bf16[208,768]{1,0:T(8,128)(2,1)}, u32[]{:S(2)}, u32[]{:S(2)}) collective-permute-start(bf16[208,768]{1,0:T(8,128)(2,1)} %pad_maximum_fusion.25), channel_id=1, source_target_pairs={{0,3},{1,2},{2,1},{3,0},{4,7},{5,6},{6,5},{7,4},{8,11},{9,10},{10,... | collective-permute-start | bytes 958472 | tf_op jit(solution)/shard_map/ppermute | solution.py:896
  124.3 14.9 %collective-permute-start.22 = (bf16[2,128,768]{2,1,0:T(8,128)(2,1)}, bf16[2,128,768]{2,1,0:T(8,128)(2,1)}, u32[]{:S(2)}, u32[]{:S(2)}) collective-permute-start(bf16[2,128,768]{2,1,0:T(8,128)(2,1)} %maximum_bitcast_fusion.4), channel_id=1, source_target_pairs={{0,8},{1,9},{2,10},{3,11},{4,12},{5,13},{6,14},{7,15},{8,0},{9,1},... | collective-permute-start | bytes 1179656 | tf_op jit(solution)/shard_map/ppermute | solution.py:896
  131.3 35.5 %collective-permute-start.24 = (bf16[8,96,384]{2,1,0:T(8,128)(2,1)S(1)}, bf16[8,96,384]{2,1,0:T(8,128)(2,1)S(1)}, u32[]{:S(2)}, u32[]{:S(2)}) collective-permute-start(bf16[8,96,384]{2,1,0:T(8,128)(2,1)S(1)} %copy-done.33), channel_id=1, source_target_pairs={{0,2},{1,3},{2,0},{3,1},{4,6},{5,7},{6,4},{7,5},{8,10},{9,11},{10,... | collective-permute-start | bytes 1769480 | tf_op jit(solution)/shard_map/ppermute | solution.py:896
  140.4 26.5 %collective-permute-start.23 = (bf16[2,8,96,768]{3,2,1,0:T(8,128)(2,1)S(1)}, bf16[2,8,96,768]{3,2,1,0:T(8,128)(2,1)}, u32[]{:S(2)}, u32[]{:S(2)}) collective-permute-start(bf16[2,8,96,768]{3,2,1,0:T(8,128)(2,1)S(1)} %pad_maximum_fusion.left_ref.right_ref.refs_2_.refs_3_), channel_id=1, source_target_pairs={{0,1},{1,0},{2,3},{3,2},{4,5},{5,4},{6,7},{7,6},{8,9},{9,8},{10,11... | collective-permute-start | bytes 7077896 | tf_op jit(solution)/shard_map/ppermute | solution.py:896
  141.1 24.2 %collective-permute-start.27 = (bf16[4,128,384]{2,1,0:T(8,128)(2,1)S(1)}, bf16[4,128,384]{2,1,0:T(8,128)(2,1)S(1)}, u32[]{:S(2)}, u32[]{:S(2)}) collective-permute-start(bf16[4,128,384]{2,1,0:T(8,128)(2,1)S(1)} %get-tuple-element.636), channel_id=1, source_target_pairs={{0,2},{1,3},{2,0},{3,1},{4,6},{5,7},{6,4},{7,5},{8,10},{9,11},{10,... | collective-permute-start | bytes 1179656 | tf_op jit(solution)/shard_map/ppermute | solution.py:896
  142.7 22.6 %collective-permute-start.26 = (bf16[4,128,384]{2,1,0:T(8,128)(2,1)S(1)}, bf16[4,128,384]{2,1,0:T(8,128)(2,1)}, u32[]{:S(2)}, u32[]{:S(2)}) collective-permute-start(bf16[4,128,384]{2,1,0:T(8,128)(2,1)S(1)} %get-tuple-element.637), channel_id=1, source_target_pairs={{0,4},{1,5},{2,6},{3,7},{4,0},{5,1},{6,2},{7,3},{8,12},{9,13},{10,... | collective-permute-start | bytes 1179656 | tf_op jit(solution)/shard_map/ppermute | solution.py:896
  167.6 20.5 %collective-permute-start.28 = (bf16[8,128,384]{2,1,0:T(8,128)(2,1)S(1)}, bf16[8,128,384]{2,1,0:T(8,128)(2,1)S(1)}, u32[]{:S(2)}, u32[]{:S(2)}) collective-permute-start(bf16[8,128,384]{2,1,0:T(8,128)(2,1)S(1)} %bitcast.482), channel_id=1, source_target_pairs={{0,2},{1,3},{2,0},{3,1},{4,6},{5,7},{6,4},{7,5},{8,10},{9,11},{10,... | collective-permute-start | bytes 2359304 | tf_op jit(solution)/shard_map/ppermute | solution.py:896
  168.2 19.5 %collective-permute-start.29 = (bf16[2,4,128,384]{3,2,1,0:T(8,128)(2,1)S(1)}, bf16[2,4,128,384]{3,2,1,0:T(8,128)(2,1)S(1)}, u32[]{:S(2)}, u32[]{:S(2)}) collective-permute-start(bf16[2,4,128,384]{3,2,1,0:T(8,128)(2,1)S(1)} %pad_maximum_fusion.19), channel_id=1, source_target_pairs={{0,4},{1,5},{2,6},{3,7},{4,0},{5,1},{6,2},{7,3},{8,12},{9,13},{10,... | collective-permute-start | bytes 2359304 | tf_op jit(solution)/shard_map/ppermute | solution.py:896
  169.0 19.6 %collective-permute-start.30 = (bf16[2,8,96,384]{3,2,1,0:T(8,128)(2,1)S(1)}, bf16[2,8,96,384]{3,2,1,0:T(8,128)(2,1)}, u32[]{:S(2)}, u32[]{:S(2)}) collective-permute-start(bf16[2,8,96,384]{3,2,1,0:T(8,128)(2,1)S(1)} %pad_maximum_fusion.10.refs_0_.refs_2_), channel_id=1, source_target_pairs={{0,1},{1,0},{2,3},{3,2},{4,5},{5,4},{6,7},{7,6},{8,9},{9,8},{10,11... | collective-permute-start | bytes 3538952 | tf_op jit(solution)/shard_map/ppermute | solution.py:896
  170.3 18.2 %collective-permute-start.31 = (bf16[2,8,96,384]{3,2,1,0:T(8,128)(2,1)S(1)}, bf16[2,8,96,384]{3,2,1,0:T(8,128)(2,1)S(1)}, u32[]{:S(2)}, u32[]{:S(2)}) collective-permute-start(bf16[2,8,96,384]{3,2,1,0:T(8,128)(2,1)S(1)} %bitcast.529), channel_id=1, source_target_pairs={{0,1},{1,0},{2,3},{3,2},{4,5},{5,4},{6,7},{7,6},{8,9},{9,8},{10,11... | collective-permute-start | bytes 3538952 | tf_op jit(solution)/shard_map/ppermute | solution.py:896
  188.6 12.2 %collective-permute-start.32 = (bf16[2,8,128,384]{3,2,1,0:T(8,128)(2,1)S(1)}, bf16[2,8,128,384]{3,2,1,0:T(8,128)(2,1)}, u32[]{:S(2)}, u32[]{:S(2)}) collective-permute-start(bf16[2,8,128,384]{3,2,1,0:T(8,128)(2,1)S(1)} %pad_maximum_fusion.3.refs_2_.refs_4_), channel_id=1, source_target_pairs={{0,1},{1,0},{2,3},{3,2},{4,5},{5,4},{6,7},{7,6},{8,9},{9,8},{10,11... | collective-permute-start | bytes 4718600 | tf_op jit(solution)/shard_map/ppermute | solution.py:896
  189.1 11.7 %collective-permute-start.33 = (bf16[2,8,128,384]{3,2,1,0:T(8,128)(2,1)S(1)}, bf16[2,8,128,384]{3,2,1,0:T(8,128)(2,1)}, u32[]{:S(2)}, u32[]{:S(2)}) collective-permute-start(bf16[2,8,128,384]{3,2,1,0:T(8,128)(2,1)S(1)} %bitcast.511), channel_id=1, source_target_pairs={{0,1},{1,0},{2,3},{3,2},{4,5},{5,4},{6,7},{7,6},{8,9},{9,8},{10,11... | collective-permute-start | bytes 4718600 | tf_op jit(solution)/shard_map/ppermute | solution.py:896
  250.8 19.2 %collective-permute-start.40 = (bf16[2,768,768]{2,1,0:T(8,128)(2,1)}, bf16[2,768,768]{2,1,0:T(8,128)(2,1)S(1)}, u32[]{:S(2)}, u32[]{:S(2)}) collective-permute-start(bf16[2,768,768]{2,1,0:T(8,128)(2,1)} %get-tuple-element.401), channel_id=1, source_target_pairs={{0,1},{1,0},{2,3},{3,2},{4,5},{5,4},{6,7},{7,6},{8,9},{9,8},{10,11... | collective-permute-start | bytes 7077896 | tf_op jit(solution)/shard_map/ppermute | solution.py:896
  250.9 19.1 %collective-permute-start.41 = (bf16[2,768,768]{2,1,0:T(8,128)(2,1)}, bf16[2,768,768]{2,1,0:T(8,128)(2,1)}, u32[]{:S(2)}, u32[]{:S(2)}) collective-permute-start(bf16[2,768,768]{2,1,0:T(8,128)(2,1)} %get-tuple-element.402), channel_id=1, source_target_pairs={{0,1},{1,0},{2,3},{3,2},{4,5},{5,4},{6,7},{7,6},{8,9},{9,8},{10,11... | collective-permute-start | bytes 7077896 | tf_op jit(solution)/shard_map/ppermute | solution.py:896
  272.7 31.9 %collective-permute-start.42 = (bf16[8,96,768]{2,1,0:T(8,128)(2,1)}, bf16[8,96,768]{2,1,0:T(8,128)(2,1)}, u32[]{:S(2)}, u32[]{:S(2)}) collective-permute-start(bf16[8,96,768]{2,1,0:T(8,128)(2,1)} %fusion), channel_id=1, source_target_pairs={{0,2},{1,3},{2,0},{3,1},{4,6},{5,7},{6,4},{7,5},{8,10},{9,11},{10,... | collective-permute-start | bytes 3538952 | tf_op jit(solution)/shard_map/ppermute | solution.py:896
  276.9 28.0 %collective-permute-start.43 = (bf16[2,4,96,768]{3,2,1,0:T(8,128)(2,1)}, bf16[2,4,96,768]{3,2,1,0:T(8,128)(2,1)}, u32[]{:S(2)}, u32[]{:S(2)}) collective-permute-start(bf16[2,4,96,768]{3,2,1,0:T(8,128)(2,1)} %fusion.1), channel_id=1, source_target_pairs={{0,4},{1,5},{2,6},{3,7},{4,0},{5,1},{6,2},{7,3},{8,12},{9,13},{10,... | collective-permute-start | bytes 3538952 | tf_op jit(solution)/shard_map/ppermute | solution.py:896
  306.1 30.8 %collective-permute-start.44 = (bf16[4,96,768]{2,1,0:T(8,128)(2,1)S(1)}, bf16[4,96,768]{2,1,0:T(8,128)(2,1)S(1)}, u32[]{:S(2)}, u32[]{:S(2)}) collective-permute-start(bf16[4,96,768]{2,1,0:T(8,128)(2,1)S(1)} %fusion.5), channel_id=1, source_target_pairs={{0,4},{1,5},{2,6},{3,7},{4,0},{5,1},{6,2},{7,3},{8,12},{9,13},{10,... | collective-permute-start | bytes 1769480 | tf_op jit(solution)/shard_map/ppermute | solution.py:896
  309.9 27.0 %collective-permute-start.45 = (bf16[4,96,768]{2,1,0:T(8,128)(2,1)}, bf16[4,96,768]{2,1,0:T(8,128)(2,1)}, u32[]{:S(2)}, u32[]{:S(2)}) collective-permute-start(bf16[4,96,768]{2,1,0:T(8,128)(2,1)} %fusion.4), channel_id=1, source_target_pairs={{0,2},{1,3},{2,0},{3,1},{4,6},{5,7},{6,4},{7,5},{8,10},{9,11},{10,... | collective-permute-start | bytes 1769480 | tf_op jit(solution)/shard_map/ppermute | solution.py:896
  310.4 26.5 %collective-permute-start.46 = (bf16[2,768,768]{2,1,0:T(8,128)(2,1)}, bf16[2,768,768]{2,1,0:T(8,128)(2,1)S(1)}, u32[]{:S(2)}, u32[]{:S(2)}) collective-permute-start(bf16[2,768,768]{2,1,0:T(8,128)(2,1)} %get-tuple-element.426), channel_id=1, source_target_pairs={{0,1},{1,0},{2,3},{3,2},{4,5},{5,4},{6,7},{7,6},{8,9},{9,8},{10,11... | collective-permute-start | bytes 7077896 | tf_op jit(solution)/shard_map/ppermute | solution.py:896
  341.6 7.5 %collective-permute-start.47 = (bf16[208,768]{1,0:T(8,128)(2,1)}, bf16[208,768]{1,0:T(8,128)(2,1)}, u32[]{:S(2)}, u32[]{:S(2)}) collective-permute-start(bf16[208,768]{1,0:T(8,128)(2,1)} %get-tuple-element.433), channel_id=1, source_target_pairs={{0,1},{1,0},{2,3},{3,2},{4,5},{5,4},{6,7},{7,6},{8,9},{9,8},{10,11... | collective-permute-start | bytes 958472 | tf_op jit(solution)/shard_map/ppermute | solution.py:896
  342.1 10.7 %collective-permute-start.48 = (bf16[208,768]{1,0:T(8,128)(2,1)}, bf16[208,768]{1,0:T(8,128)(2,1)}, u32[]{:S(2)}, u32[]{:S(2)}) collective-permute-start(bf16[208,768]{1,0:T(8,128)(2,1)} %get-tuple-element.434), channel_id=1, source_target_pairs={{0,2},{1,3},{2,0},{3,1},{4,6},{5,7},{6,4},{7,5},{8,10},{9,11},{10,... | collective-permute-start | bytes 958472 | tf_op jit(solution)/shard_map/ppermute | solution.py:896
  343.6 14.2 %collective-permute-start.49 = (bf16[208,768]{1,0:T(8,128)(2,1)}, bf16[208,768]{1,0:T(8,128)(2,1)}, u32[]{:S(2)}, u32[]{:S(2)}) collective-permute-start(bf16[208,768]{1,0:T(8,128)(2,1)} %get-tuple-element.435), channel_id=1, source_target_pairs={{0,3},{1,2},{2,1},{3,0},{4,7},{5,6},{6,5},{7,4},{8,11},{9,10},{10,... | collective-permute-start | bytes 958472 | tf_op jit(solution)/shard_map/ppermute | solution.py:896
  344.9 29.3 %collective-permute-start.50 = (bf16[2,4,96,768]{3,2,1,0:T(8,128)(2,1)S(1)}, bf16[2,4,96,768]{3,2,1,0:T(8,128)(2,1)S(1)}, u32[]{:S(2)}, u32[]{:S(2)}) collective-permute-start(bf16[2,4,96,768]{3,2,1,0:T(8,128)(2,1)S(1)} %copy-done.24), channel_id=1, source_target_pairs={{0,4},{1,5},{2,6},{3,7},{4,0},{5,1},{6,2},{7,3},{8,12},{9,13},{10,... | collective-permute-start | bytes 3538952 | tf_op jit(solution)/shard_map/ppermute | solution.py:896
  375.3 26.5 %collective-permute-start.51 = (bf16[2,768,768]{2,1,0:T(8,128)(2,1)}, bf16[2,768,768]{2,1,0:T(8,128)(2,1)}, u32[]{:S(2)}, u32[]{:S(2)}) collective-permute-start(bf16[2,768,768]{2,1,0:T(8,128)(2,1)} %get-tuple-element.450), channel_id=1, source_target_pairs={{0,1},{1,0},{2,3},{3,2},{4,5},{5,4},{6,7},{7,6},{8,9},{9,8},{10,11... | collective-permute-start | bytes 7077896 | tf_op jit(solution)/shard_map/ppermute | solution.py:896
  376.3 21.9 %collective-permute-start.53 = (bf16[1,192,768]{2,1,0:T(8,128)(2,1)S(1)}, bf16[1,192,768]{2,1,0:T(8,128)(2,1)S(1)}, u32[]{:S(2)}, u32[]{:S(2)}) collective-permute-start(bf16[1,192,768]{2,1,0:T(8,128)(2,1)S(1)} %pad_maximum_fusion.27), channel_id=1, source_target_pairs={{0,8},{1,9},{2,10},{3,11},{4,12},{5,13},{6,14},{7,15},{8,0},{9,1},... | collective-permute-start | bytes 884744 | tf_op jit(solution)/shard_map/ppermute | solution.py:896
  378.3 23.5 %collective-permute-start.54 = (bf16[1,192,768]{2,1,0:T(8,128)(2,1)S(1)}, bf16[1,192,768]{2,1,0:T(8,128)(2,1)S(1)}, u32[]{:S(2)}, u32[]{:S(2)}) collective-permute-start(bf16[1,192,768]{2,1,0:T(8,128)(2,1)S(1)} %pad_maximum_fusion.28), channel_id=1, source_target_pairs={{0,16},{1,17},{2,18},{3,19},{4,20},{5,21},{6,22},{7,23},{8,24},{9,... | collective-permute-start | bytes 884744 | tf_op jit(solution)/shard_map/ppermute | solution.py:896
  379.2 22.6 %collective-permute-start.55 = (bf16[1,192,768]{2,1,0:T(8,128)(2,1)}, bf16[1,192,768]{2,1,0:T(8,128)(2,1)S(1)}, u32[]{:S(2)}, u32[]{:S(2)}) collective-permute-start(bf16[1,192,768]{2,1,0:T(8,128)(2,1)} %pad_maximum_fusion.29), channel_id=1, source_target_pairs={{0,24},{1,25},{2,26},{3,27},{4,28},{5,29},{6,30},{7,31},{8,16},{9,... | collective-permute-start | bytes 884744 | tf_op jit(solution)/shard_map/ppermute | solution.py:896
  382.3 19.5 %collective-permute-start.52 = (bf16[4,96,768]{2,1,0:T(8,128)(2,1)S(1)}, bf16[4,96,768]{2,1,0:T(8,128)(2,1)S(1)}, u32[]{:S(2)}, u32[]{:S(2)}) collective-permute-start(bf16[4,96,768]{2,1,0:T(8,128)(2,1)S(1)} %fusion.3), channel_id=1, source_target_pairs={{0,2},{1,3},{2,0},{3,1},{4,6},{5,7},{6,4},{7,5},{8,10},{9,11},{10,... | collective-permute-start | bytes 1769480 | tf_op jit(solution)/shard_map/ppermute | solution.py:896
  407.1 20.1 %collective-permute-start.56 = (bf16[8,96,384]{2,1,0:T(8,128)(2,1)}, bf16[8,96,384]{2,1,0:T(8,128)(2,1)}, u32[]{:S(2)}, u32[]{:S(2)}) collective-permute-start(bf16[8,96,384]{2,1,0:T(8,128)(2,1)} %fusion.6), channel_id=1, source_target_pairs={{0,2},{1,3},{2,0},{3,1},{4,6},{5,7},{6,4},{7,5},{8,10},{9,11},{10,... | collective-permute-start | bytes 1769480 | tf_op jit(solution)/shard_map/ppermute | solution.py:896
  408.6 18.6 %collective-permute-start.57 = (bf16[2,4,96,384]{3,2,1,0:T(8,128)(2,1)}, bf16[2,4,96,384]{3,2,1,0:T(8,128)(2,1)}, u32[]{:S(2)}, u32[]{:S(2)}) collective-permute-start(bf16[2,4,96,384]{3,2,1,0:T(8,128)(2,1)} %fusion.7), channel_id=1, source_target_pairs={{0,4},{1,5},{2,6},{3,7},{4,0},{5,1},{6,2},{7,3},{8,12},{9,13},{10,... | collective-permute-start | bytes 1769480 | tf_op jit(solution)/shard_map/ppermute | solution.py:896
  411.5 42.3 %collective-permute-start.62 = (bf16[1,96,768]{2,1,0:T(8,128)(2,1)}, bf16[1,96,768]{2,1,0:T(8,128)(2,1)}, u32[]{:S(2)}, u32[]{:S(2)}) collective-permute-start(bf16[1,96,768]{2,1,0:T(8,128)(2,1)} %get-tuple-element.542), channel_id=1, source_target_pairs={{0,8},{1,9},{2,10},{3,11},{4,12},{5,13},{6,14},{7,15},{8,0},{9,1},... | collective-permute-start | bytes 442376 | tf_op jit(solution)/shard_map/ppermute | solution.py:896
  416.7 37.0 %collective-permute-start.63 = (bf16[1,96,768]{2,1,0:T(8,128)(2,1)}, bf16[1,96,768]{2,1,0:T(8,128)(2,1)}, u32[]{:S(2)}, u32[]{:S(2)}) collective-permute-start(bf16[1,96,768]{2,1,0:T(8,128)(2,1)} %get-tuple-element.541), channel_id=1, source_target_pairs={{0,16},{1,17},{2,18},{3,19},{4,20},{5,21},{6,22},{7,23},{8,24},{9,... | collective-permute-start | bytes 442376 | tf_op jit(solution)/shard_map/ppermute | solution.py:896
  427.2 5.9 %collective-permute-start.58 = (bf16[16,24,896]{2,1,0:T(8,128)(2,1)S(1)}, bf16[16,24,896]{2,1,0:T(8,128)(2,1)S(1)}, u32[]{:S(2)}, u32[]{:S(2)}) collective-permute-start(bf16[16,24,896]{2,1,0:T(8,128)(2,1)S(1)} %get-tuple-element.473), channel_id=1, source_target_pairs={{0,1},{1,0},{2,3},{3,2},{4,5},{5,4},{6,7},{7,6},{8,9},{9,8},{10,11... | collective-permute-start | bytes 2064392 | tf_op jit(solution)/shard_map/ppermute | solution.py:896
  434.0 8.8 %collective-permute-start.59 = (bf16[4,96,384]{2,1,0:T(8,128)(2,1)S(1)}, bf16[4,96,384]{2,1,0:T(8,128)(2,1)S(1)}, u32[]{:S(2)}, u32[]{:S(2)}) collective-permute-start(bf16[4,96,384]{2,1,0:T(8,128)(2,1)S(1)} %fusion.15), channel_id=1, source_target_pairs={{0,4},{1,5},{2,6},{3,7},{4,0},{5,1},{6,2},{7,3},{8,12},{9,13},{10,... | collective-permute-start | bytes 884744 | tf_op jit(solution)/shard_map/ppermute | solution.py:896
  435.5 9.9 %collective-permute-start.60 = (bf16[4,96,384]{2,1,0:T(8,128)(2,1)S(1)}, bf16[4,96,384]{2,1,0:T(8,128)(2,1)S(1)}, u32[]{:S(2)}, u32[]{:S(2)}) collective-permute-start(bf16[4,96,384]{2,1,0:T(8,128)(2,1)S(1)} %fusion.10), channel_id=1, source_target_pairs={{0,2},{1,3},{2,0},{3,1},{4,6},{5,7},{6,4},{7,5},{8,10},{9,11},{10,... | collective-permute-start | bytes 884744 | tf_op jit(solution)/shard_map/ppermute | solution.py:896
  436.0 15.4 %collective-permute-start.61 = (bf16[8,24,896]{2,1,0:T(8,128)(2,1)S(1)}, bf16[8,24,896]{2,1,0:T(8,128)(2,1)S(1)}, u32[]{:S(2)}, u32[]{:S(2)}) collective-permute-start(bf16[8,24,896]{2,1,0:T(8,128)(2,1)S(1)} %fusion.14), channel_id=1, source_target_pairs={{0,2},{1,3},{2,0},{3,1},{4,6},{5,7},{6,4},{7,5},{8,10},{9,11},{10,... | collective-permute-start | bytes 1032200 | tf_op jit(solution)/shard_map/ppermute | solution.py:896
  442.8 10.9 %collective-permute-start.64 = (bf16[1,96,768]{2,1,0:T(8,128)(2,1)S(1)}, bf16[1,96,768]{2,1,0:T(8,128)(2,1)S(1)}, u32[]{:S(2)}, u32[]{:S(2)}) collective-permute-start(bf16[1,96,768]{2,1,0:T(8,128)(2,1)S(1)} %get-tuple-element.540), channel_id=1, source_target_pairs={{0,24},{1,25},{2,26},{3,27},{4,28},{5,29},{6,30},{7,31},{8,16},{9,... | collective-permute-start | bytes 442376 | tf_op jit(solution)/shard_map/ppermute | solution.py:896
  453.9 10.6 %collective-permute-start.65 = (bf16[1,96,768]{2,1,0:T(8,128)(2,1)S(1)}, bf16[1,96,768]{2,1,0:T(8,128)(2,1)S(1)}, u32[]{:S(2)}, u32[]{:S(2)}) collective-permute-start(bf16[1,96,768]{2,1,0:T(8,128)(2,1)S(1)} %get-tuple-element.494), channel_id=1, source_target_pairs={{0,8},{1,9},{2,10},{3,11},{4,12},{5,13},{6,14},{7,15},{8,0},{9,1},... | collective-permute-start | bytes 442376 | tf_op jit(solution)/shard_map/ppermute | solution.py:896
  455.1 13.4 %collective-permute-start.66 = (bf16[1,96,768]{2,1,0:T(8,128)(2,1)S(1)}, bf16[1,96,768]{2,1,0:T(8,128)(2,1)S(1)}, u32[]{:S(2)}, u32[]{:S(2)}) collective-permute-start(bf16[1,96,768]{2,1,0:T(8,128)(2,1)S(1)} %get-tuple-element.495), channel_id=1, source_target_pairs={{0,16},{1,17},{2,18},{3,19},{4,20},{5,21},{6,22},{7,23},{8,24},{9,... | collective-permute-start | bytes 442376 | tf_op jit(solution)/shard_map/ppermute | solution.py:896
  457.0 11.6 %collective-permute-start.67 = (bf16[1,96,768]{2,1,0:T(8,128)(2,1)S(1)}, bf16[1,96,768]{2,1,0:T(8,128)(2,1)S(1)}, u32[]{:S(2)}, u32[]{:S(2)}) collective-permute-start(bf16[1,96,768]{2,1,0:T(8,128)(2,1)S(1)} %get-tuple-element.496), channel_id=1, source_target_pairs={{0,24},{1,25},{2,26},{3,27},{4,28},{5,29},{6,30},{7,31},{8,16},{9,... | collective-permute-start | bytes 442376 | tf_op jit(solution)/shard_map/ppermute | solution.py:896
  458.4 10.2 %collective-permute-start.68 = (bf16[4,24,896]{2,1,0:T(8,128)(2,1)S(1)}, bf16[4,24,896]{2,1,0:T(8,128)(2,1)S(1)}, u32[]{:S(2)}, u32[]{:S(2)}) collective-permute-start(bf16[4,24,896]{2,1,0:T(8,128)(2,1)S(1)} %fusion.58), channel_id=1, source_target_pairs={{0,4},{1,5},{2,6},{3,7},{4,0},{5,1},{6,2},{7,3},{8,12},{9,13},{10,... | collective-permute-start | bytes 516104 | tf_op jit(solution)/shard_map/ppermute | solution.py:896
  468.7 6.8 %collective-permute-start.69 = (bf16[1,24,896]{2,1,0:T(8,128)(2,1)S(1)}, bf16[1,24,896]{2,1,0:T(8,128)(2,1)S(1)}, u32[]{:S(2)}, u32[]{:S(2)}) collective-permute-start(bf16[1,24,896]{2,1,0:T(8,128)(2,1)S(1)} %get-tuple-element.502), channel_id=1, source_target_pairs={{0,8},{1,9},{2,10},{3,11},{4,12},{5,13},{6,14},{7,15},{8,0},{9,1},... | collective-permute-start | bytes 129032 | tf_op jit(solution)/shard_map/ppermute | solution.py:896
  472.0 5.9 %collective-permute-start.71 = (bf16[1,24,896]{2,1,0:T(8,128)(2,1)S(1)}, bf16[1,24,896]{2,1,0:T(8,128)(2,1)S(1)}, u32[]{:S(2)}, u32[]{:S(2)}) collective-permute-start(bf16[1,24,896]{2,1,0:T(8,128)(2,1)S(1)} %get-tuple-element.504), channel_id=1, source_target_pairs={{0,24},{1,25},{2,26},{3,27},{4,28},{5,29},{6,30},{7,31},{8,16},{9,... | collective-permute-start | bytes 129032 | tf_op jit(solution)/shard_map/ppermute | solution.py:896
  (81 other events, 297.6 us)

commit v7 on v6

--- a/solution.py
+++ b/solution.py
@@ -1267,11 +1267,10 @@
     d_first[0], d_normed[0] = temporal_backward(
         normed_t, d_rows, first_w[0], rows_wide, qkv_t, mixed_t, 0
     )
-    d_rows, first_own, d_normed[0], core_first, sum_second[-1], *others = tick(
-        d_rows, d_first[0], d_normed[0], core_first, sum_second[-1], *others
-    )
-    sum_up += [other[..., :rows_wide, :] for other in others]
-    sum_down += [other[..., rows_wide:, :] for other in others]
+    d_rows, first_own, d_normed[0], core_first, sum_second[-1] = tick(
+        d_rows, d_first[0], d_normed[0], core_first, sum_second[-1]
+    )
+    wide_parts = others
 
     sum_first = [blocked(first_own), blocked(core_first)]
     send_left, left = cube.cut_row([term[..., :middle] for term in sum_first])
@@ -1288,7 +1287,11 @@
         by_slot, start_slot, slot_valid, d_rows, d_normed[0], d_normed[1], norms, d_norms
     )
     send, sum_early = cube.cut([d_early.reshape(-1, rows_small, dim + 128)], 1)
-    other_left, other_right, send, token = tick(other_left, other_right, send, token)
+    other_left, other_right, send, token, *wide_parts = tick(
+        other_left, other_right, send, token, *wide_parts
+    )
+    sum_up += [other[..., :rows_wide, :] for other in wide_parts]
+    sum_down += [other[..., rows_wide:, :] for other in wide_parts]
     other = cube.swap(send, 1)
     left.append(other_left)
     right.append(other_right)

time: 514 us -> 507 us (0.986)
    unnamed x138 -> x126, local copies, waits for them, and re-layouts: 12.4 us -> 10.5 us
  transfers between devices with their start and end apart: 77 -> 77, of which waited for: 30 -> 29; matrix products, arithmetic and copies ran while one was open for 13% -> 15% of each run, Pallas kernels for 36% -> 36%
where the time goes in v7:
time: 507 us; the launch traced here: 499 us
  Pallas kernels  221 us (44%)
  starting transfers between devices  82.3 us (16%)
  waiting for transfers between devices  79.9 us (16%)
  other arithmetic  64.1 us (13%)
  local copies, waits for them, and re-layouts  38.1 us (8%)
  between operations  10 us (2%)
    pallas_call x20, Pallas kernels, call(): pl.pallas_call(kernel, grid=(steps,), in_specs=in_specs or [spec_of(value...  142 us
    ppermute x77, starting transfers between devices, swap(): return lax.ppermute(value, ALL, [(i, i ^ mask) for i in range(self.count)])  82.3 us
    ppermute x77, waiting for transfers between devices, swap(): return lax.ppermute(value, ALL, [(i, i ^ mask) for i in range(self.count)])  79.9 us
    pallas_call x4, Pallas kernels, block_call(): pl.pallas_call(with_fetches(kernel, places), grid=(2,), in_specs=specs, o...  73.2 us
    convert_element_type x24, other arithmetic, low(): return value.astype(LOWER)  24.7 us
    unnamed x126, local copies, waits for them, and re-layouts  10.5 us
  transfers between devices with their start and end apart: 77, of which 29 were waited for; matrix products, arithmetic and copies ran while one was open for 15% of the time, Pallas kernels for 36%

profile of v7, /device:TPU:0, one launch (start us, length us, event | category | flops | bytes accessed | tf_op | source)
XLA Modules:
  0.0 498.5 jit_solution(13471145521591755443)
XLA Ops:
  5.7 4.1 collective-permute-start
  15.4 1.7 gather_fusion
  20.9 1.6 collective-permute-start.1
  25.9 7.6 %collective-permute-done.3 = bf16[208,768]{1,0:T(8,128)(2,1)S(1)} collective-permute-done((bf16[208,768]{1,0:T(8,128)(2,1)S(1)}, bf16[208,768]{1,0:T(8,128)(2,1)S(1)}, u32[]{:S(2)}, u32[]{:S(2)}) %collective-permute-start.3) | collective-permute-done | bytes 319520 | tf_op jit(solution)/shard_map/ppermute | solution.py:896
  33.5 4.9 collective-permute-done.4
  44.3 3.1 collective-permute-start.11
  47.4 3.1 collective-permute-done.5
  52.3 1.6 collective-permute-start.7
  56.8 14.8 %collective-permute-done.7 = bf16[8,128,384]{2,1,0:T(8,128)(2,1)S(1)} collective-permute-done((bf16[8,128,384]{2,1,0:T(8,128)(2,1)S(1)}, bf16[8,128,384]{2,1,0:T(8,128)(2,1)S(1)}, u32[]{:S(2)}, u32[]{:S(2)}) %collective-permute-start.7) | collective-permute-done | bytes 786464 | tf_op jit(solution)/shard_map/ppermute | solution.py:896
  83.7 1.8 collective-permute-done.12.other_left.left_ref
  89.5 5.1 %embed.1 = (f32[832,768]{1,0:T(8,128)}, bf16[832,768]{1,0:T(8,128)(2,1)}) custom-call(bf16[832,768]{1,0:T(8,128)(2,1)} %pad_maximum_fusion.5.patches_ref, bf16[768,768]{1,0:T(8,128)(2,1)} %bitcast.532, f32[832,1]{1,0:T(8,128)} %copy.104.valid_ref, f32[8,768]{1,0:T(8,128)} %reshape.1638.norms_ref.refs_5_.refs_6_.refs_7_.refs_11_), custom_call_target="tpu_custom_call" | custom-call | flops 15000000512 | bytes 8388608 | tf_op jit(solution)/shard_map/embed/pallas_call | solution.py:589
  94.6 2.1 collective-permute-done.14
  101.0 10.7 %temporal_forward.1 = (bf16[4,4,576,208]{3,2,1,0:T(8,128)(2,1)}, bf16[4,832,192]{2,1,0:T(8,128)(2,1)}) custom-call(bf16[832,768]{1,0:T(8,128)(2,1)} %get-tuple-element.447.normed_ref, bf16[2,8,128,384]{3,2,1,0:T(8,128)(2,1)} %pad_maximum_fusion.1.own_left.left_ref, bf16[2,8,128,384]{3,2,1,0:T(8,128)(2,1)} %bitcast.466, ...), custom_call_target="tpu_custom_call" | custom-call | flops 40000000000 | bytes 8388608 | tf_op jit(solution)/shard_map/temporal_forward/pallas_call | solution.py:589
  128.7 2.6 convolution_multiply_fusion.start_ref
  133.1 6.1 %collective-permute-done.21.refs_3_ = bf16[208,768]{1,0:T(8,128)(2,1)} collective-permute-done((bf16[208,768]{1,0:T(8,128)(2,1)}, bf16[208,768]{1,0:T(8,128)(2,1)}, u32[]{:S(2)}, u32[]{:S(2)}) %collective-permute-start.21) | collective-permute-done | bytes 319520 | tf_op jit(solution)/shard_map/ppermute | solution.py:896
  141.1 1.6 collective-permute-start.27
  144.2 5.7 %enter_frame.1 = (f32[832,768]{1,0:T(8,128)}, bf16[832,768]{1,0:T(8,128)(2,1)}) custom-call(f32[832,768]{1,0:T(8,128)} %convolution_multiply_fusion.start_ref, bf16[208,768]{1,0:T(8,128)(2,1)} %pad_maximum_fusion.26.refs_0_, bf16[208,768]{1,0:T(8,128)(2,1)} %collective-permute-done.19.refs_1_, bf16[208,768]{1,0:T(8,128)(2,1)} %collective-permute-done.20.refs_2_, ...), custom_call_target="tpu_custom_call" | custom-call | flops 2000000000 | bytes 8388608 | tf_op jit(solution)/shard_map/enter_frame/pallas_call | solution.py:589
  149.9 15.4 %spatial_forward.2 = (bf16[2,832,576]{2,1,0:T(8,128)(2,1)}, bf16[2,832,192]{2,1,0:T(8,128)(2,1)}, bf16[2,832,192]{2,1,0:T(8,128)(2,1)}, f32[832,768]{1,0:T(8,128)}) custom-call(bf16[832,768]{1,0:T(8,128)(2,1)} %get-tuple-element.415.normed_ref.refs_0_, bf16[2,8,96,768]{3,2,1,0:T(8,128)(2,1)} %copy-done.3, bf16[2,8,96,768]{3,2,1,0:T(8,128)(2,1)} %copy-done.3, ...), custom_call_target="tpu_custom_call" | custom-call | flops 15000000512 | bytes 8388608 | tf_op jit(solution)/shard_map/spatial_forward/pallas_call | solution.py:589
  170.4 17.2 %spatial_forward.3 = (bf16[2,832,576]{2,1,0:T(8,128)(2,1)}, bf16[2,832,192]{2,1,0:T(8,128)(2,1)}, bf16[2,832,192]{2,1,0:T(8,128)(2,1)}, f32[832,768]{1,0:T(8,128)}, bf16[832,768]{1,0:T(8,128)(2,1)}) custom-call(bf16[832,768]{1,0:T(8,128)(2,1)} %get-tuple-element.415.normed_ref.refs_0_, ...), custom_call_target="tpu_custom_call" | custom-call | flops 15000000512 | bytes 8388608 | tf_op jit(solution)/shard_map/spatial_forward/pallas_call | solution.py:665
  190.9 9.9 %feed_forward.2 = (bf16[2,832,768]{2,1,0:T(8,128)(2,1)}, bf16[2,832,768]{2,1,0:T(8,128)(2,1)}, f32[832,768]{1,0:T(8,128)}) custom-call(bf16[832,768]{1,0:T(8,128)(2,1)} %get-tuple-element.391.normed_ref.refs_0_, bf16[2,8,96,384]{3,2,1,0:T(8,128)(2,1)} %copy-done.22, bf16[2,8,96,384]{3,2,1,0:T(8,128)(2,1)} %bitcast.530, bf16[2,8,128,384]{3,2,1,0:T(8,128)(2,1)} %copy-done.10, ...), custom_call_target="tpu_custom_call" | custom-call | flops 10000000000 | bytes 8388608 | tf_op jit(solution)/shard_map/feed_forward/pallas_call | solution.py:589
  200.8 12.1 %feed_forward.3 = (bf16[2,832,768]{2,1,0:T(8,128)(2,1)}, bf16[2,832,768]{2,1,0:T(8,128)(2,1)}, f32[832,768]{1,0:T(8,128)}, f32[1,768]{1,0:T(1,128)}) custom-call(bf16[832,768]{1,0:T(8,128)(2,1)} %get-tuple-element.391.normed_ref.refs_0_, bf16[2,8,96,384]{3,2,1,0:T(8,128)(2,1)} %collective-permute-done.30.refs_1_.refs_0_, bf16[2,8,96,384]{3,2,1,0:T(8,128)(2,1)} %copy-done.61, ...), custom_call_target="tpu_custom_call" | custom-call | flops 10000000000 | bytes 8388608 | tf_op jit(solution)/shard_map/feed_forward/pallas_call | solution.py:665
  219.0 1.7 collective-permute-start.37
  220.7 2.5 collective-permute-start.38
  229.3 7.3 %losses.1 = (f32[1,1]{1,0:T(1,128)}, bf16[8,768]{1,0:T(8,128)(2,1)}, bf16[8,768]{1,0:T(8,128)(2,1)}, f32[832,768]{1,0:T(8,128)}, bf16[832,768]{1,0:T(8,128)(2,1)}, /*index=5*/f32[2,768]{1,0:T(2,128)}) custom-call(s32[1]{0:T(128)} %bitcast.clip_ref, f32[8,896]{1,0:T(8,128)} %squeeze_reshape.3.facts_ref, bf16[768,768]{1,0:T(8,128)(2,1)} %bitcast.474, ...), custom_call_target="tpu_custom_call" | custom-call | flops 1000000000 | bytes 8388608 | tf_op jit(solution)/shard_map/losses/pallas_call | solution.py:589
  236.6 14.2 %feed_backward.2 = (bf16[2,768,768]{2,1,0:T(8,128)(2,1)}, bf16[2,768,768]{2,1,0:T(8,128)(2,1)}, f32[832,768]{1,0:T(8,128)}) custom-call(bf16[832,768]{1,0:T(8,128)(2,1)} %get-tuple-element.391.normed_ref.refs_0_, bf16[832,768]{1,0:T(8,128)(2,1)} %get-tuple-element.392.grad_ref.refs_1_, bf16[2,8,96,384]{3,2,1,0:T(8,128)(2,1)} %collective-permute-done.30.refs_1_.refs_0_, ...), custom_call_target="tpu_custom_call" | custom-call | flops 15000000512 | bytes 8388608 | tf_op jit(solution)/shard_map/feed_backward/pallas_call | solution.py:589
  252.6 17.4 %feed_backward.3 = (bf16[2,768,768]{2,1,0:T(8,128)(2,1)}, bf16[2,768,768]{2,1,0:T(8,128)(2,1)}, f32[832,768]{1,0:T(8,128)}, bf16[832,768]{1,0:T(8,128)(2,1)}, f32[2,768]{1,0:T(2,128)}) custom-call(bf16[832,768]{1,0:T(8,128)(2,1)} %get-tuple-element.391.normed_ref.refs_0_, bf16[832,768]{1,0:T(8,128)(2,1)} %get-tuple-element.392.grad_ref.refs_1_, ...), custom_call_target="tpu_custom_call" | custom-call | flops 15000000512 | bytes 8388608 | tf_op jit(solution)/shard_map/feed_backward/pallas_call | solution.py:665
  270.0 2.7 fusion
  274.3 2.6 fusion.1
  278.4 24.6 %spatial_backward.2 = (bf16[2,768,768]{2,1,0:T(8,128)(2,1)}, f32[832,768]{1,0:T(8,128)}) custom-call(bf16[832,768]{1,0:T(8,128)(2,1)} %get-tuple-element.415.normed_ref.refs_0_, bf16[832,768]{1,0:T(8,128)(2,1)} %get-tuple-element.416.grad_ref.refs_1_, bf16[2,8,96,768]{3,2,1,0:T(8,128)(2,1)} %collective-permute-done.23.refs_1_.refs_2_.left_ref.right_ref, ...), custom_call_target="tpu_custom_call" | custom-call | flops 30000001024 | bytes 8388608 | tf_op jit(solution)/shard_map/spatial_backward/pallas_call | solution.py:589
  303.1 1.6 copy-done.4
  307.7 2.3 fusion.4
  310.5 26.5 %spatial_backward.3 = (bf16[2,768,768]{2,1,0:T(8,128)(2,1)}, bf16[832,768]{1,0:T(8,128)(2,1)}, f32[2,768]{1,0:T(2,128)}) custom-call(bf16[832,768]{1,0:T(8,128)(2,1)} %get-tuple-element.415.normed_ref.refs_0_, bf16[832,768]{1,0:T(8,128)(2,1)} %get-tuple-element.416.grad_ref.refs_1_, bf16[2,8,96,768]{3,2,1,0:T(8,128)(2,1)} %copy-done.3, ...), custom_call_target="tpu_custom_call" | custom-call | flops 30000001024 | bytes 8388608 | tf_op jit(solution)/shard_map/spatial_backward/pallas_call | solution.py:665
  337.1 3.3 fusion.85
  346.8 1.6 fusion.44
  350.6 2.3 collective-permute-done.48
  352.9 5.0 %collective-permute-done.49 = bf16[208,768]{1,0:T(8,128)(2,1)} collective-permute-done((bf16[208,768]{1,0:T(8,128)(2,1)}, bf16[208,768]{1,0:T(8,128)(2,1)}, u32[]{:S(2)}, u32[]{:S(2)}) %collective-permute-start.49) | collective-permute-done | bytes 319520 | tf_op jit(solution)/shard_map/ppermute | solution.py:896
  357.9 2.4 pad_maximum_fusion.6.grad_ref.drows_ref
  360.3 14.1 %temporal_backward.2 = (bf16[2,768,768]{2,1,0:T(8,128)(2,1)}, f32[832,768]{1,0:T(8,128)}) custom-call(bf16[832,768]{1,0:T(8,128)(2,1)} %get-tuple-element.447.normed_ref, bf16[832,768]{1,0:T(8,128)(2,1)} %pad_maximum_fusion.6.grad_ref.drows_ref, bf16[2,8,128,384]{3,2,1,0:T(8,128)(2,1)} %collective-permute-done.12.other_left.left_ref, ...), custom_call_target="tpu_custom_call" | custom-call | flops 14000000000 | bytes 8388608 | tf_op jit(solution)/shard_map/temporal_backward/pallas_call | solution.py:589
  376.4 2.0 collective-permute-start.55
  380.8 1.6 fusion.3
  382.4 1.6 collective-permute-start.52
  384.0 14.3 %temporal_backward.3 = (bf16[2,768,768]{2,1,0:T(8,128)(2,1)}, f32[832,768]{1,0:T(8,128)}) custom-call(bf16[832,768]{1,0:T(8,128)(2,1)} %get-tuple-element.447.normed_ref, bf16[832,768]{1,0:T(8,128)(2,1)} %pad_maximum_fusion.6.grad_ref.drows_ref, bf16[2,8,128,384]{3,2,1,0:T(8,128)(2,1)} %pad_maximum_fusion.1.own_left.left_ref, ...), custom_call_target="tpu_custom_call" | custom-call | flops 14000000000 | bytes 8388608 | tf_op jit(solution)/shard_map/temporal_backward/pallas_call | solution.py:589
  398.3 2.2 fusion.82
  404.8 8.3 %embed_backward.1 = bf16[768,896]{1,0:T(8,128)(2,1)} custom-call(bf16[832,768]{1,0:T(8,128)(2,1)} %pad_maximum_fusion.5.patches_ref, f32[832,768]{1,0:T(8,128)} %get-tuple-element.460.start_ref, f32[832,1]{1,0:T(8,128)} %copy.104.valid_ref, bf16[832,768]{1,0:T(8,128)(2,1)} %pad_maximum_fusion.6.grad_ref.drows_ref, f32[832,768]{1,0:T(8,128)} %get-tuple-element.462.da_ref, ...), custom_call_target="tpu_custom_call" | custom-call | flops 30000001024 | bytes 8388608 | tf_op jit(solution)/shard_map/embed_backward/pallas_call | solution.py:589
  415.3 2.3 fusion.38
  418.9 1.8 collective-permute-start.63
  423.7 2.5 fusion.31
  426.4 1.6 collective-permute-start.59
  431.3 4.5 collective-permute-done.59
  437.8 6.6 %collective-permute-done.61 = bf16[8,24,896]{2,1,0:T(8,128)(2,1)S(1)} collective-permute-done((bf16[8,24,896]{2,1,0:T(8,128)(2,1)S(1)}, bf16[8,24,896]{2,1,0:T(8,128)(2,1)S(1)}, u32[]{:S(2)}, u32[]{:S(2)}) %collective-permute-start.61) | collective-permute-done | bytes 344096 | tf_op jit(solution)/shard_map/ppermute | solution.py:896
  447.7 1.9 collective-permute-start.66
  449.6 2.4 collective-permute-start.67
  452.5 2.0 fusion.36.refs_0_
  454.5 2.1 finish.1
  458.0 3.6 collective-permute-done.66
  461.6 2.3 collective-permute-start.69
  464.7 1.6 collective-permute-start.71
  474.4 2.9 collective-permute-start.73
  478.6 1.9 collective-permute-start.74
  480.5 1.8 collective-permute-done.74
  484.4 2.2 collective-permute-done.75
  487.2 1.7 collective-permute-start.76
  488.8 3.0 collective-permute-done.76
  492.3 5.7 %optimizer.1 = (f32[1,1]{1,0:T(1,128)}, f32[24,768]{1,0:T(8,128)}, f32[24,768]{1,0:T(8,128)}, f32[24,768]{1,0:T(8,128)}, f32[8,24]{1,0:T(8,128)}, /*index=5*/f32...) custom-call(f32[1,1]{1,0:T(1,128)S(6)} %add.1307.total_ref, ...), custom_call_target="tpu_custom_call" | custom-call | tf_op jit(solution)/shard_map/optimizer/pallas_call | solution.py:829
  (404 shorter events, 139.1 us)
Async XLA Ops:
  5.7 14.9 %collective-permute-start = (bf16[1,128,768]{2,1,0:T(8,128)(2,1)S(1)}, bf16[1,128,768]{2,1,0:T(8,128)(2,1)S(1)}, u32[]{:S(2)}, u32[]{:S(2)}) collective-permute-start(bf16[1,128,768]{2,1,0:T(8,128)(2,1)S(1)} %fusion.57), channel_id=1, source_target_pairs={{0,16},{1,17},{2,18},{3,19},{4,20},{5,21},{6,22},{7,23},{8,24},{9,... | collective-permute-start | bytes 589832 | tf_op jit(solution)/shard_map/ppermute | solution.py:896
  20.9 17.5 %collective-permute-start.1 = (bf16[2,128,768]{2,1,0:T(8,128)(2,1)S(1)}, bf16[2,128,768]{2,1,0:T(8,128)(2,1)S(1)}, u32[]{:S(2)}, u32[]{:S(2)}) collective-permute-start(bf16[2,128,768]{2,1,0:T(8,128)(2,1)S(1)} %maximum_bitcast_fusion.3), channel_id=1, source_target_pairs={{0,8},{1,9},{2,10},{3,11},{4,12},{5,13},{6,14},{7,15},{8,0},{9,1},... | collective-permute-start | bytes 1179656 | tf_op jit(solution)/shard_map/ppermute | solution.py:896
  23.1 10.4 %collective-permute-start.3 = (bf16[208,768]{1,0:T(8,128)(2,1)S(1)}, bf16[208,768]{1,0:T(8,128)(2,1)S(1)}, u32[]{:S(2)}, u32[]{:S(2)}) collective-permute-start(bf16[208,768]{1,0:T(8,128)(2,1)S(1)} %get-tuple-element.291), channel_id=1, source_target_pairs={{0,2},{1,3},{2,0},{3,1},{4,6},{5,7},{6,4},{7,5},{8,10},{9,11},{10,... | collective-permute-start | bytes 958472 | tf_op jit(solution)/shard_map/ppermute | solution.py:896
  24.6 13.8 %collective-permute-start.4 = (bf16[208,768]{1,0:T(8,128)(2,1)S(1)}, bf16[208,768]{1,0:T(8,128)(2,1)S(1)}, u32[]{:S(2)}, u32[]{:S(2)}) collective-permute-start(bf16[208,768]{1,0:T(8,128)(2,1)S(1)} %get-tuple-element.292), channel_id=1, source_target_pairs={{0,3},{1,2},{2,1},{3,0},{4,7},{5,6},{6,5},{7,4},{8,11},{9,10},{10,... | collective-permute-start | bytes 958472 | tf_op jit(solution)/shard_map/ppermute | solution.py:896
  38.7 11.9 %collective-permute-start.5 = (bf16[4,128,384]{2,1,0:T(8,128)(2,1)S(1)}, bf16[4,128,384]{2,1,0:T(8,128)(2,1)S(1)}, u32[]{:S(2)}, u32[]{:S(2)}) collective-permute-start(bf16[4,128,384]{2,1,0:T(8,128)(2,1)S(1)} %get-tuple-element.299), channel_id=1, source_target_pairs={{0,4},{1,5},{2,6},{3,7},{4,0},{5,1},{6,2},{7,3},{8,12},{9,13},{10,... | collective-permute-start | bytes 1179656 | tf_op jit(solution)/shard_map/ppermute | solution.py:896
  40.3 11.5 %collective-permute-start.6 = (bf16[4,128,384]{2,1,0:T(8,128)(2,1)S(1)}, bf16[4,128,384]{2,1,0:T(8,128)(2,1)S(1)}, u32[]{:S(2)}, u32[]{:S(2)}) collective-permute-start(bf16[4,128,384]{2,1,0:T(8,128)(2,1)S(1)} %get-tuple-element.300), channel_id=1, source_target_pairs={{0,2},{1,3},{2,0},{3,1},{4,6},{5,7},{6,4},{7,5},{8,10},{9,11},{10,... | collective-permute-start | bytes 1179656 | tf_op jit(solution)/shard_map/ppermute | solution.py:896
  43.1 33.2 %collective-permute-start.9 = (bf16[1,192,768]{2,1,0:T(8,128)(2,1)}, bf16[1,192,768]{2,1,0:T(8,128)(2,1)}, u32[]{:S(2)}, u32[]{:S(2)}) collective-permute-start(bf16[1,192,768]{2,1,0:T(8,128)(2,1)} %maximum_bitcast_fusion.5), channel_id=1, source_target_pairs={{0,8},{1,9},{2,10},{3,11},{4,12},{5,13},{6,14},{7,15},{8,0},{9,1},... | collective-permute-start | bytes 884744 | tf_op jit(solution)/shard_map/ppermute | solution.py:896
  43.5 32.8 %collective-permute-start.10 = (bf16[1,192,768]{2,1,0:T(8,128)(2,1)}, bf16[1,192,768]{2,1,0:T(8,128)(2,1)}, u32[]{:S(2)}, u32[]{:S(2)}) collective-permute-start(bf16[1,192,768]{2,1,0:T(8,128)(2,1)} %maximum_bitcast_fusion.5), channel_id=1, source_target_pairs={{0,16},{1,17},{2,18},{3,19},{4,20},{5,21},{6,22},{7,23},{8,24},{9,... | collective-permute-start | bytes 884744 | tf_op jit(solution)/shard_map/ppermute | solution.py:896
  44.3 31.9 %collective-permute-start.11 = (bf16[1,192,768]{2,1,0:T(8,128)(2,1)}, bf16[1,192,768]{2,1,0:T(8,128)(2,1)}, u32[]{:S(2)}, u32[]{:S(2)}) collective-permute-start(bf16[1,192,768]{2,1,0:T(8,128)(2,1)} %maximum_bitcast_fusion.5), channel_id=1, source_target_pairs={{0,24},{1,25},{2,26},{3,27},{4,28},{5,29},{6,30},{7,31},{8,16},{9,... | collective-permute-start | bytes 884744 | tf_op jit(solution)/shard_map/ppermute | solution.py:896
  52.3 19.3 %collective-permute-start.7 = (bf16[8,128,384]{2,1,0:T(8,128)(2,1)S(1)}, bf16[8,128,384]{2,1,0:T(8,128)(2,1)S(1)}, u32[]{:S(2)}, u32[]{:S(2)}) collective-permute-start(bf16[8,128,384]{2,1,0:T(8,128)(2,1)S(1)} %bitcast.484), channel_id=1, source_target_pairs={{0,2},{1,3},{2,0},{3,1},{4,6},{5,7},{6,4},{7,5},{8,10},{9,11},{10,... | collective-permute-start | bytes 2359304 | tf_op jit(solution)/shard_map/ppermute | solution.py:896
  53.8 19.0 %collective-permute-start.8 = (bf16[2,4,128,384]{3,2,1,0:T(8,128)(2,1)S(1)}, bf16[2,4,128,384]{3,2,1,0:T(8,128)(2,1)S(1)}, u32[]{:S(2)}, u32[]{:S(2)}) collective-permute-start(bf16[2,4,128,384]{3,2,1,0:T(8,128)(2,1)S(1)} %pad_maximum_fusion.14), channel_id=1, source_target_pairs={{0,4},{1,5},{2,6},{3,7},{4,0},{5,1},{6,2},{7,3},{8,12},{9,13},{10,... | collective-permute-start | bytes 2359304 | tf_op jit(solution)/shard_map/ppermute | solution.py:896
  79.6 5.9 %collective-permute-start.12 = (bf16[2,8,128,384]{3,2,1,0:T(8,128)(2,1)}, bf16[2,8,128,384]{3,2,1,0:T(8,128)(2,1)}, u32[]{:S(2)}, u32[]{:S(2)}) collective-permute-start(bf16[2,8,128,384]{3,2,1,0:T(8,128)(2,1)} %pad_maximum_fusion.1.own_left.left_ref), channel_id=1, source_target_pairs={{0,1},{1,0},{2,3},{3,2},{4,5},{5,4},{6,7},{7,6},{8,9},{9,8},{10,11... | collective-permute-start | bytes 4718600 | tf_op jit(solution)/shard_map/ppermute | solution.py:896
  79.6 5.9 %collective-permute-start.13 = (bf16[2,8,128,384]{3,2,1,0:T(8,128)(2,1)S(1)}, bf16[2,8,128,384]{3,2,1,0:T(8,128)(2,1)}, u32[]{:S(2)}, u32[]{:S(2)}) collective-permute-start(bf16[2,8,128,384]{3,2,1,0:T(8,128)(2,1)S(1)} %bitcast.465), channel_id=1, source_target_pairs={{0,1},{1,0},{2,3},{3,2},{4,5},{5,4},{6,7},{7,6},{8,9},{9,8},{10,11... | collective-permute-start | bytes 4718600 | tf_op jit(solution)/shard_map/ppermute | solution.py:896
  81.1 15.6 %collective-permute-start.14 = (bf16[4,192,384]{2,1,0:T(8,128)(2,1)}, bf16[4,192,384]{2,1,0:T(8,128)(2,1)}, u32[]{:S(2)}, u32[]{:S(2)}) collective-permute-start(bf16[4,192,384]{2,1,0:T(8,128)(2,1)} %get-tuple-element.335), channel_id=1, source_target_pairs={{0,4},{1,5},{2,6},{3,7},{4,0},{5,1},{6,2},{7,3},{8,12},{9,13},{10,... | collective-permute-start | bytes 1769480 | tf_op jit(solution)/shard_map/ppermute | solution.py:896
  81.6 15.3 %collective-permute-start.15 = (bf16[4,192,384]{2,1,0:T(8,128)(2,1)}, bf16[4,192,384]{2,1,0:T(8,128)(2,1)}, u32[]{:S(2)}, u32[]{:S(2)}) collective-permute-start(bf16[4,192,384]{2,1,0:T(8,128)(2,1)} %get-tuple-element.336), channel_id=1, source_target_pairs={{0,2},{1,3},{2,0},{3,1},{4,6},{5,7},{6,4},{7,5},{8,10},{9,11},{10,... | collective-permute-start | bytes 1769480 | tf_op jit(solution)/shard_map/ppermute | solution.py:896
  82.1 33.2 %collective-permute-start.18 = (bf16[1,128,768]{2,1,0:T(8,128)(2,1)}, bf16[1,128,768]{2,1,0:T(8,128)(2,1)}, u32[]{:S(2)}, u32[]{:S(2)}) collective-permute-start(bf16[1,128,768]{2,1,0:T(8,128)(2,1)} %maximum_bitcast_fusion.6), channel_id=1, source_target_pairs={{0,16},{1,17},{2,18},{3,19},{4,20},{5,21},{6,22},{7,23},{8,24},{9,... | collective-permute-start | bytes 589832 | tf_op jit(solution)/shard_map/ppermute | solution.py:896
  98.7 16.6 %collective-permute-start.16 = (bf16[8,96,384]{2,1,0:T(8,128)(2,1)S(1)}, bf16[8,96,384]{2,1,0:T(8,128)(2,1)S(1)}, u32[]{:S(2)}, u32[]{:S(2)}) collective-permute-start(bf16[8,96,384]{2,1,0:T(8,128)(2,1)S(1)} %slice.406), channel_id=1, source_target_pairs={{0,2},{1,3},{2,0},{3,1},{4,6},{5,7},{6,4},{7,5},{8,10},{9,11},{10,... | collective-permute-start | bytes 1769480 | tf_op jit(solution)/shard_map/ppermute | solution.py:896
  99.4 15.9 %collective-permute-start.17 = (bf16[2,4,96,384]{3,2,1,0:T(8,128)(2,1)S(1)}, bf16[2,4,96,384]{3,2,1,0:T(8,128)(2,1)S(1)}, u32[]{:S(2)}, u32[]{:S(2)}) collective-permute-start(bf16[2,4,96,384]{3,2,1,0:T(8,128)(2,1)S(1)} %get-tuple-element.616), channel_id=1, source_target_pairs={{0,4},{1,5},{2,6},{3,7},{4,0},{5,1},{6,2},{7,3},{8,12},{9,13},{10,... | collective-permute-start | bytes 1769480 | tf_op jit(solution)/shard_map/ppermute | solution.py:896
  113.2 53.6 %collective-permute-start.25 = (bf16[2,4,96,384]{3,2,1,0:T(8,128)(2,1)S(1)}, bf16[2,4,96,384]{3,2,1,0:T(8,128)(2,1)S(1)}, u32[]{:S(2)}, u32[]{:S(2)}) collective-permute-start(bf16[2,4,96,384]{3,2,1,0:T(8,128)(2,1)S(1)} %get-tuple-element.615), channel_id=1, source_target_pairs={{0,4},{1,5},{2,6},{3,7},{4,0},{5,1},{6,2},{7,3},{8,12},{9,13},{10,... | collective-permute-start | bytes 1769480 | tf_op jit(solution)/shard_map/ppermute | solution.py:896
  122.4 8.8 %collective-permute-start.19 = (bf16[208,768]{1,0:T(8,128)(2,1)S(1)}, bf16[208,768]{1,0:T(8,128)(2,1)}, u32[]{:S(2)}, u32[]{:S(2)}) collective-permute-start(bf16[208,768]{1,0:T(8,128)(2,1)S(1)} %pad_maximum_fusion.23), channel_id=1, source_target_pairs={{0,1},{1,0},{2,3},{3,2},{4,5},{5,4},{6,7},{7,6},{8,9},{9,8},{10,11... | collective-permute-start | bytes 958472 | tf_op jit(solution)/shard_map/ppermute | solution.py:896
  122.5 10.6 %collective-permute-start.20 = (bf16[208,768]{1,0:T(8,128)(2,1)}, bf16[208,768]{1,0:T(8,128)(2,1)}, u32[]{:S(2)}, u32[]{:S(2)}) collective-permute-start(bf16[208,768]{1,0:T(8,128)(2,1)} %pad_maximum_fusion.24), channel_id=1, source_target_pairs={{0,2},{1,3},{2,0},{3,1},{4,6},{5,7},{6,4},{7,5},{8,10},{9,11},{10,... | collective-permute-start | bytes 958472 | tf_op jit(solution)/shard_map/ppermute | solution.py:896
  124.0 15.2 %collective-permute-start.21 = (bf16[208,768]{1,0:T(8,128)(2,1)}, bf16[208,768]{1,0:T(8,128)(2,1)}, u32[]{:S(2)}, u32[]{:S(2)}) collective-permute-start(bf16[208,768]{1,0:T(8,128)(2,1)} %pad_maximum_fusion.25), channel_id=1, source_target_pairs={{0,3},{1,2},{2,1},{3,0},{4,7},{5,6},{6,5},{7,4},{8,11},{9,10},{10,... | collective-permute-start | bytes 958472 | tf_op jit(solution)/shard_map/ppermute | solution.py:896
  124.3 14.9 %collective-permute-start.22 = (bf16[2,128,768]{2,1,0:T(8,128)(2,1)}, bf16[2,128,768]{2,1,0:T(8,128)(2,1)}, u32[]{:S(2)}, u32[]{:S(2)}) collective-permute-start(bf16[2,128,768]{2,1,0:T(8,128)(2,1)} %maximum_bitcast_fusion.4), channel_id=1, source_target_pairs={{0,8},{1,9},{2,10},{3,11},{4,12},{5,13},{6,14},{7,15},{8,0},{9,1},... | collective-permute-start | bytes 1179656 | tf_op jit(solution)/shard_map/ppermute | solution.py:896
  131.3 35.6 %collective-permute-start.24 = (bf16[8,96,384]{2,1,0:T(8,128)(2,1)S(1)}, bf16[8,96,384]{2,1,0:T(8,128)(2,1)S(1)}, u32[]{:S(2)}, u32[]{:S(2)}) collective-permute-start(bf16[8,96,384]{2,1,0:T(8,128)(2,1)S(1)} %copy-done.32), channel_id=1, source_target_pairs={{0,2},{1,3},{2,0},{3,1},{4,6},{5,7},{6,4},{7,5},{8,10},{9,11},{10,... | collective-permute-start | bytes 1769480 | tf_op jit(solution)/shard_map/ppermute | solution.py:896
  140.4 26.5 %collective-permute-start.23 = (bf16[2,8,96,768]{3,2,1,0:T(8,128)(2,1)S(1)}, bf16[2,8,96,768]{3,2,1,0:T(8,128)(2,1)}, u32[]{:S(2)}, u32[]{:S(2)}) collective-permute-start(bf16[2,8,96,768]{3,2,1,0:T(8,128)(2,1)S(1)} %pad_maximum_fusion.left_ref.right_ref.refs_2_.refs_3_), channel_id=1, source_target_pairs={{0,1},{1,0},{2,3},{3,2},{4,5},{5,4},{6,7},{7,6},{8,9},{9,8},{10,11... | collective-permute-start | bytes 7077896 | tf_op jit(solution)/shard_map/ppermute | solution.py:896
  141.1 24.2 %collective-permute-start.27 = (bf16[4,128,384]{2,1,0:T(8,128)(2,1)S(1)}, bf16[4,128,384]{2,1,0:T(8,128)(2,1)S(1)}, u32[]{:S(2)}, u32[]{:S(2)}) collective-permute-start(bf16[4,128,384]{2,1,0:T(8,128)(2,1)S(1)} %get-tuple-element.636), channel_id=1, source_target_pairs={{0,2},{1,3},{2,0},{3,1},{4,6},{5,7},{6,4},{7,5},{8,10},{9,11},{10,... | collective-permute-start | bytes 1179656 | tf_op jit(solution)/shard_map/ppermute | solution.py:896
  142.7 22.7 %collective-permute-start.26 = (bf16[4,128,384]{2,1,0:T(8,128)(2,1)S(1)}, bf16[4,128,384]{2,1,0:T(8,128)(2,1)}, u32[]{:S(2)}, u32[]{:S(2)}) collective-permute-start(bf16[4,128,384]{2,1,0:T(8,128)(2,1)S(1)} %get-tuple-element.637), channel_id=1, source_target_pairs={{0,4},{1,5},{2,6},{3,7},{4,0},{5,1},{6,2},{7,3},{8,12},{9,13},{10,... | collective-permute-start | bytes 1179656 | tf_op jit(solution)/shard_map/ppermute | solution.py:896
  167.7 20.5 %collective-permute-start.28 = (bf16[8,128,384]{2,1,0:T(8,128)(2,1)S(1)}, bf16[8,128,384]{2,1,0:T(8,128)(2,1)S(1)}, u32[]{:S(2)}, u32[]{:S(2)}) collective-permute-start(bf16[8,128,384]{2,1,0:T(8,128)(2,1)S(1)} %bitcast.482), channel_id=1, source_target_pairs={{0,2},{1,3},{2,0},{3,1},{4,6},{5,7},{6,4},{7,5},{8,10},{9,11},{10,... | collective-permute-start | bytes 2359304 | tf_op jit(solution)/shard_map/ppermute | solution.py:896
  168.2 19.4 %collective-permute-start.29 = (bf16[2,4,128,384]{3,2,1,0:T(8,128)(2,1)S(1)}, bf16[2,4,128,384]{3,2,1,0:T(8,128)(2,1)S(1)}, u32[]{:S(2)}, u32[]{:S(2)}) collective-permute-start(bf16[2,4,128,384]{3,2,1,0:T(8,128)(2,1)S(1)} %pad_maximum_fusion.19), channel_id=1, source_target_pairs={{0,4},{1,5},{2,6},{3,7},{4,0},{5,1},{6,2},{7,3},{8,12},{9,13},{10,... | collective-permute-start | bytes 2359304 | tf_op jit(solution)/shard_map/ppermute | solution.py:896
  169.0 19.5 %collective-permute-start.30 = (bf16[2,8,96,384]{3,2,1,0:T(8,128)(2,1)S(1)}, bf16[2,8,96,384]{3,2,1,0:T(8,128)(2,1)}, u32[]{:S(2)}, u32[]{:S(2)}) collective-permute-start(bf16[2,8,96,384]{3,2,1,0:T(8,128)(2,1)S(1)} %pad_maximum_fusion.10.refs_0_.refs_2_), channel_id=1, source_target_pairs={{0,1},{1,0},{2,3},{3,2},{4,5},{5,4},{6,7},{7,6},{8,9},{9,8},{10,11... | collective-permute-start | bytes 3538952 | tf_op jit(solution)/shard_map/ppermute | solution.py:896
  170.3 18.2 %collective-permute-start.31 = (bf16[2,8,96,384]{3,2,1,0:T(8,128)(2,1)S(1)}, bf16[2,8,96,384]{3,2,1,0:T(8,128)(2,1)S(1)}, u32[]{:S(2)}, u32[]{:S(2)}) collective-permute-start(bf16[2,8,96,384]{3,2,1,0:T(8,128)(2,1)S(1)} %bitcast.529), channel_id=1, source_target_pairs={{0,1},{1,0},{2,3},{3,2},{4,5},{5,4},{6,7},{7,6},{8,9},{9,8},{10,11... | collective-permute-start | bytes 3538952 | tf_op jit(solution)/shard_map/ppermute | solution.py:896
  188.5 12.2 %collective-permute-start.32 = (bf16[2,8,128,384]{3,2,1,0:T(8,128)(2,1)S(1)}, bf16[2,8,128,384]{3,2,1,0:T(8,128)(2,1)}, u32[]{:S(2)}, u32[]{:S(2)}) collective-permute-start(bf16[2,8,128,384]{3,2,1,0:T(8,128)(2,1)S(1)} %pad_maximum_fusion.3.refs_2_.refs_4_), channel_id=1, source_target_pairs={{0,1},{1,0},{2,3},{3,2},{4,5},{5,4},{6,7},{7,6},{8,9},{9,8},{10,11... | collective-permute-start | bytes 4718600 | tf_op jit(solution)/shard_map/ppermute | solution.py:896
  189.1 11.7 %collective-permute-start.33 = (bf16[2,8,128,384]{3,2,1,0:T(8,128)(2,1)S(1)}, bf16[2,8,128,384]{3,2,1,0:T(8,128)(2,1)}, u32[]{:S(2)}, u32[]{:S(2)}) collective-permute-start(bf16[2,8,128,384]{3,2,1,0:T(8,128)(2,1)S(1)} %bitcast.511), channel_id=1, source_target_pairs={{0,1},{1,0},{2,3},{3,2},{4,5},{5,4},{6,7},{7,6},{8,9},{9,8},{10,11... | collective-permute-start | bytes 4718600 | tf_op jit(solution)/shard_map/ppermute | solution.py:896
  250.8 19.2 %collective-permute-start.40 = (bf16[2,768,768]{2,1,0:T(8,128)(2,1)}, bf16[2,768,768]{2,1,0:T(8,128)(2,1)S(1)}, u32[]{:S(2)}, u32[]{:S(2)}) collective-permute-start(bf16[2,768,768]{2,1,0:T(8,128)(2,1)} %get-tuple-element.401), channel_id=1, source_target_pairs={{0,1},{1,0},{2,3},{3,2},{4,5},{5,4},{6,7},{7,6},{8,9},{9,8},{10,11... | collective-permute-start | bytes 7077896 | tf_op jit(solution)/shard_map/ppermute | solution.py:896
  250.9 19.1 %collective-permute-start.41 = (bf16[2,768,768]{2,1,0:T(8,128)(2,1)}, bf16[2,768,768]{2,1,0:T(8,128)(2,1)}, u32[]{:S(2)}, u32[]{:S(2)}) collective-permute-start(bf16[2,768,768]{2,1,0:T(8,128)(2,1)} %get-tuple-element.402), channel_id=1, source_target_pairs={{0,1},{1,0},{2,3},{3,2},{4,5},{5,4},{6,7},{7,6},{8,9},{9,8},{10,11... | collective-permute-start | bytes 7077896 | tf_op jit(solution)/shard_map/ppermute | solution.py:896
  272.8 32.0 %collective-permute-start.42 = (bf16[8,96,768]{2,1,0:T(8,128)(2,1)}, bf16[8,96,768]{2,1,0:T(8,128)(2,1)}, u32[]{:S(2)}, u32[]{:S(2)}) collective-permute-start(bf16[8,96,768]{2,1,0:T(8,128)(2,1)} %fusion), channel_id=1, source_target_pairs={{0,2},{1,3},{2,0},{3,1},{4,6},{5,7},{6,4},{7,5},{8,10},{9,11},{10,... | collective-permute-start | bytes 3538952 | tf_op jit(solution)/shard_map/ppermute | solution.py:896
  276.9 28.0 %collective-permute-start.43 = (bf16[2,4,96,768]{3,2,1,0:T(8,128)(2,1)}, bf16[2,4,96,768]{3,2,1,0:T(8,128)(2,1)}, u32[]{:S(2)}, u32[]{:S(2)}) collective-permute-start(bf16[2,4,96,768]{3,2,1,0:T(8,128)(2,1)} %fusion.1), channel_id=1, source_target_pairs={{0,4},{1,5},{2,6},{3,7},{4,0},{5,1},{6,2},{7,3},{8,12},{9,13},{10,... | collective-permute-start | bytes 3538952 | tf_op jit(solution)/shard_map/ppermute | solution.py:896
  306.2 30.8 %collective-permute-start.44 = (bf16[4,96,768]{2,1,0:T(8,128)(2,1)S(1)}, bf16[4,96,768]{2,1,0:T(8,128)(2,1)S(1)}, u32[]{:S(2)}, u32[]{:S(2)}) collective-permute-start(bf16[4,96,768]{2,1,0:T(8,128)(2,1)S(1)} %fusion.5), channel_id=1, source_target_pairs={{0,4},{1,5},{2,6},{3,7},{4,0},{5,1},{6,2},{7,3},{8,12},{9,13},{10,... | collective-permute-start | bytes 1769480 | tf_op jit(solution)/shard_map/ppermute | solution.py:896
  310.0 27.0 %collective-permute-start.45 = (bf16[4,96,768]{2,1,0:T(8,128)(2,1)}, bf16[4,96,768]{2,1,0:T(8,128)(2,1)}, u32[]{:S(2)}, u32[]{:S(2)}) collective-permute-start(bf16[4,96,768]{2,1,0:T(8,128)(2,1)} %fusion.4), channel_id=1, source_target_pairs={{0,2},{1,3},{2,0},{3,1},{4,6},{5,7},{6,4},{7,5},{8,10},{9,11},{10,... | collective-permute-start | bytes 1769480 | tf_op jit(solution)/shard_map/ppermute | solution.py:896
  310.5 26.5 %collective-permute-start.46 = (bf16[2,768,768]{2,1,0:T(8,128)(2,1)}, bf16[2,768,768]{2,1,0:T(8,128)(2,1)S(1)}, u32[]{:S(2)}, u32[]{:S(2)}) collective-permute-start(bf16[2,768,768]{2,1,0:T(8,128)(2,1)} %get-tuple-element.426), channel_id=1, source_target_pairs={{0,1},{1,0},{2,3},{3,2},{4,5},{5,4},{6,7},{7,6},{8,9},{9,8},{10,11... | collective-permute-start | bytes 7077896 | tf_op jit(solution)/shard_map/ppermute | solution.py:896
  341.7 8.9 %collective-permute-start.47 = (bf16[208,768]{1,0:T(8,128)(2,1)}, bf16[208,768]{1,0:T(8,128)(2,1)}, u32[]{:S(2)}, u32[]{:S(2)}) collective-permute-start(bf16[208,768]{1,0:T(8,128)(2,1)} %get-tuple-element.433), channel_id=1, source_target_pairs={{0,1},{1,0},{2,3},{3,2},{4,5},{5,4},{6,7},{7,6},{8,9},{9,8},{10,11... | collective-permute-start | bytes 958472 | tf_op jit(solution)/shard_map/ppermute | solution.py:896
  342.2 10.7 %collective-permute-start.48 = (bf16[208,768]{1,0:T(8,128)(2,1)}, bf16[208,768]{1,0:T(8,128)(2,1)}, u32[]{:S(2)}, u32[]{:S(2)}) collective-permute-start(bf16[208,768]{1,0:T(8,128)(2,1)} %get-tuple-element.434), channel_id=1, source_target_pairs={{0,2},{1,3},{2,0},{3,1},{4,6},{5,7},{6,4},{7,5},{8,10},{9,11},{10,... | collective-permute-start | bytes 958472 | tf_op jit(solution)/shard_map/ppermute | solution.py:896
  343.7 14.2 %collective-permute-start.49 = (bf16[208,768]{1,0:T(8,128)(2,1)}, bf16[208,768]{1,0:T(8,128)(2,1)}, u32[]{:S(2)}, u32[]{:S(2)}) collective-permute-start(bf16[208,768]{1,0:T(8,128)(2,1)} %get-tuple-element.435), channel_id=1, source_target_pairs={{0,3},{1,2},{2,1},{3,0},{4,7},{5,6},{6,5},{7,4},{8,11},{9,10},{10,... | collective-permute-start | bytes 958472 | tf_op jit(solution)/shard_map/ppermute | solution.py:896
  345.0 29.4 %collective-permute-start.50 = (bf16[2,4,96,768]{3,2,1,0:T(8,128)(2,1)S(1)}, bf16[2,4,96,768]{3,2,1,0:T(8,128)(2,1)S(1)}, u32[]{:S(2)}, u32[]{:S(2)}) collective-permute-start(bf16[2,4,96,768]{3,2,1,0:T(8,128)(2,1)S(1)} %copy-done.25), channel_id=1, source_target_pairs={{0,4},{1,5},{2,6},{3,7},{4,0},{5,1},{6,2},{7,3},{8,12},{9,13},{10,... | collective-permute-start | bytes 3538952 | tf_op jit(solution)/shard_map/ppermute | solution.py:896
  375.4 22.9 %collective-permute-start.51 = (bf16[2,768,768]{2,1,0:T(8,128)(2,1)}, bf16[2,768,768]{2,1,0:T(8,128)(2,1)}, u32[]{:S(2)}, u32[]{:S(2)}) collective-permute-start(bf16[2,768,768]{2,1,0:T(8,128)(2,1)} %get-tuple-element.450), channel_id=1, source_target_pairs={{0,1},{1,0},{2,3},{3,2},{4,5},{5,4},{6,7},{7,6},{8,9},{9,8},{10,11... | collective-permute-start | bytes 7077896 | tf_op jit(solution)/shard_map/ppermute | solution.py:896
  376.4 41.3 %collective-permute-start.55 = (bf16[1,192,768]{2,1,0:T(8,128)(2,1)}, bf16[1,192,768]{2,1,0:T(8,128)(2,1)S(1)}, u32[]{:S(2)}, u32[]{:S(2)}) collective-permute-start(bf16[1,192,768]{2,1,0:T(8,128)(2,1)} %pad_maximum_fusion.27), channel_id=1, source_target_pairs={{0,8},{1,9},{2,10},{3,11},{4,12},{5,13},{6,14},{7,15},{8,0},{9,1},... | collective-permute-start | bytes 884744 | tf_op jit(solution)/shard_map/ppermute | solution.py:896
  378.4 40.5 %collective-permute-start.56 = (bf16[1,192,768]{2,1,0:T(8,128)(2,1)}, bf16[1,192,768]{2,1,0:T(8,128)(2,1)}, u32[]{:S(2)}, u32[]{:S(2)}) collective-permute-start(bf16[1,192,768]{2,1,0:T(8,128)(2,1)} %pad_maximum_fusion.28), channel_id=1, source_target_pairs={{0,16},{1,17},{2,18},{3,19},{4,20},{5,21},{6,22},{7,23},{8,24},{9,... | collective-permute-start | bytes 884744 | tf_op jit(solution)/shard_map/ppermute | solution.py:896
  379.3 41.4 %collective-permute-start.57 = (bf16[1,192,768]{2,1,0:T(8,128)(2,1)}, bf16[1,192,768]{2,1,0:T(8,128)(2,1)}, u32[]{:S(2)}, u32[]{:S(2)}) collective-permute-start(bf16[1,192,768]{2,1,0:T(8,128)(2,1)} %pad_maximum_fusion.29), channel_id=1, source_target_pairs={{0,24},{1,25},{2,26},{3,27},{4,28},{5,29},{6,30},{7,31},{8,16},{9,... | collective-permute-start | bytes 884744 | tf_op jit(solution)/shard_map/ppermute | solution.py:896
  382.4 15.9 %collective-permute-start.52 = (bf16[4,96,768]{2,1,0:T(8,128)(2,1)S(1)}, bf16[4,96,768]{2,1,0:T(8,128)(2,1)S(1)}, u32[]{:S(2)}, u32[]{:S(2)}) collective-permute-start(bf16[4,96,768]{2,1,0:T(8,128)(2,1)S(1)} %fusion.3), channel_id=1, source_target_pairs={{0,2},{1,3},{2,0},{3,1},{4,6},{5,7},{6,4},{7,5},{8,10},{9,11},{10,... | collective-permute-start | bytes 1769480 | tf_op jit(solution)/shard_map/ppermute | solution.py:896
  403.2 17.5 %collective-permute-start.53 = (bf16[8,96,384]{2,1,0:T(8,128)(2,1)}, bf16[8,96,384]{2,1,0:T(8,128)(2,1)}, u32[]{:S(2)}, u32[]{:S(2)}) collective-permute-start(bf16[8,96,384]{2,1,0:T(8,128)(2,1)} %fusion.6), channel_id=1, source_target_pairs={{0,2},{1,3},{2,0},{3,1},{4,6},{5,7},{6,4},{7,5},{8,10},{9,11},{10,... | collective-permute-start | bytes 1769480 | tf_op jit(solution)/shard_map/ppermute | solution.py:896
  403.7 17.0 %collective-permute-start.54 = (bf16[2,4,96,384]{3,2,1,0:T(8,128)(2,1)}, bf16[2,4,96,384]{3,2,1,0:T(8,128)(2,1)}, u32[]{:S(2)}, u32[]{:S(2)}) collective-permute-start(bf16[2,4,96,384]{3,2,1,0:T(8,128)(2,1)} %fusion.7), channel_id=1, source_target_pairs={{0,4},{1,5},{2,6},{3,7},{4,0},{5,1},{6,2},{7,3},{8,12},{9,13},{10,... | collective-permute-start | bytes 1769480 | tf_op jit(solution)/shard_map/ppermute | solution.py:896
  417.7 29.0 %collective-permute-start.62 = (bf16[1,96,768]{2,1,0:T(8,128)(2,1)}, bf16[1,96,768]{2,1,0:T(8,128)(2,1)S(1)}, u32[]{:S(2)}, u32[]{:S(2)}) collective-permute-start(bf16[1,96,768]{2,1,0:T(8,128)(2,1)} %get-tuple-element.542), channel_id=1, source_target_pairs={{0,8},{1,9},{2,10},{3,11},{4,12},{5,13},{6,14},{7,15},{8,0},{9,1},... | collective-permute-start | bytes 442376 | tf_op jit(solution)/shard_map/ppermute | solution.py:896
  418.9 27.8 %collective-permute-start.63 = (bf16[1,96,768]{2,1,0:T(8,128)(2,1)}, bf16[1,96,768]{2,1,0:T(8,128)(2,1)}, u32[]{:S(2)}, u32[]{:S(2)}) collective-permute-start(bf16[1,96,768]{2,1,0:T(8,128)(2,1)} %get-tuple-element.541), channel_id=1, source_target_pairs={{0,16},{1,17},{2,18},{3,19},{4,20},{5,21},{6,22},{7,23},{8,24},{9,... | collective-permute-start | bytes 442376 | tf_op jit(solution)/shard_map/ppermute | solution.py:896
  420.7 5.5 %collective-permute-start.58 = (bf16[16,24,896]{2,1,0:T(8,128)(2,1)S(1)}, bf16[16,24,896]{2,1,0:T(8,128)(2,1)S(1)}, u32[]{:S(2)}, u32[]{:S(2)}) collective-permute-start(bf16[16,24,896]{2,1,0:T(8,128)(2,1)S(1)} %get-tuple-element.473), channel_id=1, source_target_pairs={{0,1},{1,0},{2,3},{3,2},{4,5},{5,4},{6,7},{7,6},{8,9},{9,8},{10,11... | collective-permute-start | bytes 2064392 | tf_op jit(solution)/shard_map/ppermute | solution.py:896
  426.4 9.5 %collective-permute-start.59 = (bf16[4,96,384]{2,1,0:T(8,128)(2,1)S(1)}, bf16[4,96,384]{2,1,0:T(8,128)(2,1)S(1)}, u32[]{:S(2)}, u32[]{:S(2)}) collective-permute-start(bf16[4,96,384]{2,1,0:T(8,128)(2,1)S(1)} %fusion.15), channel_id=1, source_target_pairs={{0,4},{1,5},{2,6},{3,7},{4,0},{5,1},{6,2},{7,3},{8,12},{9,13},{10,... | collective-permute-start | bytes 884744 | tf_op jit(solution)/shard_map/ppermute | solution.py:896
  427.9 9.8 %collective-permute-start.60 = (bf16[4,96,384]{2,1,0:T(8,128)(2,1)S(1)}, bf16[4,96,384]{2,1,0:T(8,128)(2,1)S(1)}, u32[]{:S(2)}, u32[]{:S(2)}) collective-permute-start(bf16[4,96,384]{2,1,0:T(8,128)(2,1)S(1)} %fusion.10), channel_id=1, source_target_pairs={{0,2},{1,3},{2,0},{3,1},{4,6},{5,7},{6,4},{7,5},{8,10},{9,11},{10,... | collective-permute-start | bytes 884744 | tf_op jit(solution)/shard_map/ppermute | solution.py:896
  429.5 15.0 %collective-permute-start.61 = (bf16[8,24,896]{2,1,0:T(8,128)(2,1)S(1)}, bf16[8,24,896]{2,1,0:T(8,128)(2,1)S(1)}, u32[]{:S(2)}, u32[]{:S(2)}) collective-permute-start(bf16[8,24,896]{2,1,0:T(8,128)(2,1)S(1)} %fusion.14), channel_id=1, source_target_pairs={{0,2},{1,3},{2,0},{3,1},{4,6},{5,7},{6,4},{7,5},{8,10},{9,11},{10,... | collective-permute-start | bytes 1032200 | tf_op jit(solution)/shard_map/ppermute | solution.py:896
  435.8 10.9 %collective-permute-start.64 = (bf16[1,96,768]{2,1,0:T(8,128)(2,1)S(1)}, bf16[1,96,768]{2,1,0:T(8,128)(2,1)S(1)}, u32[]{:S(2)}, u32[]{:S(2)}) collective-permute-start(bf16[1,96,768]{2,1,0:T(8,128)(2,1)S(1)} %copy-done.48), channel_id=1, source_target_pairs={{0,24},{1,25},{2,26},{3,27},{4,28},{5,29},{6,30},{7,31},{8,16},{9,... | collective-permute-start | bytes 442376 | tf_op jit(solution)/shard_map/ppermute | solution.py:896
  447.5 10.5 %collective-permute-start.65 = (bf16[1,96,768]{2,1,0:T(8,128)(2,1)}, bf16[1,96,768]{2,1,0:T(8,128)(2,1)S(1)}, u32[]{:S(2)}, u32[]{:S(2)}) collective-permute-start(bf16[1,96,768]{2,1,0:T(8,128)(2,1)} %get-tuple-element.494), channel_id=1, source_target_pairs={{0,8},{1,9},{2,10},{3,11},{4,12},{5,13},{6,14},{7,15},{8,0},{9,1},... | collective-permute-start | bytes 442376 | tf_op jit(solution)/shard_map/ppermute | solution.py:896
  447.7 13.9 %collective-permute-start.66 = (bf16[1,96,768]{2,1,0:T(8,128)(2,1)S(1)}, bf16[1,96,768]{2,1,0:T(8,128)(2,1)S(1)}, u32[]{:S(2)}, u32[]{:S(2)}) collective-permute-start(bf16[1,96,768]{2,1,0:T(8,128)(2,1)S(1)} %get-tuple-element.495), channel_id=1, source_target_pairs={{0,16},{1,17},{2,18},{3,19},{4,20},{5,21},{6,22},{7,23},{8,24},{9,... | collective-permute-start | bytes 442376 | tf_op jit(solution)/shard_map/ppermute | solution.py:896
  449.6 11.9 %collective-permute-start.67 = (bf16[1,96,768]{2,1,0:T(8,128)(2,1)S(1)}, bf16[1,96,768]{2,1,0:T(8,128)(2,1)S(1)}, u32[]{:S(2)}, u32[]{:S(2)}) collective-permute-start(bf16[1,96,768]{2,1,0:T(8,128)(2,1)S(1)} %get-tuple-element.496), channel_id=1, source_target_pairs={{0,24},{1,25},{2,26},{3,27},{4,28},{5,29},{6,30},{7,31},{8,16},{9,... | collective-permute-start | bytes 442376 | tf_op jit(solution)/shard_map/ppermute | solution.py:896
  452.0 9.6 %collective-permute-start.68 = (bf16[4,24,896]{2,1,0:T(8,128)(2,1)S(1)}, bf16[4,24,896]{2,1,0:T(8,128)(2,1)S(1)}, u32[]{:S(2)}, u32[]{:S(2)}) collective-permute-start(bf16[4,24,896]{2,1,0:T(8,128)(2,1)S(1)} %fusion.58), channel_id=1, source_target_pairs={{0,4},{1,5},{2,6},{3,7},{4,0},{5,1},{6,2},{7,3},{8,12},{9,13},{10,... | collective-permute-start | bytes 516104 | tf_op jit(solution)/shard_map/ppermute | solution.py:896
  461.6 6.8 %collective-permute-start.69 = (bf16[1,24,896]{2,1,0:T(8,128)(2,1)S(1)}, bf16[1,24,896]{2,1,0:T(8,128)(2,1)S(1)}, u32[]{:S(2)}, u32[]{:S(2)}) collective-permute-start(bf16[1,24,896]{2,1,0:T(8,128)(2,1)S(1)} %get-tuple-element.502), channel_id=1, source_target_pairs={{0,8},{1,9},{2,10},{3,11},{4,12},{5,13},{6,14},{7,15},{8,0},{9,1},... | collective-permute-start | bytes 129032 | tf_op jit(solution)/shard_map/ppermute | solution.py:896
  464.7 5.9 %collective-permute-start.71 = (bf16[1,24,896]{2,1,0:T(8,128)(2,1)S(1)}, bf16[1,24,896]{2,1,0:T(8,128)(2,1)S(1)}, u32[]{:S(2)}, u32[]{:S(2)}) collective-permute-start(bf16[1,24,896]{2,1,0:T(8,128)(2,1)S(1)} %get-tuple-element.504), channel_id=1, source_target_pairs={{0,24},{1,25},{2,26},{3,27},{4,28},{5,29},{6,30},{7,31},{8,16},{9,... | collective-permute-start | bytes 129032 | tf_op jit(solution)/shard_map/ppermute | solution.py:896
  (75 other events, 280.6 us)
